TPU v7x, 128 devices: a whole 4x4x4 slice. The times are simulated.
128 devices in a mesh: fsdp: 32 (over y, z_lo, x), ctx: 2 (over core), tp: 2 (over z_hi).
Axes of the slice: x: 4, y: 4, z: 4 (z_hi: 2, z_lo: 2; z = z_hi * 2 + z_lo), core: 2. Of those that a mesh axis runs over, the one named last changes fastest.
Arguments:
- tokens: bfloat16 [8192, 768], P(('fsdp', 'ctx')), may hold values from -6 to 6
- cotangent: bfloat16 [8192, 768], P(('fsdp', 'ctx')), may hold values from -16 to 16
- doc_lens: int32 [32, 4], P('fsdp'), may hold values from 1 to 192, as said below
- block_pos: int32 [32, 4], P('fsdp'), may hold values from 0 to 3, each once within a row
- w_qkv: bfloat16 [2, 768, 2304], P(None, 'fsdp', 'tp'), may hold values from -0.21875 to 0.21875
- w_out: bfloat16 [2, 768, 768], P(None, 'tp', 'fsdp'), may hold values from -1.75 to 1.75
- w_up: bfloat16 [2, 768, 3072], P(None, 'fsdp', 'tp'), may hold values from -0.21875 to 0.21875
- w_down: bfloat16 [2, 3072, 768], P(None, 'tp', 'fsdp'), may hold values from -0.109375 to 0.109375
- b_qkv: bfloat16 [2, 2304], P(None, ('tp', 'fsdp')), may hold values from -1.796875 to 1.796875
- b_up: bfloat16 [2, 3072], P(None, ('tp', 'fsdp')), may hold values from -1.796875 to 1.796875
- out_bias: bfloat16 [2, 2, 768], P(None, None, 'fsdp'), may hold values from -1.796875 to 1.796875
- norm_gain: bfloat16 [2, 2, 768], P(None, None, 'fsdp'), may hold values from 0.25 to 1.75
- norm_bias: bfloat16 [2, 2, 768], P(None, None, 'fsdp'), may hold values from -1.796875 to 1.796875
Outputs:
- output: bfloat16 [8192, 768], P(('fsdp', 'ctx'))
- grad_tokens: bfloat16 [8192, 768], P(('fsdp', 'ctx'))
- grad_w_qkv: float32 [2, 768, 2304], P(None, 'fsdp', 'tp')
- grad_w_out: float32 [2, 768, 768], P(None, 'tp', 'fsdp')
- grad_w_up: float32 [2, 768, 3072], P(None, 'fsdp', 'tp')
- grad_w_down: float32 [2, 3072, 768], P(None, 'tp', 'fsdp')
- grad_b_qkv: float32 [2, 2304], P(None, ('tp', 'fsdp'))
- grad_b_up: float32 [2, 3072], P(None, ('tp', 'fsdp'))
- grad_out_bias: float32 [2, 2, 768], P(None, None, 'fsdp')
- grad_norm_gain: float32 [2, 2, 768], P(None, None, 'fsdp')
- grad_norm_bias: float32 [2, 2, 768], P(None, None, 'fsdp')
Inputs may be any that keep to these rules, and one draw needn't show every extreme that they name: `doc_lens`: in each group's row one entry, at a place drawn from the seed, is exactly 192; every entry is at least 1, and the row sums to at most 256. `block_pos`: each group's row is a permutation of the 4 position blocks.
All inputs are finite; a program needn't handle non-finite values.
Results may differ from a plain program's by a relative error of at most 0.019.
Values may be sent and summed in bfloat16 or wider, within the bound.
No kernel may reach another device: no remote copies, remote signals or barrier semaphores. Data moves between devices by JAX's collectives and lax.ppermute only.
A program may use at most 192 MiB of HBM per device.

v0:
```python
import jax
import jax.numpy as jnp
from jax import lax
from jax.sharding import PartitionSpec as P

HS = 64
ROT = 16


EPSILON = 1e-05
MASKED = -1e30


def side_by_side(arrays, axis, dim, along):
    ends, at = ([], 0)
    for a in arrays[:-1]:
        at += a.shape[along]
        ends.append(at)
    both = jnp.concatenate(arrays, axis=along)
    return tuple(jnp.split(lax.all_gather(both, axis, axis=dim, tiled=True), ends, axis=along))


def from_everyone(array, axis):
    count = lax.axis_size(axis)
    return lax.all_to_all(
        jnp.broadcast_to(array[None], (count, *array.shape)), axis, 0, 0, tiled=True
    )


def of_everyone(array, axis):
    return from_everyone(array, axis).astype(jnp.float32).sum(axis=0)


def split_up(array, dim, count):
    shape = array.shape
    blocks = array.reshape(*shape[:dim], count, shape[dim] // count, *shape[dim + 1 :])
    return jnp.moveaxis(blocks, dim, 0)


def sent_and_summed(array, axis, dim):
    count = lax.axis_size(axis)
    blocks = lax.all_to_all(split_up(array, dim, count), axis, 0, 0, tiled=True)
    return jnp.sum(blocks.astype(jnp.float32), axis=0)


def in_one_piece(arrays, axis, dim, along):
    ends, at = ([], 0)
    for a in arrays[:-1]:
        at += a.shape[along]
        ends.append(at)
    both = jnp.concatenate(arrays, axis=along)
    return tuple(jnp.split(sent_and_summed(both, axis, dim), ends, axis=along))


def side_by_side_2(arrays, axis, dim, along):
    widths = [a.shape[along] for a in arrays]
    both = jnp.concatenate(arrays, axis=along)
    result = lax.psum_scatter(both, axis, scatter_dimension=dim, tiled=True)
    return tuple(jnp.split(result, [sum(widths[:k]) for k in range(1, len(widths))], axis=along))


def contract_rows(left, right):
    return lax.dot_general(
        left, right, (((0,), (0,)), ((), ())), preferred_element_type=jnp.float32
    )


def contract_cols(left, right):
    return lax.dot_general(
        left, right, (((1,), (1,)), ((), ())), preferred_element_type=jnp.float32
    )


def gelu_exact(values):
    return jax.nn.gelu(values, approximate=False)


def angles(positions):
    exponents = jnp.arange(ROT // 2, dtype=jnp.float32) * (2.0 / ROT)
    inverse = jnp.power(10000.0, -exponents)
    phase = positions.astype(jnp.float32)[:, None] * inverse[None, :]
    return (jnp.cos(phase), jnp.sin(phase))


def rotate(values, cos_table, sin_table):
    half_rot = ROT // 2
    first_half = values[..., :half_rot]
    second_half = values[..., half_rot:ROT]
    cos_wide = cos_table[:, None, :]
    sin_wide = sin_table[:, None, :]
    return jnp.concatenate(
        [
            first_half * cos_wide - second_half * sin_wide,
            second_half * cos_wide + first_half * sin_wide,
            values[..., ROT:],
        ],
        axis=-1,
    )


def normalize(values, gain_row, shift_row):
    row_mean = jnp.mean(values, axis=-1, keepdims=True)
    centered = values - row_mean
    inv_std = lax.rsqrt(jnp.mean(centered * centered, axis=-1, keepdims=True) + EPSILON)
    normed = centered * inv_std
    return (normed * gain_row + shift_row, normed, inv_std)


def norm_back(grad_out, normed, inv_std, gain_row):
    grad_hat = grad_out * gain_row
    grad_in = inv_std * (
        grad_hat
        - jnp.mean(grad_hat, axis=-1, keepdims=True)
        - normed * jnp.mean(grad_hat * normed, axis=-1, keepdims=True)
    )
    return (grad_in, jnp.sum(grad_out * normed, axis=0), jnp.sum(grad_out, axis=0))


def layer_forward(hidden, weights, allowed, cos_table, sin_table):
    w_qkv, w_out, w_up, w_down, b_qkv, b_up, b_out, norm_gain, norm_shift = weights
    row_count = hidden.shape[0]
    head_count = w_qkv.shape[1] // (3 * HS)
    gains = norm_gain.astype(jnp.float32)
    shifts = norm_shift.astype(jnp.float32)
    normed_a, hat_a, rstd_a = normalize(hidden, gains[0], shifts[0])
    attn_in = normed_a.astype(jnp.bfloat16)
    projected = jnp.dot(attn_in, w_qkv, preferred_element_type=jnp.float32) + b_qkv.astype(
        jnp.float32
    )
    projected = projected.reshape(row_count, head_count, 3, HS)
    queries = rotate(projected[:, :, 0], cos_table, sin_table).astype(jnp.bfloat16)
    key_part = (
        rotate(projected[:, :, 1], cos_table, sin_table)
        .astype(jnp.bfloat16)
        .reshape(row_count, head_count * HS)
    )
    value_part = projected[:, :, 2].astype(jnp.bfloat16).reshape(row_count, head_count * HS)
    keys_all, values_all = side_by_side((key_part, value_part), "ctx", 0, 1)
    keys_all = keys_all.reshape(-1, head_count, HS)
    values_all = values_all.reshape(-1, head_count, HS)
    scores = jnp.einsum(
        "qhd,khd->hqk", queries, keys_all, preferred_element_type=jnp.float32
    ) * HS ** (-0.5)
    scores = jnp.where(allowed[None], scores, MASKED)
    row_max = jnp.max(scores, axis=2, keepdims=True)
    exponent = jnp.exp(scores - row_max)
    denominator = jnp.sum(exponent, axis=2, keepdims=True)
    attention = (exponent / denominator).astype(jnp.bfloat16)
    log_total = row_max + jnp.log(denominator)
    attended = jnp.einsum("hqk,khd->qhd", attention, values_all, preferred_element_type=jnp.float32)
    attn_out = attended.astype(jnp.bfloat16).reshape(row_count, head_count * HS)
    normed_b, hat_b, rstd_b = normalize(hidden, gains[1], shifts[1])
    mlp_in = normed_b.astype(jnp.bfloat16)
    up_value = jnp.dot(mlp_in, w_up, preferred_element_type=jnp.float32) + b_up.astype(jnp.float32)
    activated = gelu_exact(up_value).astype(jnp.bfloat16)
    local_sum = jnp.dot(attn_out, w_out, preferred_element_type=jnp.float32) + jnp.dot(
        activated, w_down, preferred_element_type=jnp.float32
    )
    branch = of_everyone(local_sum.astype(jnp.bfloat16), "tp").astype(jnp.float32)
    biases = b_out.astype(jnp.float32)
    following = hidden + branch + biases[0] + biases[1]
    state = (
        hat_a,
        rstd_a,
        attn_in,
        hat_b,
        rstd_b,
        mlp_in,
        queries,
        keys_all,
        values_all,
        log_total,
        attn_out,
        up_value,
        activated,
    )
    return (following, state)


def layer_backward(grad_next, state, weights, allowed, cos_table, sin_table):
    w_qkv, w_out, w_up, w_down, b_qkv, b_up, b_out, norm_gain, norm_shift = weights
    (
        hat_a,
        rstd_a,
        attn_in,
        hat_b,
        rstd_b,
        mlp_in,
        queries,
        keys_all,
        values_all,
        log_total,
        attn_out,
        up_value,
        activated,
    ) = state
    row_count = grad_next.shape[0]
    head_count = queries.shape[1]
    scale_factor = HS ** (-0.5)
    low_grad = grad_next.astype(jnp.bfloat16)
    grad_w_out = contract_rows(attn_out, low_grad)
    grad_w_down = contract_rows(activated, low_grad)
    grad_attended = (
        contract_cols(low_grad, w_out).astype(jnp.bfloat16).reshape(row_count, head_count, HS)
    )
    grad_activated = contract_cols(low_grad, w_down)
    unused_value, gelu_back = jax.vjp(gelu_exact, up_value)
    low_grad_up = gelu_back(grad_activated)[0].astype(jnp.bfloat16)
    grad_w_up = contract_rows(mlp_in, low_grad_up)
    grad_b_up = jnp.sum(low_grad_up.astype(jnp.float32), axis=0)
    part_mlp = contract_cols(low_grad_up, w_up)
    scores = (
        jnp.einsum("qhd,khd->hqk", queries, keys_all, preferred_element_type=jnp.float32)
        * scale_factor
    )
    scores = jnp.where(allowed[None], scores, MASKED)
    attention = jnp.exp(scores - log_total)
    grad_attention = jnp.einsum(
        "qhd,khd->hqk", grad_attended, values_all, preferred_element_type=jnp.float32
    )
    grad_values = jnp.einsum(
        "hqk,qhd->khd",
        attention.astype(jnp.bfloat16),
        grad_attended,
        preferred_element_type=jnp.float32,
    )
    row_dot = jnp.sum(attention * grad_attention, axis=2, keepdims=True)
    low_scores = (attention * (grad_attention - row_dot)).astype(jnp.bfloat16)
    grad_queries = (
        jnp.einsum("hqk,khd->qhd", low_scores, keys_all, preferred_element_type=jnp.float32)
        * scale_factor
    )
    grad_keys = (
        jnp.einsum("hqk,qhd->khd", low_scores, queries, preferred_element_type=jnp.float32)
        * scale_factor
    )
    grad_keys, grad_values = in_one_piece(
        (
            grad_keys.reshape(-1, head_count * HS).astype(jnp.bfloat16),
            grad_values.reshape(-1, head_count * HS).astype(jnp.bfloat16),
        ),
        "ctx",
        0,
        1,
    )
    grad_queries = rotate(grad_queries, cos_table, -sin_table)
    grad_keys = rotate(grad_keys.reshape(row_count, head_count, HS), cos_table, -sin_table)
    grad_values = grad_values.reshape(row_count, head_count, HS)
    low_grad_qkv = (
        jnp.stack([grad_queries, grad_keys, grad_values], axis=2)
        .astype(jnp.bfloat16)
        .reshape(row_count, head_count * 3 * HS)
    )
    grad_w_qkv = contract_rows(attn_in, low_grad_qkv)
    grad_b_qkv = jnp.sum(low_grad_qkv.astype(jnp.float32), axis=0)
    part_attn = contract_cols(low_grad_qkv, w_qkv)
    grad_norm_a, grad_norm_b = (
        of_everyone(part_attn.astype(jnp.bfloat16), "tp").astype(jnp.float32),
        of_everyone(part_mlp.astype(jnp.bfloat16), "tp").astype(jnp.float32),
    )
    gains = norm_gain.astype(jnp.float32)
    back_a, gain_grad_a, shift_grad_a = norm_back(grad_norm_a, hat_a, rstd_a, gains[0])
    back_b, gain_grad_b, shift_grad_b = norm_back(grad_norm_b, hat_b, rstd_b, gains[1])
    grad_prev = grad_next + back_a + back_b
    bias_grad = jnp.sum(grad_next, axis=0)
    grads = (
        grad_w_qkv,
        grad_w_out,
        grad_w_up,
        grad_w_down,
        grad_b_qkv,
        grad_b_up,
        jnp.stack([bias_grad, bias_grad]),
        jnp.stack([gain_grad_a, gain_grad_b]),
        jnp.stack([shift_grad_a, shift_grad_b]),
    )
    return (grad_prev, grads)


def owners(grad_parts):
    (
        part_qkv,
        part_out,
        part_up,
        part_down,
        part_bqkv,
        part_bup,
        part_obias,
        part_gain,
        part_shift,
    ) = grad_parts
    shares = (
        lax.psum_scatter(part_qkv, ("fsdp", "ctx"), scatter_dimension=1, tiled=True),
        lax.psum_scatter(part_out, ("fsdp", "ctx"), scatter_dimension=2, tiled=True),
        lax.psum_scatter(part_up, ("fsdp", "ctx"), scatter_dimension=1, tiled=True),
        lax.psum_scatter(part_down, ("fsdp", "ctx"), scatter_dimension=2, tiled=True),
        lax.psum_scatter(part_bqkv, ("fsdp", "ctx"), scatter_dimension=1, tiled=True),
        lax.psum_scatter(part_bup, ("fsdp", "ctx"), scatter_dimension=1, tiled=True),
        *side_by_side_2((part_obias, part_gain, part_shift), ("fsdp", "ctx"), 2, 0),
    )
    (
        share_qkv,
        share_out,
        share_up,
        share_down,
        share_bqkv,
        share_bup,
        share_obias,
        share_gain,
        share_shift,
    ) = shares
    return (
        lax.all_gather(share_qkv.astype(jnp.bfloat16), "ctx", axis=1, tiled=True).astype(
            share_qkv.dtype
        ),
        lax.all_gather(share_out.astype(jnp.bfloat16), "ctx", axis=2, tiled=True).astype(
            share_out.dtype
        ),
        lax.all_gather(share_up.astype(jnp.bfloat16), "ctx", axis=1, tiled=True).astype(
            share_up.dtype
        ),
        lax.all_gather(share_down.astype(jnp.bfloat16), "ctx", axis=2, tiled=True).astype(
            share_down.dtype
        ),
        lax.all_gather(share_bqkv.astype(jnp.bfloat16), "ctx", axis=1, tiled=True).astype(
            share_bqkv.dtype
        ),
        lax.all_gather(share_bup.astype(jnp.bfloat16), "ctx", axis=1, tiled=True).astype(
            share_bup.dtype
        ),
        *tuple(
            (
                part.astype(jnp.float32)
                for part in side_by_side(
                    (
                        share_obias.astype(jnp.bfloat16),
                        share_gain.astype(jnp.bfloat16),
                        share_shift.astype(jnp.bfloat16),
                    ),
                    "ctx",
                    2,
                    0,
                )
            )
        ),
    )


def per_device(
    tokens,
    cotangent,
    doc_lens,
    block_pos,
    w_qkv,
    w_out,
    w_up,
    w_down,
    b_qkv,
    b_up,
    out_bias,
    norm_gain,
    norm_bias,
):
    row_count = tokens.shape[0]
    block_rows = row_count // 2
    ctx_index = lax.axis_index("ctx")
    offsets = jnp.arange(block_rows, dtype=jnp.int32)
    key_pos = (block_pos[0][:, None] * block_rows + offsets[None, :]).reshape(-1)
    query_pos = lax.dynamic_slice_in_dim(key_pos, ctx_index * row_count, row_count)
    doc_ends = jnp.cumsum(doc_lens[0])
    key_doc = jnp.sum((key_pos[:, None] >= doc_ends[None, :]).astype(jnp.int32), axis=1)
    query_doc = lax.dynamic_slice_in_dim(key_doc, ctx_index * row_count, row_count)
    allowed = (query_doc[:, None] == key_doc[None, :]) & (key_pos[None, :] <= query_pos[:, None])
    cos_table, sin_table = angles(query_pos)
    layer_count = w_qkv.shape[0]

    def fetch(layer_index):
        return (
            lax.all_gather(w_qkv[layer_index], "fsdp", axis=0, tiled=True),
            lax.all_gather(w_out[layer_index], "fsdp", axis=1, tiled=True),
            lax.all_gather(w_up[layer_index], "fsdp", axis=0, tiled=True),
            lax.all_gather(w_down[layer_index], "fsdp", axis=1, tiled=True),
            lax.all_gather(b_qkv[layer_index], "fsdp", axis=0, tiled=True),
            lax.all_gather(b_up[layer_index], "fsdp", axis=0, tiled=True),
            *side_by_side(
                (out_bias[layer_index], norm_gain[layer_index], norm_bias[layer_index]),
                "fsdp",
                1,
                0,
            ),
        )

    hidden = tokens.astype(jnp.float32)
    saved_states = []
    kept_weights = []
    for layer_index in range(layer_count):
        weights = fetch(layer_index)
        hidden, state = layer_forward(hidden, weights, allowed, cos_table, sin_table)
        saved_states.append(state)
        kept_weights.append(weights)
    result = hidden.astype(jnp.bfloat16)
    grad_hidden = cotangent.astype(jnp.float32)
    layer_grads = [None] * layer_count
    for layer_index in reversed(range(layer_count)):
        weights = fetch(layer_index)
        grad_hidden, grads = layer_backward(
            grad_hidden, saved_states[layer_index], weights, allowed, cos_table, sin_table
        )
        expanded = tuple((grad_piece[None] for grad_piece in grads))
        layer_grads[layer_index] = expanded
    merged = tuple(
        (
            jnp.concatenate(
                [layer_grads[layer_pos][member_pos] for layer_pos in range(layer_count)], axis=0
            )
            for member_pos in range(9)
        )
    )
    merged = owners(merged)
    return (
        result,
        grad_hidden.astype(jnp.bfloat16),
        merged[0],
        merged[1],
        merged[2],
        merged[3],
        merged[4],
        merged[5],
        merged[6],
        merged[7],
        merged[8],
    )


def solution(mesh):
    in_specs = (
        P(("fsdp", "ctx"), None),
        P(("fsdp", "ctx"), None),
        P("fsdp", None),
        P("fsdp", None),
        P(None, "fsdp", "tp"),
        P(None, "tp", "fsdp"),
        P(None, "fsdp", "tp"),
        P(None, "tp", "fsdp"),
        P(None, ("tp", "fsdp")),
        P(None, ("tp", "fsdp")),
        P(None, None, "fsdp"),
        P(None, None, "fsdp"),
        P(None, None, "fsdp"),
    )
    out_specs = (
        P(("fsdp", "ctx"), None),
        P(("fsdp", "ctx"), None),
        P(None, "fsdp", "tp"),
        P(None, "tp", "fsdp"),
        P(None, "fsdp", "tp"),
        P(None, "tp", "fsdp"),
        P(None, ("tp", "fsdp")),
        P(None, ("tp", "fsdp")),
        P(None, None, "fsdp"),
        P(None, None, "fsdp"),
        P(None, None, "fsdp"),
    )
    return jax.shard_map(
        per_device, mesh=mesh, in_specs=in_specs, out_specs=out_specs, check_vma=False
    )
```

profile of v0, /device:TPU:1, one launch (start us, length us, event | category | flops | bytes accessed | tf_op | source)
XLA Modules:
  0.0 1514.0 jit_solution(8534992257897441745)
XLA Ops:
  15.3 69.9 %all-gather.12 = bf16[32,24,6]{1,2,0:T(8,128)(2,1)S(1)} all-gather(bf16[1,24,6]{1,2,0:T(8,128)(2,1)S(1)} %maximum_bitcast_fusion.10), channel_id=1, replica_groups=mesh['fsdp'=32,'ctx'=2,'tp'=2] {'fsdp'}, dimensions={0}, use_global_device_ids=true | all-gather | bytes 9504 | tf_op jit(solution)/shard_map/all_gather | solution.py:20
  90.3 127.4 %all-reduce.12 = (bf16[1152]{0:T(1024)(128)(2,1)S(1)}, bf16[1152]{0:T(1024)(128)(2,1)S(1)}, bf16[1536]{0:T(1024)(128)(2,1)S(1)}, bf16[1536]{0:T(1024)(128)(2,1)S(1)}) all-reduce(bf16[1152]{0:T(1024)(128)(2,1)S(1)} %dynamic-update-slice.2, bf16[1152]{0:T(1024)(128)(2,1)S(1)} %dynamic-update-slice, ...), channel_id=9, replica_groups=mesh['fsdp'=32,'ctx'=2,'tp'=2] {'fsdp'}, use_global_device_ids=true, to_apply=%add.2 | all-reduce | flops 5376 | bytes 21504
  222.7 68.2 %all-gather.2 = bf16[1,384,768]{1,2,0:T(8,128)(2,1)S(1)} all-gather(bf16[1,384,24]{1,2,0:T(8,128)(2,1)S(1)} %get-tuple-element.161), channel_id=4, replica_groups=mesh['fsdp'=32,'ctx'=2,'tp'=2] {'fsdp'}, dimensions={2}, use_global_device_ids=true | all-gather | bytes 608256 | tf_op jit(solution)/shard_map/all_gather | solution.py:380
  290.9 69.7 %all-gather.8 = bf16[1,384,768]{1,2,0:T(8,128)(2,1)S(1)} all-gather(bf16[1,384,24]{1,2,0:T(8,128)(2,1)S(1)} %get-tuple-element.160), channel_id=10, replica_groups=mesh['fsdp'=32,'ctx'=2,'tp'=2] {'fsdp'}, dimensions={2}, use_global_device_ids=true | all-gather | bytes 608256 | tf_op jit(solution)/shard_map/all_gather | solution.py:380
  361.0 62.7 %all-gather.13 = bf16[32,24,6]{1,2,0:T(8,128)(2,1)S(1)} all-gather(bf16[1,24,6]{1,2,0:T(8,128)(2,1)S(1)} %maximum_bitcast_fusion.11), channel_id=1, replica_groups=mesh['fsdp'=32,'ctx'=2,'tp'=2] {'fsdp'}, dimensions={0}, use_global_device_ids=true | all-gather | bytes 9504 | tf_op jit(solution)/shard_map/all_gather | solution.py:20
  429.7 2.0 convolution_add_fusion.1
  432.1 75.8 %all_gather.82 = bf16[256,768]{0,1:T(8,128)(2,1)S(1)} all-gather(bf16[128,768]{0,1:T(8,128)(2,1)S(1)} %pad_maximum_fusion.6), channel_id=1, replica_groups=mesh['fsdp'=32,'ctx'=2,'tp'=2] {'ctx'}, dimensions={0}, use_global_device_ids=true | all-gather | bytes 589824 | tf_op jit(solution)/shard_map/all_gather | solution.py:20
  509.6 4.8 multiply_convert_fusion.3
  514.4 2.7 fusion.45
  517.9 5.4 all-to-all-start
  523.9 7.3 all-to-all-done
  531.7 81.4 %all-gather.29.cloned.1.call-done = bf16[1,768,1152]{2,1,0:T(8,128)(2,1)} async-done(((bf16[1,24,1152]{2,1,0:T(8,128)(2,1)}), bf16[1,768,1152]{2,1,0:T(8,128)(2,1)}) %all-gather.29.cloned.1.call-update) | async-done | bytes 1769488 | tf_op jit(solution)/shard_map/all_gather | solution.py:379
  613.2 1.9 convolution_add_fusion
  618.3 22.9 %all_gather.90 = bf16[256,768]{0,1:T(8,128)(2,1)S(1)} all-gather(bf16[128,768]{0,1:T(8,128)(2,1)S(1)} %pad_maximum_fusion.7), channel_id=1, replica_groups=mesh['fsdp'=32,'ctx'=2,'tp'=2] {'ctx'}, dimensions={0}, use_global_device_ids=true | all-gather | bytes 589824 | tf_op jit(solution)/shard_map/all_gather | solution.py:20
  652.9 4.3 all_to_all.40
  660.1 4.2 all-to-all-start.3
  664.3 104.8 %all-gather.31.cloned.1.call-done = bf16[1,768,1536]{2,1,0:T(8,128)(2,1)} async-done(((bf16[1,24,1536]{2,1,0:T(8,128)(2,1)}), bf16[1,768,1536]{2,1,0:T(8,128)(2,1)}) %all-gather.31.cloned.1.call-update) | async-done | bytes 2359312 | tf_op jit(solution)/shard_map/all_gather | solution.py:381
  769.1 4.8 multiply_convert_fusion.2
  773.9 3.0 convolution_bitcast_fusion
  778.4 146.0 %all-gather.33.cloned.1.call-done = bf16[1,1536,768]{1,2,0:T(8,128)(2,1)} async-done(((bf16[1,1536,24]{1,2,0:T(8,128)(2,1)}), bf16[1,1536,768]{1,2,0:T(8,128)(2,1)}) %all-gather.33.cloned.1.call-update) | async-done | bytes 2359312 | tf_op jit(solution)/shard_map/all_gather | solution.py:382
  924.4 2.9 convert_reduce_fusion.8
  930.6 2.4 convolution_bitcast_fusion.4
  933.0 2.9 convolution_bitcast_fusion.2
  936.8 4.2 all-to-all-start.4
  945.3 2.0 all-to-all-done.4
  956.0 26.4 %all_to_all.41 = bf16[2,128,768]{1,2,0:T(8,128)(2,1)S(1)} all-to-all(bf16[2,128,768]{1,2,0:T(8,128)(2,1)S(1)} %pad_maximum_fusion.5), channel_id=1, replica_groups=mesh['fsdp'=32,'ctx'=2,'tp'=2] {'ctx'}, dimensions={0} | all-to-all | bytes 786432 | tf_op jit(solution)/shard_map/all_to_all | solution.py:42
  983.2 4.5 all-to-all-start.1
  989.5 2.9 convolution_bitcast_fusion.1
  994.7 3.4 pad_maximum_fusion.2
  998.1 11.4 copy.129
  1009.5 2.8 pad_maximum_fusion.3
  1012.3 5.6 copy.130
  1017.9 2.5 convert_reduce_fusion.9
  1020.5 3.0 convolution_bitcast_fusion.3
  1023.5 4.8 pad_maximum_fusion
  1028.3 22.1 %copy.131 = f32[2,768,1536]{2,0,1:T(2,128)} copy(f32[2,768,1536]{2,1,0:T(8,128)S(1)} %pad_maximum_fusion) | data formatting | bytes 18874368 | tf_op jit(solution)/shard_map/concatenate | solution.py:413
  1050.4 6.7 pad_maximum_fusion.1
  1057.2 14.9 copy.132
  1074.0 2.7 fusion.34
  1078.2 4.2 all-to-all-start.7
  1083.5 6.1 all-to-all-done.7
  1090.3 3.5 all-to-all-start.6
  1094.0 6.1 all-to-all-done.6
  1100.7 377.7 %all-reduce.14 = (bf16[2,768,1152]{2,0,1:T(2,128)(2,1)}, bf16[2,384,768]{1,0,2:T(2,128)(2,1)}, bf16[2,768,1536]{2,0,1:T(2,128)(2,1)}, bf16[2,1536,768]{1,0,2:T(2...) all-reduce(f32[2,768,1152]{2,0,1:T(2,128)} %copy.129, ...), channel_id=14, replica_groups=mesh['fsdp'=32,'ctx'=2,'tp'=2] {'fsdp','ctx'}, use_global_device_ids=true, to_apply=%region_28.29.clone | all-reduce | flops 7092480 | bytes 42554880
  1479.2 6.4 all_gather.95
  1487.0 1.8 all_gather.96
  1490.4 1.9 all_gather.97
  1494.0 1.9 all_gather.98
  (404 shorter events, 87.7 us)
Async XLA Ops:
  7.2 353.4 %copy-start.7 = (bf16[128,768]{1,0:T(8,128)(2,1)S(1)}, bf16[128,768]{1,0:T(8,128)(2,1)}, u32[]{:S(2)}) copy-start(bf16[128,768]{1,0:T(8,128)(2,1)} %param.14) | copy-start | bytes 589828
  7.2 422.4 %all-gather.23.cloned.1.call-start = ((), (), s32[]{:S(2)}) async-start(), calls=%async_computation.8 | async-start | bytes 1824768 | tf_op jit(solution)/shard_map/all_gather | solution.py:379
  8.8 417.5 %copy-start.86 = (u32[128]{0:T(128)S(1)}, u32[128]{0:T(128)}, u32[]{:S(2)}) copy-start(u32[128]{0:T(128)} %constant.142) | copy-start | bytes 1540
  8.8 420.9 %copy-start = (bf16[128,768]{1,0:T(8,128)(2,1)S(1)}, bf16[128,768]{1,0:T(8,128)(2,1)}, u32[]{:S(2)}) copy-start(bf16[128,768]{1,0:T(8,128)(2,1)} %param.13) | copy-start | bytes 589828
  8.8 500.8 %all-gather.25.cloned.1.call-start = ((), (), s32[]{:S(2)}) async-start(), calls=%async_computation.9 | async-start | bytes 2433024 | tf_op jit(solution)/shard_map/all_gather | solution.py:381
  10.5 504.0 %all-gather.27.cloned.1.call-start = ((), (), s32[]{:S(2)}) async-start(), calls=%async_computation.10 | async-start | bytes 2433024 | tf_op jit(solution)/shard_map/all_gather | solution.py:382
  12.1 601.0 %all-gather.29.cloned.1.call-start = ((), (), s32[]{:S(2)}) async-start(), calls=%async_computation.11 | async-start | bytes 1824768 | tf_op jit(solution)/shard_map/all_gather | solution.py:379
  12.7 756.3 %all-gather.31.cloned.1.call-start = ((), (), s32[]{:S(2)}) async-start(), calls=%async_computation.12 | async-start | bytes 2433024 | tf_op jit(solution)/shard_map/all_gather | solution.py:381
  13.3 911.1 %all-gather.33.cloned.1.call-start = ((), (), s32[]{:S(2)}) async-start(), calls=%async_computation.13 | async-start | bytes 2433024 | tf_op jit(solution)/shard_map/all_gather | solution.py:382
  217.8 213.8 %copy-start.53 = (f32[768]{0:T(1024)}, f32[768]{0:T(1024)S(1)}, u32[]{:S(2)}) copy-start(f32[768]{0:T(1024)S(1)} %get-tuple-element.101) | copy-start | bytes 9220
  217.8 291.7 %copy-start.75 = (f32[768]{0:T(1024)}, f32[768]{0:T(1024)S(1)}, u32[]{:S(2)}) copy-start(f32[768]{0:T(1024)S(1)} %get-tuple-element.100) | copy-start | bytes 9220
  217.9 291.7 %copy-start.40 = (f32[768]{0:T(1024)}, f32[768]{0:T(1024)S(1)}, u32[]{:S(2)}) copy-start(f32[768]{0:T(1024)S(1)} %get-tuple-element.98) | copy-start | bytes 9220
  218.9 290.7 %copy-start.61 = (f32[128]{0:T(128)}, f32[128]{0:T(128)S(1)}, u32[]{:S(2)}) copy-start(f32[128]{0:T(128)S(1)} %broadcast_multiply_fusion.9) | copy-start | bytes 1540
  220.1 289.5 %copy-start.79 = (f32[128]{0:T(128)}, f32[128]{0:T(128)S(1)}, u32[]{:S(2)}) copy-start(f32[128]{0:T(128)S(1)} %add_rsqrt_fusion.1) | copy-start | bytes 1540
  360.6 71.3 %copy-start.4 = (bf16[1,384,768]{1,2,0:T(8,128)(2,1)}, bf16[1,384,768]{1,2,0:T(8,128)(2,1)S(1)}, u32[]{:S(2)}) copy-start(bf16[1,384,768]{1,2,0:T(8,128)(2,1)S(1)} %all-gather.8) | copy-start | bytes 1769476
  424.5 188.7 %copy-start.57 = (f32[768]{0:T(1024)}, f32[768]{0:T(1024)S(1)}, u32[]{:S(2)}) copy-start(f32[768]{0:T(1024)S(1)} %get-tuple-element.97) | copy-start | bytes 9220
  425.1 188.1 %copy-start.36 = (f32[768]{0:T(1024)}, f32[768]{0:T(1024)S(1)}, u32[]{:S(2)}) copy-start(f32[768]{0:T(1024)S(1)} %get-tuple-element.95) | copy-start | bytes 9220
  432.0 76.7 %copy-start.32 = (bf16[128,6,48]{0,2,1:T(8,128)(2,1)}, bf16[128,6,48]{0,2,1:T(8,128)(2,1)S(1)}, u32[]{:S(2)}) copy-start(bf16[128,6,48]{0,2,1:T(8,128)(2,1)S(1)} %slice.375) | copy-start | bytes 221188
  432.0 77.1 %copy-start.44 = (bf16[128,6,8]{0,2,1:T(8,128)(2,1)}, bf16[128,6,8]{0,2,1:T(8,128)(2,1)S(1)}, u32[]{:S(2)}) copy-start(bf16[128,6,8]{0,2,1:T(8,128)(2,1)S(1)} %get-tuple-element.147) | copy-start | bytes 36868
  432.0 77.1 %copy-start.46 = (bf16[128,6,8]{0,2,1:T(8,128)(2,1)}, bf16[128,6,8]{0,2,1:T(8,128)(2,1)S(1)}, u32[]{:S(2)}) copy-start(bf16[128,6,8]{0,2,1:T(8,128)(2,1)S(1)} %get-tuple-element.148) | copy-start | bytes 36868
  517.9 13.3 all-to-all-start
  531.6 84.5 %copy-start.85 = (f32[128]{0:T(128)}, f32[128]{0:T(128)S(1)}, u32[]{:S(2)}) copy-start(f32[128]{0:T(128)S(1)} %add_rsqrt_fusion) | copy-start | bytes 1540
  618.2 24.1 %copy-start.48 = (bf16[128,6,8]{0,2,1:T(8,128)(2,1)}, bf16[128,6,8]{0,2,1:T(8,128)(2,1)S(1)}, u32[]{:S(2)}) copy-start(bf16[128,6,8]{0,2,1:T(8,128)(2,1)S(1)} %get-tuple-element.143) | copy-start | bytes 36868
  618.2 25.5 %copy-start.50 = (bf16[128,6,8]{0,2,1:T(8,128)(2,1)}, bf16[128,6,8]{0,2,1:T(8,128)(2,1)S(1)}, u32[]{:S(2)}) copy-start(bf16[128,6,8]{0,2,1:T(8,128)(2,1)S(1)} %get-tuple-element.144) | copy-start | bytes 36868
  618.2 24.0 %copy-start.34 = (bf16[128,6,48]{0,2,1:T(8,128)(2,1)}, bf16[128,6,48]{0,2,1:T(8,128)(2,1)S(1)}, u32[]{:S(2)}) copy-start(bf16[128,6,48]{0,2,1:T(8,128)(2,1)S(1)} %slice.373) | copy-start | bytes 221188
  657.8 111.3 %copy-start.42 = (f32[768]{0:T(1024)S(1)}, f32[768]{0:T(1024)}, u32[]{:S(2)}) copy-start(f32[768]{0:T(1024)} %get-tuple-element.94) | copy-start | bytes 9220
  657.8 111.3 %copy-start.77 = (f32[768]{0:T(1024)S(1)}, f32[768]{0:T(1024)}, u32[]{:S(2)}) copy-start(f32[768]{0:T(1024)} %get-tuple-element.96) | copy-start | bytes 9220
  657.8 111.3 %copy-start.84 = (f32[1536]{0:T(1024)S(1)}, f32[1536]{0:T(1024)}, u32[]{:S(2)}) copy-start(f32[1536]{0:T(1024)} %convert_element_type.395) | copy-start | bytes 18436
  660.1 275.8 %all-to-all-start.3 = ((bf16[2,128,768]{2,1,0:T(8,128)(2,1)}), bf16[2,128,768]{2,1,0:T(8,128)(2,1)}, u32[]{:S(2)}, u32[]{:S(2)}) async-start(bf16[2,128,768]{2,1,0:T(8,128)(2,1)} %broadcast_in_dim.76), calls=%async_computation.3 | async-start | bytes 786432 | tf_op jit(solution)/shard_map/all_to_all | solution.py:25
  936.8 10.5 all-to-all-start.4
  955.6 26.8 %copy-start.21 = (bf16[128,768]{1,0:T(8,128)(2,1)S(1)}, bf16[128,768]{1,0:T(8,128)(2,1)}, u32[]{:S(2)}) copy-start(bf16[128,768]{1,0:T(8,128)(2,1)} %fusion.42) | copy-start | bytes 589828
  955.9 31.9 %copy-start.25 = (bf16[256,384]{0,1:T(8,128)(2,1)S(1)}, bf16[256,384]{0,1:T(8,128)(2,1)}, u32[]{:S(2)}) copy-start(bf16[256,384]{0,1:T(8,128)(2,1)} %copy-done.24) | copy-start | bytes 589828
  956.0 32.1 %copy-start.56 = (f32[128,8]{0,1:T(8,128)S(1)}, f32[128,8]{0,1:T(8,128)}, u32[]{:S(2)}) copy-start(f32[128,8]{0,1:T(8,128)} %get-tuple-element.179) | copy-start | bytes 12292
  956.0 32.2 %copy-start.10 = (bf16[128,768]{1,0:T(8,128)(2,1)S(1)}, bf16[128,768]{1,0:T(8,128)(2,1)}, u32[]{:S(2)}) copy-start(bf16[128,768]{1,0:T(8,128)(2,1)} %copy-done.9) | copy-start | bytes 589828
  956.0 32.2 %copy-start.29 = (bf16[6,64,128]{2,1,0:T(8,128)(2,1)S(1)}, bf16[6,64,128]{2,1,0:T(8,128)(2,1)}, u32[]{:S(2)}) copy-start(bf16[6,64,128]{2,1,0:T(8,128)(2,1)} %copy-done.28) | copy-start | bytes 294916
  983.2 94.2 %all-to-all-start.1 = ((bf16[2,128,768]{2,1,0:T(8,128)(2,1)}), bf16[2,128,768]{2,1,0:T(8,128)(2,1)}, u32[]{:S(2)}, u32[]{:S(2)}) async-start(bf16[2,128,768]{2,1,0:T(8,128)(2,1)} %broadcast_in_dim.75), calls=%async_computation.1 | async-start | bytes 786432 | tf_op jit(solution)/shard_map/all_to_all | solution.py:25
  1023.5 26.9 %slice-start = ((s8[4718592]{0:T(1024)(128)(4,1)}), s8[4194304]{0:T(1024)(128)(4,1)S(1)}, s32[]{:S(2)}) async-start(s8[4718592]{0:T(1024)(128)(4,1)} %bitcast.277), calls=%async_computation.14 | async-start | bytes 8388608
  1028.3 22.2 %slice-start.1 = ((s8[4718592]{0:T(1024)(128)(4,1)}), s8[524288]{0:T(1024)(128)(4,1)S(1)}, s32[]{:S(2)}) async-start(s8[4718592]{0:T(1024)(128)(4,1)} %bitcast.277), calls=%async_computation.15 | async-start | bytes 1048576
  1057.1 16.3 %copy-start.72 = (f32[768]{0:T(1024)S(1)}, f32[768]{0:T(1024)}, u32[]{:S(2)}) copy-start(f32[768]{0:T(1024)} %get-tuple-element.88) | copy-start | bytes 9220
  1057.1 16.3 %copy-start.71 = (f32[768]{0:T(1024)S(1)}, f32[768]{0:T(1024)}, u32[]{:S(2)}) copy-start(f32[768]{0:T(1024)} %get-tuple-element.66) | copy-start | bytes 9220
  1057.2 16.8 %copy-start.70 = (f32[768]{0:T(1024)S(1)}, f32[768]{0:T(1024)}, u32[]{:S(2)}) copy-start(f32[768]{0:T(1024)} %get-tuple-element.80) | copy-start | bytes 9220
  1057.2 16.8 %copy-start.69 = (f32[768]{0:T(1024)S(1)}, f32[768]{0:T(1024)}, u32[]{:S(2)}) copy-start(f32[768]{0:T(1024)} %get-tuple-element.78) | copy-start | bytes 9220
  1076.7 17.1 %copy-start.82 = (f32[1,768]{1,0:T(1,128)S(1)}, f32[1,768]{1,0:T(1,128)}, u32[]{:S(2)}) copy-start(f32[1,768]{1,0:T(1,128)} %stack.76) | copy-start | bytes 9220
  1078.2 11.4 all-to-all-start.7
  1082.4 18.2 %copy-start.81 = (f32[1,768]{1,0:T(1,128)S(1)}, f32[1,768]{1,0:T(1,128)}, u32[]{:S(2)}) copy-start(f32[1,768]{1,0:T(1,128)} %stack.81) | copy-start | bytes 9220
  1090.3 9.7 all-to-all-start.6
  1478.3 27.4 %copy-start.63 = (f32[768]{0:T(1024)S(1)}, f32[768]{0:T(1024)}, u32[]{:S(2)}) copy-start(f32[768]{0:T(1024)} %get-tuple-element.92) | copy-start | bytes 9220
  1478.3 27.4 %copy-start.64 = (f32[768]{0:T(1024)S(1)}, f32[768]{0:T(1024)}, u32[]{:S(2)}) copy-start(f32[768]{0:T(1024)} %get-tuple-element.93) | copy-start | bytes 9220
  (54 other events, 235.8 us)
Sparse Core Ops, SparseCore 0:
  10.2 134.8 all-gather.22
  147.4 155.2 all-gather.24
  304.9 153.2 all-gather.26
  460.3 152.8 all-gather.28
  615.2 153.7 all-gather.30
  770.6 153.8 all-gather.32
where the time goes:
time: 1520 us; the launch traced here: 1510 us
  blocking collectives  922 us (61%)
  waiting for transfers between devices  355 us (23%)
  local copies, waits for them, and re-layouts  98.7 us (6%)
  matrix products  54 us (4%)
  other arithmetic  38.1 us (3%)
  starting transfers between devices  26.1 us (2%)
  between operations  19.4 us (1%)
    unnamed x2, blocking collectives  505 us
    all_gather x5, blocking collectives, side_by_side(): lax.all_gather(both, axis, axis=dim, tiled=True)  233 us
    all_gather x2, waiting for transfers between devices, fetch(): lax.all_gather(w_down[layer_index], 'fsdp', axis=1, tiled=True)  146 us
    all_gather x2, blocking collectives, fetch(): lax.all_gather(w_out[layer_index], 'fsdp', axis=1, tiled=True)  138 us
    all_gather x2, waiting for transfers between devices, fetch(): lax.all_gather(w_up[layer_index], 'fsdp', axis=0, tiled=True)  105 us
    all_gather x2, waiting for transfers between devices, fetch(): lax.all_gather(w_qkv[layer_index], 'fsdp', axis=0, tiled=True)  81.5 us
    concatenate x4, local copies, waits for them, and re-layouts, per_device(): jnp.concatenate([layer_grads[layer_pos][member_pos] for layer_pos in rang...  54 us
    all_to_all x2, blocking collectives, sent_and_summed(): blocks = lax.all_to_all(split_up(array, dim, count), axis, 0, 0, tiled=True)  30.8 us
  transfers between devices with their start and end apart: 12, of which 7 were waited for; matrix products, arithmetic and copies ran while one was open for 11% of the time, Pallas kernels for 0%

commit v1 on v0

v1 whole, which is shorter than its diff:
```python
import jax
import jax.numpy as jnp
from jax import lax
from jax.sharding import PartitionSpec as P

HS = 64
ROT = 16
EPSILON = 1e-05
MASKED = -1e30
F32 = jnp.float32
BF = jnp.bfloat16
SWAP = [(0, 1), (1, 0)]


def other_core(values):
    return lax.ppermute(values, "ctx", SWAP)


def other_half(values):
    return lax.ppermute(values, "tp", SWAP)


def to_all(block):
    count = lax.axis_size("fsdp")
    return lax.all_to_all(
        jnp.broadcast_to(block[None], (count, *block.shape)), "fsdp", 0, 0, tiled=True
    )


def summed(blocks):
    got = lax.all_to_all(blocks, "fsdp", 0, 0, tiled=True)
    return jnp.sum(got.astype(F32), axis=0)


def own_rows_summed(part):
    half = part.shape[0] // 2
    mine = part[:half] + other_core(part[half:].astype(BF)).astype(F32)
    mine = mine.astype(BF)
    return mine.astype(F32) + other_half(mine).astype(F32)


def with_other_rows(total):
    return jnp.concatenate([total, other_core(total.astype(BF)).astype(F32)], axis=0)


def rows_by_rows(left, right):
    return lax.dot_general(
        left, right, (((0,), (0,)), ((), ())), preferred_element_type=F32
    )


def cols_by_cols(left, right):
    return lax.dot_general(
        left, right, (((1,), (1,)), ((), ())), preferred_element_type=F32
    )


def product(left, right):
    return jnp.dot(left, right, preferred_element_type=F32)


def gelu_exact(values):
    return jax.nn.gelu(values, approximate=False)


def angles(positions):
    exponents = jnp.arange(ROT // 2, dtype=F32) * (2.0 / ROT)
    inverse = jnp.power(10000.0, -exponents)
    phase = positions.astype(F32)[:, None] * inverse[None, :]
    return (jnp.cos(phase), jnp.sin(phase))


def rotate(values, cos_table, sin_table):
    half_rot = ROT // 2
    first_half = values[..., :half_rot]
    second_half = values[..., half_rot:ROT]
    cos_wide = cos_table[:, None, :]
    sin_wide = sin_table[:, None, :]
    return jnp.concatenate(
        [
            first_half * cos_wide - second_half * sin_wide,
            second_half * cos_wide + first_half * sin_wide,
            values[..., ROT:],
        ],
        axis=-1,
    )


def standardize(values):
    centered = values - jnp.mean(values, axis=-1, keepdims=True)
    inv_std = lax.rsqrt(jnp.mean(centered * centered, axis=-1, keepdims=True) + EPSILON)
    return (centered * inv_std, inv_std)


def layer_forward(hidden, weights, allowed, cos_table, sin_table):
    w_qkv, w_out_t, w_up, w_down_t, b_qkv, b_up, b_out, gains, shifts = weights
    rows = hidden.shape[0]
    heads = w_qkv.shape[1] // (3 * HS)
    normed, inv_std = standardize(hidden)
    attn_in = (normed * gains[0] + shifts[0]).astype(BF)
    mlp_in = (normed * gains[1] + shifts[1]).astype(BF)
    projected = (product(attn_in, w_qkv) + b_qkv).reshape(rows, heads, 3, HS)
    queries = rotate(projected[:, :, 0], cos_table, sin_table).astype(BF)
    keys = rotate(projected[:, :, 1], cos_table, sin_table).astype(BF)
    values = projected[:, :, 2].astype(BF)
    scores = jnp.einsum("qhd,khd->hqk", queries, keys, preferred_element_type=F32)
    scores = jnp.where(allowed[None], scores * HS ** (-0.5), MASKED)
    exponent = jnp.exp(scores - jnp.max(scores, axis=2, keepdims=True))
    attention = exponent / jnp.sum(exponent, axis=2, keepdims=True)
    attended = jnp.einsum(
        "hqk,khd->qhd", attention.astype(BF), values, preferred_element_type=F32
    )
    attn_out = attended.astype(BF).reshape(rows, heads * HS)
    up_value = product(mlp_in, w_up) + b_up
    activated = gelu_exact(up_value).astype(BF)
    part = cols_by_cols(attn_out, w_out_t) + cols_by_cols(activated, w_down_t)
    state = (normed, inv_std, attn_in, mlp_in, queries, keys, values, attention, attn_out)
    return (part, (*state, up_value, activated))


def layer_backward(grad_next, state, weights, cos_table, sin_table):
    w_qkv, w_out_t, w_up, w_down_t, b_qkv, b_up, b_out, gains, shifts = weights
    normed, inv_std, attn_in, mlp_in, queries, keys, values, attention, attn_out = state[:9]
    up_value, activated = state[9:]
    rows = grad_next.shape[0]
    heads = queries.shape[1]
    scale = HS ** (-0.5)
    low_grad = grad_next.astype(BF)
    grad_w_out = rows_by_rows(low_grad, attn_out)
    grad_w_down = rows_by_rows(low_grad, activated)
    grad_attended = product(low_grad, w_out_t).astype(BF).reshape(rows, heads, HS)
    grad_activated = product(low_grad, w_down_t)
    unused_value, gelu_back = jax.vjp(gelu_exact, up_value)
    low_grad_up = gelu_back(grad_activated)[0].astype(BF)
    grad_w_up = rows_by_rows(mlp_in, low_grad_up)
    grad_b_up = jnp.sum(low_grad_up.astype(F32), axis=0)
    part_mlp = cols_by_cols(low_grad_up, w_up)
    grad_attention = jnp.einsum("qhd,khd->hqk", grad_attended, values, preferred_element_type=F32)
    grad_values = jnp.einsum(
        "hqk,qhd->khd", attention.astype(BF), grad_attended, preferred_element_type=F32
    )
    row_dot = jnp.sum(attention * grad_attention, axis=2, keepdims=True)
    low_scores = (attention * (grad_attention - row_dot)).astype(BF)
    grad_queries = scale * jnp.einsum(
        "hqk,khd->qhd", low_scores, keys, preferred_element_type=F32
    )
    grad_keys = scale * jnp.einsum(
        "hqk,qhd->khd", low_scores, queries, preferred_element_type=F32
    )
    grad_queries = rotate(grad_queries, cos_table, -sin_table)
    grad_keys = rotate(grad_keys, cos_table, -sin_table)
    low_grad_qkv = (
        jnp.stack([grad_queries, grad_keys, grad_values], axis=2)
        .astype(BF)
        .reshape(rows, heads * 3 * HS)
    )
    grad_w_qkv = rows_by_rows(attn_in, low_grad_qkv)
    grad_b_qkv = jnp.sum(low_grad_qkv.astype(F32), axis=0)
    part_attn = cols_by_cols(low_grad_qkv, w_qkv)
    part = part_attn * gains[0] + part_mlp * gains[1]
    slab = jnp.concatenate([grad_w_qkv, grad_w_out, grad_w_up, grad_w_down], axis=1).astype(BF)
    sums = (
        jnp.sum(grad_next, axis=0) * 0.25,
        jnp.sum(part_attn * normed, axis=0),
        jnp.sum(part_mlp * normed, axis=0),
        jnp.sum(part_attn, axis=0),
        jnp.sum(part_mlp, axis=0),
    )
    return (part, slab, sums, grad_b_qkv, grad_b_up)


def norm_back(total, normed, inv_std):
    return inv_std * (
        total
        - jnp.mean(total, axis=-1, keepdims=True)
        - normed * jnp.mean(total * normed, axis=-1, keepdims=True)
    )


def per_device(
    tokens,
    cotangent,
    doc_lens,
    block_pos,
    w_qkv,
    w_out,
    w_up,
    w_down,
    b_qkv,
    b_up,
    out_bias,
    norm_gain,
    norm_bias,
):
    row_count = tokens.shape[0]
    block_rows = row_count // 2
    core = lax.axis_index("ctx")
    owners = lax.axis_size("fsdp")
    layers, depth, width_qkv = w_qkv.shape
    width_qkv, width_out, width_up = (n // 2 for n in (width_qkv, w_out.shape[1], w_up.shape[2]))

    def mine(array, axis, width):
        return lax.dynamic_slice_in_dim(array, core * width, width, axis)

    slabs = jnp.concatenate(
        [
            mine(w_qkv, 2, width_qkv),
            mine(w_out, 1, width_out).transpose(0, 2, 1),
            mine(w_up, 2, width_up),
            mine(w_down, 1, width_up).transpose(0, 2, 1),
        ],
        axis=2,
    )
    vectors = jnp.concatenate([out_bias, norm_gain, norm_bias], axis=1).reshape(-1, depth)
    bias_qkv = jnp.pad(b_qkv, ((0, 0), (0, 2 * depth - b_qkv.shape[1]))).reshape(-1, depth)
    bias_up = b_up.reshape(-1, depth)
    small = jnp.concatenate([vectors, bias_qkv, bias_up], axis=0)
    small = jnp.pad(small, ((0, 128 - small.shape[0]), (0, 0))).T
    first = to_all(jnp.concatenate([slabs[0], small], axis=1)).reshape(owners * depth, -1)
    later = to_all(slabs[1]).reshape(owners * depth, -1)
    width = slabs.shape[2]
    small = first[:, width:].T.reshape(128, owners, depth)[: 10 * layers].astype(F32)
    vectors = small[: 6 * layers].reshape(layers, 3, 2, owners * depth)
    bias_qkv, bias_up = (
        small[at * layers : (at + 2) * layers]
        .reshape(layers, 2, owners, depth)
        .transpose(0, 2, 1, 3)
        .reshape(layers, owners, 2 * depth)
        for at in (6, 8)
    )
    bias_qkv = mine(bias_qkv[:, :, : b_qkv.shape[1]].reshape(layers, -1), 1, width_qkv)
    bias_up = mine(bias_up.reshape(layers, -1), 1, width_up)

    cuts = (0, width_qkv, width_qkv + width_out, width_qkv + width_out + width_up, width)
    weights = []
    for layer, slab in enumerate((first, later)):
        matrices = (slab[:, a:b] for a, b in zip(cuts[:-1], cuts[1:]))
        weights.append((*matrices, bias_qkv[layer], bias_up[layer], *vectors[layer]))

    both = jnp.stack([tokens, cotangent])
    hidden, grad = jnp.concatenate([both, other_core(both)], axis=1).astype(F32)
    offsets = jnp.arange(block_rows, dtype=jnp.int32)
    positions = (block_pos[0][:, None] * block_rows + offsets[None, :]).reshape(2, row_count)
    positions = jnp.where(core == 0, positions, positions[::-1]).reshape(-1)
    doc_ends = jnp.cumsum(doc_lens[0])
    docs = jnp.sum((positions[:, None] >= doc_ends[None, :]).astype(jnp.int32), axis=1)
    allowed = (docs[:, None] == docs[None, :]) & (positions[None, :] <= positions[:, None])
    cos_table, sin_table = angles(positions)

    states = []
    for layer in range(layers):
        part, state = layer_forward(hidden, weights[layer], allowed, cos_table, sin_table)
        states.append(state)
        total = own_rows_summed(part)
        b_out = weights[layer][6]
        if layer + 1 < layers:
            hidden = hidden + with_other_rows(total) + b_out[0] + b_out[1]
        else:
            result = (hidden[:row_count] + total + b_out[0] + b_out[1]).astype(BF)

    all_sums, pieces = [None] * layers, [None] * layers
    for layer in reversed(range(layers)):
        state = states[layer]
        part, slab, sums, grad_b_qkv, grad_b_up = layer_backward(
            grad, state, weights[layer], cos_table, sin_table
        )
        bias_grads = []
        for vector, whole in ((grad_b_qkv, 2 * depth), (grad_b_up, 2 * depth)):
            empty = jnp.zeros_like(vector)
            spread = jnp.where(
                core == 0, jnp.concatenate([vector, empty]), jnp.concatenate([empty, vector])
            ).reshape(owners, -1)
            spread = jnp.pad(spread, ((0, 0), (0, whole - spread.shape[1])))
            bias_grads.append(spread.reshape(owners, 2, depth).transpose(1, 0, 2).reshape(2, -1))
        all_sums[layer] = jnp.concatenate([jnp.stack(sums), *bias_grads], axis=0)
        if layer == 0:
            rows = jnp.concatenate(all_sums, axis=0)
            rows = jnp.pad(rows, ((0, 128 - rows.shape[0]), (0, 0))).astype(BF)
            slab = jnp.concatenate([slab, rows.T], axis=1)
        pieces[layer] = summed(slab.reshape(owners, depth, -1))
        total = own_rows_summed(part)
        if layer > 0:
            total = with_other_rows(total)
            grad = grad + norm_back(total, state[0], state[1])
        else:
            normed, inv_std = state[0][:row_count], state[1][:row_count]
            grad_tokens = (grad[:row_count] + norm_back(total, normed, inv_std)).astype(BF)

    small = pieces[0][:, width:].T[: 9 * layers].astype(BF).astype(F32)
    small = small + other_half(small)
    own_small = pieces[0][:, width:].T[: 9 * layers].astype(BF).astype(F32)
    small = small.reshape(layers, 9, depth)
    own_small = own_small.reshape(layers, 9, depth)
    small = jnp.concatenate([small[:, :5], own_small[:, 5:]], axis=1)
    small = small + other_core(small)
    matrices = jnp.stack([pieces[0][:, :width], pieces[1]]).astype(BF)
    theirs = other_core(matrices)
    low = jnp.where(core == 0, matrices, theirs).astype(F32)
    high = jnp.where(core == 0, theirs, matrices).astype(F32)
    joined = []
    for k, (a, b) in enumerate(zip(cuts[:-1], cuts[1:])):
        joined.append(jnp.concatenate([low[:, :, a:b], high[:, :, a:b]], axis=2))
    grad_qkv, grad_out, grad_up, grad_down = joined
    return (
        result,
        grad_tokens,
        grad_qkv,
        grad_out.transpose(0, 2, 1),
        grad_up,
        grad_down.transpose(0, 2, 1),
        small[:, 5:7].reshape(layers, -1)[:, : b_qkv.shape[1]],
        small[:, 7:9].reshape(layers, -1),
        jnp.stack([small[:, 0], small[:, 0]], axis=1),
        small[:, 1:3],
        small[:, 3:5],
    )


def solution(mesh):
    in_specs = (
        P(("fsdp", "ctx"), None),
        P(("fsdp", "ctx"), None),
        P("fsdp", None),
        P("fsdp", None),
        P(None, "fsdp", "tp"),
        P(None, "tp", "fsdp"),
        P(None, "fsdp", "tp"),
        P(None, "tp", "fsdp"),
        P(None, ("tp", "fsdp")),
        P(None, ("tp", "fsdp")),
        P(None, None, "fsdp"),
        P(None, None, "fsdp"),
        P(None, None, "fsdp"),
    )
    out_specs = (P(("fsdp", "ctx"), None), P(("fsdp", "ctx"), None), *in_specs[4:])
    return jax.shard_map(
        per_device, mesh=mesh, in_specs=in_specs, out_specs=out_specs, check_vma=False
    )
```

time: 1520 us -> 340 us (0.22)
  blocking collectives: 922 us -> 0 us
  waiting for transfers between devices: 355 us -> 104 us
  starting transfers between devices: 26.1 us -> 56.6 us
  local copies, waits for them, and re-layouts: 98.7 us -> 69.4 us
  matrix products: 54 us -> 71.5 us
  between operations: 19.4 us -> 2.04 us
    unnamed x2 -> x0, blocking collectives: 505 us -> none
    all_gather x13 -> x0, blocking collectives: 387 us -> none  [the longest x5 233 us: side_by_side(): lax.all_gather(both, axis, axis=dim, tiled=True)]
    all_gather x6 -> x0, waiting for transfers between devices: 332 us -> none  [the longest x2 146 us: fetch(): lax.all_gather(w_down[layer_index], 'fsdp', axis=1, tiled=True)]
    ppermute x0 -> x14, waiting for transfers between devices: none -> 63.4 us  [the longest x5 61.7 us: other_half(): return lax.ppermute(values, 'tp', SWAP)]
    concatenate x4 -> x5, local copies, waits for them, and re-layouts: 54 us -> 19 us  [the longest x1 6.74 us: layer_backward(): jnp.concatenate([grad_w_qkv, grad_w_out, grad_w_up, grad_w_down], axis=1)]
    all_to_all x2 -> x0, blocking collectives: 30.8 us -> none  [sent_and_summed(): blocks = lax.all_to_all(split_up(array, dim, count), axis, 0, 0, tiled=True)]
    all_to_all x6 -> x4, waiting for transfers between devices: 21.4 us -> 40.7 us  [the longest x2 40.7 us: to_all(): lax.all_to_all(jnp.broadcast_to(block[None], (count, *block.shape)), 'fsd...]
    ppermute x0 -> x14, starting transfers between devices: none -> 17.4 us  [the longest x5 10.1 us: other_half(): return lax.ppermute(values, 'tp', SWAP)]
  transfers between devices with their start and end apart: 12 -> 18, of which waited for: 7 -> 8; matrix products, arithmetic and copies ran while one was open for 11% -> 33% of each run, Pallas kernels for 0% -> 0%
where the time goes in v1:
time: 340 us; the launch traced here: 337 us
  waiting for transfers between devices  104 us (31%)
  matrix products  71.5 us (21%)
  local copies, waits for them, and re-layouts  69.4 us (20%)
  starting transfers between devices  56.6 us (17%)
  other arithmetic  33.7 us (10%)
    ppermute x5, waiting for transfers between devices, other_half(): return lax.ppermute(values, 'tp', SWAP)  61.7 us
    all_to_all x2, waiting for transfers between devices, to_all(): lax.all_to_all(jnp.broadcast_to(block[None], (count, *block.shape)), 'fsd...  40.7 us
    dot_general x8, matrix products, product(): return jnp.dot(left, right, preferred_element_type=F32)  21.6 us
    all_to_all x2, starting transfers between devices, summed(): got = lax.all_to_all(blocks, 'fsdp', 0, 0, tiled=True)  19.9 us
    all_to_all x2, starting transfers between devices, to_all(): lax.all_to_all(jnp.broadcast_to(block[None], (count, *block.shape)), 'fsd...  19.3 us
    dot_general x8, matrix products, rows_by_rows(): lax.dot_general(left, right, (((0,), (0,)), ((), ())), preferred_element_...  18 us
    dot_general x8, matrix products, cols_by_cols(): lax.dot_general(left, right, (((1,), (1,)), ((), ())), preferred_element_...  16.1 us
    ppermute x5, starting transfers between devices, other_half(): return lax.ppermute(values, 'tp', SWAP)  10.1 us
  transfers between devices with their start and end apart: 18, of which 8 were waited for; matrix products, arithmetic and copies ran while one was open for 33% of the time, Pallas kernels for 0%

profile of v1, /device:TPU:1, one launch (start us, length us, event | category | flops | bytes accessed | tf_op | source)
XLA Modules:
  0.0 337.2 jit_solution(12770941948533119222)
XLA Ops:
  6.1 2.1 broadcast_in_dim.18
  8.2 9.5 %all-to-all-start = ((bf16[32,24,2432]{2,1,0:T(8,128)(2,1)}), bf16[32,24,2432]{2,1,0:T(8,128)(2,1)}, u32[]{:S(2)}, u32[]{:S(2)}) async-start(bf16[32,24,2432]{2,1,0:T(8,128)(2,1)} %broadcast_in_dim.18), calls=%async_computation | async-start | bytes 7471104 | tf_op jit(solution)/shard_map/all_to_all | solution.py:25
  22.3 40.7 %all-to-all-done = bf16[32,24,2432]{2,1,0:T(8,128)(2,1)} async-done(((bf16[32,24,2432]{2,1,0:T(8,128)(2,1)}), bf16[32,24,2432]{2,1,0:T(8,128)(2,1)}, u32[]{:S(2)}, u32[]{:S(2)}) %all-to-all-start) | async-done | bytes 3735584 | tf_op jit(solution)/shard_map/all_to_all | solution.py:25
  63.0 2.0 broadcast_in_dim.22
  65.0 9.8 %all-to-all-start.1 = ((bf16[32,24,2304]{2,1,0:T(8,128)(2,1)}), bf16[32,24,2304]{2,1,0:T(8,128)(2,1)}, u32[]{:S(2)}, u32[]{:S(2)}) async-start(bf16[32,24,2304]{2,1,0:T(8,128)(2,1)} %broadcast_in_dim.22), calls=%async_computation.1 | async-start | bytes 7077888 | tf_op jit(solution)/shard_map/all_to_all | solution.py:25
  75.8 3.0 slice_reduce_fusion.3
  85.6 2.2 fusion.146
  91.0 4.4 %multiply_convert_fusion.3 = (bf16[256,768]{1,0:T(8,128)(2,1)S(1)}, f32[256,768]{1,0:T(8,128)}, f32[256,768]{1,0:T(8,128)}) fusion(f32[768]{0:T(1024)S(1)} %get-tuple-element.38, bf16[768,2432]{1,0:T(8,128)(2,1)} %bitcast.7, f32[256,768]{1,0:T(8,128)S(1)} %fusion.60, f32[768]{0:T(1024)S(1)} %copy-done.62, f32[768]{0:T(1024)S(1)} %copy-done.64), kind=kOutput, calls=%fused_computation.115 | convolution fusion | flops 315555840 | bytes 3941376 | tf_op jit(solution)/shard_map/dot_general | solution.py:59
  95.4 1.9 convolution_add_fusion.2
  102.8 3.4 %collective-permute-start.2 = (bf16[128,768]{1,0:T(8,128)(2,1)S(1)}, bf16[128,768]{1,0:T(8,128)(2,1)S(1)}, u32[]{:S(2)}, u32[]{:S(2)}) collective-permute-start(bf16[128,768]{1,0:T(8,128)(2,1)S(1)} %fusion.73), channel_id=1, source_target_pairs={{0,1},{1,0},{2,3},{3,2},{4,5},{5,4},{6,7},{7,6},{8,9},{9,8},{10,11... | collective-permute-start | bytes 589832 | tf_op jit(solution)/shard_map/ppermute | solution.py:20
  107.4 14.8 %collective-permute-done.2 = bf16[128,768]{1,0:T(8,128)(2,1)S(1)} collective-permute-done((bf16[128,768]{1,0:T(8,128)(2,1)S(1)}, bf16[128,768]{1,0:T(8,128)(2,1)S(1)}, u32[]{:S(2)}, u32[]{:S(2)}) %collective-permute-start.2) | collective-permute-done | bytes 196640 | tf_op jit(solution)/shard_map/ppermute | solution.py:20
  123.4 2.2 convolution_convert_fusion.9
  127.7 1.8 convolution_add_fusion.4
  130.4 1.9 fusion.147
  137.1 1.7 fusion.28
  138.9 4.3 %multiply_convert_fusion.2 = (bf16[256,768]{1,0:T(8,128)(2,1)}, f32[256,768]{1,0:T(8,128)S(1)}, f32[256,768]{1,0:T(8,128)S(1)}) fusion(f32[768]{0:T(1024)S(1)} %copy-done.81, bf16[768,2304]{1,0:T(8,128)(2,1)} %bitcast.22, f32[768]{0:T(1024)S(1)} %copy-done.70, f32[768]{0:T(1024)S(1)} %copy-done.56, f32[256]{0:T(256)S(1)} %copy-done.72, ...), kind=kOutput, calls=%fused_computation.99 | convolution fusion | flops 315949056 | bytes 3943424 | tf_op jit(solution)/shard_map/dot_general | solution.py:59
  143.2 2.0 convert_reduce_fusion
  145.2 2.8 multiply_add_fusion.1
  150.8 1.9 copy.223
  154.2 2.7 convolution_convert_fusion
  156.9 2.5 convolution_convert_fusion.4
  162.2 2.3 convolution_convert_fusion.10
  164.5 4.4 %collective-permute-done.7 = bf16[128,768]{1,0:T(8,128)(2,1)} collective-permute-done((bf16[128,768]{1,0:T(8,128)(2,1)}, bf16[128,768]{1,0:T(8,128)(2,1)}, u32[]{:S(2)}, u32[]{:S(2)}) %collective-permute-start.7) | collective-permute-done | bytes 196640 | tf_op jit(solution)/shard_map/ppermute | solution.py:20
  168.9 1.8 fusion.129
  172.0 1.9 convolution_convert_fusion.6
  174.8 2.6 multiply_reduce_fusion
  178.4 1.9 convolution_convert_fusion.8
  182.8 1.9 copy.225
  184.7 2.7 convolution_convert_fusion.1
  187.4 6.7 %concatenate.155 = bf16[32,24,2304]{2,1,0:T(8,128)(2,1)} concatenate(bf16[32,24,576]{2,1,0:T(8,128)(2,1)} %convolution_convert_fusion.4, bf16[32,24,192]{2,1,0:T(8,128)(2,1)} %convolution_convert_fusion.6, bf16[32,24,768]{2,1,0:T(8,128)(2,1)} %convolution_convert_fusion.1, bf16[32,24,768]{2,1,0:T(8,128)(2,1)} %convolution_convert_fusion), dimensions={2} | concatenate | bytes 7077888 | tf_op jit(solution)/shard_map/concatenate | solution.py:161
  194.1 12.0 %all-to-all-start.3 = ((bf16[32,24,2304]{2,1,0:T(8,128)(2,1)}), bf16[32,24,2304]{2,1,0:T(8,128)(2,1)}, u32[]{:S(2)}, u32[]{:S(2)}) async-start(bf16[32,24,2304]{2,1,0:T(8,128)(2,1)} %concatenate.155), calls=%async_computation.3 | async-start | bytes 7077888 | tf_op jit(solution)/shard_map/all_to_all | solution.py:31
  211.5 1.7 fusion.31
  213.3 3.2 convert_reduce_fusion.1
  216.5 2.9 fusion.133
  239.6 5.4 %concatenate.153 = bf16[18,768]{1,0:T(8,128)(2,1)} concatenate(bf16[1,768]{1,0:T(2,128)(2,1)} %mul.657, bf16[1,768]{1,0:T(2,128)(2,1)} %stack.93, bf16[1,768]{1,0:T(2,128)(2,1)} %stack.94, bf16[1,768]{1,0:T(2,128)(2,1)} %stack.95, bf16[1,768]{1,0:T(2,128)(2,1)} %stack.96, bf16[2,768]{1,0:T(2,128)(2,1)} %reshape.673, bf16[2,768]{1,0:T(2,128)(2,1)} %reshape.675, ...), dimensions={0} | concatenate | bytes 55296 | tf_op jit(solution)/shard_map/concatenate | solution.py:277
  245.0 2.5 fusion.4
  247.5 2.6 fusion.11
  254.0 6.1 %copy.222 = bf16[768,2432]{1,0:T(8,128)(2,1)} copy(bf16[768,2432]{0,1:T(8,128)(2,1)} %bitcast_dynamic-update-slice_fusion) | data formatting | bytes 7471104 | tf_op jit(solution)/shard_map/concatenate | solution.py:279
  260.0 7.9 %all-to-all-start.2 = ((bf16[32,24,2432]{2,1,0:T(8,128)(2,1)}), bf16[32,24,2432]{2,1,0:T(8,128)(2,1)}, u32[]{:S(2)}, u32[]{:S(2)}) async-start(bf16[32,24,2432]{2,1,0:T(8,128)(2,1)} %bitcast.189), calls=%async_computation.2 | async-start | bytes 7471104 | tf_op jit(solution)/shard_map/all_to_all | solution.py:31
  269.6 1.8 convolution_add_fusion
  274.5 2.4 collective-permute-start.10
  277.0 30.6 %collective-permute-done.5 = bf16[128,768]{1,0:T(8,128)(2,1)S(1)} collective-permute-done((bf16[128,768]{1,0:T(8,128)(2,1)S(1)}, bf16[128,768]{1,0:T(8,128)(2,1)S(1)}, u32[]{:S(2)}, u32[]{:S(2)}) %collective-permute-start.5) | collective-permute-done | bytes 196640 | tf_op jit(solution)/shard_map/ppermute | solution.py:20
  308.4 10.0 %collective-permute-done.10 = bf16[128,768]{1,0:T(8,128)(2,1)S(1)} collective-permute-done((bf16[128,768]{1,0:T(8,128)(2,1)S(1)}, bf16[128,768]{1,0:T(8,128)(2,1)S(1)}, u32[]{:S(2)}, u32[]{:S(2)}) %collective-permute-start.10) | collective-permute-done | bytes 196640 | tf_op jit(solution)/shard_map/ppermute | solution.py:20
  319.4 2.5 reduce.5
  321.9 2.7 reduce.4
  324.6 2.2 collective-permute-start.12
  326.9 1.8 collective-permute-done.12
  328.9 1.7 collective-permute-start.13
  (377 shorter events, 90.9 us)
Async XLA Ops:
  8.2 9.5 %copy-start.21 = (bf16[128,768]{1,0:T(8,128)(2,1)S(1)}, bf16[128,768]{1,0:T(8,128)(2,1)}, u32[]{:S(2)}) copy-start(bf16[128,768]{1,0:T(8,128)(2,1)} %param.14) | copy-start | bytes 589828
  8.2 9.5 %copy-start.22 = (bf16[128,768]{1,0:T(8,128)(2,1)S(1)}, bf16[128,768]{1,0:T(8,128)(2,1)}, u32[]{:S(2)}) copy-start(bf16[128,768]{1,0:T(8,128)(2,1)} %param.13) | copy-start | bytes 589828
  8.2 10.7 %copy-start.82 = (s32[1,4]{1,0:T(1,128)S(1)}, s32[1,4]{1,0:T(1,128)}, u32[]{:S(2)}) copy-start(s32[1,4]{1,0:T(1,128)} %param.16) | copy-start | bytes 52
  8.2 11.8 %copy-start.83 = (s32[1,4]{1,0:T(1,128)S(1)}, s32[1,4]{1,0:T(1,128)}, u32[]{:S(2)}) copy-start(s32[1,4]{1,0:T(1,128)} %param.15) | copy-start | bytes 52
  8.2 54.8 %all-to-all-start = ((bf16[32,24,2432]{2,1,0:T(8,128)(2,1)}), bf16[32,24,2432]{2,1,0:T(8,128)(2,1)}, u32[]{:S(2)}, u32[]{:S(2)}) async-start(bf16[32,24,2432]{2,1,0:T(8,128)(2,1)} %broadcast_in_dim.18), calls=%async_computation | async-start | bytes 7471104 | tf_op jit(solution)/shard_map/all_to_all | solution.py:25
  17.8 3.3 collective-permute-start
  21.9 43.1 %copy-start.74 = (f32[256]{0:T(256)}, f32[256]{0:T(256)S(1)}, u32[]{:S(2)}) copy-start(f32[256]{0:T(256)S(1)} %broadcast_multiply_fusion.3) | copy-start | bytes 3076
  22.1 42.9 %copy-start.78 = (f32[256]{0:T(256)}, f32[256]{0:T(256)S(1)}, u32[]{:S(2)}) copy-start(f32[256]{0:T(256)S(1)} %add_rsqrt_fusion.1) | copy-start | bytes 3076
  65.0 58.5 %all-to-all-start.1 = ((bf16[32,24,2304]{2,1,0:T(8,128)(2,1)}), bf16[32,24,2304]{2,1,0:T(8,128)(2,1)}, u32[]{:S(2)}, u32[]{:S(2)}) async-start(bf16[32,24,2304]{2,1,0:T(8,128)(2,1)} %broadcast_in_dim.22), calls=%async_computation.1 | async-start | bytes 7077888 | tf_op jit(solution)/shard_map/all_to_all | solution.py:25
  82.0 7.3 %copy-start.11 = (f32[256,576]{0,1:T(8,128)}, f32[256,576]{0,1:T(8,128)S(1)}, u32[]{:S(2)}) copy-start(f32[256,576]{0,1:T(8,128)S(1)} %convolution_add_fusion.5) | copy-start | bytes 1769476
  98.2 3.5 %collective-permute-start.1 = (bf16[128,768]{1,0:T(8,128)(2,1)S(1)}, bf16[128,768]{1,0:T(8,128)(2,1)S(1)}, u32[]{:S(2)}, u32[]{:S(2)}) collective-permute-start(bf16[128,768]{1,0:T(8,128)(2,1)S(1)} %slice.657), channel_id=1, source_target_pairs={{0,2},{2,0},{1,3},{3,1},{4,6},{6,4},{5,7},{7,5},{8,10},{10,8},{9,1... | collective-permute-start | bytes 589832 | tf_op jit(solution)/shard_map/ppermute | solution.py:16
  102.8 19.5 %collective-permute-start.2 = (bf16[128,768]{1,0:T(8,128)(2,1)S(1)}, bf16[128,768]{1,0:T(8,128)(2,1)S(1)}, u32[]{:S(2)}, u32[]{:S(2)}) collective-permute-start(bf16[128,768]{1,0:T(8,128)(2,1)S(1)} %fusion.73), channel_id=1, source_target_pairs={{0,1},{1,0},{2,3},{3,2},{4,5},{5,4},{6,7},{7,6},{8,9},{9,8},{10,11... | collective-permute-start | bytes 589832 | tf_op jit(solution)/shard_map/ppermute | solution.py:20
  123.0 2.6 collective-permute-start.3
  129.6 7.0 %copy-start.34 = (bf16[256,3,48]{0,2,1:T(8,128)(2,1)}, bf16[256,3,48]{0,2,1:T(8,128)(2,1)S(1)}, u32[]{:S(2)}) copy-start(bf16[256,3,48]{0,2,1:T(8,128)(2,1)S(1)} %slice.658) | copy-start | bytes 221188
  129.7 6.6 %copy-start.49 = (bf16[256,3,8]{0,2,1:T(8,128)(2,1)}, bf16[256,3,8]{0,2,1:T(8,128)(2,1)S(1)}, u32[]{:S(2)}) copy-start(bf16[256,3,8]{0,2,1:T(8,128)(2,1)S(1)} %get-tuple-element.87) | copy-start | bytes 36868
  129.7 6.6 %copy-start.50 = (bf16[256,3,8]{0,2,1:T(8,128)(2,1)}, bf16[256,3,8]{0,2,1:T(8,128)(2,1)S(1)}, u32[]{:S(2)}) copy-start(bf16[256,3,8]{0,2,1:T(8,128)(2,1)S(1)} %get-tuple-element.88) | copy-start | bytes 36868
  129.7 6.9 %copy-start.51 = (bf16[256,3,8]{0,2,1:T(8,128)(2,1)}, bf16[256,3,8]{0,2,1:T(8,128)(2,1)S(1)}, u32[]{:S(2)}) copy-start(bf16[256,3,8]{0,2,1:T(8,128)(2,1)S(1)} %get-tuple-element.107) | copy-start | bytes 36868
  129.7 6.9 %copy-start.52 = (bf16[256,3,8]{0,2,1:T(8,128)(2,1)}, bf16[256,3,8]{0,2,1:T(8,128)(2,1)S(1)}, u32[]{:S(2)}) copy-start(bf16[256,3,8]{0,2,1:T(8,128)(2,1)S(1)} %get-tuple-element.108) | copy-start | bytes 36868
  143.2 6.6 %copy-start.17 = (f32[1,128,768]{2,1,0:T(8,128)S(1)}, f32[1,128,768]{2,1,0:T(8,128)}, u32[]{:S(2)}) copy-start(f32[1,128,768]{2,1,0:T(8,128)} %get-tuple-element.97) | copy-start | bytes 1179652
  143.2 6.6 %copy-start.53 = (f32[768]{0:T(1024)S(1)}, f32[768]{0:T(1024)}, u32[]{:S(2)}) copy-start(f32[768]{0:T(1024)} %get-tuple-element.31) | copy-start | bytes 9220
  149.7 9.7 %collective-permute-start.6 = (bf16[128,768]{1,0:T(8,128)(2,1)}, bf16[128,768]{1,0:T(8,128)(2,1)}, u32[]{:S(2)}, u32[]{:S(2)}) collective-permute-start(bf16[128,768]{1,0:T(8,128)(2,1)} %slice.655), channel_id=1, source_target_pairs={{0,2},{2,0},{1,3},{3,1},{4,6},{6,4},{5,7},{7,5},{8,10},{10,8},{9,1... | collective-permute-start | bytes 589832 | tf_op jit(solution)/shard_map/ppermute | solution.py:16
  159.4 12.7 %copy-start.14 = (bf16[768,256]{1,0:T(8,128)(2,1)S(1)}, bf16[768,256]{1,0:T(8,128)(2,1)}, u32[]{:S(2)}) copy-start(bf16[768,256]{1,0:T(8,128)(2,1)} %copy.224) | copy-start | bytes 1179652
  161.1 7.9 %collective-permute-start.7 = (bf16[128,768]{1,0:T(8,128)(2,1)}, bf16[128,768]{1,0:T(8,128)(2,1)}, u32[]{:S(2)}, u32[]{:S(2)}) collective-permute-start(bf16[128,768]{1,0:T(8,128)(2,1)} %fusion.68), channel_id=1, source_target_pairs={{0,1},{1,0},{2,3},{3,2},{4,5},{5,4},{6,7},{7,6},{8,9},{9,8},{10,11... | collective-permute-start | bytes 589832 | tf_op jit(solution)/shard_map/ppermute | solution.py:20
  164.5 10.3 %copy-start.6 = (f32[256,768]{1,0:T(8,128)S(1)}, f32[256,768]{1,0:T(8,128)}, u32[]{:S(2)}) copy-start(f32[256,768]{1,0:T(8,128)} %copy-done.5) | copy-start | bytes 2359300
  164.5 10.3 %copy-start.7 = (f32[256,768]{1,0:T(8,128)S(1)}, f32[256,768]{1,0:T(8,128)}, u32[]{:S(2)}) copy-start(f32[256,768]{1,0:T(8,128)} %get-tuple-element.123) | copy-start | bytes 2359300
  164.5 13.0 %copy-start.59 = (f32[256]{0:T(256)S(1)}, f32[256]{0:T(256)}, u32[]{:S(2)}) copy-start(f32[256]{0:T(256)} %copy-done.57) | copy-start | bytes 3076
  164.5 13.0 %copy-start.73 = (f32[256]{0:T(256)S(1)}, f32[256]{0:T(256)}, u32[]{:S(2)}) copy-start(f32[256]{0:T(256)} %copy-done.71) | copy-start | bytes 3076
  170.8 3.2 collective-permute-start.8
  194.1 65.9 %all-to-all-start.3 = ((bf16[32,24,2304]{2,1,0:T(8,128)(2,1)}), bf16[32,24,2304]{2,1,0:T(8,128)(2,1)}, u32[]{:S(2)}, u32[]{:S(2)}) async-start(bf16[32,24,2304]{2,1,0:T(8,128)(2,1)} %concatenate.155), calls=%async_computation.3 | async-start | bytes 7077888 | tf_op jit(solution)/shard_map/all_to_all | solution.py:31
  213.2 8.6 %copy-start.75 = (bf16[576]{0:T(1024)(128)(2,1)S(1)}, bf16[576]{0:T(1024)(128)(2,1)}, u32[]{:S(2)}) copy-start(bf16[576]{0:T(1024)(128)(2,1)} %reduce_sum.292) | copy-start | bytes 3460
  216.5 31.1 %copy-start.16 = (f32[1,128,768]{2,1,0:T(8,128)S(1)}, f32[1,128,768]{2,1,0:T(8,128)}, u32[]{:S(2)}) copy-start(f32[1,128,768]{2,1,0:T(8,128)} %get-tuple-element.72) | copy-start | bytes 1179652
  239.6 10.5 %copy-start.63 = (f32[768]{0:T(1024)S(1)}, f32[768]{0:T(1024)}, u32[]{:S(2)}) copy-start(f32[768]{0:T(1024)} %get-tuple-element.33) | copy-start | bytes 9220
  239.6 10.5 %copy-start.66 = (f32[768]{0:T(1024)S(1)}, f32[768]{0:T(1024)}, u32[]{:S(2)}) copy-start(f32[768]{0:T(1024)} %get-tuple-element.34) | copy-start | bytes 9220
  260.0 8.0 %copy-start.31 = (bf16[3,64,256]{2,1,0:T(8,128)(2,1)S(1)}, bf16[3,64,256]{2,1,0:T(8,128)(2,1)}, u32[]{:S(2)}) copy-start(bf16[3,64,256]{2,1,0:T(8,128)(2,1)} %convolution_convert_fusion.10) | copy-start | bytes 294916
  260.0 9.6 %copy-start.18 = (bf16[256,768]{1,0:T(8,128)(2,1)S(1)}, bf16[256,768]{1,0:T(8,128)(2,1)}, u32[]{:S(2)}) copy-start(bf16[256,768]{1,0:T(8,128)(2,1)} %get-tuple-element.47) | copy-start | bytes 1179652
  260.0 61.9 %all-to-all-start.2 = ((bf16[32,24,2432]{2,1,0:T(8,128)(2,1)}), bf16[32,24,2432]{2,1,0:T(8,128)(2,1)}, u32[]{:S(2)}, u32[]{:S(2)}) async-start(bf16[32,24,2432]{2,1,0:T(8,128)(2,1)} %bitcast.189), calls=%async_computation.2 | async-start | bytes 7471104 | tf_op jit(solution)/shard_map/all_to_all | solution.py:31
  268.0 39.6 %copy-start.60 = (f32[768]{0:T(1024)S(1)}, f32[768]{0:T(1024)}, u32[]{:S(2)}) copy-start(f32[768]{0:T(1024)} %get-tuple-element.25) | copy-start | bytes 9220
  268.0 39.6 %copy-start.61 = (f32[768]{0:T(1024)S(1)}, f32[768]{0:T(1024)}, u32[]{:S(2)}) copy-start(f32[768]{0:T(1024)} %get-tuple-element.26) | copy-start | bytes 9220
  269.6 49.0 %copy-start.4 = (f32[256,768]{1,0:T(8,128)S(1)}, f32[256,768]{1,0:T(8,128)}, u32[]{:S(2)}) copy-start(f32[256,768]{1,0:T(8,128)} %copy-done.2) | copy-start | bytes 2359300
  269.6 49.0 %slice-start = ((f32[256]{0:T(256)}), f32[128]{0:T(128)S(1)}, s32[]{:S(2)}) async-start(f32[256]{0:T(256)} %copy-done.78), calls=%async_computation.4 | async-start | bytes 1024 | tf_op jit(solution)/shard_map/slice | solution.py:286
  271.5 2.0 collective-permute-start.4
  272.5 2.1 collective-permute-start.9
  273.5 34.1 %collective-permute-start.5 = (bf16[128,768]{1,0:T(8,128)(2,1)S(1)}, bf16[128,768]{1,0:T(8,128)(2,1)S(1)}, u32[]{:S(2)}, u32[]{:S(2)}) collective-permute-start(bf16[128,768]{1,0:T(8,128)(2,1)S(1)} %fusion.69), channel_id=1, source_target_pairs={{0,1},{1,0},{2,3},{3,2},{4,5},{5,4},{6,7},{7,6},{8,9},{9,8},{10,11... | collective-permute-start | bytes 589832 | tf_op jit(solution)/shard_map/ppermute | solution.py:20
  274.5 43.8 %collective-permute-start.10 = (bf16[128,768]{1,0:T(8,128)(2,1)S(1)}, bf16[128,768]{1,0:T(8,128)(2,1)S(1)}, u32[]{:S(2)}, u32[]{:S(2)}) collective-permute-start(bf16[128,768]{1,0:T(8,128)(2,1)S(1)} %fusion.66), channel_id=1, source_target_pairs={{0,1},{1,0},{2,3},{3,2},{4,5},{5,4},{6,7},{7,6},{8,9},{9,8},{10,11... | collective-permute-start | bytes 589832 | tf_op jit(solution)/shard_map/ppermute | solution.py:20
  321.9 15.3 %copy-start.1 = (bf16[2,24,1536]{2,1,0:T(8,128)(2,1)S(1)}, bf16[2,24,1536]{2,1,0:T(8,128)(2,1)}, u32[]{:S(2)}) copy-start(bf16[2,24,1536]{2,1,0:T(8,128)(2,1)} %param.19) | copy-start | bytes 442372
  324.6 4.1 %collective-permute-start.12 = (f32[18,24]{0,1:T(8,128)S(1)}, f32[18,24]{0,1:T(8,128)S(1)}, u32[]{:S(2)}, u32[]{:S(2)}) collective-permute-start(f32[18,24]{0,1:T(8,128)S(1)} %slice_convert_fusion.10), channel_id=1, source_target_pairs={{0,1},{1,0},{2,3},{3,2},{4,5},{5,4},{6,7},{7,6},{8,9},{9,8},{10,11... | collective-permute-start | bytes 5192 | tf_op jit(solution)/shard_map/ppermute | solution.py:20
  328.9 2.6 collective-permute-start.13
  330.6 3.3 collective-permute-start.11
  (55 other events, 201.7 us)

commit v2 on v1

v2 whole, which is shorter than its diff:
```python
import functools

import jax
import jax.numpy as jnp
from jax import lax
from jax.experimental import pallas as pl
from jax.experimental.pallas import tpu as pltpu
from jax.sharding import PartitionSpec as P

HS = 64
ROT = 16
EPSILON = 1e-05
MASKED = -1e30
F32 = jnp.float32
BF = jnp.bfloat16
SWAP = [(0, 1), (1, 0)]
LANES = 128
CHUNK = 32
HEAD = 4 * HS
SCALE = HS ** (-0.5)
VMEM_BYTES = 50 * 1024 * 1024
GAIN_A, GAIN_B, SHIFT_A, SHIFT_B, BIAS_QKV, BIAS_UP, BIAS_OUT = range(7)
VECTORS = 8
SUM_OUT, SUM_GAIN_A, SUM_GAIN_B, SUM_SHIFT_A, SUM_SHIFT_B, SUM_QKV, SUM_UP = range(7)


def other_core(values):
    return lax.ppermute(values, "ctx", SWAP)


def other_half(values):
    return lax.ppermute(values, "tp", SWAP)


def to_all(block):
    count = lax.axis_size("fsdp")
    return lax.all_to_all(
        jnp.broadcast_to(block[None], (count, *block.shape)), "fsdp", 0, 0, tiled=True
    )


def summed(blocks):
    got = lax.all_to_all(blocks, "fsdp", 0, 0, tiled=True)
    return jnp.sum(got.astype(F32), axis=0)


def dot(left, right, along=(1, 0)):
    dims = (((along[0],), (along[1],)), ((), ()))
    return lax.dot_general(left, right, dims, preferred_element_type=F32)


def over_rows(rows, step, carry=None, start=0):
    def body(at, kept):
        return step(pl.ds(pl.multiple_of(at * CHUNK, CHUNK), CHUNK), kept)

    return lax.fori_loop(start // CHUNK, rows // CHUNK, body, carry)


def by_eights(values):
    return values.reshape(-1, 8, values.shape[-1]).sum(axis=0)


def whole_sum(eights):
    return jnp.sum(eights, axis=0, keepdims=True)


def turned(tile, cos, left, right):
    return (
        tile * cos
        + pltpu.roll(tile, LANES - ROT // 2, 1) * left
        + pltpu.roll(tile, ROT // 2, 1) * right
    )


def row_norm(values):
    centered = values - jnp.mean(values, axis=-1, keepdims=True)
    inv_std = lax.rsqrt(jnp.mean(centered * centered, axis=-1, keepdims=True) + EPSILON)
    return centered * inv_std, inv_std


def row_norm_back(total, normed, inv_std):
    return inv_std * (
        total
        - jnp.mean(total, axis=-1, keepdims=True)
        - normed * jnp.mean(total * normed, axis=-1, keepdims=True)
    )


def one_hot(place_ref, at, width):
    rows = lax.broadcasted_iota(jnp.int32, (width, place_ref.shape[1]), 0)
    return (rows == place_ref[at : at + 1, :]).astype(F32).astype(BF)


class State:
    names = ("normed", "inv_std", "a", "m", "qk", "v", "p", "o", "gl", "slope")

    def __init__(self, refs):
        for name, ref in zip(self.names, refs, strict=True):
            setattr(self, name, ref)

    @staticmethod
    def shapes(rows, depth, heads, hidden):
        return (
            jax.ShapeDtypeStruct((rows, depth), F32),
            jax.ShapeDtypeStruct((rows, 1), F32),
            jax.ShapeDtypeStruct((rows, depth), BF),
            jax.ShapeDtypeStruct((rows, depth), BF),
            jax.ShapeDtypeStruct((rows, heads * 2 * HS), BF),
            jax.ShapeDtypeStruct((rows, heads * HS), BF),
            jax.ShapeDtypeStruct((heads, rows, rows), F32),
            jax.ShapeDtypeStruct((rows, heads * HEAD), BF),
            jax.ShapeDtypeStruct((rows, hidden), BF),
            jax.ShapeDtypeStruct((rows, hidden), F32),
        )


def forward(state, vec_ref, w_ref, table_ref, mask_ref, part_ref, wide_ref):
    rows, depth = state.normed.shape
    heads = state.v.shape[1] // HS
    attn, hidden = heads * HEAD, state.gl.shape[1]

    def affine(at, _):
        normed = state.normed[at, :]
        state.a[at, :] = (
            normed * vec_ref[GAIN_A : GAIN_A + 1, :] + vec_ref[SHIFT_A : SHIFT_A + 1, :]
        ).astype(BF)
        state.m[at, :] = (
            normed * vec_ref[GAIN_B : GAIN_B + 1, :] + vec_ref[SHIFT_B : SHIFT_B + 1, :]
        ).astype(BF)

    over_rows(rows, affine)
    wide_ref[...] = dot(state.a[...], w_ref[:, :attn])
    state.o[...] = jnp.zeros_like(state.o)
    for head in range(heads):
        at = head * HEAD
        bias = vec_ref[BIAS_QKV : BIAS_QKV + 1, at : at + HEAD]
        tile = wide_ref[:, at : at + LANES] + bias[:, :LANES]
        tile = turned(tile, table_ref[0], table_ref[1], table_ref[2]).astype(BF)
        value = wide_ref[:, at + 2 * HS : at + 3 * HS] + bias[:, 2 * HS : 3 * HS]
        value = value.astype(BF)
        state.qk[:, head * LANES : (head + 1) * LANES] = tile
        state.v[:, head * HS : (head + 1) * HS] = value
        half = rows // 2
        for top in (0, half):
            scores = dot(tile[top : top + half, :HS], tile[:, HS:], (1, 1))
            scores = scores * SCALE + mask_ref[top : top + half, :]
            exponent = jnp.exp(scores - jnp.max(scores, axis=1, keepdims=True))
            share = exponent * (1.0 / jnp.sum(exponent, axis=1, keepdims=True))
            state.p[head, top : top + half, :] = share
            state.o[top : top + half, at + 3 * HS : at + HEAD] = dot(
                share.astype(BF), value
            ).astype(BF)
    wide_ref[:, :hidden] = dot(state.m[...], w_ref[:, attn : attn + hidden])

    def gelu(at, _):
        up = wide_ref[at, :hidden] + vec_ref[BIAS_UP : BIAS_UP + 1, :hidden]
        below = 0.5 + 0.5 * lax.erf(up * (0.5**0.5))
        state.gl[at, :] = (up * below).astype(BF)
        state.slope[at, :] = below + up * (jnp.exp(-0.5 * up * up) * 0.3989422804014327)

    over_rows(rows, gelu)
    part = dot(state.o[...], w_ref[:, :attn], (1, 1))
    part = part + dot(state.gl[...], w_ref[:, attn + hidden : attn + 2 * hidden], (1, 1))
    part_ref[...] = part.astype(BF)


def backward(
    state, grad_ref, vec_ref, w_ref, table_ref, part_ref, slab_ref, sums_ref, scratch
):
    low_ref, up_ref, qkv_ref, wide_ref, deep_ref = scratch
    rows, depth = state.normed.shape
    heads = state.v.shape[1] // HS
    attn, hidden = heads * HEAD, state.gl.shape[1]

    def lower(at, total):
        grad = grad_ref[at, :].astype(F32)
        low_ref[at, :] = grad.astype(BF)
        return total + by_eights(grad)

    total = over_rows(rows, lower, jnp.zeros((8, depth), F32))
    sums_ref[SUM_OUT : SUM_OUT + 1, :] = whole_sum(total) * 0.25
    low = low_ref[...]
    wide_ref[:, :hidden] = dot(low, w_ref[:, attn + hidden : attn + 2 * hidden])

    def through_gelu(at, total):
        up = (wide_ref[at, :hidden] * state.slope[at, :]).astype(BF)
        up_ref[at, :] = up
        return total + by_eights(up.astype(F32))

    total = over_rows(rows, through_gelu, jnp.zeros((8, hidden), F32))
    sums_ref[SUM_UP : SUM_UP + 1, :hidden] = whole_sum(total)
    wide_ref[...] = dot(low, w_ref[:, :attn])
    for head in range(heads):
        at = head * HEAD
        tile = state.qk[:, head * LANES : (head + 1) * LANES]
        query, key = tile[:, :HS], tile[:, HS:]
        value = state.v[:, head * HS : (head + 1) * HS]
        out = wide_ref[:, at + 3 * HS : at + HEAD].astype(BF)
        half = rows // 2
        grad_value, grad_key, grad_query = 0.0, 0.0, []
        for top in (0, half):
            share = state.p[head, top : top + half, :]
            grad = dot(out[top : top + half], value, (1, 1))
            delta = jnp.sum(share * grad, axis=1, keepdims=True)
            low_scores = (share * (grad - delta)).astype(BF)
            grad_value = grad_value + dot(share.astype(BF), out[top : top + half], (0, 0))
            grad_query.append(dot(low_scores, key))
            grad_key = grad_key + dot(low_scores, query[top : top + half], (0, 0))
        both = jnp.concatenate([jnp.concatenate(grad_query, axis=0), grad_key], axis=1) * SCALE
        both = turned(both, table_ref[0], -table_ref[1], -table_ref[2])
        qkv_ref[:, at : at + LANES] = both.astype(BF)
        qkv_ref[:, at + LANES : at + HEAD] = jnp.concatenate(
            [grad_value, jnp.zeros_like(grad_value)], axis=1
        ).astype(BF)

    def count_qkv(at, total):
        return total + by_eights(qkv_ref[at, :].astype(F32))

    total = over_rows(rows, count_qkv, jnp.zeros((8, attn), F32))
    sums_ref[SUM_QKV : SUM_QKV + 1, :] = whole_sum(total)
    wide_ref[...] = dot(qkv_ref[...], w_ref[:, :attn], (1, 1))
    deep_ref[...] = dot(up_ref[...], w_ref[:, attn : attn + hidden], (1, 1))

    def through_norm(at, totals):
        first, second, normed = wide_ref[at, :], deep_ref[at, :], state.normed[at, :]
        part_ref[at, :] = (
            first * vec_ref[GAIN_A : GAIN_A + 1, :] + second * vec_ref[GAIN_B : GAIN_B + 1, :]
        ).astype(BF)
        new = (first * normed, second * normed, first, second)
        return tuple(old + by_eights(term) for old, term in zip(totals, new, strict=True))

    totals = over_rows(rows, through_norm, (jnp.zeros((8, depth), F32),) * 4)
    for row, total in enumerate(totals):
        sums_ref[SUM_GAIN_A + row : SUM_GAIN_A + row + 1, :] = whole_sum(total)
    slab = dot(state.a[...], qkv_ref[...], (0, 0)) + dot(low, state.o[...], (0, 0))
    slab_ref[:, :attn] = slab.astype(BF)
    slab_ref[:, attn : attn + hidden] = dot(state.m[...], up_ref[...], (0, 0)).astype(BF)
    slab_ref[:, attn + hidden : attn + 2 * hidden] = dot(low, state.gl[...], (0, 0)).astype(BF)


def first_kernel(layers, tokens_ref, w_ref, place_ref, table_ref, mask_ref, *rest):
    part_ref, vec_ref, *state, wide_ref = rest
    state = State(state)
    attn = state.o.shape[1]
    hidden = state.gl.shape[1]
    small = jnp.transpose(w_ref[:, attn + 2 * hidden :].astype(F32))
    at = 6 * layers
    biases = small[at : at + 4 * layers].astype(BF)
    bias_qkv = dot(biases[:layers], one_hot(place_ref, 0, attn), (1, 1)) + dot(
        biases[layers : 2 * layers], one_hot(place_ref, 1, attn), (1, 1)
    )
    bias_up = dot(biases[2 * layers : 3 * layers], one_hot(place_ref, 2, attn), (1, 1)) + dot(
        biases[3 * layers :], one_hot(place_ref, 3, attn), (1, 1)
    )
    for layer in range(layers):
        rows = small[6 * layer : 6 * layer + 6]
        vec_ref[layer, GAIN_A : SHIFT_B + 1, :] = rows[2:]
        vec_ref[layer, BIAS_QKV : BIAS_QKV + 1, :] = bias_qkv[layer : layer + 1]
        vec_ref[layer, BIAS_UP : BIAS_UP + 1, :] = bias_up[layer : layer + 1]
        vec_ref[layer, BIAS_OUT : BIAS_OUT + 1, :] = rows[0:1] + rows[1:2]
        vec_ref[layer, BIAS_OUT + 1 : VECTORS, :] = rows[0:1]

    def enter(at, _):
        normed, inv_std = row_norm(tokens_ref[at, :].astype(F32))
        state.normed[at, :] = normed
        state.inv_std[at, :] = inv_std

    over_rows(tokens_ref.shape[0], enter)
    forward(state, vec_ref.at[0], w_ref, table_ref, mask_ref, part_ref, wide_ref)


def last_kernel(
    tokens_ref, mine_ref, theirs_ref, other_ref, grad_ref, vec_ref, w_ref, table_ref, mask_ref, *rest
):
    ahead_ref, part_ref, slab_ref, sums_ref, hidden_ref, normed_ref, inv_std_ref, *rest = rest
    state, scratch = State([normed_ref, inv_std_ref, *rest[:8]]), rest[8:]
    own = mine_ref.shape[0]
    bias = vec_ref[0, BIAS_OUT : BIAS_OUT + 1, :]

    def keep(at, values):
        normed, inv_std = row_norm(values)
        normed_ref[at, :] = normed
        inv_std_ref[at, :] = inv_std

    def enter_own(at, _):
        total = mine_ref[at, :].astype(F32) + theirs_ref[at, :].astype(F32)
        values = tokens_ref[at, :].astype(F32) + total + bias
        hidden_ref[at, :] = values + vec_ref[1, BIAS_OUT : BIAS_OUT + 1, :]
        keep(at, values)

    def enter_other(at, _):
        there = pl.ds(pl.multiple_of(at.start + own, CHUNK), CHUNK)
        keep(there, tokens_ref[there, :].astype(F32) + other_ref[at, :].astype(F32) + bias)

    over_rows(own, enter_own)
    over_rows(own, enter_other)
    forward(state, vec_ref.at[1], w_ref, table_ref, mask_ref, ahead_ref, scratch[3])
    backward(
        state, grad_ref, vec_ref.at[1], w_ref, table_ref, part_ref, slab_ref, sums_ref, scratch
    )


def back_kernel(
    layers, grad_ref, mine_ref, theirs_ref, other_ref, normed_ref, inv_std_ref, later_ref, *rest
):
    vec_ref, w_ref, place_ref, table_ref, *rest = rest
    state, rest = State(rest[:10]), rest[10:]
    part_ref, slab_ref, kept_ref, sums_ref, below_ref, *scratch = rest
    own = mine_ref.shape[0]
    attn, hidden = state.o.shape[1], state.gl.shape[1]

    def enter_own(at, _):
        total = mine_ref[at, :].astype(F32) + theirs_ref[at, :].astype(F32)
        grad = row_norm_back(total, normed_ref[at, :], inv_std_ref[at, :])
        grad = grad + grad_ref[at, :].astype(F32)
        kept_ref[at, :] = grad
        below_ref[at, :] = grad

    def enter_other(at, _):
        there = pl.ds(pl.multiple_of(at.start + own, CHUNK), CHUNK)
        total = other_ref[at, :].astype(F32)
        grad = row_norm_back(total, normed_ref[there, :], inv_std_ref[there, :])
        below_ref[there, :] = grad + grad_ref[there, :].astype(F32)

    over_rows(own, enter_own)
    over_rows(own, enter_other)
    backward(
        state, below_ref, vec_ref.at[0], w_ref, table_ref, part_ref, slab_ref, sums_ref, scratch
    )
    both = [sums_ref, later_ref]
    pad = jnp.zeros((8 - layers, attn), F32)
    qkv = jnp.concatenate([ref[SUM_QKV : SUM_QKV + 1, :] for ref in both] + [pad], axis=0)
    up = jnp.concatenate([ref[SUM_UP : SUM_UP + 1, :] for ref in both] + [pad], axis=0)
    spread = [
        dot(values.astype(BF), one_hot(place_ref, at, attn))[:layers]
        for values, at in ((qkv, 0), (qkv, 1), (up, 2), (up, 3))
    ]
    small = [ref[: SUM_SHIFT_B + 1, :] for ref in both] + spread
    used = 9 * layers
    small = jnp.concatenate(small + [jnp.zeros((LANES - used, attn), F32)], axis=0)
    slab_ref[:, attn + 2 * hidden :] = jnp.transpose(small).astype(BF)


def call(kernel, outs, scratch, flops, *args):
    return pl.pallas_call(
        kernel,
        out_shape=outs,
        in_specs=[pl.BlockSpec(memory_space=pltpu.VMEM)] * len(args),
        out_specs=jax.tree.map(lambda _: pl.BlockSpec(memory_space=pltpu.VMEM), outs),
        scratch_shapes=scratch,
        compiler_params=pltpu.CompilerParams(vmem_limit_bytes=VMEM_BYTES),
        cost_estimate=pl.CostEstimate(flops=flops, bytes_accessed=8_000_000, transcendentals=0),
    )(*args)


def own_rows_summed(part):
    half = part.shape[0] // 2
    mine = part[:half].astype(F32) + other_core(part[half:]).astype(F32)
    mine = mine.astype(BF)
    return mine, other_half(mine)


def other_rows(mine, theirs):
    return other_core((mine.astype(F32) + theirs.astype(F32)).astype(BF))


def rotation(positions):
    exponents = jnp.arange(ROT // 2, dtype=F32) * (2.0 / ROT)
    inverse = jnp.power(10000.0, -exponents)
    phase = positions.astype(F32)[:, None] * inverse[None, :]
    cos, sin = jnp.cos(phase), jnp.sin(phase)
    none = jnp.zeros_like(sin)
    rest = jnp.zeros((positions.shape[0], HS - ROT), F32)
    tables = [[cos, cos, rest + 1.0], [-sin, none, rest], [none, sin, rest]]
    return jnp.stack([jnp.concatenate(t + t, axis=1) for t in tables])


def bias_places(core, owners, depth, width_qkv, width_up, shard_qkv, shard_up):
    owner = jnp.arange(owners * depth, dtype=jnp.int32) // depth
    inner = jnp.arange(owners * depth, dtype=jnp.int32) % depth
    rows = []
    for width, shard, head in ((width_qkv, shard_qkv, 3 * HS), (width_up, shard_up, None)):
        for first in (0, depth):
            at = owner * shard + inner + first - core * width
            fits = (inner + first < shard) & (at >= 0) & (at < width)
            if head is not None:
                at = at // head * HEAD + at % head
            rows.append(jnp.where(fits, at, -1))
    return jnp.stack(rows + rows)


def per_device(
    tokens,
    cotangent,
    doc_lens,
    block_pos,
    w_qkv,
    w_out,
    w_up,
    w_down,
    b_qkv,
    b_up,
    out_bias,
    norm_gain,
    norm_bias,
):
    row_count = tokens.shape[0]
    block_rows = row_count // 2
    core = lax.axis_index("ctx")
    owners = lax.axis_size("fsdp")
    layers, depth, width_qkv = w_qkv.shape
    width_qkv, width_out, hidden = (n // 2 for n in (width_qkv, w_out.shape[1], w_up.shape[2]))
    heads = width_out // HS
    attn = heads * HEAD
    width = attn + 2 * hidden
    wide = owners * depth
    rows = 2 * row_count

    def mine_of(array, axis, size):
        return lax.dynamic_slice_in_dim(array, core * size, size, axis)

    qkv = mine_of(w_qkv, 2, width_qkv).reshape(layers, depth, heads, 3 * HS)
    out = mine_of(w_out, 1, width_out).transpose(0, 2, 1).reshape(layers, depth, heads, HS)
    slabs = jnp.concatenate(
        [
            jnp.concatenate([qkv, out], axis=3).reshape(layers, depth, attn),
            mine_of(w_up, 2, hidden),
            mine_of(w_down, 1, hidden).transpose(0, 2, 1),
        ],
        axis=2,
    )
    vectors = jnp.concatenate([out_bias, norm_gain, norm_bias], axis=1).reshape(-1, depth)
    bias_qkv = jnp.pad(b_qkv, ((0, 0), (0, 2 * depth - b_qkv.shape[1])))
    biases = [b[:, at : at + depth] for b in (bias_qkv, b_up) for at in (0, depth)]
    small = jnp.concatenate([vectors, *biases], axis=0)
    small = jnp.pad(small, ((0, LANES - small.shape[0]), (0, 0))).T
    first = to_all(jnp.concatenate([slabs[0], small], axis=1)).reshape(wide, -1)
    second = to_all(slabs[1]).reshape(wide, -1)

    both = jnp.stack([tokens, cotangent])
    start, grad = jnp.concatenate([both, other_core(both)], axis=1)
    offsets = jnp.arange(block_rows, dtype=jnp.int32)
    positions = (block_pos[0][:, None] * block_rows + offsets[None, :]).reshape(2, row_count)
    positions = jnp.where(core == 0, positions, positions[::-1]).reshape(-1)
    doc_ends = jnp.cumsum(doc_lens[0])
    docs = jnp.sum((positions[:, None] >= doc_ends[None, :]).astype(jnp.int32), axis=1)
    allowed = (docs[:, None] == docs[None, :]) & (positions[None, :] <= positions[:, None])
    mask = jnp.where(allowed, 0.0, MASKED).astype(F32)
    table = rotation(positions)
    place = bias_places(core, owners, depth, width_qkv, hidden, b_qkv.shape[1], b_up.shape[1])

    sds = jax.ShapeDtypeStruct
    flops = 2 * rows * wide * width
    part, vec, *state = call(
        functools.partial(first_kernel, layers),
        (sds((rows, wide), BF), sds((layers, VECTORS, wide), F32), *State.shapes(rows, wide, heads, hidden)),
        [pltpu.VMEM((rows, wide), F32)],
        flops,
        start,
        first,
        place,
        table,
        mask,
    )
    mine, theirs = own_rows_summed(part)
    kept = State.shapes(rows, wide, heads, hidden)
    scratch = [
        pltpu.VMEM((rows, wide), BF),
        pltpu.VMEM((rows, hidden), BF),
        pltpu.VMEM((rows, attn), BF),
        pltpu.VMEM((rows, wide), F32),
        pltpu.VMEM((rows, wide), F32),
    ]
    ahead, part, slab, later_sums, result, normed, inv_std = call(
        last_kernel,
        (
            sds((rows, wide), BF),
            sds((rows, wide), BF),
            sds((wide, width), BF),
            sds((8, wide), F32),
            sds((row_count, wide), F32),
            *kept[:2],
        ),
        [pltpu.VMEM(s.shape, s.dtype) for s in kept[2:]] + scratch,
        3 * flops,
        start,
        mine,
        theirs,
        other_rows(mine, theirs),
        grad,
        vec,
        second,
        table,
        mask,
    )
    pieces = [None, summed(slab.reshape(owners, depth, -1))]
    mine, theirs = own_rows_summed(part)
    part, slab, grad_below = call(
        functools.partial(back_kernel, layers),
        (sds((rows, wide), BF), sds((wide, width + LANES), BF), sds((row_count, wide), F32)),
        [pltpu.VMEM((8, wide), F32), pltpu.VMEM((rows, wide), F32)] + scratch,
        2 * flops,
        grad,
        mine,
        theirs,
        other_rows(mine, theirs),
        normed,
        inv_std,
        later_sums,
        vec,
        first,
        place,
        table,
        *state,
    )
    pieces[0] = summed(slab.reshape(owners, depth, -1))
    mine, theirs = own_rows_summed(ahead)
    result = (result + mine.astype(F32) + theirs.astype(F32)).astype(BF)
    mine, theirs = own_rows_summed(part)
    total = mine.astype(F32) + theirs.astype(F32)
    total = row_norm_back(total, state[0][:row_count], state[1][:row_count])
    grad_tokens = (grad_below + total).astype(BF)

    small = pieces[0][:, width:].T[: 9 * layers].astype(BF).astype(F32)
    vectors = small[: 5 * layers]
    vectors = vectors + other_half(vectors)
    small = jnp.concatenate([vectors, small[5 * layers :]], axis=0)
    small = small + other_core(small)
    vectors = small[: 5 * layers].reshape(layers, 5, depth)
    low, high, up_low, up_high = (small[at * layers : (at + 1) * layers] for at in (5, 6, 7, 8))
    matrices = jnp.stack([pieces[0][:, :width], pieces[1]]).astype(BF)
    theirs = other_core(matrices)
    low_half = jnp.where(core == 0, matrices, theirs).astype(F32)
    high_half = jnp.where(core == 0, theirs, matrices).astype(F32)
    halves = (low_half, high_half)
    heads_of = [h[:, :, :attn].reshape(layers, depth, heads, HEAD) for h in halves]
    grad_qkv = jnp.concatenate(
        [h[..., : 3 * HS].reshape(layers, depth, width_qkv) for h in heads_of], axis=2
    )
    grad_out = jnp.concatenate(
        [h[..., 3 * HS :].reshape(layers, depth, width_out) for h in heads_of], axis=2
    )
    grad_up = jnp.concatenate([h[:, :, attn : attn + hidden] for h in halves], axis=2)
    grad_down = jnp.concatenate([h[:, :, attn + hidden :] for h in halves], axis=2)
    return (
        result,
        grad_tokens,
        grad_qkv,
        grad_out.transpose(0, 2, 1),
        grad_up,
        grad_down.transpose(0, 2, 1),
        jnp.concatenate([low, high], axis=1)[:, : b_qkv.shape[1]],
        jnp.concatenate([up_low, up_high], axis=1),
        jnp.stack([vectors[:, 0], vectors[:, 0]], axis=1),
        vectors[:, 1:3],
        vectors[:, 3:5],
    )


def solution(mesh):
    in_specs = (
        P(("fsdp", "ctx"), None),
        P(("fsdp", "ctx"), None),
        P("fsdp", None),
        P("fsdp", None),
        P(None, "fsdp", "tp"),
        P(None, "tp", "fsdp"),
        P(None, "fsdp", "tp"),
        P(None, "tp", "fsdp"),
        P(None, ("tp", "fsdp")),
        P(None, ("tp", "fsdp")),
        P(None, None, "fsdp"),
        P(None, None, "fsdp"),
        P(None, None, "fsdp"),
    )
    out_specs = (P(("fsdp", "ctx"), None), P(("fsdp", "ctx"), None), *in_specs[4:])
    return jax.shard_map(
        per_device, mesh=mesh, in_specs=in_specs, out_specs=out_specs, check_vma=False
    )
```

time: 340 us -> 289 us (0.85)
  matrix products: 71.5 us -> 0 us
  blocking collectives: 0 us -> 53.3 us
  local copies, waits for them, and re-layouts: 69.4 us -> 21.2 us
  Pallas kernels: 0 us -> 36.5 us
  other arithmetic: 33.7 us -> 15 us
  waiting for transfers between devices: 104 us -> 117 us
  starting transfers between devices: 56.6 us -> 43.8 us
    dot_general x34 -> x0, matrix products: 67.3 us -> none  [the longest x8 21.6 us: product(): return jnp.dot(left, right, preferred_element_type=F32)]
    all_to_all x0 -> x1, blocking collectives: none -> 53.3 us  [to_all(): lax.all_to_all(jnp.broadcast_to(block[None], (count, *block.shape)), 'fsd...]
    ppermute x5, waiting for transfers between devices: 61.7 us -> 111 us  [other_half(): return lax.ppermute(values, 'tp', SWAP)]
    all_to_all x2 -> x1, waiting for transfers between devices: 40.7 us -> 0.01 us  [to_all(): lax.all_to_all(jnp.broadcast_to(block[None], (count, *block.shape)), 'fsd...]
    pallas_call x0 -> x3, Pallas kernels: none -> 36.5 us  [call(): pl.pallas_call(kernel, out_shape=outs, in_specs=[pl.BlockSpec(memory_spac...]
    concatenate x5 -> x4, local copies, waits for them, and re-layouts: 19 us -> 0.84 us  [the longest x3 0.75 us: rotation(): return jnp.stack([jnp.concatenate(t + t, axis=1) for t in tables])]
    all_to_all x2 -> x1, starting transfers between devices: 19.3 us -> 4.97 us  [to_all(): lax.all_to_all(jnp.broadcast_to(block[None], (count, *block.shape)), 'fsd...]
    reshape x19 -> x10, local copies, waits for them, and re-layouts: 9.13 us -> 0.98 us  [the longest x2 0.29 us: per_device(): h[..., :3 * HS].reshape(layers, depth, width_qkv)]
  transfers between devices with their start and end apart: 18 -> 17, of which waited for: 8 -> 11; matrix products, arithmetic and copies ran while one was open for 33% -> 4% of each run, Pallas kernels for 0% -> 8%
where the time goes in v2:
time: 289 us; the launch traced here: 288 us
  waiting for transfers between devices  117 us (40%)
  blocking collectives  53.3 us (18%)
  starting transfers between devices  43.8 us (15%)
  Pallas kernels  36.5 us (13%)
  local copies, waits for them, and re-layouts  21.2 us (7%)
  other arithmetic  15 us (5%)
    ppermute x5, waiting for transfers between devices, other_half(): return lax.ppermute(values, 'tp', SWAP)  111 us
    all_to_all x1, blocking collectives, to_all(): lax.all_to_all(jnp.broadcast_to(block[None], (count, *block.shape)), 'fsd...  53.3 us
    pallas_call x3, Pallas kernels, call(): pl.pallas_call(kernel, out_shape=outs, in_specs=[pl.BlockSpec(memory_spac...  36.5 us
    all_to_all x2, starting transfers between devices, summed(): got = lax.all_to_all(blocks, 'fsdp', 0, 0, tiled=True)  22.4 us
    unnamed x49, local copies, waits for them, and re-layouts  10.3 us
    ppermute x5, starting transfers between devices, other_half(): return lax.ppermute(values, 'tp', SWAP)  8.71 us
    ppermute x9, starting transfers between devices, other_core(): return lax.ppermute(values, 'ctx', SWAP)  7.76 us
    ppermute x9, waiting for transfers between devices, other_core(): return lax.ppermute(values, 'ctx', SWAP)  6.52 us
  transfers between devices with their start and end apart: 17, of which 11 were waited for; matrix products, arithmetic and copies ran while one was open for 4% of the time, Pallas kernels for 8%

profile of v2, /device:TPU:1, one launch (start us, length us, event | category | flops | bytes accessed | tf_op | source)
XLA Modules:
  0.0 288.0 jit_solution(15416621583943741634)
XLA Ops:
  0.7 1.0 constant_dynamic-slice_fusion.1
  1.7 0.8 dynamic-slice_bitcast_fusion.1
  2.9 0.9 dynamic-slice_bitcast_fusion
  3.8 0.8 fusion.9
  4.8 0.8 copy.93
  5.6 0.7 pad_maximum_fusion.10
  6.5 0.7 copy.95
  7.6 53.3 %all_to_all.20 = bf16[32,24,2432]{2,1,0:T(8,128)(2,1)} all-to-all(bf16[32,24,2432]{2,1,0:T(8,128)(2,1)S(1)} %broadcast_in_dim.40), channel_id=1, replica_groups=mesh['fsdp'=32,'ctx'=2,'tp'=2] {'fsdp'}, dimensions={0} | all-to-all | bytes 7471104 | tf_op jit(solution)/shard_map/all_to_all | solution.py:37
  60.9 2.1 broadcast_in_dim.46
  63.0 5.0 %all-to-all-start.1 = ((bf16[32,24,2304]{2,1,0:T(8,128)(2,1)}), bf16[32,24,2304]{2,1,0:T(8,128)(2,1)}, u32[]{:S(2)}, u32[]{:S(2)}) async-start(bf16[32,24,2304]{2,1,0:T(8,128)(2,1)} %broadcast_in_dim.46), calls=%async_computation.1 | async-start | bytes 7077888 | tf_op jit(solution)/shard_map/all_to_all | solution.py:37
  68.0 2.9 %collective-permute-start = (bf16[2,128,768]{2,1,0:T(8,128)(2,1)S(1)}, bf16[2,128,768]{2,1,0:T(8,128)(2,1)S(1)}, u32[]{:S(2)}, u32[]{:S(2)}) collective-permute-start(bf16[2,128,768]{2,1,0:T(8,128)(2,1)S(1)} %pad_maximum_fusion.1), channel_id=1, source_target_pairs={{0,2},{2,0},{1,3},{3,1},{4,6},{6,4},{5,7},{7,5},{8,10},{10,8},{9,1... | collective-permute-start | bytes 1179656 | tf_op jit(solution)/shard_map/ppermute | solution.py:28
  73.5 9.4 %shard_map.212 = (bf16[256,768]{1,0:T(8,128)(2,1)S(1)}, f32[2,8,768]{2,1,0:T(8,128)S(1)}, f32[256,768]{1,0:T(8,128)}, f32[256,1]{1,0:T(8,128)S(1)}, bf16[256,768...) custom-call(bf16[256,768]{1,0:T(8,128)(2,1)S(1)} %get-tuple-element., ...), custom_call_target="tpu_custom_call" | custom-call | flops 905969664 | bytes 8000000 | tf_op jit(solution)/shard_map/pallas_call | solution.py:345
  84.3 1.4 collective-permute-done.1
  85.7 3.4 %collective-permute-start.2 = (bf16[128,768]{1,0:T(8,128)(2,1)S(1)}, bf16[128,768]{1,0:T(8,128)(2,1)S(1)}, u32[]{:S(2)}, u32[]{:S(2)}) collective-permute-start(bf16[128,768]{1,0:T(8,128)(2,1)S(1)} %add_convert_fusion.7.mine_ref), channel_id=1, source_target_pairs={{0,1},{1,0},{2,3},{3,2},{4,5},{5,4},{6,7},{7,6},{8,9},{9,8},{10,11... | collective-permute-start | bytes 589832 | tf_op jit(solution)/shard_map/ppermute | solution.py:32
  89.1 26.4 %collective-permute-done.2.theirs_ref = bf16[128,768]{1,0:T(8,128)(2,1)S(1)} collective-permute-done((bf16[128,768]{1,0:T(8,128)(2,1)S(1)}, bf16[128,768]{1,0:T(8,128)(2,1)S(1)}, u32[]{:S(2)}, u32[]{:S(2)}) %collective-permute-start.2) | collective-permute-done | bytes 196640 | tf_op jit(solution)/shard_map/ppermute | solution.py:32
  115.6 0.7 add_convert_fusion.6
  116.8 1.3 collective-permute-done.3.other_ref
  118.8 0.9 copy-done.7
  119.7 0.8 copy-done.15
  120.5 0.9 copy-done.18
  121.4 14.9 %shard_map.213 = (bf16[256,768]{1,0:T(8,128)(2,1)S(1)}, bf16[256,768]{1,0:T(8,128)(2,1)S(1)}, bf16[768,2304]{1,0:T(8,128)(2,1)}, f32[8,768]{1,0:T(8,128)S(1)}, f...) custom-call(bf16[256,768]{1,0:T(8,128)(2,1)S(1)} %get-tuple-element.115.tokens_ref, ...), custom_call_target="tpu_custom_call" | custom-call | flops 2717908992 | bytes 8000000 | tf_op jit(solution)/shard_map/pallas_call | solution.py:345
  136.3 0.7 copy-done.2
  137.0 0.8 copy-done.4
  138.4 8.5 %all-to-all-start.3 = ((bf16[32,24,2304]{2,1,0:T(8,128)(2,1)}), bf16[32,24,2304]{2,1,0:T(8,128)(2,1)}, u32[]{:S(2)}, u32[]{:S(2)}) async-start(bf16[32,24,2304]{2,1,0:T(8,128)(2,1)} %bitcast.46), calls=%async_computation.3 | async-start | bytes 7077888 | tf_op jit(solution)/shard_map/all_to_all | solution.py:43
  147.0 0.7 collective-permute-start.6
  147.7 1.1 collective-permute-done.6
  148.8 1.3 collective-permute-start.7
  150.2 34.6 %collective-permute-done.7.theirs_ref = bf16[128,768]{1,0:T(8,128)(2,1)S(1)} collective-permute-done((bf16[128,768]{1,0:T(8,128)(2,1)S(1)}, bf16[128,768]{1,0:T(8,128)(2,1)S(1)}, u32[]{:S(2)}, u32[]{:S(2)}) %collective-permute-start.7) | collective-permute-done | bytes 196640 | tf_op jit(solution)/shard_map/ppermute | solution.py:32
  185.4 1.2 collective-permute-done.8.other_ref
  186.6 0.9 copy-done.9
  187.5 0.9 copy-done.11
  188.4 0.9 copy-done.13
  189.3 12.3 %shard_map.214 = (bf16[256,768]{1,0:T(8,128)(2,1)S(1)}, bf16[768,2432]{1,0:T(8,128)(2,1)}, f32[128,768]{1,0:T(8,128)S(1)}) custom-call(bf16[256,768]{1,0:T(8,128)(2,1)S(1)} %get-tuple-element.114.grad_ref, bf16[128,768]{1,0:T(8,128)(2,1)S(1)} %add_convert_fusion.3.mine_ref, bf16[128,768]{1,0:T(8,128)(2,1)S(1)} %collective-permute-done.7.theirs_ref, ...), custom_call_target="tpu_custom_call" | custom-call | flops 1811939328 | bytes 8000000 | tf_op jit(solution)/shard_map/pallas_call | solution.py:345
  201.6 13.9 %all-to-all-start.2 = ((bf16[32,24,2432]{2,1,0:T(8,128)(2,1)}), bf16[32,24,2432]{2,1,0:T(8,128)(2,1)}, u32[]{:S(2)}, u32[]{:S(2)}) async-start(bf16[32,24,2432]{2,1,0:T(8,128)(2,1)} %bitcast.45), calls=%async_computation.2 | async-start | bytes 7471104 | tf_op jit(solution)/shard_map/all_to_all | solution.py:43
  215.6 0.7 collective-permute-start.4
  216.5 0.8 collective-permute-done.4
  217.4 3.0 %collective-permute-start.5 = (bf16[128,768]{1,0:T(8,128)(2,1)S(1)}, bf16[128,768]{1,0:T(8,128)(2,1)S(1)}, u32[]{:S(2)}, u32[]{:S(2)}) collective-permute-start(bf16[128,768]{1,0:T(8,128)(2,1)S(1)} %add_convert_fusion.5), channel_id=1, source_target_pairs={{0,1},{1,0},{2,3},{3,2},{4,5},{5,4},{6,7},{7,6},{8,9},{9,8},{10,11... | collective-permute-start | bytes 589832 | tf_op jit(solution)/shard_map/ppermute | solution.py:32
  221.0 34.4 %collective-permute-done.5 = bf16[128,768]{1,0:T(8,128)(2,1)S(1)} collective-permute-done((bf16[128,768]{1,0:T(8,128)(2,1)S(1)}, bf16[128,768]{1,0:T(8,128)(2,1)S(1)}, u32[]{:S(2)}, u32[]{:S(2)}) %collective-permute-start.5) | collective-permute-done | bytes 196640 | tf_op jit(solution)/shard_map/ppermute | solution.py:32
  255.5 0.7 add_convert_fusion.4
  256.2 11.5 %collective-permute-done.10 = bf16[128,768]{1,0:T(8,128)(2,1)S(1)} collective-permute-done((bf16[128,768]{1,0:T(8,128)(2,1)S(1)}, bf16[128,768]{1,0:T(8,128)(2,1)S(1)}, u32[]{:S(2)}, u32[]{:S(2)}) %collective-permute-start.10) | collective-permute-done | bytes 196640 | tf_op jit(solution)/shard_map/ppermute | solution.py:32
  267.9 0.8 add_convert_fusion
  268.7 2.5 reduce.1
  271.2 2.6 reduce
  274.4 3.6 %collective-permute-done.12 = f32[10,24]{0,1:T(8,128)S(1)} collective-permute-done((f32[10,24]{0,1:T(8,128)S(1)}, f32[10,24]{0,1:T(8,128)S(1)}, u32[]{:S(2)}, u32[]{:S(2)}) %collective-permute-start.12) | collective-permute-done | bytes 992 | tf_op jit(solution)/shard_map/ppermute | solution.py:32
  278.1 2.0 collective-permute-start.13
  285.1 0.7 maximum_bitcast_fusion
  285.8 0.7 pad_maximum_fusion.3
  287.3 0.8 pad_maximum_fusion.6
  (142 shorter events, 14.8 us)
Async XLA Ops:
  0.6 2.2 copy-start
  63.0 5.0 %copy-start.20 = (bf16[128,768]{1,0:T(8,128)(2,1)S(1)}, bf16[128,768]{1,0:T(8,128)(2,1)}, u32[]{:S(2)}) copy-start(bf16[128,768]{1,0:T(8,128)(2,1)} %param.14) | copy-start | bytes 589828
  63.0 5.0 %copy-start.21 = (bf16[128,768]{1,0:T(8,128)(2,1)S(1)}, bf16[128,768]{1,0:T(8,128)(2,1)}, u32[]{:S(2)}) copy-start(bf16[128,768]{1,0:T(8,128)(2,1)} %param.13) | copy-start | bytes 589828
  63.0 8.0 %copy-start.22 = (s32[1,4]{1,0:T(1,128)S(1)}, s32[1,4]{1,0:T(1,128)}, u32[]{:S(2)}) copy-start(s32[1,4]{1,0:T(1,128)} %param.16) | copy-start | bytes 52
  63.0 8.4 %copy-start.23 = (s32[1,4]{1,0:T(1,128)S(1)}, s32[1,4]{1,0:T(1,128)}, u32[]{:S(2)}) copy-start(s32[1,4]{1,0:T(1,128)} %param.15) | copy-start | bytes 52
  63.0 53.8 %all-to-all-start.1 = ((bf16[32,24,2304]{2,1,0:T(8,128)(2,1)}), bf16[32,24,2304]{2,1,0:T(8,128)(2,1)}, u32[]{:S(2)}, u32[]{:S(2)}) async-start(bf16[32,24,2304]{2,1,0:T(8,128)(2,1)} %broadcast_in_dim.46), calls=%async_computation.1 | async-start | bytes 7077888 | tf_op jit(solution)/shard_map/all_to_all | solution.py:37
  68.0 5.3 %collective-permute-start = (bf16[2,128,768]{2,1,0:T(8,128)(2,1)S(1)}, bf16[2,128,768]{2,1,0:T(8,128)(2,1)S(1)}, u32[]{:S(2)}, u32[]{:S(2)}) collective-permute-start(bf16[2,128,768]{2,1,0:T(8,128)(2,1)S(1)} %pad_maximum_fusion.1), channel_id=1, source_target_pairs={{0,2},{2,0},{1,3},{3,1},{4,6},{6,4},{5,7},{7,5},{8,10},{10,8},{9,1... | collective-permute-start | bytes 1179656 | tf_op jit(solution)/shard_map/ppermute | solution.py:28
  82.8 0.7 copy-start.8
  83.5 0.6 copy-start.14
  84.1 31.4 %copy-start.1 = (bf16[256,768]{1,0:T(8,128)(2,1)}, bf16[256,768]{1,0:T(8,128)(2,1)S(1)}, u32[]{:S(2)}) copy-start(bf16[256,768]{1,0:T(8,128)(2,1)S(1)} %get-tuple-element.49.rest_12_) | copy-start | bytes 1179652
  84.1 32.2 %copy-start.10 = (bf16[256,192]{1,0:T(8,128)(2,1)}, bf16[256,192]{1,0:T(8,128)(2,1)S(1)}, u32[]{:S(2)}) copy-start(bf16[256,192]{1,0:T(8,128)(2,1)S(1)} %get-tuple-element.46.rest_9_) | copy-start | bytes 294916
  84.2 1.5 collective-permute-start.1
  85.7 29.8 %collective-permute-start.2 = (bf16[128,768]{1,0:T(8,128)(2,1)S(1)}, bf16[128,768]{1,0:T(8,128)(2,1)S(1)}, u32[]{:S(2)}, u32[]{:S(2)}) collective-permute-start(bf16[128,768]{1,0:T(8,128)(2,1)S(1)} %add_convert_fusion.7.mine_ref), channel_id=1, source_target_pairs={{0,1},{1,0},{2,3},{3,2},{4,5},{5,4},{6,7},{7,6},{8,9},{9,8},{10,11... | collective-permute-start | bytes 589832 | tf_op jit(solution)/shard_map/ppermute | solution.py:32
  115.5 3.2 %copy-start.6 = (bf16[128,768]{1,0:T(8,128)(2,1)}, bf16[128,768]{1,0:T(8,128)(2,1)S(1)}, u32[]{:S(2)}) copy-start(bf16[128,768]{1,0:T(8,128)(2,1)S(1)} %collective-permute-done.2.theirs_ref) | copy-start | bytes 589828
  116.3 1.8 collective-permute-start.3
  118.1 0.7 copy-start.17
  118.7 0.9 copy-start.7
  119.7 0.8 copy-start.15
  120.5 0.9 copy-start.18
  136.3 0.7 copy-start.2
  137.0 0.8 copy-start.4
  137.8 0.7 copy-start.12
  138.4 8.5 %copy-start.3 = (bf16[256,768]{1,0:T(8,128)(2,1)S(1)}, bf16[256,768]{1,0:T(8,128)(2,1)}, u32[]{:S(2)}) copy-start(bf16[256,768]{1,0:T(8,128)(2,1)} %copy-done.2) | copy-start | bytes 1179652
  138.4 48.2 %copy-start.16 = (f32[2,8,768]{2,1,0:T(8,128)S(1)}, f32[2,8,768]{2,1,0:T(8,128)}, u32[]{:S(2)}) copy-start(f32[2,8,768]{2,1,0:T(8,128)} %copy-done.14) | copy-start | bytes 147460
  138.4 63.2 %all-to-all-start.3 = ((bf16[32,24,2304]{2,1,0:T(8,128)(2,1)}), bf16[32,24,2304]{2,1,0:T(8,128)(2,1)}, u32[]{:S(2)}, u32[]{:S(2)}) async-start(bf16[32,24,2304]{2,1,0:T(8,128)(2,1)} %bitcast.46), calls=%async_computation.3 | async-start | bytes 7077888 | tf_op jit(solution)/shard_map/all_to_all | solution.py:43
  147.0 1.8 collective-permute-start.6
  148.8 36.0 %collective-permute-start.7 = (bf16[128,768]{1,0:T(8,128)(2,1)S(1)}, bf16[128,768]{1,0:T(8,128)(2,1)S(1)}, u32[]{:S(2)}, u32[]{:S(2)}) collective-permute-start(bf16[128,768]{1,0:T(8,128)(2,1)S(1)} %add_convert_fusion.3.mine_ref), channel_id=1, source_target_pairs={{0,1},{1,0},{2,3},{3,2},{4,5},{5,4},{6,7},{7,6},{8,9},{9,8},{10,11... | collective-permute-start | bytes 589832 | tf_op jit(solution)/shard_map/ppermute | solution.py:32
  184.9 1.7 collective-permute-start.8
  186.6 0.9 copy-start.9
  187.5 0.9 copy-start.11
  188.4 0.9 copy-start.13
  201.6 53.8 %copy-start.5 = (f32[128,768]{1,0:T(8,128)S(1)}, f32[128,768]{1,0:T(8,128)}, u32[]{:S(2)}) copy-start(f32[128,768]{1,0:T(8,128)} %copy-done.4) | copy-start | bytes 1179652
  201.6 66.1 %copy-start.19 = (f32[256,768]{1,0:T(8,128)S(1)}, f32[256,768]{1,0:T(8,128)}, u32[]{:S(2)}) copy-start(f32[256,768]{1,0:T(8,128)} %get-tuple-element.41.rest_4_) | copy-start | bytes 2359300
  201.6 69.6 %all-to-all-start.2 = ((bf16[32,24,2432]{2,1,0:T(8,128)(2,1)}), bf16[32,24,2432]{2,1,0:T(8,128)(2,1)}, u32[]{:S(2)}, u32[]{:S(2)}) async-start(bf16[32,24,2432]{2,1,0:T(8,128)(2,1)} %bitcast.45), calls=%async_computation.2 | async-start | bytes 7471104 | tf_op jit(solution)/shard_map/all_to_all | solution.py:43
  215.6 1.8 collective-permute-start.4
  216.4 4.0 %collective-permute-start.9 = (bf16[128,768]{1,0:T(8,128)(2,1)S(1)}, bf16[128,768]{1,0:T(8,128)(2,1)S(1)}, u32[]{:S(2)}, u32[]{:S(2)}) collective-permute-start(bf16[128,768]{1,0:T(8,128)(2,1)S(1)} %slice.139), channel_id=1, source_target_pairs={{0,2},{2,0},{1,3},{3,1},{4,6},{6,4},{5,7},{7,5},{8,10},{10,8},{9,1... | collective-permute-start | bytes 589832 | tf_op jit(solution)/shard_map/ppermute | solution.py:28
  217.4 38.0 %collective-permute-start.5 = (bf16[128,768]{1,0:T(8,128)(2,1)S(1)}, bf16[128,768]{1,0:T(8,128)(2,1)S(1)}, u32[]{:S(2)}, u32[]{:S(2)}) collective-permute-start(bf16[128,768]{1,0:T(8,128)(2,1)S(1)} %add_convert_fusion.5), channel_id=1, source_target_pairs={{0,1},{1,0},{2,3},{3,2},{4,5},{5,4},{6,7},{7,6},{8,9},{9,8},{10,11... | collective-permute-start | bytes 589832 | tf_op jit(solution)/shard_map/ppermute | solution.py:32
  220.5 47.2 %collective-permute-start.10 = (bf16[128,768]{1,0:T(8,128)(2,1)S(1)}, bf16[128,768]{1,0:T(8,128)(2,1)S(1)}, u32[]{:S(2)}, u32[]{:S(2)}) collective-permute-start(bf16[128,768]{1,0:T(8,128)(2,1)S(1)} %add_convert_fusion.1), channel_id=1, source_target_pairs={{0,1},{1,0},{2,3},{3,2},{4,5},{5,4},{6,7},{7,6},{8,9},{9,8},{10,11... | collective-permute-start | bytes 589832 | tf_op jit(solution)/shard_map/ppermute | solution.py:32
  273.9 4.1 %collective-permute-start.12 = (f32[10,24]{0,1:T(8,128)S(1)}, f32[10,24]{0,1:T(8,128)S(1)}, u32[]{:S(2)}, u32[]{:S(2)}) collective-permute-start(f32[10,24]{0,1:T(8,128)S(1)} %bitcast.59), channel_id=1, source_target_pairs={{0,1},{1,0},{2,3},{3,2},{4,5},{5,4},{6,7},{7,6},{8,9},{9,8},{10,11... | collective-permute-start | bytes 2888 | tf_op jit(solution)/shard_map/ppermute | solution.py:32
  278.1 2.9 collective-permute-start.13
  280.1 3.8 %collective-permute-start.11 = (bf16[2,24,2304]{2,1,0:T(8,128)(2,1)S(1)}, bf16[2,24,2304]{2,1,0:T(8,128)(2,1)S(1)}, u32[]{:S(2)}, u32[]{:S(2)}) collective-permute-start(bf16[2,24,2304]{2,1,0:T(8,128)(2,1)S(1)} %pad_maximum_fusion.5), channel_id=1, source_target_pairs={{0,2},{2,0},{1,3},{3,1},{4,6},{6,4},{5,7},{7,5},{8,10},{10,8},{9,1... | collective-permute-start | bytes 663560 | tf_op jit(solution)/shard_map/ppermute | solution.py:28

commit v3 on v2

v3 whole, which is shorter than its diff:
```python
import functools

import jax
import jax.numpy as jnp
from jax import lax
from jax.experimental import pallas as pl
from jax.experimental.pallas import tpu as pltpu
from jax.sharding import PartitionSpec as P

HS = 64
ROT = 16
EPSILON = 1e-05
MASKED = -1e30
F32 = jnp.float32
BF = jnp.bfloat16
SWAP = [(0, 1), (1, 0)]
NEAR = 4
LANES = 128
CHUNK = 128
HEAD = 4 * HS
SCALE = HS ** (-0.5)
VMEM_BYTES = 62 * 1024 * 1024
GAIN_A, GAIN_B, SHIFT_A, SHIFT_B, BIAS_QKV, BIAS_UP, BIAS_OUT = range(7)
VECTORS = 8
SUM_OUT, SUM_GAIN_A, SUM_GAIN_B, SUM_SHIFT_A, SUM_SHIFT_B, SUM_QKV, SUM_UP = range(7)


def other_core(values):
    return lax.ppermute(values, "ctx", SWAP)


def other_half(values):
    return lax.ppermute(values, "tp", SWAP)


def other_core_and_half(values):
    return lax.ppermute(values, ("ctx", "tp"), [(0, 3), (1, 2), (2, 1), (3, 0)])


def near_group(values):
    owners = lax.axis_size("fsdp")
    return lax.ppermute(values, "fsdp", [(f, f ^ NEAR) for f in range(owners)])


def near_other_half(values):
    owners = lax.axis_size("fsdp")
    pairs = [(2 * f + t, 2 * (f ^ NEAR) + 1 - t) for f in range(owners) for t in (0, 1)]
    return lax.ppermute(values, ("fsdp", "tp"), pairs)


def exchanged(blocks):
    return lax.all_to_all(blocks, "fsdp", 0, 0, tiled=True)


def dot(left, right, along=(1, 0)):
    dims = (((along[0],), (along[1],)), ((), ()))
    return lax.dot_general(left, right, dims, preferred_element_type=F32)


def over_rows(rows, step, carry=None, start=0):
    def body(at, kept):
        return step(pl.ds(pl.multiple_of(at * CHUNK, CHUNK), CHUNK), kept)

    return lax.fori_loop(start // CHUNK, rows // CHUNK, body, carry)


def by_eights(values):
    return values.reshape(-1, 8, values.shape[-1]).sum(axis=0)


def whole_sum(eights):
    return jnp.sum(eights, axis=0, keepdims=True)


def turned(tile, cos, left, right):
    return (
        tile * cos
        + pltpu.roll(tile, LANES - ROT // 2, 1) * left
        + pltpu.roll(tile, ROT // 2, 1) * right
    )


def row_norm(values):
    centered = values - jnp.mean(values, axis=-1, keepdims=True)
    inv_std = lax.rsqrt(jnp.mean(centered * centered, axis=-1, keepdims=True) + EPSILON)
    return centered * inv_std, inv_std


def row_norm_back(total, normed, inv_std):
    return inv_std * (
        total
        - jnp.mean(total, axis=-1, keepdims=True)
        - normed * jnp.mean(total * normed, axis=-1, keepdims=True)
    )


def one_hot(place_ref, at, width):
    rows = lax.broadcasted_iota(jnp.int32, (width, place_ref.shape[1]), 0)
    return (rows == place_ref[at : at + 1, :]).astype(F32).astype(BF)


class Slab:
    def __init__(self, far_ref, heads_ref, w_ref, arrived):
        attn, width = heads_ref.shape[1], heads_ref.shape[1] + w_ref.shape[1]
        self.heads_ref, self.w_ref = heads_ref, w_ref
        self.copies = [
            pltpu.make_async_copy(far_ref.at[:, :attn], heads_ref, arrived.at[0]),
            pltpu.make_async_copy(far_ref.at[:, attn:width], w_ref, arrived.at[1]),
        ]
        for copy in self.copies:
            copy.start()

    def wait(self):
        for copy in self.copies:
            copy.wait()
        return self.heads_ref, self.w_ref

    def give(self, far_ref, sent):
        attn, width = self.heads_ref.shape[1], self.heads_ref.shape[1] + self.w_ref.shape[1]
        copies = [
            pltpu.make_async_copy(self.heads_ref, far_ref.at[:, :attn], sent.at[0]),
            pltpu.make_async_copy(self.w_ref, far_ref.at[:, attn:width], sent.at[1]),
        ]
        for copy in copies:
            copy.start()
        for copy in copies:
            copy.wait()


class Copies:
    def __init__(self, semaphores):
        self.semaphores, self.started = semaphores, []

    def start(self, src, dst):
        copy = pltpu.make_async_copy(src, dst, self.semaphores.at[len(self.started)])
        copy.start()
        self.started.append(copy)

    def wait(self, begin=0, end=None):
        for copy in self.started[begin:end]:
            copy.wait()


class State:
    names = ("normed", "inv_std", "a", "m", "qk", "v", "p", "o", "gl", "slope")

    def __init__(self, refs, copies=None, far=()):
        for name, ref in zip(self.names, refs, strict=True):
            setattr(self, name, ref)
        self.copies, self.far = copies, dict(zip(self.names, far))

    def ready(self, *names):
        for name in names:
            if name in self.far:
                self.copies.start(getattr(self, name), self.far[name])

    @staticmethod
    def shapes(rows, depth, heads, hidden):
        group = rows // 2
        return (
            jax.ShapeDtypeStruct((rows, depth), F32),
            jax.ShapeDtypeStruct((rows, 1), F32),
            jax.ShapeDtypeStruct((group, depth), BF),
            jax.ShapeDtypeStruct((rows, depth), BF),
            jax.ShapeDtypeStruct((group, heads * 2 * HS), BF),
            jax.ShapeDtypeStruct((group, heads * HS), BF),
            jax.ShapeDtypeStruct((heads, group, group), F32),
            jax.ShapeDtypeStruct((group, heads * HEAD), BF),
            jax.ShapeDtypeStruct((rows, hidden), BF),
            jax.ShapeDtypeStruct((rows, hidden), F32),
        )


def places(rows):
    quarter = rows // 4
    return [(0, 0, 0), (quarter, 1, 0), (2 * quarter, 0, quarter), (3 * quarter, 1, quarter)]


def forward(state, vec_ref, slab, near_copies, table_ref, mask_ref, parts, wide_ref):
    rows, depth = state.normed.shape
    group = rows // 2
    heads = state.v.shape[1] // HS
    hidden = state.gl.shape[1]

    def affine_a(at, _):
        state.a[at, :] = (
            state.normed[at, :] * vec_ref[GAIN_A : GAIN_A + 1, :]
            + vec_ref[SHIFT_A : SHIFT_A + 1, :]
        ).astype(BF)

    def affine_b(at, _):
        state.m[at, :] = (
            state.normed[at, :] * vec_ref[GAIN_B : GAIN_B + 1, :]
            + vec_ref[SHIFT_B : SHIFT_B + 1, :]
        ).astype(BF)

    state.ready("normed", "inv_std")
    over_rows(group, affine_a)
    over_rows(rows, affine_b)
    state.ready("a", "m")
    heads_ref, w_ref = slab.wait()
    near_copies.wait()
    wide_ref[:group, :] = dot(state.a[...], heads_ref[...])
    state.o[...] = jnp.zeros_like(state.o)
    for head in range(heads):
        at = head * HEAD
        bias = vec_ref[BIAS_QKV : BIAS_QKV + 1, at : at + HEAD]
        tile = wide_ref[:group, at : at + LANES] + bias[:, :LANES]
        tile = turned(tile, table_ref[0], table_ref[1], table_ref[2]).astype(BF)
        value = wide_ref[:group, at + 2 * HS : at + 3 * HS] + bias[:, 2 * HS : 3 * HS]
        value = value.astype(BF)
        state.qk[:, head * LANES : (head + 1) * LANES] = tile
        state.v[:, head * HS : (head + 1) * HS] = value
        half = group // 2
        for top in (0, half):
            scores = dot(tile[top : top + half, :HS], tile[:, HS:], (1, 1))
            scores = scores * SCALE + mask_ref[top : top + half, :]
            exponent = jnp.exp(scores - jnp.max(scores, axis=1, keepdims=True))
            share = exponent * (1.0 / jnp.sum(exponent, axis=1, keepdims=True))
            state.p[head, top : top + half, :] = share
            state.o[top : top + half, at + 3 * HS : at + HEAD] = dot(
                share.astype(BF), value
            ).astype(BF)
    state.ready("qk", "v", "p", "o")
    wide_ref[:, :hidden] = dot(state.m[...], w_ref[:, :hidden])

    def gelu(at, _):
        up = wide_ref[at, :hidden] + vec_ref[BIAS_UP : BIAS_UP + 1, :hidden]
        below = 0.5 + 0.5 * lax.erf(up * (0.5**0.5))
        state.gl[at, :] = (up * below).astype(BF)
        state.slope[at, :] = below + up * (jnp.exp(-0.5 * up * up) * 0.3989422804014327)

    over_rows(rows, gelu)
    state.ready("gl", "slope")
    down = w_ref[:, hidden : 2 * hidden]
    part = dot(state.o[...], heads_ref[...], (1, 1))
    half = group // 2
    part = (part + dot(state.gl[:group, :], down, (1, 1))).astype(BF)
    near = dot(state.gl[group:, :], down, (1, 1)).astype(BF)
    for core, part_ref in enumerate(parts):
        at = core * half
        part_ref[:half, :] = part[at : at + half]
        part_ref[half:, :] = near[at : at + half]


def backward(
    state, grad_ref, vec_ref, slab, table_ref, parts, sums_ref, scratch, put, far_parts
):
    low_ref, up_ref, qkv_ref, wide_ref, deep_ref = scratch
    heads_ref, w_ref = slab.heads_ref, slab.w_ref
    rows, depth = state.normed.shape
    group = rows // 2
    heads = state.v.shape[1] // HS
    attn, hidden = heads * HEAD, state.gl.shape[1]

    def lower(at, total):
        grad = grad_ref[at, :].astype(F32)
        low_ref[at, :] = grad.astype(BF)
        return total + by_eights(grad)

    total = over_rows(rows, lower, jnp.zeros((8, depth), F32))
    sums_ref[SUM_OUT : SUM_OUT + 1, :] = whole_sum(total) * 0.125
    low = low_ref[...]
    wide_ref[:, :hidden] = dot(low, w_ref[:, hidden : 2 * hidden])

    def through_gelu(at, total):
        up = (wide_ref[at, :hidden] * state.slope[at, :]).astype(BF)
        up_ref[at, :] = up
        return total + by_eights(up.astype(F32))

    total = over_rows(rows, through_gelu, jnp.zeros((8, hidden), F32))
    sums_ref[SUM_UP : SUM_UP + 1, :hidden] = whole_sum(total)
    wide_ref[:group, :] = dot(low_ref[:group, :], heads_ref[...])
    for head in range(heads):
        at = head * HEAD
        tile = state.qk[:, head * LANES : (head + 1) * LANES]
        query, key = tile[:, :HS], tile[:, HS:]
        value = state.v[:, head * HS : (head + 1) * HS]
        out = wide_ref[:group, at + 3 * HS : at + HEAD].astype(BF)
        half = group // 2
        grad_value, grad_key, grad_query = 0.0, 0.0, []
        for top in (0, half):
            share = state.p[head, top : top + half, :]
            grad = dot(out[top : top + half], value, (1, 1))
            delta = jnp.sum(share * grad, axis=1, keepdims=True)
            low_scores = (share * (grad - delta)).astype(BF)
            grad_value = grad_value + dot(share.astype(BF), out[top : top + half], (0, 0))
            grad_query.append(dot(low_scores, key))
            grad_key = grad_key + dot(low_scores, query[top : top + half], (0, 0))
        both = jnp.concatenate([jnp.concatenate(grad_query, axis=0), grad_key], axis=1) * SCALE
        both = turned(both, table_ref[0], -table_ref[1], -table_ref[2])
        qkv_ref[:, at : at + LANES] = both.astype(BF)
        qkv_ref[:, at + LANES : at + HEAD] = jnp.concatenate(
            [grad_value, jnp.zeros_like(grad_value)], axis=1
        ).astype(BF)

    def count_qkv(at, total):
        return total + by_eights(qkv_ref[at, :].astype(F32))

    total = over_rows(group, count_qkv, jnp.zeros((8, attn), F32))
    sums_ref[SUM_QKV : SUM_QKV + 1, :] = whole_sum(total)
    wide_ref[:group, :] = dot(qkv_ref[...], heads_ref[...], (1, 1))
    deep_ref[...] = dot(up_ref[...], w_ref[:, :hidden], (1, 1))

    def through_norms(with_first, part_ref, begin, to):
        def step(at, totals):
            there, at = moved(at, to), moved(at, begin)
            second, normed = deep_ref[at, :], state.normed[at, :]
            total, new = second * vec_ref[GAIN_B : GAIN_B + 1, :], (second * normed, second)
            if with_first:
                first = wide_ref[at, :]
                total = total + first * vec_ref[GAIN_A : GAIN_A + 1, :]
                new = (*new, first * normed, first)
            part_ref[there, :] = total.astype(BF)
            return tuple(old + by_eights(term) for old, term in zip(totals, new, strict=True))

        return step

    totals = (jnp.zeros((8, depth), F32),) * 4
    for begin, core, to in places(rows):
        count = 4 if begin < group else 2
        step = through_norms(begin < group, parts[core], begin, to)
        totals = (*over_rows(rows // 4, step, totals[:count]), *totals[count:])
    for row, total in zip((SUM_GAIN_B, SUM_SHIFT_B, SUM_GAIN_A, SUM_SHIFT_A), totals, strict=True):
        sums_ref[row : row + 1, :] = whole_sum(total)
    for ref, far_part_ref in zip(parts, far_parts, strict=True):
        put.start(ref, far_part_ref)
    heads_grad = dot(state.a[...], qkv_ref[...], (0, 0))
    heads_grad = heads_grad + dot(low_ref[:group, :], state.o[...], (0, 0))
    heads_ref[...] = heads_grad.astype(BF)
    w_ref[:, :hidden] = dot(state.m[...], up_ref[...], (0, 0)).astype(BF)
    w_ref[:, hidden : 2 * hidden] = dot(low, state.gl[...], (0, 0)).astype(BF)


def first_kernel(layers, *refs):
    inputs, (far_ref, place_ref, far_table_ref, far_mask_ref, *rest) = refs[:4], refs[4:]
    far_parts, vec_ref, far_state, rest = rest[:2], rest[2], rest[3:13], rest[13:]
    parts, (table_ref, mask_ref, get, put), rest = rest[:2], rest[2:6], rest[6:]
    wide_ref, small_ref, heads_ref, w_ref, arrived, *state = rest
    get, put = Copies(get), Copies(put)
    state = State(state, put, far_state)
    attn = state.o.shape[1]
    hidden = state.gl.shape[1]
    columns = attn + 2 * hidden
    copy = pltpu.make_async_copy(far_ref.at[:, columns:], small_ref, arrived.at[2])
    copy.start()
    slab = Slab(far_ref, heads_ref, w_ref, arrived)
    get.start(far_table_ref, table_ref)
    get.start(far_mask_ref, mask_ref)
    copy.wait()
    small = jnp.transpose(small_ref[...].astype(F32))
    at = 6 * layers
    biases = small[at : at + 4 * layers].astype(BF)
    bias_qkv = dot(biases[:layers], one_hot(place_ref, 0, attn), (1, 1)) + dot(
        biases[layers : 2 * layers], one_hot(place_ref, 1, attn), (1, 1)
    )
    bias_up = dot(biases[2 * layers : 3 * layers], one_hot(place_ref, 2, hidden), (1, 1)) + dot(
        biases[3 * layers :], one_hot(place_ref, 3, hidden), (1, 1)
    )
    for layer in range(layers):
        rows = small[6 * layer : 6 * layer + 6]
        vec_ref[layer, GAIN_A : SHIFT_B + 1, :] = rows[2:]
        vec_ref[layer, BIAS_QKV : BIAS_QKV + 1, :] = bias_qkv[layer : layer + 1]
        vec_ref[layer, BIAS_UP : BIAS_UP + 1, :hidden] = bias_up[layer : layer + 1]
        vec_ref[layer, BIAS_OUT : BIAS_OUT + 1, :] = rows[0:1] + rows[1:2]
        vec_ref[layer, BIAS_OUT + 1 : VECTORS, :] = rows[0:1]

    for quarter, ref in enumerate(inputs):

        def enter(at, _, ref=ref, begin=quarter * ref.shape[0]):
            normed, inv_std = row_norm(ref[at, :].astype(F32))
            state.normed[moved(at, begin), :] = normed
            state.inv_std[moved(at, begin), :] = inv_std

        over_rows(ref.shape[0], enter)
    forward(state, vec_ref.at[0], slab, get, table_ref, mask_ref, parts, wide_ref)
    for ref, far_part_ref in zip(parts, far_parts, strict=True):
        put.start(ref, far_part_ref)
    put.wait()


def summed_rows(parts, at, there):
    mine, half, near, near_half = parts
    first = mine[at, :].astype(F32) + half[at, :].astype(F32)
    return first + (near[there, :].astype(F32) + near_half[there, :].astype(F32))


def moved(at, by):
    return pl.ds(pl.multiple_of(at.start + by, CHUNK), CHUNK)


def over_totals(parts, other_ref, inputs, take):
    own = parts[0].shape[0] // 2

    def own_core(at, _):
        take(at, summed_rows(parts, at, moved(at, own)), inputs[0][at, :])

    def near_own_core(at, _):
        total = summed_rows(parts, moved(at, own), at)
        take(moved(at, 2 * own), total, inputs[2][at, :])

    def other(at, _):
        take(moved(at, own), other_ref[at, :].astype(F32), inputs[1][at, :])

    def near_other(at, _):
        total = other_ref[moved(at, own), :].astype(F32)
        take(moved(at, 3 * own), total, inputs[3][at, :])

    for step in (own_core, near_own_core, other, near_other):
        over_rows(own, step)


def last_kernel(*refs):
    inputs, far_ends, parts, refs = refs[:4], refs[4:8], refs[8:12], refs[12:]
    other_ref, vec_ref, far_ref, far_table_ref, far_mask_ref, *rest = refs
    far_parts, rest = rest[:4], rest[4:]
    slab_ref, sums_ref, far_hidden_ref, far_normed_ref, far_inv_std_ref, *rest = rest
    (table_ref, mask_ref, hidden_ref, get, put), rest = rest[:5], rest[5:]
    ahead, back, rest = rest[:2], rest[2:4], rest[4:]
    get, put = Copies(get), Copies(put)
    state, rest = State(rest[:10], put, (far_normed_ref, far_inv_std_ref)), rest[10:]
    grad_ref, heads_ref, w_ref, arrived, *scratch = rest
    slab = Slab(far_ref, heads_ref, w_ref, arrived)
    get.start(far_table_ref, table_ref)
    get.start(far_mask_ref, mask_ref)
    own = hidden_ref.shape[0]
    for quarter, ref in enumerate(far_ends):
        get.start(ref, grad_ref.at[quarter * own : (quarter + 1) * own, :])
    bias = vec_ref[0, BIAS_OUT : BIAS_OUT + 1, :]

    def enter(at, total, tokens):
        values = tokens.astype(F32) + total + bias
        scratch[3][at, :] = values
        normed, inv_std = row_norm(values)
        state.normed[at, :] = normed
        state.inv_std[at, :] = inv_std

    over_totals(parts, other_ref, inputs, enter)
    hidden_ref[...] = scratch[3][:own, :] + vec_ref[1, BIAS_OUT : BIAS_OUT + 1, :]
    put.start(hidden_ref, far_hidden_ref)
    forward(state, vec_ref.at[1], slab, get, table_ref, mask_ref, ahead, scratch[3])
    for ref, far_part_ref in zip(ahead, far_parts[:2], strict=True):
        put.start(ref, far_part_ref)
    backward(state, grad_ref, vec_ref.at[1], slab, table_ref, back, sums_ref, scratch, put, far_parts[2:])
    slab.give(slab_ref, arrived)
    put.wait()


def back_kernel(layers, *refs):
    inputs, parts, refs = refs[:4], refs[4:8], refs[8:]
    other_ref, normed_ref, inv_std_ref, later_ref, vec_ref, far_ref, place_ref, far_table_ref, *rest = refs
    far_state, rest = rest[:10], rest[10:]
    far_back, (slab_ref, kept_ref, table_ref, get, put, *rest) = rest[:2], rest[2:]
    back, state, rest = rest[:2], State(rest[2:12]), rest[12:]
    sums_ref, below_ref, small_ref, heads_ref, w_ref, arrived, *scratch = rest
    get, put = Copies(get), Copies(put)
    slab = Slab(far_ref, heads_ref, w_ref, arrived)
    get.start(far_table_ref, table_ref)
    for name, ref in zip(State.names, far_state, strict=True):
        get.start(ref, getattr(state, name))
    attn, hidden = state.o.shape[1], state.gl.shape[1]

    def enter(at, total, cotangent):
        grad = row_norm_back(total, normed_ref[at, :], inv_std_ref[at, :])
        below_ref[at, :] = grad + cotangent.astype(F32)

    over_totals(parts, other_ref, inputs, enter)
    kept_ref[...] = below_ref[: kept_ref.shape[0], :]
    slab.wait()
    get.wait()
    backward(state, below_ref, vec_ref.at[0], slab, table_ref, back, sums_ref, scratch, put, far_back)
    both = [sums_ref, later_ref]
    pad = jnp.zeros((8 - layers, attn), F32)
    qkv = jnp.concatenate([ref[SUM_QKV : SUM_QKV + 1, :] for ref in both] + [pad], axis=0)
    up = [ref[SUM_UP : SUM_UP + 1, :hidden] for ref in both] + [pad[:, :hidden]]
    up = jnp.concatenate(up, axis=0)
    spread = [
        dot(values.astype(BF), one_hot(place_ref, at, values.shape[1]))[:layers]
        for values, at in ((qkv, 0), (qkv, 1), (up, 2), (up, 3))
    ]
    small = [ref[: SUM_SHIFT_B + 1, :] for ref in both] + spread
    used = 9 * layers
    small = jnp.concatenate(small + [jnp.zeros((LANES - used, attn), F32)], axis=0)
    small_ref[...] = jnp.transpose(small).astype(BF)
    columns = attn + 2 * hidden
    copy = pltpu.make_async_copy(small_ref, slab_ref.at[:, columns:], arrived.at[2])
    copy.start()
    slab.give(slab_ref, arrived)
    copy.wait()
    put.wait()


def slabs_kernel(layers, core_ref, *refs):
    far, sends, refs = refs[:9], refs[9 : 9 + layers], refs[9 + layers :]
    local, (rows_ref, bias_ref, arrived) = refs[:9], refs[9:]
    copies = [
        pltpu.make_async_copy(src, dst, arrived.at[i])
        for i, (src, dst) in enumerate(zip(far, local, strict=True))
    ]
    for copy in copies:
        copy.start()
    for copy in copies:
        copy.wait()
    (qkv_ref, out_ref, up_ref, down_ref), vectors, biases = local[:4], local[4:7], local[7:9]
    depth, width_out = qkv_ref.shape[1], out_ref.shape[2] // 2
    hidden = up_ref.shape[2] // 4
    low = core_ref[0] == 0

    def half(values):
        width = values.shape[1] // 2
        return jnp.where(low, values[:, :width], values[:, width:])

    rows_ref[...] = jnp.zeros_like(rows_ref)
    at = 0
    for layer in range(layers):
        for ref in vectors:
            rows_ref[at : at + 2, :depth] = ref[layer].astype(F32)
            at += 2
    lanes = lax.broadcasted_iota(jnp.int32, bias_ref.shape, 1)
    for ref in biases:
        bias_ref[...] = jnp.zeros_like(bias_ref)
        bias_ref[:layers, : ref.shape[1]] = ref[...].astype(F32)
        for values in (bias_ref[...], pltpu.roll(bias_ref[...], LANES - depth, 1)):
            rows_ref[at : at + layers, :] = jnp.where(lanes < depth, values, 0.0)[:layers]
            at += layers
    small = jnp.transpose(rows_ref[...])[:depth].astype(BF)
    for layer, send_ref in enumerate(sends):
        qkv, out = half(qkv_ref[layer]), half(out_ref[layer])
        up, down = half(up_ref[layer]), half(down_ref[layer])
        attn = []
        for head in range(width_out // HS):
            at = head * 3 * HS
            attn += [qkv[:, at : at + 3 * HS], out[:, head * HS : (head + 1) * HS]]
        attn = jnp.concatenate(attn, axis=1)
        for z in (0, 1):
            at = slice(z * hidden, (z + 1) * hidden)
            block = [attn, up[:, at], down[:, at]] + ([small] if layer == 0 else [])
            block = jnp.concatenate(block, axis=1)
            for owner in range(send_ref.shape[0]):
                if owner // NEAR % 2 == z:
                    send_ref[owner] = block


def gather_kernel(layers, *refs):
    got, (all_ref, small_ref, pad_ref) = refs[:layers], refs[layers:]
    owners, depth, width = got[1].shape
    hidden = (all_ref.shape[2] - width) // 2
    attn = width - 2 * hidden

    def sums_of(got_ref, columns):
        sums = []
        for z in (0, 1):
            senders = [owner for owner in range(owners) if owner // NEAR % 2 == z]
            total = got_ref[senders[0], :, columns].astype(F32)
            for owner in senders[1:]:
                total = total + got_ref[owner, :, columns].astype(F32)
            sums.append(total)
        return sums

    for layer in range(layers):
        first, second = sums_of(got[layer], slice(0, attn))
        all_ref[layer, :, :attn] = (first + second).astype(BF)
        for kind in (0, 1):
            begin = attn + kind * hidden
            first, second = sums_of(got[layer], slice(begin, begin + hidden))
            begin = attn + 2 * kind * hidden
            all_ref[layer, :, begin : begin + hidden] = first.astype(BF)
            all_ref[layer, :, begin + hidden : begin + 2 * hidden] = second.astype(BF)
    first, second = sums_of(got[0], slice(width, width + LANES))
    pad_ref[...] = jnp.zeros_like(pad_ref)
    pad_ref[:depth, :] = first + second
    small_ref[...] = jnp.transpose(pad_ref[...])[: small_ref.shape[0]]


def finish_kernel(layers, core_ref, mine_ref, theirs_ref, *rest):
    smalls, (qkv_ref, out_ref, up_ref, down_ref, *vectors) = rest[:4], rest[4:]
    bias_qkv_ref, bias_up_ref, bias_out_ref, gain_ref, shift_ref = vectors
    width_qkv, width_out, width_up = (r.shape[2] // 2 for r in (qkv_ref, out_ref, up_ref))
    depth, heads = qkv_ref.shape[1], width_out // HS
    attn = heads * HEAD
    low = core_ref[0] == 0
    for layer in range(layers):
        mine, theirs = mine_ref[layer].astype(F32), theirs_ref[layer].astype(F32)
        sides = (jnp.where(low, mine, theirs), jnp.where(low, theirs, mine))
        for side, values in enumerate(sides):
            at = side * width_up
            up_ref[layer, :, at : at + width_up] = values[:, attn : attn + width_up]
            down_ref[layer, :, at : at + width_up] = values[:, attn + width_up :]
        starts = [(values, head * HEAD) for values in sides for head in range(heads)]
        qkv_ref[layer] = jnp.concatenate([v[:, at : at + 3 * HS] for v, at in starts], axis=1)
        out_ref[layer] = jnp.concatenate([v[:, at + 3 * HS : at + HEAD] for v, at in starts], axis=1)
    mine, core, half, core_half = (ref[...] for ref in smalls)
    vectors = (mine + half) + (core + core_half)
    for layer in range(layers):
        rows = vectors[5 * layer : 5 * layer + 5, :depth]
        bias_out_ref[layer, 0:1, :] = rows[:1]
        bias_out_ref[layer, 1:2, :] = rows[:1]
        gain_ref[layer] = rows[1:3]
        shift_ref[layer] = rows[3:5]
    biases = mine + core
    at = 5 * layers
    for ref in (bias_qkv_ref, bias_up_ref):
        first, second = biases[at : at + layers], biases[at + layers : at + 2 * layers]
        lanes = lax.broadcasted_iota(jnp.int32, first.shape, 1)
        both = jnp.where(lanes < depth, first, pltpu.roll(second, depth, 1))
        ref[...] = both[:, : ref.shape[1]]
        at += 2 * layers


def call(kernel, outs, scratch, flops, *args, far=(), far_outs=(), limit=VMEM_BYTES, **more):
    def space(at, arg, far):
        if at in far:
            return pltpu.HBM
        return pltpu.SMEM if arg.shape == (1,) else pltpu.VMEM

    return pl.pallas_call(
        kernel,
        out_shape=outs,
        in_specs=[pl.BlockSpec(memory_space=space(at, arg, far)) for at, arg in enumerate(args)],
        out_specs=[
            pl.BlockSpec(memory_space=space(at, out, far_outs)) for at, out in enumerate(outs)
        ],
        scratch_shapes=scratch,
        compiler_params=pltpu.CompilerParams(vmem_limit_bytes=limit),
        cost_estimate=pl.CostEstimate(flops=flops, bytes_accessed=8_000_000, transcendentals=0),
        **more,
    )(*args)


def core_rows_summed(kept, sent):
    return (kept.astype(F32) + other_core(sent).astype(F32)).astype(BF)


def parts_of_sum(mine):
    return mine, other_half(mine), near_group(mine), near_other_half(mine)


def other_rows(parts):
    mine, half, near, near_half = (p.astype(F32).reshape(2, -1, p.shape[1]) for p in parts)
    total = (mine + half) + (near[::-1] + near_half[::-1])
    return other_core(total.astype(BF).reshape(parts[0].shape))


def own_parts(kept, sent):
    mine = core_rows_summed(kept, sent)
    own = mine.shape[0] // 2
    return mine[:own], other_half(mine[:own]), near_group(mine[own:]), near_other_half(mine[own:])


def total_of(parts):
    mine, half, near, near_half = (part.astype(F32) for part in parts)
    return (mine + half) + (near + near_half)


def rotation(positions):
    exponents = jnp.arange(ROT // 2, dtype=F32) * (2.0 / ROT)
    inverse = jnp.power(10000.0, -exponents)
    phase = positions.astype(F32)[:, None] * inverse[None, :]
    cos, sin = jnp.cos(phase), jnp.sin(phase)
    none = jnp.zeros_like(sin)
    rest = jnp.zeros((positions.shape[0], HS - ROT), F32)
    tables = [[cos, cos, rest + 1.0], [-sin, none, rest], [none, sin, rest]]
    return jnp.stack([jnp.concatenate(t + t, axis=1) for t in tables])


def bias_places(owners, depth, starts, widths, shards):
    owner = jnp.arange(owners * depth, dtype=jnp.int32) // depth
    inner = jnp.arange(owners * depth, dtype=jnp.int32) % depth
    rows = []
    for start, width, shard, head in zip(starts, widths, shards, (3 * HS, None), strict=True):
        for first in (0, depth):
            at = owner * shard + inner + first - start
            fits = (inner + first < shard) & (at >= 0) & (at < width)
            if head is not None:
                at = at // head * HEAD + at % head
            rows.append(jnp.where(fits, at, -1))
    return jnp.stack(rows + rows)


def per_device(
    tokens,
    cotangent,
    doc_lens,
    block_pos,
    w_qkv,
    w_out,
    w_up,
    w_down,
    b_qkv,
    b_up,
    out_bias,
    norm_gain,
    norm_bias,
):
    row_count = tokens.shape[0]
    block_rows = row_count // 2
    core = lax.axis_index("ctx")
    owners = lax.axis_size("fsdp")
    layers, depth, width_qkv = w_qkv.shape
    width_qkv, width_out, hidden = width_qkv // 2, w_out.shape[1] // 2, w_up.shape[2] // 4
    place_z = lax.axis_index("fsdp") // NEAR % 2
    heads = width_out // HS
    attn = heads * HEAD
    width = attn + 2 * hidden
    wide = owners * depth
    rows = 4 * row_count

    core_at = core.astype(jnp.int32).reshape(1)
    sds = jax.ShapeDtypeStruct
    raw = (
        w_qkv,
        w_out.transpose(0, 2, 1),
        w_up,
        w_down.transpose(0, 2, 1),
        out_bias,
        norm_gain,
        norm_bias,
        b_qkv,
        b_up,
    )
    sends = call(
        functools.partial(slabs_kernel, layers),
        (
            sds((owners, depth, width + LANES), BF),
            sds((owners, depth, width), BF),
        ),
        [pltpu.VMEM(a.shape, a.dtype) for a in raw]
        + [pltpu.VMEM((LANES, LANES), F32), pltpu.VMEM((8, LANES), F32)]
        + [pltpu.SemaphoreType.DMA((len(raw),))],
        1000,
        core_at,
        *raw,
        far=range(1, 1 + len(raw)),
    )
    first, second = (exchanged(blocks).reshape(wide, -1) for blocks in sends)
    starts, ends = ((own, near_other_half(own)) for own in (tokens, cotangent))
    starts, ends = ((o, other_core(o), n, other_core(n)) for o, n in (starts, ends))
    offsets = jnp.arange(block_rows, dtype=jnp.int32)
    positions = (block_pos[0][:, None] * block_rows + offsets[None, :]).reshape(2, row_count)
    positions = jnp.where(core == 0, positions, positions[::-1]).reshape(-1)
    doc_ends = jnp.cumsum(doc_lens[0])
    docs = jnp.sum((positions[:, None] >= doc_ends[None, :]).astype(jnp.int32), axis=1)
    allowed = (docs[:, None] == docs[None, :]) & (positions[None, :] <= positions[:, None])
    mask = jnp.where(allowed, 0.0, MASKED).astype(F32)
    table = rotation(positions)
    place = bias_places(
        owners,
        depth,
        (core * width_qkv, (2 * core + place_z) * hidden),
        (width_qkv, hidden),
        (b_qkv.shape[1], b_up.shape[1]),
    )

    flops = 2 * rows * wide * width
    part = sds((rows // 2, wide), BF)
    kept = State.shapes(rows, wide, heads, hidden)

    def vmem(*arrays):
        return [pltpu.VMEM(array.shape, array.dtype) for array in arrays]

    def copies(*counts):
        return [pltpu.SemaphoreType.DMA((count,)) for count in counts]

    slab_scratch = [
        pltpu.VMEM((wide, attn), BF),
        pltpu.VMEM((wide, 2 * hidden), BF),
        pltpu.SemaphoreType.DMA((3,)),
    ]
    kept_part, sent_part, vec, *state = call(
        functools.partial(first_kernel, layers),
        (part, part, sds((layers, VECTORS, wide), F32), *State.shapes(rows, wide, heads, hidden)),
        [
            *vmem(part, part, table, mask),
            *copies(2, 12),
            pltpu.VMEM((rows, wide), F32),
            pltpu.VMEM((wide, LANES), BF),
            *slab_scratch,
            *vmem(*kept),
        ],
        flops,
        *starts,
        first,
        place,
        table,
        mask,
        far=(4, 6, 7),
        far_outs=(0, 1, *range(3, 13)),
    )
    parts = parts_of_sum(core_rows_summed(kept_part, sent_part))
    scratch = [
        pltpu.VMEM((rows, wide), BF),
        pltpu.VMEM((rows, hidden), BF),
        pltpu.VMEM((rows // 2, attn), BF),
        pltpu.VMEM((rows, wide), F32),
        pltpu.VMEM((rows, wide), F32),
    ]
    *sums, slab, later_sums, result, normed, inv_std = call(
        last_kernel,
        (
            *(part,) * 4,
            sds((wide, width), BF),
            sds((8, wide), F32),
            sds((row_count, wide), F32),
            *kept[:2],
        ),
        [
            *vmem(table, mask, sds((row_count, wide), F32)),
            *copies(6, 7),
            *vmem(part, part, part, part, *kept, sds((rows, wide), BF)),
            *slab_scratch,
            *scratch,
        ],
        3 * flops,
        *starts,
        *ends,
        *parts,
        other_rows(parts),
        vec,
        second,
        table,
        mask,
        far=(4, 5, 6, 7, 14, 15, 16),
        far_outs=(0, 1, 2, 3, 4, 6, 7, 8),
    )
    parts = parts_of_sum(core_rows_summed(*sums[2:]))
    slab, *sums = lax.optimization_barrier((slab, *sums[:2], *parts))
    ahead, parts = own_parts(*sums[:2]), sums[2:]
    later = exchanged(slab.reshape(owners, depth, -1))
    kept_part, sent_part, slab, grad_below = call(
        functools.partial(back_kernel, layers),
        (part, part, sds((wide, width + LANES), BF), sds((row_count, wide), F32)),
        [
            *vmem(table),
            *copies(11, 2),
            *vmem(part, part, *kept, later_sums, sds((rows, wide), F32), sds((wide, LANES), BF)),
            *slab_scratch,
            *scratch,
        ],
        2 * flops,
        *ends,
        *parts,
        other_rows(parts),
        normed,
        inv_std,
        later_sums,
        vec,
        first,
        place,
        table,
        *state,
        far=(13, *range(15, 26)),
        far_outs=(0, 1, 2),
    )
    earlier = exchanged(slab.reshape(owners, depth, -1))
    below = own_parts(kept_part, sent_part)

    mine, small = call(
        functools.partial(gather_kernel, layers),
        (sds((layers, depth, width + 2 * hidden), BF), sds((24, LANES), F32)),
        [pltpu.VMEM((LANES, LANES), F32)],
        1000,
        earlier,
        later,
    )
    result = (result + total_of(ahead)).astype(BF)
    mine, small, below = lax.optimization_barrier((mine, small, below))
    total = row_norm_back(total_of(below), state[0][:row_count], state[1][:row_count])
    grad_tokens = (grad_below + total).astype(BF)
    grad_qkv, grad_out, grad_up, grad_down, *vectors = call(
        functools.partial(finish_kernel, layers),
        tuple(
            sds(shape, F32)
            for shape in (
                w_qkv.shape,
                (layers, depth, w_out.shape[1]),
                w_up.shape,
                (layers, depth, w_down.shape[1]),
                b_qkv.shape,
                b_up.shape,
                out_bias.shape,
                norm_gain.shape,
                norm_bias.shape,
            )
        ),
        [],
        1000,
        core_at,
        mine,
        other_core(mine),
        small,
        other_core(small),
        other_half(small),
        other_core_and_half(small),
    )
    return (
        result,
        grad_tokens,
        grad_qkv,
        grad_out.transpose(0, 2, 1),
        grad_up,
        grad_down.transpose(0, 2, 1),
        *vectors,
    )


def solution(mesh):
    in_specs = (
        P(("fsdp", "ctx"), None),
        P(("fsdp", "ctx"), None),
        P("fsdp", None),
        P("fsdp", None),
        P(None, "fsdp", "tp"),
        P(None, "tp", "fsdp"),
        P(None, "fsdp", "tp"),
        P(None, "tp", "fsdp"),
        P(None, ("tp", "fsdp")),
        P(None, ("tp", "fsdp")),
        P(None, None, "fsdp"),
        P(None, None, "fsdp"),
        P(None, None, "fsdp"),
    )
    out_specs = (P(("fsdp", "ctx"), None), P(("fsdp", "ctx"), None), *in_specs[4:])
    return jax.shard_map(
        per_device, mesh=mesh, in_specs=in_specs, out_specs=out_specs, check_vma=False
    )
```

time: 289 us -> 249 us (0.86)
  blocking collectives: 53.3 us -> 0 us
  starting transfers between devices: 43.8 us -> 67.7 us
  local copies, waits for them, and re-layouts: 21.2 us -> 7.78 us
  Pallas kernels: 36.5 us -> 48.5 us
  other arithmetic: 15 us -> 9.65 us
  waiting for transfers between devices: 117 us -> 113 us
    ppermute x5, waiting for transfers between devices: 111 us -> 47.4 us  [other_half(): return lax.ppermute(values, 'tp', SWAP)]
    all_to_all x1 -> x0, blocking collectives: 53.3 us -> none  [to_all(): lax.all_to_all(jnp.broadcast_to(block[None], (count, *block.shape)), 'fsd...]
    all_to_all x3 -> x4, waiting for transfers between devices: 0.01 us -> 34.2 us  [exchanged(): return lax.all_to_all(blocks, 'fsdp', 0, 0, tiled=True)]
    ppermute x0 -> x11, waiting for transfers between devices: none -> 25.8 us  [the longest x4 22.4 us: near_group(): return lax.ppermute(values, 'fsdp', [(f, f ^ NEAR) for f in range(owners)])]
    ppermute x0 -> x11, starting transfers between devices: none -> 16 us  [the longest x6 9.85 us: near_other_half(): return lax.ppermute(values, ('fsdp', 'tp'), pairs)]
    pallas_call x3 -> x6, Pallas kernels: 36.5 us -> 48.5 us  [call(): pl.pallas_call(kernel, out_shape=outs, in_specs=[pl.BlockSpec(memory_spac...]
    unnamed x49 -> x56, local copies, waits for them, and re-layouts: 10.3 us -> 4.33 us
    all_to_all x3 -> x4, starting transfers between devices: 27.4 us -> 32.9 us  [exchanged(): return lax.all_to_all(blocks, 'fsdp', 0, 0, tiled=True)]
  transfers between devices with their start and end apart: 17 -> 32, of which waited for: 11 -> 15; matrix products, arithmetic and copies ran while one was open for 4% -> 5% of each run, Pallas kernels for 8% -> 11%
where the time goes in v3:
time: 249 us; the launch traced here: 248 us
  waiting for transfers between devices  113 us (45%)
  starting transfers between devices  67.7 us (27%)
  Pallas kernels  48.5 us (19%)
  other arithmetic  9.65 us (4%)
  local copies, waits for them, and re-layouts  7.78 us (3%)
    pallas_call x6, Pallas kernels, call(): pl.pallas_call(kernel, out_shape=outs, in_specs=[pl.BlockSpec(memory_spac...  48.5 us
    ppermute x5, waiting for transfers between devices, other_half(): return lax.ppermute(values, 'tp', SWAP)  47.4 us
    all_to_all x4, waiting for transfers between devices, exchanged(): return lax.all_to_all(blocks, 'fsdp', 0, 0, tiled=True)  34.2 us
    all_to_all x4, starting transfers between devices, exchanged(): return lax.all_to_all(blocks, 'fsdp', 0, 0, tiled=True)  32.9 us
    ppermute x4, waiting for transfers between devices, near_group(): return lax.ppermute(values, 'fsdp', [(f, f ^ NEAR) for f in range(owners)])  22.4 us
    ppermute x6, starting transfers between devices, near_other_half(): return lax.ppermute(values, ('fsdp', 'tp'), pairs)  9.85 us
    ppermute x12, starting transfers between devices, other_core(): return lax.ppermute(values, 'ctx', SWAP)  9.69 us
    ppermute x5, starting transfers between devices, other_half(): return lax.ppermute(values, 'tp', SWAP)  9.14 us
  transfers between devices with their start and end apart: 32, of which 15 were waited for; matrix products, arithmetic and copies ran while one was open for 5% of the time, Pallas kernels for 11%

profile of v3, /device:TPU:1, one launch (start us, length us, event | category | flops | bytes accessed | tf_op | source)
XLA Modules:
  0.0 248.4 jit_solution(12882533619786785829)
XLA Ops:
  0.7 3.8 %shard_map.212 = (bf16[32,24,1664]{2,1,0:T(8,128)(2,1)}, bf16[32,24,1536]{2,1,0:T(8,128)(2,1)}) custom-call(s32[1]{0:T(128)} %bitcast.core_ref, bf16[2,24,1152]{2,1,0:T(8,128)(2,1)} %refs_0_.4, bf16[2,24,384]{2,1,0:T(8,128)(2,1)} %bitcast.45, bf16[2,24,1536]{2,1,0:T(8,128)(2,1)} %refs_2_.1, bf16[2,24,1536]{2,1,0:T(8,128)(2,1)} %bitcast.44, ...), custom_call_target="tpu_custom_call" | custom-call | flops 1000 | bytes 8000000 | tf_op jit(solution)/shard_map/pallas_call | solution.py:616
  4.5 9.4 %all-to-all-start = ((bf16[32,24,1664]{2,1,0:T(8,128)(2,1)}), bf16[32,24,1664]{2,1,0:T(8,128)(2,1)S(1)}, u32[]{:S(2)}, u32[]{:S(2)}) async-start(bf16[32,24,1664]{2,1,0:T(8,128)(2,1)} %get-tuple-element.63), calls=%async_computation | async-start | bytes 5111808 | tf_op jit(solution)/shard_map/all_to_all | solution.py:52
  13.9 3.4 %collective-permute-start.1 = (bf16[128,768]{1,0:T(8,128)(2,1)S(1)}, bf16[128,768]{1,0:T(8,128)(2,1)}, u32[]{:S(2)}, u32[]{:S(2)}) collective-permute-start(bf16[128,768]{1,0:T(8,128)(2,1)S(1)} %copy-done.24), channel_id=1, source_target_pairs={{0,17},{1,16},{4,21},{5,20},{8,25},{9,24},{12,29},{13,28},{16,1},{... | collective-permute-start | bytes 589832 | tf_op jit(solution)/shard_map/ppermute | solution.py:48
  17.3 1.5 collective-permute-start
  22.4 0.8 collective-permute-start.2
  23.3 22.5 %all-to-all-done = bf16[32,24,1664]{2,1,0:T(8,128)(2,1)S(1)} async-done(((bf16[32,24,1664]{2,1,0:T(8,128)(2,1)}), bf16[32,24,1664]{2,1,0:T(8,128)(2,1)S(1)}, u32[]{:S(2)}, u32[]{:S(2)}) %all-to-all-start) | async-done | bytes 2555936 | tf_op jit(solution)/shard_map/all_to_all | solution.py:52
  45.8 1.5 copy-done
  47.2 7.6 %all-to-all-start.1 = ((bf16[32,24,1536]{2,1,0:T(8,128)(2,1)}), bf16[32,24,1536]{2,1,0:T(8,128)(2,1)}, u32[]{:S(2)}, u32[]{:S(2)}) async-start(bf16[32,24,1536]{2,1,0:T(8,128)(2,1)} %get-tuple-element.67), calls=%async_computation.1 | async-start | bytes 4718592 | tf_op jit(solution)/shard_map/all_to_all | solution.py:52
  54.8 0.8 and_select_fusion.refs_7_.refs_16_
  56.4 8.7 %shard_map.213 = (bf16[256,768]{1,0:T(8,128)(2,1)}, bf16[256,768]{1,0:T(8,128)(2,1)}, f32[2,8,768]{2,1,0:T(8,128)}, f32[512,768]{1,0:T(8,128)}, f32[512,1]{1,0:T...) custom-call(bf16[128,768]{1,0:T(8,128)(2,1)} %refs_0_.6, ...), custom_call_target="tpu_custom_call" | custom-call | flops 1207959552 | bytes 8000000 | tf_op jit(solution)/shard_map/pallas_call | solution.py:616
  65.1 1.6 collective-permute-start.6
  66.7 1.6 collective-permute-done.6
  68.2 1.1 add_convert_fusion.5.refs_8_
  69.3 1.5 collective-permute-start.8
  70.9 2.2 collective-permute-start.9
  73.1 1.1 collective-permute-start.7
  74.2 2.1 collective-permute-start.4
  76.3 15.8 %collective-permute-done.8.refs_10_ = bf16[256,768]{1,0:T(8,128)(2,1)S(1)} collective-permute-done((bf16[256,768]{1,0:T(8,128)(2,1)S(1)}, bf16[256,768]{1,0:T(8,128)(2,1)S(1)}, u32[]{:S(2)}, u32[]{:S(2)}) %collective-permute-start.8) | collective-permute-done | bytes 393248 | tf_op jit(solution)/shard_map/ppermute | solution.py:42
  92.2 10.1 %collective-permute-done.7.refs_9_ = bf16[256,768]{1,0:T(8,128)(2,1)S(1)} collective-permute-done((bf16[256,768]{1,0:T(8,128)(2,1)S(1)}, bf16[256,768]{1,0:T(8,128)(2,1)S(1)}, u32[]{:S(2)}, u32[]{:S(2)}) %collective-permute-start.7) | collective-permute-done | bytes 393248 | tf_op jit(solution)/shard_map/ppermute | solution.py:33
  103.6 1.1 collective-permute-done.3.refs_5_.refs_1_
  105.8 15.7 %shard_map.214 = (bf16[256,768]{1,0:T(8,128)(2,1)}, bf16[256,768]{1,0:T(8,128)(2,1)}, bf16[256,768]{1,0:T(8,128)(2,1)}, bf16[256,768]{1,0:T(8,128)(2,1)}, bf16[7...) custom-call(bf16[128,768]{1,0:T(8,128)(2,1)} %refs_0_.6, ...), custom_call_target="tpu_custom_call" | custom-call | flops 3623878656 | bytes 8000000 | tf_op jit(solution)/shard_map/pallas_call | solution.py:616
  122.0 1.6 collective-permute-done.11
  123.5 1.1 add_convert_fusion.3.refs_4_
  124.7 1.2 collective-permute-start.13
  125.9 2.1 collective-permute-start.14
  128.1 8.5 %collective-permute-done.12.refs_5_ = bf16[256,768]{1,0:T(8,128)(2,1)S(1)} collective-permute-done((bf16[256,768]{1,0:T(8,128)(2,1)S(1)}, bf16[256,768]{1,0:T(8,128)(2,1)S(1)}, u32[]{:S(2)}, u32[]{:S(2)}) %collective-permute-start.12) | collective-permute-done | bytes 393248 | tf_op jit(solution)/shard_map/ppermute | solution.py:33
  136.6 6.7 %collective-permute-done.13.refs_6_ = bf16[256,768]{1,0:T(8,128)(2,1)S(1)} collective-permute-done((bf16[256,768]{1,0:T(8,128)(2,1)S(1)}, bf16[256,768]{1,0:T(8,128)(2,1)S(1)}, u32[]{:S(2)}, u32[]{:S(2)}) %collective-permute-start.13) | collective-permute-done | bytes 393248 | tf_op jit(solution)/shard_map/ppermute | solution.py:42
  143.3 2.4 collective-permute-done.14.refs_7_
  145.7 7.8 %all-to-all-start.3 = ((bf16[32,24,1536]{2,1,0:T(8,128)(2,1)}), bf16[32,24,1536]{2,1,0:T(8,128)(2,1)}, u32[]{:S(2)}, u32[]{:S(2)}) async-start(bf16[32,24,1536]{2,1,0:T(8,128)(2,1)} %bitcast.34), calls=%async_computation.3 | async-start | bytes 4718592 | tf_op jit(solution)/shard_map/all_to_all | solution.py:52
  153.9 1.1 collective-permute-start.19
  155.0 1.3 collective-permute-done.19.refs_8_
  157.1 14.4 %shard_map.215 = (bf16[256,768]{1,0:T(8,128)(2,1)}, bf16[256,768]{1,0:T(8,128)(2,1)}, bf16[768,1664]{1,0:T(8,128)(2,1)}, f32[128,768]{1,0:T(8,128)}) custom-call(bf16[128,768]{1,0:T(8,128)(2,1)} %refs_0_.7, bf16[128,768]{1,0:T(8,128)(2,1)} %copy-done.16, bf16[128,768]{1,0:T(8,128)(2,1)} %copy-done.15, bf16[128,768]{1,0:T(8,128)(2,1)} %copy-done.17, ...), custom_call_target="tpu_custom_call" | custom-call | flops 2415919104 | bytes 8000000 | tf_op jit(solution)/shard_map/pallas_call | solution.py:616
  171.5 11.7 %all-to-all-done.3.refs_1_ = bf16[32,24,1536]{2,1,0:T(8,128)(2,1)} async-done(((bf16[32,24,1536]{2,1,0:T(8,128)(2,1)}), bf16[32,24,1536]{2,1,0:T(8,128)(2,1)}, u32[]{:S(2)}, u32[]{:S(2)}) %all-to-all-start.3) | async-done | bytes 2359328 | tf_op jit(solution)/shard_map/all_to_all | solution.py:52
  183.2 8.1 %all-to-all-start.2 = ((bf16[32,24,1664]{2,1,0:T(8,128)(2,1)}), bf16[32,24,1664]{2,1,0:T(8,128)(2,1)}, u32[]{:S(2)}, u32[]{:S(2)}) async-start(bf16[32,24,1664]{2,1,0:T(8,128)(2,1)} %bitcast.33), calls=%async_computation.2 | async-start | bytes 5111808 | tf_op jit(solution)/shard_map/all_to_all | solution.py:52
  191.3 1.2 collective-permute-start.15
  192.6 0.9 slice_reduce_fusion
  194.1 1.5 collective-permute-start.17
  195.6 1.9 collective-permute-start.16
  198.3 1.4 collective-permute-start.22
  199.7 28.7 %collective-permute-done.16 = bf16[128,768]{1,0:T(8,128)(2,1)S(1)} collective-permute-done((bf16[128,768]{1,0:T(8,128)(2,1)S(1)}, bf16[128,768]{1,0:T(8,128)(2,1)S(1)}, u32[]{:S(2)}, u32[]{:S(2)}) %collective-permute-start.16) | collective-permute-done | bytes 196640 | tf_op jit(solution)/shard_map/ppermute | solution.py:33
  228.4 3.4 %collective-permute-start.21 = (bf16[128,768]{1,0:T(8,128)(2,1)S(1)}, bf16[128,768]{1,0:T(8,128)(2,1)}, u32[]{:S(2)}, u32[]{:S(2)}) collective-permute-start(bf16[128,768]{1,0:T(8,128)(2,1)S(1)} %get-tuple-element.100), channel_id=1, source_target_pairs={{0,1},{1,0},{2,3},{3,2},{4,5},{5,4},{6,7},{7,6},{8,9},{9,8},{10,11... | collective-permute-start | bytes 589832 | tf_op jit(solution)/shard_map/ppermute | solution.py:33
  232.6 3.9 %shard_map.216 = (bf16[2,24,2304]{2,1,0:T(8,128)(2,1)}, f32[24,128]{1,0:T(8,128)}) custom-call(bf16[32,24,1664]{2,1,0:T(8,128)(2,1)} %all-to-all-done.2.refs_0_, bf16[32,24,1536]{2,1,0:T(8,128)(2,1)} %all-to-all-done.3.refs_1_), custom_call_target="tpu_custom_call" | custom-call | flops 1000 | bytes 8000000 | tf_op jit(solution)/shard_map/pallas_call | solution.py:616
  236.5 1.6 collective-permute-start.25
  238.1 2.7 %collective-permute-start.26 = (f32[24,128]{1,0:T(8,128)}, f32[24,128]{1,0:T(8,128)S(1)}, u32[]{:S(2)}, u32[]{:S(2)}) collective-permute-start(f32[24,128]{1,0:T(8,128)} %get-tuple-element.105.rest_0_), channel_id=1, source_target_pairs={{0,1},{1,0},{2,3},{3,2},{4,5},{5,4},{6,7},{7,6},{8,9},{9,8},{10,11... | collective-permute-start | bytes 36872 | tf_op jit(solution)/shard_map/ppermute | solution.py:33
  241.5 1.2 fusion.3
  242.7 2.0 add_convert_fusion.6
  244.7 0.9 collective-permute-done.27.rest_3_
  246.2 2.1 shard_map.217
  (122 shorter events, 11.8 us)
Async XLA Ops:
  4.5 9.4 %copy-start.24 = (bf16[128,768]{1,0:T(8,128)(2,1)S(1)}, bf16[128,768]{1,0:T(8,128)(2,1)}, u32[]{:S(2)}) copy-start(bf16[128,768]{1,0:T(8,128)(2,1)} %refs_0_.6) | copy-start | bytes 589828
  4.5 14.4 %copy-start.26 = (s32[1,4]{1,0:T(1,128)S(1)}, s32[1,4]{1,0:T(1,128)}, u32[]{:S(2)}) copy-start(s32[1,4]{1,0:T(1,128)} %param.16) | copy-start | bytes 52
  4.5 41.3 %all-to-all-start = ((bf16[32,24,1664]{2,1,0:T(8,128)(2,1)}), bf16[32,24,1664]{2,1,0:T(8,128)(2,1)S(1)}, u32[]{:S(2)}, u32[]{:S(2)}) async-start(bf16[32,24,1664]{2,1,0:T(8,128)(2,1)} %get-tuple-element.63), calls=%async_computation | async-start | bytes 5111808 | tf_op jit(solution)/shard_map/all_to_all | solution.py:52
  13.9 8.5 %collective-permute-start.1 = (bf16[128,768]{1,0:T(8,128)(2,1)S(1)}, bf16[128,768]{1,0:T(8,128)(2,1)}, u32[]{:S(2)}, u32[]{:S(2)}) collective-permute-start(bf16[128,768]{1,0:T(8,128)(2,1)S(1)} %copy-done.24), channel_id=1, source_target_pairs={{0,17},{1,16},{4,21},{5,20},{8,25},{9,24},{12,29},{13,28},{16,1},{... | collective-permute-start | bytes 589832 | tf_op jit(solution)/shard_map/ppermute | solution.py:48
  17.3 38.4 %collective-permute-start = (bf16[128,768]{1,0:T(8,128)(2,1)S(1)}, bf16[128,768]{1,0:T(8,128)(2,1)}, u32[]{:S(2)}, u32[]{:S(2)}) collective-permute-start(bf16[128,768]{1,0:T(8,128)(2,1)S(1)} %copy-done.24), channel_id=1, source_target_pairs={{0,2},{2,0},{1,3},{3,1},{4,6},{6,4},{5,7},{7,5},{8,10},{10,8},{9,1... | collective-permute-start | bytes 589832 | tf_op jit(solution)/shard_map/ppermute | solution.py:29
  22.4 33.3 %collective-permute-start.2 = (bf16[128,768]{1,0:T(8,128)(2,1)}, bf16[128,768]{1,0:T(8,128)(2,1)S(1)}, u32[]{:S(2)}, u32[]{:S(2)}) collective-permute-start(bf16[128,768]{1,0:T(8,128)(2,1)} %collective-permute-done.1.refs_2_), channel_id=1, source_target_pairs={{0,2},{2,0},{1,3},{3,1},{4,6},{6,4},{5,7},{7,5},{8,10},{10,8},{9,1... | collective-permute-start | bytes 589832 | tf_op jit(solution)/shard_map/ppermute | solution.py:29
  47.2 57.8 %all-to-all-start.1 = ((bf16[32,24,1536]{2,1,0:T(8,128)(2,1)}), bf16[32,24,1536]{2,1,0:T(8,128)(2,1)}, u32[]{:S(2)}, u32[]{:S(2)}) async-start(bf16[32,24,1536]{2,1,0:T(8,128)(2,1)} %get-tuple-element.67), calls=%async_computation.1 | async-start | bytes 4718592 | tf_op jit(solution)/shard_map/all_to_all | solution.py:52
  56.4 17.8 %copy-start.14 = (bf16[128,768]{1,0:T(8,128)(2,1)S(1)}, bf16[128,768]{1,0:T(8,128)(2,1)}, u32[]{:S(2)}) copy-start(bf16[128,768]{1,0:T(8,128)(2,1)} %refs_0_.7) | copy-start | bytes 589828
  65.1 3.1 %collective-permute-start.6 = (bf16[256,768]{1,0:T(8,128)(2,1)}, bf16[256,768]{1,0:T(8,128)(2,1)S(1)}, u32[]{:S(2)}, u32[]{:S(2)}) collective-permute-start(bf16[256,768]{1,0:T(8,128)(2,1)} %get-tuple-element.65), channel_id=1, source_target_pairs={{0,2},{2,0},{1,3},{3,1},{4,6},{6,4},{5,7},{7,5},{8,10},{10,8},{9,1... | collective-permute-start | bytes 1179656 | tf_op jit(solution)/shard_map/ppermute | solution.py:29
  69.3 33.2 %copy-start.6 = (bf16[256,768]{1,0:T(8,128)(2,1)}, bf16[256,768]{1,0:T(8,128)(2,1)S(1)}, u32[]{:S(2)}) copy-start(bf16[256,768]{1,0:T(8,128)(2,1)S(1)} %add_convert_fusion.5.refs_8_) | copy-start | bytes 1179652
  69.3 22.7 %collective-permute-start.8 = (bf16[256,768]{1,0:T(8,128)(2,1)S(1)}, bf16[256,768]{1,0:T(8,128)(2,1)S(1)}, u32[]{:S(2)}, u32[]{:S(2)}) collective-permute-start(bf16[256,768]{1,0:T(8,128)(2,1)S(1)} %add_convert_fusion.5.refs_8_), channel_id=1, source_target_pairs={{0,16},{4,20},{8,24},{12,28},{16,0},{20,4},{24,8},{28,12},{32,48},... | collective-permute-start | bytes 1179656 | tf_op jit(solution)/shard_map/ppermute | solution.py:42
  70.9 21.2 %collective-permute-start.9 = (bf16[256,768]{1,0:T(8,128)(2,1)S(1)}, bf16[256,768]{1,0:T(8,128)(2,1)S(1)}, u32[]{:S(2)}, u32[]{:S(2)}) collective-permute-start(bf16[256,768]{1,0:T(8,128)(2,1)S(1)} %add_convert_fusion.5.refs_8_), channel_id=1, source_target_pairs={{0,17},{1,16},{4,21},{5,20},{8,25},{9,24},{12,29},{13,28},{16,1},{... | collective-permute-start | bytes 1179656 | tf_op jit(solution)/shard_map/ppermute | solution.py:48
  73.1 29.2 %collective-permute-start.7 = (bf16[256,768]{1,0:T(8,128)(2,1)S(1)}, bf16[256,768]{1,0:T(8,128)(2,1)S(1)}, u32[]{:S(2)}, u32[]{:S(2)}) collective-permute-start(bf16[256,768]{1,0:T(8,128)(2,1)S(1)} %add_convert_fusion.5.refs_8_), channel_id=1, source_target_pairs={{0,1},{1,0},{2,3},{3,2},{4,5},{5,4},{6,7},{7,6},{8,9},{9,8},{10,11... | collective-permute-start | bytes 1179656 | tf_op jit(solution)/shard_map/ppermute | solution.py:33
  74.2 29.0 %collective-permute-start.4 = (bf16[128,768]{1,0:T(8,128)(2,1)S(1)}, bf16[128,768]{1,0:T(8,128)(2,1)S(1)}, u32[]{:S(2)}, u32[]{:S(2)}) collective-permute-start(bf16[128,768]{1,0:T(8,128)(2,1)S(1)} %copy-done.14), channel_id=1, source_target_pairs={{0,17},{1,16},{4,21},{5,20},{8,25},{9,24},{12,29},{13,28},{16,1},{... | collective-permute-start | bytes 589832 | tf_op jit(solution)/shard_map/ppermute | solution.py:48
  92.0 10.5 %copy-start.10 = (bf16[256,768]{1,0:T(8,128)(2,1)}, bf16[256,768]{1,0:T(8,128)(2,1)S(1)}, u32[]{:S(2)}) copy-start(bf16[256,768]{1,0:T(8,128)(2,1)S(1)} %collective-permute-done.8.refs_10_) | copy-start | bytes 1179652
  92.1 10.5 %copy-start.12 = (bf16[256,768]{1,0:T(8,128)(2,1)}, bf16[256,768]{1,0:T(8,128)(2,1)S(1)}, u32[]{:S(2)}) copy-start(bf16[256,768]{1,0:T(8,128)(2,1)S(1)} %collective-permute-done.9.refs_11_) | copy-start | bytes 1179652
  102.6 2.5 %collective-permute-start.10 = (bf16[256,768]{1,0:T(8,128)(2,1)S(1)}, bf16[256,768]{1,0:T(8,128)(2,1)S(1)}, u32[]{:S(2)}, u32[]{:S(2)}) collective-permute-start(bf16[256,768]{1,0:T(8,128)(2,1)S(1)} %bitcast.42), channel_id=1, source_target_pairs={{0,2},{2,0},{1,3},{3,1},{4,6},{6,4},{5,7},{7,5},{8,10},{10,8},{9,1... | collective-permute-start | bytes 1179656 | tf_op jit(solution)/shard_map/ppermute | solution.py:29
  103.1 1.6 collective-permute-start.3
  103.2 1.8 collective-permute-start.5
  121.5 2.0 collective-permute-start.11
  124.6 29.1 %copy-start.1 = (bf16[256,768]{1,0:T(8,128)(2,1)}, bf16[256,768]{1,0:T(8,128)(2,1)S(1)}, u32[]{:S(2)}) copy-start(bf16[256,768]{1,0:T(8,128)(2,1)S(1)} %add_convert_fusion.3.refs_4_) | copy-start | bytes 1179652
  124.6 12.0 %collective-permute-start.12 = (bf16[256,768]{1,0:T(8,128)(2,1)S(1)}, bf16[256,768]{1,0:T(8,128)(2,1)S(1)}, u32[]{:S(2)}, u32[]{:S(2)}) collective-permute-start(bf16[256,768]{1,0:T(8,128)(2,1)S(1)} %add_convert_fusion.3.refs_4_), channel_id=1, source_target_pairs={{0,1},{1,0},{2,3},{3,2},{4,5},{5,4},{6,7},{7,6},{8,9},{9,8},{10,11... | collective-permute-start | bytes 1179656 | tf_op jit(solution)/shard_map/ppermute | solution.py:33
  124.7 18.5 %collective-permute-start.13 = (bf16[256,768]{1,0:T(8,128)(2,1)S(1)}, bf16[256,768]{1,0:T(8,128)(2,1)S(1)}, u32[]{:S(2)}, u32[]{:S(2)}) collective-permute-start(bf16[256,768]{1,0:T(8,128)(2,1)S(1)} %add_convert_fusion.3.refs_4_), channel_id=1, source_target_pairs={{0,16},{4,20},{8,24},{12,28},{16,0},{20,4},{24,8},{28,12},{32,48},... | collective-permute-start | bytes 1179656 | tf_op jit(solution)/shard_map/ppermute | solution.py:42
  125.9 19.8 %collective-permute-start.14 = (bf16[256,768]{1,0:T(8,128)(2,1)S(1)}, bf16[256,768]{1,0:T(8,128)(2,1)S(1)}, u32[]{:S(2)}, u32[]{:S(2)}) collective-permute-start(bf16[256,768]{1,0:T(8,128)(2,1)S(1)} %add_convert_fusion.3.refs_4_), channel_id=1, source_target_pairs={{0,17},{1,16},{4,21},{5,20},{8,25},{9,24},{12,29},{13,28},{16,1},{... | collective-permute-start | bytes 1179656 | tf_op jit(solution)/shard_map/ppermute | solution.py:48
  136.6 17.1 %copy-start.3 = (bf16[256,768]{1,0:T(8,128)(2,1)}, bf16[256,768]{1,0:T(8,128)(2,1)S(1)}, u32[]{:S(2)}) copy-start(bf16[256,768]{1,0:T(8,128)(2,1)S(1)} %collective-permute-done.12.refs_5_) | copy-start | bytes 1179652
  143.3 10.3 %copy-start.4 = (bf16[256,768]{1,0:T(8,128)(2,1)}, bf16[256,768]{1,0:T(8,128)(2,1)S(1)}, u32[]{:S(2)}) copy-start(bf16[256,768]{1,0:T(8,128)(2,1)S(1)} %collective-permute-done.13.refs_6_) | copy-start | bytes 1179652
  145.7 7.9 %copy-start.5 = (bf16[256,768]{1,0:T(8,128)(2,1)}, bf16[256,768]{1,0:T(8,128)(2,1)S(1)}, u32[]{:S(2)}) copy-start(bf16[256,768]{1,0:T(8,128)(2,1)S(1)} %collective-permute-done.14.refs_7_) | copy-start | bytes 1179652
  145.7 37.5 %all-to-all-start.3 = ((bf16[32,24,1536]{2,1,0:T(8,128)(2,1)}), bf16[32,24,1536]{2,1,0:T(8,128)(2,1)}, u32[]{:S(2)}, u32[]{:S(2)}) async-start(bf16[32,24,1536]{2,1,0:T(8,128)(2,1)} %bitcast.34), calls=%async_computation.3 | async-start | bytes 4718592 | tf_op jit(solution)/shard_map/all_to_all | solution.py:52
  153.9 2.4 collective-permute-start.19
  183.2 8.1 %copy-start.21 = (bf16[256,768]{1,0:T(8,128)(2,1)S(1)}, bf16[256,768]{1,0:T(8,128)(2,1)}, u32[]{:S(2)}) copy-start(bf16[256,768]{1,0:T(8,128)(2,1)} %get-tuple-element.75) | copy-start | bytes 1179652
  183.2 10.3 %copy-start.22 = (bf16[256,768]{1,0:T(8,128)(2,1)S(1)}, bf16[256,768]{1,0:T(8,128)(2,1)}, u32[]{:S(2)}) copy-start(bf16[256,768]{1,0:T(8,128)(2,1)} %get-tuple-element.99) | copy-start | bytes 1179652
  183.2 10.7 %copy-start.9 = (bf16[256,768]{1,0:T(8,128)(2,1)S(1)}, bf16[256,768]{1,0:T(8,128)(2,1)}, u32[]{:S(2)}) copy-start(bf16[256,768]{1,0:T(8,128)(2,1)} %get-tuple-element.74) | copy-start | bytes 1179652
  183.2 14.3 %copy-start.11 = (bf16[256,768]{1,0:T(8,128)(2,1)S(1)}, bf16[256,768]{1,0:T(8,128)(2,1)}, u32[]{:S(2)}) copy-start(bf16[256,768]{1,0:T(8,128)(2,1)} %get-tuple-element.98) | copy-start | bytes 1179652
  183.2 49.4 %all-to-all-start.2 = ((bf16[32,24,1664]{2,1,0:T(8,128)(2,1)}), bf16[32,24,1664]{2,1,0:T(8,128)(2,1)}, u32[]{:S(2)}, u32[]{:S(2)}) async-start(bf16[32,24,1664]{2,1,0:T(8,128)(2,1)} %bitcast.33), calls=%async_computation.2 | async-start | bytes 5111808 | tf_op jit(solution)/shard_map/all_to_all | solution.py:52
  191.3 40.4 %copy-start.8 = (f32[128,768]{1,0:T(8,128)S(1)}, f32[128,768]{1,0:T(8,128)}, u32[]{:S(2)}) copy-start(f32[128,768]{1,0:T(8,128)} %get-tuple-element.68) | copy-start | bytes 1179652
  191.3 2.6 %collective-permute-start.15 = (bf16[256,768]{1,0:T(8,128)(2,1)S(1)}, bf16[256,768]{1,0:T(8,128)(2,1)S(1)}, u32[]{:S(2)}, u32[]{:S(2)}) collective-permute-start(bf16[256,768]{1,0:T(8,128)(2,1)S(1)} %copy-done.21), channel_id=1, source_target_pairs={{0,2},{2,0},{1,3},{3,1},{4,6},{6,4},{5,7},{7,5},{8,10},{10,8},{9,1... | collective-permute-start | bytes 1179656 | tf_op jit(solution)/shard_map/ppermute | solution.py:29
  193.5 3.9 %collective-permute-start.20 = (bf16[256,768]{1,0:T(8,128)(2,1)S(1)}, bf16[256,768]{1,0:T(8,128)(2,1)S(1)}, u32[]{:S(2)}, u32[]{:S(2)}) collective-permute-start(bf16[256,768]{1,0:T(8,128)(2,1)S(1)} %copy-done.22), channel_id=1, source_target_pairs={{0,2},{2,0},{1,3},{3,1},{4,6},{6,4},{5,7},{7,5},{8,10},{10,8},{9,1... | collective-permute-start | bytes 1179656 | tf_op jit(solution)/shard_map/ppermute | solution.py:29
  194.1 37.7 %collective-permute-start.17 = (bf16[128,768]{1,0:T(8,128)(2,1)S(1)}, bf16[128,768]{1,0:T(8,128)(2,1)S(1)}, u32[]{:S(2)}, u32[]{:S(2)}) collective-permute-start(bf16[128,768]{1,0:T(8,128)(2,1)S(1)} %get-tuple-element.122), channel_id=1, source_target_pairs={{0,16},{4,20},{8,24},{12,28},{16,0},{20,4},{24,8},{28,12},{32,48},... | collective-permute-start | bytes 589832 | tf_op jit(solution)/shard_map/ppermute | solution.py:42
  195.6 36.2 %collective-permute-start.18 = (bf16[128,768]{1,0:T(8,128)(2,1)S(1)}, bf16[128,768]{1,0:T(8,128)(2,1)S(1)}, u32[]{:S(2)}, u32[]{:S(2)}) collective-permute-start(bf16[128,768]{1,0:T(8,128)(2,1)S(1)} %get-tuple-element.122), channel_id=1, source_target_pairs={{0,17},{1,16},{4,21},{5,20},{8,25},{9,24},{12,29},{13,28},{16,1},{... | collective-permute-start | bytes 589832 | tf_op jit(solution)/shard_map/ppermute | solution.py:48
  195.6 32.8 %collective-permute-start.16 = (bf16[128,768]{1,0:T(8,128)(2,1)S(1)}, bf16[128,768]{1,0:T(8,128)(2,1)S(1)}, u32[]{:S(2)}, u32[]{:S(2)}) collective-permute-start(bf16[128,768]{1,0:T(8,128)(2,1)S(1)} %get-tuple-element.121), channel_id=1, source_target_pairs={{0,1},{1,0},{2,3},{3,2},{4,5},{5,4},{6,7},{7,6},{8,9},{9,8},{10,11... | collective-permute-start | bytes 589832 | tf_op jit(solution)/shard_map/ppermute | solution.py:33
  198.3 38.2 %collective-permute-start.22 = (bf16[128,768]{1,0:T(8,128)(2,1)}, bf16[128,768]{1,0:T(8,128)(2,1)S(1)}, u32[]{:S(2)}, u32[]{:S(2)}) collective-permute-start(bf16[128,768]{1,0:T(8,128)(2,1)} %get-tuple-element.119), channel_id=1, source_target_pairs={{0,16},{4,20},{8,24},{12,28},{16,0},{20,4},{24,8},{28,12},{32,48},... | collective-permute-start | bytes 589832 | tf_op jit(solution)/shard_map/ppermute | solution.py:42
  199.7 36.8 %collective-permute-start.23 = (bf16[128,768]{1,0:T(8,128)(2,1)}, bf16[128,768]{1,0:T(8,128)(2,1)}, u32[]{:S(2)}, u32[]{:S(2)}) collective-permute-start(bf16[128,768]{1,0:T(8,128)(2,1)} %get-tuple-element.119), channel_id=1, source_target_pairs={{0,17},{1,16},{4,21},{5,20},{8,25},{9,24},{12,29},{13,28},{16,1},{... | collective-permute-start | bytes 589832 | tf_op jit(solution)/shard_map/ppermute | solution.py:48
  228.4 8.1 %collective-permute-start.21 = (bf16[128,768]{1,0:T(8,128)(2,1)S(1)}, bf16[128,768]{1,0:T(8,128)(2,1)}, u32[]{:S(2)}, u32[]{:S(2)}) collective-permute-start(bf16[128,768]{1,0:T(8,128)(2,1)S(1)} %get-tuple-element.100), channel_id=1, source_target_pairs={{0,1},{1,0},{2,3},{3,2},{4,5},{5,4},{6,7},{7,6},{8,9},{9,8},{10,11... | collective-permute-start | bytes 589832 | tf_op jit(solution)/shard_map/ppermute | solution.py:33
  232.6 8.9 %copy-start.2 = (f32[512,768]{1,0:T(8,128)S(1)}, f32[512,768]{1,0:T(8,128)}, u32[]{:S(2)}) copy-start(f32[512,768]{1,0:T(8,128)} %get-tuple-element.83.refs_16_) | copy-start | bytes 4718596
  236.5 8.2 %collective-permute-start.25 = (f32[24,128]{1,0:T(8,128)}, f32[24,128]{1,0:T(8,128)S(1)}, u32[]{:S(2)}, u32[]{:S(2)}) collective-permute-start(f32[24,128]{1,0:T(8,128)} %get-tuple-element.105.rest_0_), channel_id=1, source_target_pairs={{0,2},{2,0},{1,3},{3,1},{4,6},{6,4},{5,7},{7,5},{8,10},{10,8},{9,1... | collective-permute-start | bytes 36872 | tf_op jit(solution)/shard_map/ppermute | solution.py:29
  238.1 6.6 %collective-permute-start.26 = (f32[24,128]{1,0:T(8,128)}, f32[24,128]{1,0:T(8,128)S(1)}, u32[]{:S(2)}, u32[]{:S(2)}) collective-permute-start(f32[24,128]{1,0:T(8,128)} %get-tuple-element.105.rest_0_), channel_id=1, source_target_pairs={{0,1},{1,0},{2,3},{3,2},{4,5},{5,4},{6,7},{7,6},{8,9},{9,8},{10,11... | collective-permute-start | bytes 36872 | tf_op jit(solution)/shard_map/ppermute | solution.py:33
  240.8 4.8 %collective-permute-start.27 = (f32[24,128]{1,0:T(8,128)}, f32[24,128]{1,0:T(8,128)S(1)}, u32[]{:S(2)}, u32[]{:S(2)}) collective-permute-start(f32[24,128]{1,0:T(8,128)} %get-tuple-element.105.rest_0_), channel_id=1, source_target_pairs={{0,3},{1,2},{2,1},{3,0},{4,7},{5,6},{6,5},{7,4},{8,11},{9,10},{10,... | collective-permute-start | bytes 36872 | tf_op jit(solution)/shard_map/ppermute | solution.py:37
  241.3 4.3 %collective-permute-start.24 = (bf16[2,24,2304]{2,1,0:T(8,128)(2,1)}, bf16[2,24,2304]{2,1,0:T(8,128)(2,1)}, u32[]{:S(2)}, u32[]{:S(2)}) collective-permute-start(bf16[2,24,2304]{2,1,0:T(8,128)(2,1)} %get-tuple-element.104.mine_ref), channel_id=1, source_target_pairs={{0,2},{2,0},{1,3},{3,1},{4,6},{6,4},{5,7},{7,5},{8,10},{10,8},{9,1... | collective-permute-start | bytes 663560 | tf_op jit(solution)/shard_map/ppermute | solution.py:29
  (12 other events, 18.6 us)

commit v4 on v3

--- a/solution.py
+++ b/solution.py
@@ -100,12 +100,11 @@
 
 
 class Slab:
-    def __init__(self, far_ref, heads_ref, w_ref, arrived):
-        attn, width = heads_ref.shape[1], heads_ref.shape[1] + w_ref.shape[1]
+    def __init__(self, far_heads_ref, far_ref, heads_ref, w_ref, arrived):
         self.heads_ref, self.w_ref = heads_ref, w_ref
         self.copies = [
-            pltpu.make_async_copy(far_ref.at[:, :attn], heads_ref, arrived.at[0]),
-            pltpu.make_async_copy(far_ref.at[:, attn:width], w_ref, arrived.at[1]),
+            pltpu.make_async_copy(far_heads_ref, heads_ref, arrived.at[0]),
+            pltpu.make_async_copy(far_ref, w_ref, arrived.at[1]),
         ]
         for copy in self.copies:
             copy.start()
@@ -115,11 +114,10 @@
             copy.wait()
         return self.heads_ref, self.w_ref
 
-    def give(self, far_ref, sent):
-        attn, width = self.heads_ref.shape[1], self.heads_ref.shape[1] + self.w_ref.shape[1]
+    def give(self, far_heads_ref, far_ref, sent):
         copies = [
-            pltpu.make_async_copy(self.heads_ref, far_ref.at[:, :attn], sent.at[0]),
-            pltpu.make_async_copy(self.w_ref, far_ref.at[:, attn:width], sent.at[1]),
+            pltpu.make_async_copy(self.heads_ref, far_heads_ref, sent.at[0]),
+            pltpu.make_async_copy(self.w_ref, far_ref, sent.at[1]),
         ]
         for copy in copies:
             copy.start()
@@ -341,10 +339,10 @@
     state = State(state, put, far_state)
     attn = state.o.shape[1]
     hidden = state.gl.shape[1]
-    columns = attn + 2 * hidden
-    copy = pltpu.make_async_copy(far_ref.at[:, columns:], small_ref, arrived.at[2])
+    width = attn + 2 * hidden
+    copy = pltpu.make_async_copy(far_ref.at[:, width:], small_ref, arrived.at[2])
     copy.start()
-    slab = Slab(far_ref, heads_ref, w_ref, arrived)
+    slab = Slab(far_ref.at[:, :attn], far_ref.at[:, attn:width], heads_ref, w_ref, arrived)
     get.start(far_table_ref, table_ref)
     get.start(far_mask_ref, mask_ref)
     copy.wait()
@@ -420,7 +418,8 @@
     get, put = Copies(get), Copies(put)
     state, rest = State(rest[:10], put, (far_normed_ref, far_inv_std_ref)), rest[10:]
     grad_ref, heads_ref, w_ref, arrived, *scratch = rest
-    slab = Slab(far_ref, heads_ref, w_ref, arrived)
+    attn, width = heads_ref.shape[1], heads_ref.shape[1] + w_ref.shape[1]
+    slab = Slab(far_ref.at[:, :attn], far_ref.at[:, attn:width], heads_ref, w_ref, arrived)
     get.start(far_table_ref, table_ref)
     get.start(far_mask_ref, mask_ref)
     own = hidden_ref.shape[0]
@@ -442,7 +441,7 @@
     for ref, far_part_ref in zip(ahead, far_parts[:2], strict=True):
         put.start(ref, far_part_ref)
     backward(state, grad_ref, vec_ref.at[1], slab, table_ref, back, sums_ref, scratch, put, far_parts[2:])
-    slab.give(slab_ref, arrived)
+    slab.give(slab_ref.at[:, :attn], slab_ref.at[:, attn:width], arrived)
     put.wait()
 
 
@@ -454,7 +453,8 @@
     back, state, rest = rest[:2], State(rest[2:12]), rest[12:]
     sums_ref, below_ref, small_ref, heads_ref, w_ref, arrived, *scratch = rest
     get, put = Copies(get), Copies(put)
-    slab = Slab(far_ref, heads_ref, w_ref, arrived)
+    attn, width = heads_ref.shape[1], heads_ref.shape[1] + w_ref.shape[1]
+    slab = Slab(far_ref.at[:, :attn], far_ref.at[:, attn:width], heads_ref, w_ref, arrived)
     get.start(far_table_ref, table_ref)
     for name, ref in zip(State.names, far_state, strict=True):
         get.start(ref, getattr(state, name))
@@ -482,10 +482,9 @@
     used = 9 * layers
     small = jnp.concatenate(small + [jnp.zeros((LANES - used, attn), F32)], axis=0)
     small_ref[...] = jnp.transpose(small).astype(BF)
-    columns = attn + 2 * hidden
-    copy = pltpu.make_async_copy(small_ref, slab_ref.at[:, columns:], arrived.at[2])
+    copy = pltpu.make_async_copy(small_ref, slab_ref.at[:, width:], arrived.at[2])
     copy.start()
-    slab.give(slab_ref, arrived)
+    slab.give(slab_ref.at[:, :attn], slab_ref.at[:, attn:width], arrived)
     copy.wait()
     put.wait()
 
@@ -524,63 +523,87 @@
             rows_ref[at : at + layers, :] = jnp.where(lanes < depth, values, 0.0)[:layers]
             at += layers
     small = jnp.transpose(rows_ref[...])[:depth].astype(BF)
-    for layer, send_ref in enumerate(sends):
+    heads, wide = [], ([], [])
+    for layer in range(layers):
         qkv, out = half(qkv_ref[layer]), half(out_ref[layer])
         up, down = half(up_ref[layer]), half(down_ref[layer])
         attn = []
         for head in range(width_out // HS):
             at = head * 3 * HS
             attn += [qkv[:, at : at + 3 * HS], out[:, head * HS : (head + 1) * HS]]
-        attn = jnp.concatenate(attn, axis=1)
+        heads.append(jnp.concatenate(attn, axis=1))
         for z in (0, 1):
             at = slice(z * hidden, (z + 1) * hidden)
-            block = [attn, up[:, at], down[:, at]] + ([small] if layer == 0 else [])
+            wide[z].append(jnp.concatenate([up[:, at], down[:, at]], axis=1))
+    for z in (0, 1):
+        for layer, send_ref in enumerate(sends):
+            block = [heads[layer], wide[z][layer]] + ([small] if layer == 0 else [])
             block = jnp.concatenate(block, axis=1)
             for owner in range(send_ref.shape[0]):
                 if owner // NEAR % 2 == z:
                     send_ref[owner] = block
 
 
-def gather_kernel(layers, *refs):
-    got, (all_ref, small_ref, pad_ref) = refs[:layers], refs[layers:]
-    owners, depth, width = got[1].shape
-    hidden = (all_ref.shape[2] - width) // 2
-    attn = width - 2 * hidden
-
-    def sums_of(got_ref, columns):
-        sums = []
-        for z in (0, 1):
-            senders = [owner for owner in range(owners) if owner // NEAR % 2 == z]
-            total = got_ref[senders[0], :, columns].astype(F32)
-            for owner in senders[1:]:
-                total = total + got_ref[owner, :, columns].astype(F32)
-            sums.append(total)
-        return sums
-
-    for layer in range(layers):
-        first, second = sums_of(got[layer], slice(0, attn))
-        all_ref[layer, :, :attn] = (first + second).astype(BF)
-        for kind in (0, 1):
-            begin = attn + kind * hidden
-            first, second = sums_of(got[layer], slice(begin, begin + hidden))
-            begin = attn + 2 * kind * hidden
-            all_ref[layer, :, begin : begin + hidden] = first.astype(BF)
-            all_ref[layer, :, begin + hidden : begin + 2 * hidden] = second.astype(BF)
-    first, second = sums_of(got[0], slice(width, width + LANES))
+def sums_of(got_ref, columns):
+    sums = []
+    for z in (0, 1):
+        senders = [owner for owner in range(got_ref.shape[0]) if owner // NEAR % 2 == z]
+        total = got_ref[senders[0], :, columns].astype(F32)
+        for owner in senders[1:]:
+            total = total + got_ref[owner, :, columns].astype(F32)
+        sums.append(total)
+    return sums
+
+
+def put_sums(attn, got_ref, all_ref):
+    hidden = (all_ref.shape[1] - attn) // 4
+    first, second = sums_of(got_ref, slice(0, attn))
+    all_ref[:, :attn] = (first + second).astype(BF)
+    for kind in (0, 1):
+        at = attn + kind * hidden
+        for z, total in enumerate(sums_of(got_ref, slice(at, at + hidden))):
+            at_z = attn + (2 * kind + z) * hidden
+            all_ref[:, at_z : at_z + hidden] = total.astype(BF)
+
+
+def total_of(refs):
+    mine, half, near, near_half = (ref[...].astype(F32) for ref in refs)
+    return (mine + half) + (near + near_half)
+
+
+def gather_late_kernel(attn, got_ref, all_ref):
+    put_sums(attn, got_ref, all_ref)
+
+
+def gather_kernel(attn, got_ref, all_ref, small_ref, pad_ref):
+    depth, width = got_ref.shape[1], got_ref.shape[2] - LANES
+    put_sums(attn, got_ref, all_ref.at[:, : all_ref.shape[1] - LANES])
+    first, second = sums_of(got_ref, slice(width, width + LANES))
     pad_ref[...] = jnp.zeros_like(pad_ref)
     pad_ref[:depth, :] = first + second
-    small_ref[...] = jnp.transpose(pad_ref[...])[: small_ref.shape[0]]
-
-
-def finish_kernel(layers, core_ref, mine_ref, theirs_ref, *rest):
-    smalls, (qkv_ref, out_ref, up_ref, down_ref, *vectors) = rest[:4], rest[4:]
+    small = jnp.transpose(pad_ref[...])[: small_ref.shape[0]].astype(BF)
+    small_ref[...] = small
+    all_ref[:, all_ref.shape[1] - LANES :] = small
+
+
+def finish_kernel(layers, core_ref, *rest):
+    pairs, (half_ref, core_half_ref), rest = (rest[:2], rest[2:4]), rest[4:6], rest[6:]
+    parts, (below_ref, far_normed_ref, far_inv_std_ref, *rest) = rest[:4], rest[4:]
+    ahead, hidden_ref, rest = rest[:4], rest[4], rest[5:]
+    result_ref, grad_ref, qkv_ref, out_ref, up_ref, down_ref, *vectors = rest[:11]
+    normed_ref, inv_std_ref, get = rest[11:]
+    get = Copies(get)
+    own = pl.ds(0, normed_ref.shape[0])
+    get.start(far_normed_ref.at[own, :], normed_ref)
+    get.start(far_inv_std_ref.at[own, :], inv_std_ref)
     bias_qkv_ref, bias_up_ref, bias_out_ref, gain_ref, shift_ref = vectors
     width_qkv, width_out, width_up = (r.shape[2] // 2 for r in (qkv_ref, out_ref, up_ref))
     depth, heads = qkv_ref.shape[1], width_out // HS
     attn = heads * HEAD
+    width = attn + 2 * width_up
     low = core_ref[0] == 0
-    for layer in range(layers):
-        mine, theirs = mine_ref[layer].astype(F32), theirs_ref[layer].astype(F32)
+    for layer, pair in enumerate(pairs):
+        mine, theirs = (ref[:, :width].astype(F32) for ref in pair)
         sides = (jnp.where(low, mine, theirs), jnp.where(low, theirs, mine))
         for side, values in enumerate(sides):
             at = side * width_up
@@ -589,7 +612,8 @@
         starts = [(values, head * HEAD) for values in sides for head in range(heads)]
         qkv_ref[layer] = jnp.concatenate([v[:, at : at + 3 * HS] for v, at in starts], axis=1)
         out_ref[layer] = jnp.concatenate([v[:, at + 3 * HS : at + HEAD] for v, at in starts], axis=1)
-    mine, core, half, core_half = (ref[...] for ref in smalls)
+    mine, core = (ref[:, width:].astype(F32) for ref in pairs[0])
+    half, core_half = half_ref[...].astype(F32), core_half_ref[...].astype(F32)
     vectors = (mine + half) + (core + core_half)
     for layer in range(layers):
         rows = vectors[5 * layer : 5 * layer + 5, :depth]
@@ -605,6 +629,10 @@
         both = jnp.where(lanes < depth, first, pltpu.roll(second, depth, 1))
         ref[...] = both[:, : ref.shape[1]]
         at += 2 * layers
+    result_ref[...] = (hidden_ref[...] + total_of(ahead)).astype(BF)
+    get.wait()
+    total = row_norm_back(total_of(parts), normed_ref[...], inv_std_ref[...])
+    grad_ref[...] = (below_ref[...] + total).astype(BF)
 
 
 def call(kernel, outs, scratch, flops, *args, far=(), far_outs=(), limit=VMEM_BYTES, **more):
@@ -641,15 +669,9 @@
     return other_core(total.astype(BF).reshape(parts[0].shape))
 
 
-def own_parts(kept, sent):
-    mine = core_rows_summed(kept, sent)
+def own_parts(mine):
     own = mine.shape[0] // 2
     return mine[:own], other_half(mine[:own]), near_group(mine[own:]), near_other_half(mine[own:])
-
-
-def total_of(parts):
-    mine, half, near, near_half = (part.astype(F32) for part in parts)
-    return (mine + half) + (near + near_half)
 
 
 def rotation(positions):
@@ -824,7 +846,7 @@
     )
     parts = parts_of_sum(core_rows_summed(*sums[2:]))
     slab, *sums = lax.optimization_barrier((slab, *sums[:2], *parts))
-    ahead, parts = own_parts(*sums[:2]), sums[2:]
+    ahead, parts = own_parts(core_rows_summed(*sums[:2])), sums[2:]
     later = exchanged(slab.reshape(owners, depth, -1))
     kept_part, sent_part, slab, grad_below = call(
         functools.partial(back_kernel, layers),
@@ -832,7 +854,8 @@
         [
             *vmem(table),
             *copies(11, 2),
-            *vmem(part, part, *kept, later_sums, sds((rows, wide), F32), sds((wide, LANES), BF)),
+            *vmem(part, part, *kept, later_sums, sds((rows, wide), F32)),
+            *vmem(sds((wide, LANES), BF)),
             *slab_scratch,
             *scratch,
         ],
@@ -851,24 +874,30 @@
         far=(13, *range(15, 26)),
         far_outs=(0, 1, 2),
     )
+    slab, later = lax.optimization_barrier((slab, later))
     earlier = exchanged(slab.reshape(owners, depth, -1))
-    below = own_parts(kept_part, sent_part)
-
+    below = core_rows_summed(kept_part, sent_part)
+
+    (late,) = call(
+        functools.partial(gather_late_kernel, attn),
+        (sds((depth, attn + 4 * hidden), BF),),
+        [],
+        flops // 8,
+        later,
+    )
+    below, late = lax.optimization_barrier((below, late))
+    below = own_parts(below)
     mine, small = call(
-        functools.partial(gather_kernel, layers),
-        (sds((layers, depth, width + 2 * hidden), BF), sds((24, LANES), F32)),
+        functools.partial(gather_kernel, attn),
+        (sds((depth, attn + 4 * hidden + LANES), BF), sds((depth, LANES), BF)),
         [pltpu.VMEM((LANES, LANES), F32)],
         1000,
         earlier,
-        later,
-    )
-    result = (result + total_of(ahead)).astype(BF)
-    mine, small, below = lax.optimization_barrier((mine, small, below))
-    total = row_norm_back(total_of(below), state[0][:row_count], state[1][:row_count])
-    grad_tokens = (grad_below + total).astype(BF)
-    grad_qkv, grad_out, grad_up, grad_down, *vectors = call(
+    )
+    result, grad_tokens, grad_qkv, grad_out, grad_up, grad_down, *vectors = call(
         functools.partial(finish_kernel, layers),
-        tuple(
+        (sds(tokens.shape, BF),) * 2
+        + tuple(
             sds(shape, F32)
             for shape in (
                 w_qkv.shape,
@@ -882,15 +911,22 @@
                 norm_bias.shape,
             )
         ),
-        [],
+        [*vmem(sds((row_count, wide), F32), sds((row_count, 1), F32)), *copies(2)],
         1000,
         core_at,
         mine,
         other_core(mine),
-        small,
-        other_core(small),
+        late,
+        other_core(late),
         other_half(small),
         other_core_and_half(small),
+        *below,
+        grad_below,
+        state[0],
+        state[1],
+        *ahead,
+        result,
+        far=(12, 13),
     )
     return (
         result,

time: 249 us -> 244 us (0.980)
  waiting for transfers between devices: 113 us -> 107 us
  other arithmetic: 9.65 us -> 5.6 us
  starting transfers between devices: 67.7 us -> 71.1 us
  Pallas kernels: 48.5 us -> 51.8 us
    ppermute x5, waiting for transfers between devices: 47.4 us -> 23 us  [other_half(): return lax.ppermute(values, 'tp', SWAP)]
    ppermute x4, waiting for transfers between devices: 22.4 us -> 36.2 us  [near_group(): return lax.ppermute(values, 'fsdp', [(f, f ^ NEAR) for f in range(owners)])]
    ppermute x6, waiting for transfers between devices: 2.43 us -> 7.69 us  [near_other_half(): return lax.ppermute(values, ('fsdp', 'tp'), pairs)]
    ppermute x4, starting transfers between devices: 5.63 us -> 2.12 us  [near_group(): return lax.ppermute(values, 'fsdp', [(f, f ^ NEAR) for f in range(owners)])]
    ppermute x12, starting transfers between devices: 9.69 us -> 13 us  [other_core(): return lax.ppermute(values, 'ctx', SWAP)]
    pallas_call x6 -> x7, Pallas kernels: 48.5 us -> 51.8 us  [call(): pl.pallas_call(kernel, out_shape=outs, in_specs=[pl.BlockSpec(memory_spac...]
    convert_element_type x2 -> x0, other arithmetic: 2.81 us -> none  [the longest x1 2 us: per_device(): grad_tokens = (grad_below + total).astype(BF)]
  transfers between devices with their start and end apart: 32 -> 32, of which waited for: 15 -> 15; matrix products, arithmetic and copies ran while one was open for 5% -> 3% of each run, Pallas kernels for 11% -> 12%
where the time goes in v4:
time: 244 us; the launch traced here: 243 us
  waiting for transfers between devices  107 us (44%)
  starting transfers between devices  71.1 us (29%)
  Pallas kernels  51.8 us (21%)
  local copies, waits for them, and re-layouts  6.17 us (3%)
  other arithmetic  5.6 us (2%)
    pallas_call x7, Pallas kernels, call(): pl.pallas_call(kernel, out_shape=outs, in_specs=[pl.BlockSpec(memory_spac...  51.8 us
    ppermute x4, waiting for transfers between devices, near_group(): return lax.ppermute(values, 'fsdp', [(f, f ^ NEAR) for f in range(owners)])  36.2 us
    all_to_all x4, starting transfers between devices, exchanged(): return lax.all_to_all(blocks, 'fsdp', 0, 0, tiled=True)  33 us
    all_to_all x4, waiting for transfers between devices, exchanged(): return lax.all_to_all(blocks, 'fsdp', 0, 0, tiled=True)  32.2 us
    ppermute x5, waiting for transfers between devices, other_half(): return lax.ppermute(values, 'tp', SWAP)  23 us
    ppermute x12, starting transfers between devices, other_core(): return lax.ppermute(values, 'ctx', SWAP)  13 us
    ppermute x6, starting transfers between devices, near_other_half(): return lax.ppermute(values, ('fsdp', 'tp'), pairs)  11.3 us
    ppermute x5, starting transfers between devices, other_half(): return lax.ppermute(values, 'tp', SWAP)  9.92 us
  transfers between devices with their start and end apart: 32, of which 15 were waited for; matrix products, arithmetic and copies ran while one was open for 3% of the time, Pallas kernels for 12%

profile of v4, /device:TPU:1, one launch (start us, length us, event | category | flops | bytes accessed | tf_op | source)
XLA Modules:
  0.0 243.2 jit_solution(3883936703005431819)
XLA Ops:
  0.7 3.8 %shard_map.212 = (bf16[32,24,1664]{2,1,0:T(8,128)(2,1)}, bf16[32,24,1536]{2,1,0:T(8,128)(2,1)}) custom-call(s32[1]{0:T(128)} %bitcast.core_ref, bf16[2,24,1152]{2,1,0:T(8,128)(2,1)} %refs_0_.4, bf16[2,24,384]{2,1,0:T(8,128)(2,1)} %bitcast.45, bf16[2,24,1536]{2,1,0:T(8,128)(2,1)} %refs_2_.1, bf16[2,24,1536]{2,1,0:T(8,128)(2,1)} %bitcast.44, ...), custom_call_target="tpu_custom_call" | custom-call | flops 1000 | bytes 8000000 | tf_op jit(solution)/shard_map/pallas_call | solution.py:644
  4.5 9.4 %all-to-all-start = ((bf16[32,24,1664]{2,1,0:T(8,128)(2,1)}), bf16[32,24,1664]{2,1,0:T(8,128)(2,1)S(1)}, u32[]{:S(2)}, u32[]{:S(2)}) async-start(bf16[32,24,1664]{2,1,0:T(8,128)(2,1)} %get-tuple-element.63), calls=%async_computation | async-start | bytes 5111808 | tf_op jit(solution)/shard_map/all_to_all | solution.py:52
  13.9 3.4 %collective-permute-start.4 = (bf16[128,768]{1,0:T(8,128)(2,1)S(1)}, bf16[128,768]{1,0:T(8,128)(2,1)}, u32[]{:S(2)}, u32[]{:S(2)}) collective-permute-start(bf16[128,768]{1,0:T(8,128)(2,1)S(1)} %copy-done.31), channel_id=1, source_target_pairs={{0,17},{1,16},{4,21},{5,20},{8,25},{9,24},{12,29},{13,28},{16,1},{... | collective-permute-start | bytes 589832 | tf_op jit(solution)/shard_map/ppermute | solution.py:48
  17.3 1.5 collective-permute-start.3
  22.5 0.8 collective-permute-start.5
  23.3 22.5 %all-to-all-done = bf16[32,24,1664]{2,1,0:T(8,128)(2,1)S(1)} async-done(((bf16[32,24,1664]{2,1,0:T(8,128)(2,1)}), bf16[32,24,1664]{2,1,0:T(8,128)(2,1)S(1)}, u32[]{:S(2)}, u32[]{:S(2)}) %all-to-all-start) | async-done | bytes 2555936 | tf_op jit(solution)/shard_map/all_to_all | solution.py:52
  45.8 1.4 copy-done
  47.2 7.6 %all-to-all-start.1 = ((bf16[32,24,1536]{2,1,0:T(8,128)(2,1)}), bf16[32,24,1536]{2,1,0:T(8,128)(2,1)}, u32[]{:S(2)}, u32[]{:S(2)}) async-start(bf16[32,24,1536]{2,1,0:T(8,128)(2,1)} %get-tuple-element.67), calls=%async_computation.1 | async-start | bytes 4718592 | tf_op jit(solution)/shard_map/all_to_all | solution.py:52
  54.8 0.8 and_select_fusion.refs_7_.refs_16_
  56.4 8.8 %shard_map.213 = (bf16[256,768]{1,0:T(8,128)(2,1)}, bf16[256,768]{1,0:T(8,128)(2,1)}, f32[2,8,768]{2,1,0:T(8,128)}, f32[512,768]{1,0:T(8,128)}, f32[512,1]{1,0:T...) custom-call(bf16[128,768]{1,0:T(8,128)(2,1)} %refs_0_.6, ...), custom_call_target="tpu_custom_call" | custom-call | flops 1207959552 | bytes 8000000 | tf_op jit(solution)/shard_map/pallas_call | solution.py:644
  65.1 1.6 collective-permute-start.6
  66.7 1.6 collective-permute-done.6
  68.3 1.1 add_convert_fusion.5.refs_8_
  69.4 1.5 collective-permute-start.8
  70.9 2.2 collective-permute-start.9
  73.1 1.1 collective-permute-start.7
  74.2 2.1 collective-permute-start.1
  76.3 15.7 %collective-permute-done.8.refs_10_ = bf16[256,768]{1,0:T(8,128)(2,1)S(1)} collective-permute-done((bf16[256,768]{1,0:T(8,128)(2,1)S(1)}, bf16[256,768]{1,0:T(8,128)(2,1)S(1)}, u32[]{:S(2)}, u32[]{:S(2)}) %collective-permute-start.8) | collective-permute-done | bytes 393248 | tf_op jit(solution)/shard_map/ppermute | solution.py:42
  92.2 10.1 %collective-permute-done.7.refs_9_ = bf16[256,768]{1,0:T(8,128)(2,1)S(1)} collective-permute-done((bf16[256,768]{1,0:T(8,128)(2,1)S(1)}, bf16[256,768]{1,0:T(8,128)(2,1)S(1)}, u32[]{:S(2)}, u32[]{:S(2)}) %collective-permute-start.7) | collective-permute-done | bytes 393248 | tf_op jit(solution)/shard_map/ppermute | solution.py:33
  103.7 1.1 collective-permute-done.refs_5_.refs_1_
  105.9 15.7 %shard_map.214 = (bf16[256,768]{1,0:T(8,128)(2,1)}, bf16[256,768]{1,0:T(8,128)(2,1)}, bf16[256,768]{1,0:T(8,128)(2,1)}, bf16[256,768]{1,0:T(8,128)(2,1)}, bf16[7...) custom-call(bf16[128,768]{1,0:T(8,128)(2,1)} %refs_0_.6, ...), custom_call_target="tpu_custom_call" | custom-call | flops 3623878656 | bytes 8000000 | tf_op jit(solution)/shard_map/pallas_call | solution.py:644
  122.0 1.6 collective-permute-done.11
  123.6 1.1 add_convert_fusion.3.refs_4_
  125.8 2.8 %collective-permute-start.12 = (bf16[256,768]{1,0:T(8,128)(2,1)S(1)}, bf16[256,768]{1,0:T(8,128)(2,1)S(1)}, u32[]{:S(2)}, u32[]{:S(2)}) collective-permute-start(bf16[256,768]{1,0:T(8,128)(2,1)S(1)} %add_convert_fusion.3.refs_4_), channel_id=1, source_target_pairs={{0,1},{1,0},{2,3},{3,2},{4,5},{5,4},{6,7},{7,6},{8,9},{9,8},{10,11... | collective-permute-start | bytes 1179656 | tf_op jit(solution)/shard_map/ppermute | solution.py:33
  128.6 7.7 %collective-permute-done.14.refs_7_ = bf16[256,768]{1,0:T(8,128)(2,1)S(1)} collective-permute-done((bf16[256,768]{1,0:T(8,128)(2,1)S(1)}, bf16[256,768]{1,0:T(8,128)(2,1)S(1)}, u32[]{:S(2)}, u32[]{:S(2)}) %collective-permute-start.14) | collective-permute-done | bytes 393248 | tf_op jit(solution)/shard_map/ppermute | solution.py:48
  136.3 9.3 %collective-permute-done.12.refs_5_ = bf16[256,768]{1,0:T(8,128)(2,1)S(1)} collective-permute-done((bf16[256,768]{1,0:T(8,128)(2,1)S(1)}, bf16[256,768]{1,0:T(8,128)(2,1)S(1)}, u32[]{:S(2)}, u32[]{:S(2)}) %collective-permute-start.12) | collective-permute-done | bytes 393248 | tf_op jit(solution)/shard_map/ppermute | solution.py:33
  145.6 7.8 %all-to-all-start.2 = ((bf16[32,24,1536]{2,1,0:T(8,128)(2,1)}), bf16[32,24,1536]{2,1,0:T(8,128)(2,1)}, u32[]{:S(2)}, u32[]{:S(2)}) async-start(bf16[32,24,1536]{2,1,0:T(8,128)(2,1)} %bitcast.34), calls=%async_computation.2 | async-start | bytes 4718592 | tf_op jit(solution)/shard_map/all_to_all | solution.py:52
  153.8 2.1 collective-permute-start.15
  155.9 1.3 collective-permute-done.15.refs_8_
  158.0 14.3 %shard_map.215 = (bf16[256,768]{1,0:T(8,128)(2,1)}, bf16[256,768]{1,0:T(8,128)(2,1)}, bf16[768,1664]{1,0:T(8,128)(2,1)}, f32[128,768]{1,0:T(8,128)}) custom-call(bf16[128,768]{1,0:T(8,128)(2,1)} %refs_0_.7, bf16[128,768]{1,0:T(8,128)(2,1)} %copy-done.22, bf16[128,768]{1,0:T(8,128)(2,1)} %copy-done.21, bf16[128,768]{1,0:T(8,128)(2,1)} %copy-done.23, ...), custom_call_target="tpu_custom_call" | custom-call | flops 2415919104 | bytes 8000000 | tf_op jit(solution)/shard_map/pallas_call | solution.py:644
  172.4 9.7 %all-to-all-done.2.got_ref = bf16[32,24,1536]{2,1,0:T(8,128)(2,1)} async-done(((bf16[32,24,1536]{2,1,0:T(8,128)(2,1)}), bf16[32,24,1536]{2,1,0:T(8,128)(2,1)}, u32[]{:S(2)}, u32[]{:S(2)}) %all-to-all-start.2) | async-done | bytes 2359328 | tf_op jit(solution)/shard_map/all_to_all | solution.py:52
  182.1 8.2 %all-to-all-start.3 = ((bf16[32,24,1664]{2,1,0:T(8,128)(2,1)}), bf16[32,24,1664]{2,1,0:T(8,128)(2,1)}, u32[]{:S(2)}, u32[]{:S(2)}) async-start(bf16[32,24,1664]{2,1,0:T(8,128)(2,1)} %bitcast.33), calls=%async_computation.3 | async-start | bytes 5111808 | tf_op jit(solution)/shard_map/all_to_all | solution.py:52
  190.3 2.3 collective-permute-start.24
  192.6 1.2 collective-permute-done.24
  194.0 1.4 collective-permute-start.27
  195.7 2.3 collective-permute-start.25
  198.1 2.6 %shard_map.217.rest_2_ = bf16[24,2304]{1,0:T(8,128)(2,1)} custom-call(bf16[32,24,1536]{2,1,0:T(8,128)(2,1)} %all-to-all-done.2.got_ref), custom_call_target="tpu_custom_call" | custom-call | flops 150994944 | bytes 8000000 | tf_op jit(solution)/shard_map/pallas_call | solution.py:644
  200.7 1.4 collective-permute-start.23
  202.2 2.5 %collective-permute-start.21 = (bf16[128,768]{1,0:T(8,128)(2,1)S(1)}, bf16[128,768]{1,0:T(8,128)(2,1)S(1)}, u32[]{:S(2)}, u32[]{:S(2)}) collective-permute-start(bf16[128,768]{1,0:T(8,128)(2,1)S(1)} %get-tuple-element.120.rest_6_), channel_id=1, source_target_pairs={{0,1},{1,0},{2,3},{3,2},{4,5},{5,4},{6,7},{7,6},{8,9},{9,8},{10,11... | collective-permute-start | bytes 589832 | tf_op jit(solution)/shard_map/ppermute | solution.py:33
  204.7 20.5 %collective-permute-done.26.rest_15_ = bf16[128,768]{1,0:T(8,128)(2,1)S(1)} collective-permute-done((bf16[128,768]{1,0:T(8,128)(2,1)S(1)}, bf16[128,768]{1,0:T(8,128)(2,1)S(1)}, u32[]{:S(2)}, u32[]{:S(2)}) %collective-permute-start.26) | collective-permute-done | bytes 196640 | tf_op jit(solution)/shard_map/ppermute | solution.py:42
  225.2 1.3 collective-permute-start.18
  226.5 2.7 %shard_map.216 = (bf16[24,2432]{1,0:T(8,128)(2,1)}, bf16[24,128]{1,0:T(8,128)(2,1)}) custom-call(bf16[32,24,1664]{2,1,0:T(8,128)(2,1)} %all-to-all-done.3.got_ref), custom_call_target="tpu_custom_call" | custom-call | flops 1000 | bytes 8000000 | tf_op jit(solution)/shard_map/pallas_call | solution.py:644
  229.2 1.8 collective-permute-start.16
  231.0 1.8 collective-permute-start.20
  232.8 1.2 collective-permute-start.19
  233.9 3.5 %collective-permute-done.21.rest_7_ = bf16[128,768]{1,0:T(8,128)(2,1)S(1)} collective-permute-done((bf16[128,768]{1,0:T(8,128)(2,1)S(1)}, bf16[128,768]{1,0:T(8,128)(2,1)S(1)}, u32[]{:S(2)}, u32[]{:S(2)}) %collective-permute-start.21) | collective-permute-done | bytes 196640 | tf_op jit(solution)/shard_map/ppermute | solution.py:33
  237.5 0.9 collective-permute-done.20.rest_5_
  239.0 4.0 %shard_map.218 = (bf16[128,768]{1,0:T(8,128)(2,1)}, bf16[128,768]{1,0:T(8,128)(2,1)}, f32[2,24,1152]{2,1,0:T(8,128)}, f32[2,24,384]{2,1,0:T(8,128)}, f32[2,24,15...) custom-call(s32[1]{0:T(128)} %bitcast.core_ref, ...), custom_call_target="tpu_custom_call" | custom-call | flops 1000 | bytes 8000000 | tf_op jit(solution)/shard_map/pallas_call | solution.py:644
  (131 shorter events, 10.6 us)
Async XLA Ops:
  4.5 14.4 %copy-start.33 = (s32[1,4]{1,0:T(1,128)S(1)}, s32[1,4]{1,0:T(1,128)}, u32[]{:S(2)}) copy-start(s32[1,4]{1,0:T(1,128)} %param.15) | copy-start | bytes 52
  4.5 14.5 %copy-start.34 = (s32[1,4]{1,0:T(1,128)S(1)}, s32[1,4]{1,0:T(1,128)}, u32[]{:S(2)}) copy-start(s32[1,4]{1,0:T(1,128)} %param.16) | copy-start | bytes 52
  4.5 41.3 %all-to-all-start = ((bf16[32,24,1664]{2,1,0:T(8,128)(2,1)}), bf16[32,24,1664]{2,1,0:T(8,128)(2,1)S(1)}, u32[]{:S(2)}, u32[]{:S(2)}) async-start(bf16[32,24,1664]{2,1,0:T(8,128)(2,1)} %get-tuple-element.63), calls=%async_computation | async-start | bytes 5111808 | tf_op jit(solution)/shard_map/all_to_all | solution.py:52
  13.9 8.6 %collective-permute-start.4 = (bf16[128,768]{1,0:T(8,128)(2,1)S(1)}, bf16[128,768]{1,0:T(8,128)(2,1)}, u32[]{:S(2)}, u32[]{:S(2)}) collective-permute-start(bf16[128,768]{1,0:T(8,128)(2,1)S(1)} %copy-done.31), channel_id=1, source_target_pairs={{0,17},{1,16},{4,21},{5,20},{8,25},{9,24},{12,29},{13,28},{16,1},{... | collective-permute-start | bytes 589832 | tf_op jit(solution)/shard_map/ppermute | solution.py:48
  17.3 38.4 %collective-permute-start.3 = (bf16[128,768]{1,0:T(8,128)(2,1)S(1)}, bf16[128,768]{1,0:T(8,128)(2,1)}, u32[]{:S(2)}, u32[]{:S(2)}) collective-permute-start(bf16[128,768]{1,0:T(8,128)(2,1)S(1)} %copy-done.31), channel_id=1, source_target_pairs={{0,2},{2,0},{1,3},{3,1},{4,6},{6,4},{5,7},{7,5},{8,10},{10,8},{9,1... | collective-permute-start | bytes 589832 | tf_op jit(solution)/shard_map/ppermute | solution.py:29
  22.5 33.2 %collective-permute-start.5 = (bf16[128,768]{1,0:T(8,128)(2,1)}, bf16[128,768]{1,0:T(8,128)(2,1)S(1)}, u32[]{:S(2)}, u32[]{:S(2)}) collective-permute-start(bf16[128,768]{1,0:T(8,128)(2,1)} %collective-permute-done.4.refs_2_), channel_id=1, source_target_pairs={{0,2},{2,0},{1,3},{3,1},{4,6},{6,4},{5,7},{7,5},{8,10},{10,8},{9,1... | collective-permute-start | bytes 589832 | tf_op jit(solution)/shard_map/ppermute | solution.py:29
  47.2 57.8 %all-to-all-start.1 = ((bf16[32,24,1536]{2,1,0:T(8,128)(2,1)}), bf16[32,24,1536]{2,1,0:T(8,128)(2,1)}, u32[]{:S(2)}, u32[]{:S(2)}) async-start(bf16[32,24,1536]{2,1,0:T(8,128)(2,1)} %get-tuple-element.67), calls=%async_computation.1 | async-start | bytes 4718592 | tf_op jit(solution)/shard_map/all_to_all | solution.py:52
  56.4 17.9 %copy-start.20 = (bf16[128,768]{1,0:T(8,128)(2,1)S(1)}, bf16[128,768]{1,0:T(8,128)(2,1)}, u32[]{:S(2)}) copy-start(bf16[128,768]{1,0:T(8,128)(2,1)} %refs_0_.7) | copy-start | bytes 589828
  65.1 3.2 %collective-permute-start.6 = (bf16[256,768]{1,0:T(8,128)(2,1)}, bf16[256,768]{1,0:T(8,128)(2,1)S(1)}, u32[]{:S(2)}, u32[]{:S(2)}) collective-permute-start(bf16[256,768]{1,0:T(8,128)(2,1)} %get-tuple-element.65), channel_id=1, source_target_pairs={{0,2},{2,0},{1,3},{3,1},{4,6},{6,4},{5,7},{7,5},{8,10},{10,8},{9,1... | collective-permute-start | bytes 1179656 | tf_op jit(solution)/shard_map/ppermute | solution.py:29
  69.4 33.2 %copy-start.5 = (bf16[256,768]{1,0:T(8,128)(2,1)}, bf16[256,768]{1,0:T(8,128)(2,1)S(1)}, u32[]{:S(2)}) copy-start(bf16[256,768]{1,0:T(8,128)(2,1)S(1)} %add_convert_fusion.5.refs_8_) | copy-start | bytes 1179652
  69.4 22.6 %collective-permute-start.8 = (bf16[256,768]{1,0:T(8,128)(2,1)S(1)}, bf16[256,768]{1,0:T(8,128)(2,1)S(1)}, u32[]{:S(2)}, u32[]{:S(2)}) collective-permute-start(bf16[256,768]{1,0:T(8,128)(2,1)S(1)} %add_convert_fusion.5.refs_8_), channel_id=1, source_target_pairs={{0,16},{4,20},{8,24},{12,28},{16,0},{20,4},{24,8},{28,12},{32,48},... | collective-permute-start | bytes 1179656 | tf_op jit(solution)/shard_map/ppermute | solution.py:42
  70.9 21.2 %collective-permute-start.9 = (bf16[256,768]{1,0:T(8,128)(2,1)S(1)}, bf16[256,768]{1,0:T(8,128)(2,1)S(1)}, u32[]{:S(2)}, u32[]{:S(2)}) collective-permute-start(bf16[256,768]{1,0:T(8,128)(2,1)S(1)} %add_convert_fusion.5.refs_8_), channel_id=1, source_target_pairs={{0,17},{1,16},{4,21},{5,20},{8,25},{9,24},{12,29},{13,28},{16,1},{... | collective-permute-start | bytes 1179656 | tf_op jit(solution)/shard_map/ppermute | solution.py:48
  73.1 29.2 %collective-permute-start.7 = (bf16[256,768]{1,0:T(8,128)(2,1)S(1)}, bf16[256,768]{1,0:T(8,128)(2,1)S(1)}, u32[]{:S(2)}, u32[]{:S(2)}) collective-permute-start(bf16[256,768]{1,0:T(8,128)(2,1)S(1)} %add_convert_fusion.5.refs_8_), channel_id=1, source_target_pairs={{0,1},{1,0},{2,3},{3,2},{4,5},{5,4},{6,7},{7,6},{8,9},{9,8},{10,11... | collective-permute-start | bytes 1179656 | tf_op jit(solution)/shard_map/ppermute | solution.py:33
  74.2 29.0 %collective-permute-start.1 = (bf16[128,768]{1,0:T(8,128)(2,1)S(1)}, bf16[128,768]{1,0:T(8,128)(2,1)S(1)}, u32[]{:S(2)}, u32[]{:S(2)}) collective-permute-start(bf16[128,768]{1,0:T(8,128)(2,1)S(1)} %copy-done.20), channel_id=1, source_target_pairs={{0,17},{1,16},{4,21},{5,20},{8,25},{9,24},{12,29},{13,28},{16,1},{... | collective-permute-start | bytes 589832 | tf_op jit(solution)/shard_map/ppermute | solution.py:48
  92.0 10.5 %copy-start.10 = (bf16[256,768]{1,0:T(8,128)(2,1)}, bf16[256,768]{1,0:T(8,128)(2,1)S(1)}, u32[]{:S(2)}) copy-start(bf16[256,768]{1,0:T(8,128)(2,1)S(1)} %collective-permute-done.8.refs_10_) | copy-start | bytes 1179652
  92.1 10.5 %copy-start.12 = (bf16[256,768]{1,0:T(8,128)(2,1)}, bf16[256,768]{1,0:T(8,128)(2,1)S(1)}, u32[]{:S(2)}) copy-start(bf16[256,768]{1,0:T(8,128)(2,1)S(1)} %collective-permute-done.9.refs_11_) | copy-start | bytes 1179652
  102.6 2.5 %collective-permute-start.10 = (bf16[256,768]{1,0:T(8,128)(2,1)S(1)}, bf16[256,768]{1,0:T(8,128)(2,1)S(1)}, u32[]{:S(2)}, u32[]{:S(2)}) collective-permute-start(bf16[256,768]{1,0:T(8,128)(2,1)S(1)} %bitcast.42), channel_id=1, source_target_pairs={{0,2},{2,0},{1,3},{3,1},{4,6},{6,4},{5,7},{7,5},{8,10},{10,8},{9,1... | collective-permute-start | bytes 1179656 | tf_op jit(solution)/shard_map/ppermute | solution.py:29
  103.1 1.6 collective-permute-start
  103.2 1.8 collective-permute-start.2
  121.6 2.0 collective-permute-start.11
  124.7 28.9 %copy-start.1 = (bf16[256,768]{1,0:T(8,128)(2,1)}, bf16[256,768]{1,0:T(8,128)(2,1)S(1)}, u32[]{:S(2)}) copy-start(bf16[256,768]{1,0:T(8,128)(2,1)S(1)} %add_convert_fusion.3.refs_4_) | copy-start | bytes 1179652
  124.7 11.6 %collective-permute-start.14 = (bf16[256,768]{1,0:T(8,128)(2,1)S(1)}, bf16[256,768]{1,0:T(8,128)(2,1)S(1)}, u32[]{:S(2)}, u32[]{:S(2)}) collective-permute-start(bf16[256,768]{1,0:T(8,128)(2,1)S(1)} %add_convert_fusion.3.refs_4_), channel_id=1, source_target_pairs={{0,17},{1,16},{4,21},{5,20},{8,25},{9,24},{12,29},{13,28},{16,1},{... | collective-permute-start | bytes 1179656 | tf_op jit(solution)/shard_map/ppermute | solution.py:48
  125.4 10.9 %collective-permute-start.13 = (bf16[256,768]{1,0:T(8,128)(2,1)S(1)}, bf16[256,768]{1,0:T(8,128)(2,1)S(1)}, u32[]{:S(2)}, u32[]{:S(2)}) collective-permute-start(bf16[256,768]{1,0:T(8,128)(2,1)S(1)} %add_convert_fusion.3.refs_4_), channel_id=1, source_target_pairs={{0,16},{4,20},{8,24},{12,28},{16,0},{20,4},{24,8},{28,12},{32,48},... | collective-permute-start | bytes 1179656 | tf_op jit(solution)/shard_map/ppermute | solution.py:42
  125.8 19.8 %collective-permute-start.12 = (bf16[256,768]{1,0:T(8,128)(2,1)S(1)}, bf16[256,768]{1,0:T(8,128)(2,1)S(1)}, u32[]{:S(2)}, u32[]{:S(2)}) collective-permute-start(bf16[256,768]{1,0:T(8,128)(2,1)S(1)} %add_convert_fusion.3.refs_4_), channel_id=1, source_target_pairs={{0,1},{1,0},{2,3},{3,2},{4,5},{5,4},{6,7},{7,6},{8,9},{9,8},{10,11... | collective-permute-start | bytes 1179656 | tf_op jit(solution)/shard_map/ppermute | solution.py:33
  136.3 17.1 %copy-start.2 = (bf16[256,768]{1,0:T(8,128)(2,1)}, bf16[256,768]{1,0:T(8,128)(2,1)S(1)}, u32[]{:S(2)}) copy-start(bf16[256,768]{1,0:T(8,128)(2,1)S(1)} %collective-permute-done.14.refs_7_) | copy-start | bytes 1179652
  136.3 17.2 %copy-start.3 = (bf16[256,768]{1,0:T(8,128)(2,1)}, bf16[256,768]{1,0:T(8,128)(2,1)S(1)}, u32[]{:S(2)}) copy-start(bf16[256,768]{1,0:T(8,128)(2,1)S(1)} %collective-permute-done.13.refs_6_) | copy-start | bytes 1179652
  145.6 36.5 %all-to-all-start.2 = ((bf16[32,24,1536]{2,1,0:T(8,128)(2,1)}), bf16[32,24,1536]{2,1,0:T(8,128)(2,1)}, u32[]{:S(2)}, u32[]{:S(2)}) async-start(bf16[32,24,1536]{2,1,0:T(8,128)(2,1)} %bitcast.34), calls=%async_computation.2 | async-start | bytes 4718592 | tf_op jit(solution)/shard_map/all_to_all | solution.py:52
  153.8 3.5 %collective-permute-start.15 = (bf16[256,768]{1,0:T(8,128)(2,1)S(1)}, bf16[256,768]{1,0:T(8,128)(2,1)S(1)}, u32[]{:S(2)}, u32[]{:S(2)}) collective-permute-start(bf16[256,768]{1,0:T(8,128)(2,1)S(1)} %bitcast.43), channel_id=1, source_target_pairs={{0,2},{2,0},{1,3},{3,1},{4,6},{6,4},{5,7},{7,5},{8,10},{10,8},{9,1... | collective-permute-start | bytes 1179656 | tf_op jit(solution)/shard_map/ppermute | solution.py:29
  182.1 10.5 %copy-start.29 = (bf16[256,768]{1,0:T(8,128)(2,1)S(1)}, bf16[256,768]{1,0:T(8,128)(2,1)}, u32[]{:S(2)}) copy-start(bf16[256,768]{1,0:T(8,128)(2,1)} %get-tuple-element.95) | copy-start | bytes 1179652
  182.1 11.8 %copy-start.9 = (bf16[256,768]{1,0:T(8,128)(2,1)S(1)}, bf16[256,768]{1,0:T(8,128)(2,1)}, u32[]{:S(2)}) copy-start(bf16[256,768]{1,0:T(8,128)(2,1)} %get-tuple-element.101) | copy-start | bytes 1179652
  182.1 15.9 %copy-start.11 = (bf16[256,768]{1,0:T(8,128)(2,1)S(1)}, bf16[256,768]{1,0:T(8,128)(2,1)}, u32[]{:S(2)}) copy-start(bf16[256,768]{1,0:T(8,128)(2,1)} %get-tuple-element.94) | copy-start | bytes 1179652
  182.1 44.4 %all-to-all-start.3 = ((bf16[32,24,1664]{2,1,0:T(8,128)(2,1)}), bf16[32,24,1664]{2,1,0:T(8,128)(2,1)}, u32[]{:S(2)}, u32[]{:S(2)}) async-start(bf16[32,24,1664]{2,1,0:T(8,128)(2,1)} %bitcast.33), calls=%async_computation.3 | async-start | bytes 5111808 | tf_op jit(solution)/shard_map/all_to_all | solution.py:52
  190.3 3.6 %collective-permute-start.24 = (bf16[256,768]{1,0:T(8,128)(2,1)S(1)}, bf16[256,768]{1,0:T(8,128)(2,1)S(1)}, u32[]{:S(2)}, u32[]{:S(2)}) collective-permute-start(bf16[256,768]{1,0:T(8,128)(2,1)S(1)} %copy-done.28), channel_id=1, source_target_pairs={{0,2},{2,0},{1,3},{3,1},{4,6},{6,4},{5,7},{7,5},{8,10},{10,8},{9,1... | collective-permute-start | bytes 1179656 | tf_op jit(solution)/shard_map/ppermute | solution.py:29
  192.5 5.4 %collective-permute-start.17 = (bf16[256,768]{1,0:T(8,128)(2,1)S(1)}, bf16[256,768]{1,0:T(8,128)(2,1)S(1)}, u32[]{:S(2)}, u32[]{:S(2)}) collective-permute-start(bf16[256,768]{1,0:T(8,128)(2,1)S(1)} %copy-done.29), channel_id=1, source_target_pairs={{0,2},{2,0},{1,3},{3,1},{4,6},{6,4},{5,7},{7,5},{8,10},{10,8},{9,1... | collective-permute-start | bytes 1179656 | tf_op jit(solution)/shard_map/ppermute | solution.py:29
  194.0 35.1 %copy-start.6 = (bf16[128,768]{1,0:T(8,128)(2,1)}, bf16[128,768]{1,0:T(8,128)(2,1)S(1)}, u32[]{:S(2)}) copy-start(bf16[128,768]{1,0:T(8,128)(2,1)S(1)} %get-tuple-element.118.rest_13_) | copy-start | bytes 589828
  194.0 8.1 %collective-permute-start.27 = (bf16[128,768]{1,0:T(8,128)(2,1)S(1)}, bf16[128,768]{1,0:T(8,128)(2,1)S(1)}, u32[]{:S(2)}, u32[]{:S(2)}) collective-permute-start(bf16[128,768]{1,0:T(8,128)(2,1)S(1)} %get-tuple-element.117), channel_id=1, source_target_pairs={{0,17},{1,16},{4,21},{5,20},{8,25},{9,24},{12,29},{13,28},{16,1},{... | collective-permute-start | bytes 589832 | tf_op jit(solution)/shard_map/ppermute | solution.py:48
  195.5 29.7 %collective-permute-start.26 = (bf16[128,768]{1,0:T(8,128)(2,1)S(1)}, bf16[128,768]{1,0:T(8,128)(2,1)S(1)}, u32[]{:S(2)}, u32[]{:S(2)}) collective-permute-start(bf16[128,768]{1,0:T(8,128)(2,1)S(1)} %get-tuple-element.117), channel_id=1, source_target_pairs={{0,16},{4,20},{8,24},{12,28},{16,0},{20,4},{24,8},{28,12},{32,48},... | collective-permute-start | bytes 589832 | tf_op jit(solution)/shard_map/ppermute | solution.py:42
  195.7 33.5 %collective-permute-start.25 = (bf16[128,768]{1,0:T(8,128)(2,1)S(1)}, bf16[128,768]{1,0:T(8,128)(2,1)S(1)}, u32[]{:S(2)}, u32[]{:S(2)}) collective-permute-start(bf16[128,768]{1,0:T(8,128)(2,1)S(1)} %get-tuple-element.118.rest_13_), channel_id=1, source_target_pairs={{0,1},{1,0},{2,3},{3,2},{4,5},{5,4},{6,7},{7,6},{8,9},{9,8},{10,11... | collective-permute-start | bytes 589832 | tf_op jit(solution)/shard_map/ppermute | solution.py:33
  200.7 37.7 %copy-start.7 = (bf16[128,768]{1,0:T(8,128)(2,1)}, bf16[128,768]{1,0:T(8,128)(2,1)S(1)}, u32[]{:S(2)}) copy-start(bf16[128,768]{1,0:T(8,128)(2,1)S(1)} %get-tuple-element.120.rest_6_) | copy-start | bytes 589828
  200.7 32.0 %collective-permute-start.23 = (bf16[128,768]{1,0:T(8,128)(2,1)S(1)}, bf16[128,768]{1,0:T(8,128)(2,1)S(1)}, u32[]{:S(2)}, u32[]{:S(2)}) collective-permute-start(bf16[128,768]{1,0:T(8,128)(2,1)S(1)} %get-tuple-element.119), channel_id=1, source_target_pairs={{0,17},{1,16},{4,21},{5,20},{8,25},{9,24},{12,29},{13,28},{16,1},{... | collective-permute-start | bytes 589832 | tf_op jit(solution)/shard_map/ppermute | solution.py:48
  202.2 31.8 %collective-permute-start.22 = (bf16[128,768]{1,0:T(8,128)(2,1)S(1)}, bf16[128,768]{1,0:T(8,128)(2,1)S(1)}, u32[]{:S(2)}, u32[]{:S(2)}) collective-permute-start(bf16[128,768]{1,0:T(8,128)(2,1)S(1)} %get-tuple-element.119), channel_id=1, source_target_pairs={{0,16},{4,20},{8,24},{12,28},{16,0},{20,4},{24,8},{28,12},{32,48},... | collective-permute-start | bytes 589832 | tf_op jit(solution)/shard_map/ppermute | solution.py:42
  202.2 36.2 %copy-start.14 = (bf16[128,768]{1,0:T(8,128)(2,1)}, bf16[128,768]{1,0:T(8,128)(2,1)S(1)}, u32[]{:S(2)}) copy-start(bf16[128,768]{1,0:T(8,128)(2,1)S(1)} %collective-permute-done.27.rest_16_) | copy-start | bytes 589828
  202.2 35.3 %collective-permute-start.21 = (bf16[128,768]{1,0:T(8,128)(2,1)S(1)}, bf16[128,768]{1,0:T(8,128)(2,1)S(1)}, u32[]{:S(2)}, u32[]{:S(2)}) collective-permute-start(bf16[128,768]{1,0:T(8,128)(2,1)S(1)} %get-tuple-element.120.rest_6_), channel_id=1, source_target_pairs={{0,1},{1,0},{2,3},{3,2},{4,5},{5,4},{6,7},{7,6},{8,9},{9,8},{10,11... | collective-permute-start | bytes 589832 | tf_op jit(solution)/shard_map/ppermute | solution.py:33
  225.2 13.2 %copy-start.15 = (bf16[128,768]{1,0:T(8,128)(2,1)}, bf16[128,768]{1,0:T(8,128)(2,1)S(1)}, u32[]{:S(2)}) copy-start(bf16[128,768]{1,0:T(8,128)(2,1)S(1)} %collective-permute-done.26.rest_15_) | copy-start | bytes 589828
  225.2 5.8 %collective-permute-start.18 = (bf16[24,2304]{1,0:T(8,128)(2,1)}, bf16[24,2304]{1,0:T(8,128)(2,1)S(1)}, u32[]{:S(2)}, u32[]{:S(2)}) collective-permute-start(bf16[24,2304]{1,0:T(8,128)(2,1)} %shard_map.217.rest_2_), channel_id=1, source_target_pairs={{0,2},{2,0},{1,3},{3,1},{4,6},{6,4},{5,7},{7,5},{8,10},{10,8},{9,1... | collective-permute-start | bytes 331784 | tf_op jit(solution)/shard_map/ppermute | solution.py:29
  229.2 9.2 %collective-permute-start.16 = (bf16[24,2432]{1,0:T(8,128)(2,1)}, bf16[24,2432]{1,0:T(8,128)(2,1)S(1)}, u32[]{:S(2)}, u32[]{:S(2)}) collective-permute-start(bf16[24,2432]{1,0:T(8,128)(2,1)} %get-tuple-element.93.rest_0_), channel_id=1, source_target_pairs={{0,2},{2,0},{1,3},{3,1},{4,6},{6,4},{5,7},{7,5},{8,10},{10,8},{9,1... | collective-permute-start | bytes 350216 | tf_op jit(solution)/shard_map/ppermute | solution.py:29
  231.0 7.4 %collective-permute-start.20 = (bf16[24,128]{1,0:T(8,128)(2,1)}, bf16[24,128]{1,0:T(8,128)(2,1)S(1)}, u32[]{:S(2)}, u32[]{:S(2)}) collective-permute-start(bf16[24,128]{1,0:T(8,128)(2,1)} %get-tuple-element.98), channel_id=1, source_target_pairs={{0,3},{1,2},{2,1},{3,0},{4,7},{5,6},{6,5},{7,4},{8,11},{9,10},{10,... | collective-permute-start | bytes 18440 | tf_op jit(solution)/shard_map/ppermute | solution.py:37
  232.8 5.6 %collective-permute-start.19 = (bf16[24,128]{1,0:T(8,128)(2,1)}, bf16[24,128]{1,0:T(8,128)(2,1)S(1)}, u32[]{:S(2)}, u32[]{:S(2)}) collective-permute-start(bf16[24,128]{1,0:T(8,128)(2,1)} %get-tuple-element.98), channel_id=1, source_target_pairs={{0,1},{1,0},{2,3},{3,2},{4,5},{5,4},{6,7},{7,6},{8,9},{9,8},{10,11... | collective-permute-start | bytes 18440 | tf_op jit(solution)/shard_map/ppermute | solution.py:33
  (19 other events, 65.0 us)

commit v5 on v4

--- a/solution.py
+++ b/solution.py
@@ -48,8 +48,31 @@
     return lax.ppermute(values, ("fsdp", "tp"), pairs)
 
 
+def near_other_core(values):
+    owners = lax.axis_size("fsdp")
+    pairs = [(2 * f + c, 2 * (f ^ NEAR) + 1 - c) for f in range(owners) for c in (0, 1)]
+    return lax.ppermute(values, ("fsdp", "ctx"), pairs)
+
+
 def exchanged(blocks):
     return lax.all_to_all(blocks, "fsdp", 0, 0, tiled=True)
+
+
+def exchanged_in_plane(blocks):
+    owners = lax.axis_size("fsdp")
+    planes = [[f for f in range(owners) if f // NEAR % 2 == z] for z in (0, 1)]
+    return lax.all_to_all(blocks, "fsdp", 0, 0, axis_index_groups=planes, tiled=True)
+
+
+def pairs_together(slab, owners):
+    blocks = slab.reshape(owners // (2 * NEAR), 2, NEAR, -1, slab.shape[1])
+    return blocks.transpose(0, 2, 1, 3, 4).reshape(owners // 2, -1, slab.shape[1])
+
+
+def owners_in_order(blocks, owners):
+    width = blocks.shape[2]
+    blocks = blocks.reshape(owners // (2 * NEAR), NEAR, 2, -1, width)
+    return blocks.transpose(0, 2, 1, 3, 4).reshape(-1, width)
 
 
 def dot(left, right, along=(1, 0)):
@@ -378,9 +401,8 @@
 
 
 def summed_rows(parts, at, there):
-    mine, half, near, near_half = parts
-    first = mine[at, :].astype(F32) + half[at, :].astype(F32)
-    return first + (near[there, :].astype(F32) + near_half[there, :].astype(F32))
+    mine, near = parts
+    return mine[at, :].astype(F32) + near[there, :].astype(F32)
 
 
 def moved(at, by):
@@ -409,7 +431,7 @@
 
 
 def last_kernel(*refs):
-    inputs, far_ends, parts, refs = refs[:4], refs[4:8], refs[8:12], refs[12:]
+    inputs, far_ends, parts, refs = refs[:4], refs[4:8], refs[8:10], refs[10:]
     other_ref, vec_ref, far_ref, far_table_ref, far_mask_ref, *rest = refs
     far_parts, rest = rest[:4], rest[4:]
     slab_ref, sums_ref, far_hidden_ref, far_normed_ref, far_inv_std_ref, *rest = rest
@@ -446,7 +468,7 @@
 
 
 def back_kernel(layers, *refs):
-    inputs, parts, refs = refs[:4], refs[4:8], refs[8:]
+    inputs, parts, refs = refs[:4], refs[4:6], refs[6:]
     other_ref, normed_ref, inv_std_ref, later_ref, vec_ref, far_ref, place_ref, far_table_ref, *rest = refs
     far_state, rest = rest[:10], rest[10:]
     far_back, (slab_ref, kept_ref, table_ref, get, put, *rest) = rest[:2], rest[2:]
@@ -489,8 +511,8 @@
     put.wait()
 
 
-def slabs_kernel(layers, core_ref, *refs):
-    far, sends, refs = refs[:9], refs[9 : 9 + layers], refs[9 + layers :]
+def slabs_kernel(layers, core_ref, place_ref, *refs):
+    far, (send_ref, own_ref, near_ref), refs = refs[:9], refs[9:12], refs[12:]
     local, (rows_ref, bias_ref, arrived) = refs[:9], refs[9:]
     copies = [
         pltpu.make_async_copy(src, dst, arrived.at[i])
@@ -536,103 +558,120 @@
             at = slice(z * hidden, (z + 1) * hidden)
             wide[z].append(jnp.concatenate([up[:, at], down[:, at]], axis=1))
     for z in (0, 1):
-        for layer, send_ref in enumerate(sends):
-            block = [heads[layer], wide[z][layer]] + ([small] if layer == 0 else [])
-            block = jnp.concatenate(block, axis=1)
-            for owner in range(send_ref.shape[0]):
-                if owner // NEAR % 2 == z:
-                    send_ref[owner] = block
-
-
-def sums_of(got_ref, columns):
-    sums = []
-    for z in (0, 1):
-        senders = [owner for owner in range(got_ref.shape[0]) if owner // NEAR % 2 == z]
-        total = got_ref[senders[0], :, columns].astype(F32)
-        for owner in senders[1:]:
-            total = total + got_ref[owner, :, columns].astype(F32)
-        sums.append(total)
-    return sums
-
-
-def put_sums(attn, got_ref, all_ref):
-    hidden = (all_ref.shape[1] - attn) // 4
-    first, second = sums_of(got_ref, slice(0, attn))
-    all_ref[:, :attn] = (first + second).astype(BF)
-    for kind in (0, 1):
-        at = attn + kind * hidden
-        for z, total in enumerate(sums_of(got_ref, slice(at, at + hidden))):
-            at_z = attn + (2 * kind + z) * hidden
-            all_ref[:, at_z : at_z + hidden] = total.astype(BF)
+        block = jnp.concatenate([heads[0], wide[z][0], small], axis=1)
+        for owner in range(send_ref.shape[0]):
+            if owner // NEAR % 2 == z:
+                send_ref[owner] = block
+    first = place_ref[0] == 0
+    own_ref[...] = jnp.concatenate([heads[1], jnp.where(first, *wide_of(wide, 0, 1))], axis=1)
+    near_ref[...] = jnp.concatenate([heads[1], jnp.where(first, *wide_of(wide, 1, 0))], axis=1)
+
+
+def wide_of(wide, *at):
+    return [wide[z][1] for z in at]
+
+
+def sum_of(got_ref, columns):
+    total = got_ref[0, :, columns].astype(F32)
+    for sender in range(1, got_ref.shape[0]):
+        total = total + got_ref[sender, :, columns].astype(F32)
+    return total
+
+
+def put_sums(place_ref, got_ref, own_ref, near_ref):
+    depth = own_ref.shape[0]
+    step = 3 * LANES
+    for begin in range(0, own_ref.shape[1], step):
+        at = slice(begin, begin + step)
+        total = sum_of(got_ref, at)
+        low, high = total[:depth], total[depth:]
+        own_ref[:, at] = jnp.where(place_ref[0] == 0, low, high).astype(BF)
+        near_ref[:, at] = jnp.where(place_ref[0] == 0, high, low).astype(BF)
 
 
 def total_of(refs):
-    mine, half, near, near_half = (ref[...].astype(F32) for ref in refs)
-    return (mine + half) + (near + near_half)
-
-
-def gather_late_kernel(attn, got_ref, all_ref):
-    put_sums(attn, got_ref, all_ref)
-
-
-def gather_kernel(attn, got_ref, all_ref, small_ref, pad_ref):
-    depth, width = got_ref.shape[1], got_ref.shape[2] - LANES
-    put_sums(attn, got_ref, all_ref.at[:, : all_ref.shape[1] - LANES])
-    first, second = sums_of(got_ref, slice(width, width + LANES))
+    mine, near = refs
+    return mine[...].astype(F32) + near[...].astype(F32)
+
+
+def gather_late_kernel(place_ref, got_ref, own_ref, near_ref):
+    put_sums(place_ref, got_ref, own_ref, near_ref)
+
+
+def gather_kernel(place_ref, got_ref, own_ref, near_ref, pad_ref):
+    depth, width = own_ref.shape[0], own_ref.shape[1] - LANES
+    put_sums(place_ref, got_ref, own_ref.at[:, :width], near_ref.at[:, :width])
     pad_ref[...] = jnp.zeros_like(pad_ref)
-    pad_ref[:depth, :] = first + second
-    small = jnp.transpose(pad_ref[...])[: small_ref.shape[0]].astype(BF)
-    small_ref[...] = small
-    all_ref[:, all_ref.shape[1] - LANES :] = small
-
-
-def finish_kernel(layers, core_ref, *rest):
-    pairs, (half_ref, core_half_ref), rest = (rest[:2], rest[2:4]), rest[4:6], rest[6:]
-    parts, (below_ref, far_normed_ref, far_inv_std_ref, *rest) = rest[:4], rest[4:]
-    ahead, hidden_ref, rest = rest[:4], rest[4], rest[5:]
-    result_ref, grad_ref, qkv_ref, out_ref, up_ref, down_ref, *vectors = rest[:11]
-    normed_ref, inv_std_ref, get = rest[11:]
+    pad_ref[: 2 * depth, :] = sum_of(got_ref, slice(width, width + LANES))
+    low = jnp.transpose(pad_ref[...])[:depth]
+    high = pltpu.roll(low, LANES - depth, 1)
+    own_ref[:, width:] = jnp.where(place_ref[0] == 0, low, high).astype(BF)
+    near_ref[:, width:] = jnp.where(place_ref[0] == 0, high, low).astype(BF)
+
+
+def finish_kernel(layers, core_ref, place_ref, *rest):
+    groups, rest = (rest[:4], rest[4:8]), rest[8:]
+    parts, (below_ref, far_normed_ref, far_inv_std_ref, *rest) = rest[:2], rest[2:]
+    hidden_ref, *rest = rest
+    result_ref, grad_ref, qkv_ref, out_ref, up_ref, down_ref, *biases = rest[:8]
+    normed_ref, inv_std_ref, get = rest[8:]
     get = Copies(get)
     own = pl.ds(0, normed_ref.shape[0])
     get.start(far_normed_ref.at[own, :], normed_ref)
     get.start(far_inv_std_ref.at[own, :], inv_std_ref)
-    bias_qkv_ref, bias_up_ref, bias_out_ref, gain_ref, shift_ref = vectors
     width_qkv, width_out, width_up = (r.shape[2] // 2 for r in (qkv_ref, out_ref, up_ref))
     depth, heads = qkv_ref.shape[1], width_out // HS
     attn = heads * HEAD
-    width = attn + 2 * width_up
-    low = core_ref[0] == 0
-    for layer, pair in enumerate(pairs):
-        mine, theirs = (ref[:, :width].astype(F32) for ref in pair)
-        sides = (jnp.where(low, mine, theirs), jnp.where(low, theirs, mine))
-        for side, values in enumerate(sides):
-            at = side * width_up
-            up_ref[layer, :, at : at + width_up] = values[:, attn : attn + width_up]
-            down_ref[layer, :, at : at + width_up] = values[:, attn + width_up :]
+    low, first = core_ref[0] == 0, place_ref[0] == 0
+
+    def both_places(own, near):
+        return jnp.where(first, own, near), jnp.where(first, near, own)
+
+    hidden = width_up // 2
+    for layer, group in enumerate(groups):
+        mine, core, near, core_near = (ref[:, : attn + width_up].astype(F32) for ref in group)
+        attention = (mine[:, :attn] + near[:, :attn], core[:, :attn] + core_near[:, :attn])
+        sides = (jnp.where(low, *attention), jnp.where(low, *attention[::-1]))
         starts = [(values, head * HEAD) for values in sides for head in range(heads)]
         qkv_ref[layer] = jnp.concatenate([v[:, at : at + 3 * HS] for v, at in starts], axis=1)
         out_ref[layer] = jnp.concatenate([v[:, at + 3 * HS : at + HEAD] for v, at in starts], axis=1)
-    mine, core = (ref[:, width:].astype(F32) for ref in pairs[0])
-    half, core_half = half_ref[...].astype(F32), core_half_ref[...].astype(F32)
-    vectors = (mine + half) + (core + core_half)
+        for z, (ours, theirs) in enumerate(
+            zip(both_places(mine, near), both_places(core, core_near), strict=True)
+        ):
+            for side, values in enumerate((jnp.where(low, ours, theirs), jnp.where(low, theirs, ours))):
+                at = side * width_up + z * hidden
+                up_ref[layer, :, at : at + hidden] = values[:, attn : attn + hidden]
+                down_ref[layer, :, at : at + hidden] = values[:, attn + hidden : attn + 2 * hidden]
+    rows = small_sum([ref[:, attn + width_up :] for ref in groups[0]])
+    at = 5 * layers
+    for ref in biases:
+        low_rows, high_rows = rows[at : at + layers], rows[at + layers : at + 2 * layers]
+        lanes = lax.broadcasted_iota(jnp.int32, low_rows.shape, 1)
+        both = jnp.where(lanes < depth, low_rows, pltpu.roll(high_rows, depth, 1))
+        ref[...] = both[:, : ref.shape[1]]
+        at += 2 * layers
+    totals = total_of(parts)
+    count = hidden_ref.shape[0]
+    result_ref[...] = (hidden_ref[...] + totals[:count]).astype(BF)
+    get.wait()
+    total = row_norm_back(totals[count:], normed_ref[...], inv_std_ref[...])
+    grad_ref[...] = (below_ref[...] + total).astype(BF)
+
+
+def small_sum(parts):
+    mine, core, near, core_near = (part.astype(F32) for part in parts)
+    return (mine + near) + (core + core_near)
+
+
+def vectors_kernel(layers, mine_ref, half_ref, bias_out_ref, gain_ref, shift_ref):
+    vectors = mine_ref[...] + half_ref[...]
+    depth = gain_ref.shape[2]
     for layer in range(layers):
         rows = vectors[5 * layer : 5 * layer + 5, :depth]
         bias_out_ref[layer, 0:1, :] = rows[:1]
         bias_out_ref[layer, 1:2, :] = rows[:1]
         gain_ref[layer] = rows[1:3]
         shift_ref[layer] = rows[3:5]
-    biases = mine + core
-    at = 5 * layers
-    for ref in (bias_qkv_ref, bias_up_ref):
-        first, second = biases[at : at + layers], biases[at + layers : at + 2 * layers]
-        lanes = lax.broadcasted_iota(jnp.int32, first.shape, 1)
-        both = jnp.where(lanes < depth, first, pltpu.roll(second, depth, 1))
-        ref[...] = both[:, : ref.shape[1]]
-        at += 2 * layers
-    result_ref[...] = (hidden_ref[...] + total_of(ahead)).astype(BF)
-    get.wait()
-    total = row_norm_back(total_of(parts), normed_ref[...], inv_std_ref[...])
-    grad_ref[...] = (below_ref[...] + total).astype(BF)
 
 
 def call(kernel, outs, scratch, flops, *args, far=(), far_outs=(), limit=VMEM_BYTES, **more):
@@ -659,19 +698,23 @@
     return (kept.astype(F32) + other_core(sent).astype(F32)).astype(BF)
 
 
-def parts_of_sum(mine):
-    return mine, other_half(mine), near_group(mine), near_other_half(mine)
-
-
-def other_rows(parts):
-    mine, half, near, near_half = (p.astype(F32).reshape(2, -1, p.shape[1]) for p in parts)
-    total = (mine + half) + (near[::-1] + near_half[::-1])
-    return other_core(total.astype(BF).reshape(parts[0].shape))
-
-
-def own_parts(mine):
-    own = mine.shape[0] // 2
-    return mine[:own], other_half(mine[:own]), near_group(mine[own:]), near_other_half(mine[own:])
+def turned_groups(values):
+    return values.reshape(2, -1, values.shape[1])[::-1].reshape(values.shape)
+
+
+def pair_sum(mine):
+    theirs = turned_groups(near_other_half(mine))
+    return (mine.astype(F32) + theirs.astype(F32)).astype(BF)
+
+
+def other_rows(mine, near):
+    return other_core((mine.astype(F32) + turned_groups(near).astype(F32)).astype(BF))
+
+
+def own_parts(*mines):
+    count = mines[0].shape[0] // 2
+    own = jnp.concatenate([mine[:count] for mine in mines])
+    return own, near_group(jnp.concatenate([mine[count:] for mine in mines]))
 
 
 def rotation(positions):
@@ -728,6 +771,7 @@
     rows = 4 * row_count
 
     core_at = core.astype(jnp.int32).reshape(1)
+    place_at = place_z.astype(jnp.int32).reshape(1)
     sds = jax.ShapeDtypeStruct
     raw = (
         w_qkv,
@@ -740,23 +784,30 @@
         b_qkv,
         b_up,
     )
-    sends = call(
+    send, own_block, near_block = call(
         functools.partial(slabs_kernel, layers),
         (
             sds((owners, depth, width + LANES), BF),
-            sds((owners, depth, width), BF),
+            sds((depth, width), BF),
+            sds((depth, width), BF),
         ),
         [pltpu.VMEM(a.shape, a.dtype) for a in raw]
         + [pltpu.VMEM((LANES, LANES), F32), pltpu.VMEM((8, LANES), F32)]
         + [pltpu.SemaphoreType.DMA((len(raw),))],
         1000,
         core_at,
+        place_at,
         *raw,
-        far=range(1, 1 + len(raw)),
-    )
-    first, second = (exchanged(blocks).reshape(wide, -1) for blocks in sends)
+        far=range(2, 2 + len(raw)),
+    )
     starts, ends = ((own, near_other_half(own)) for own in (tokens, cotangent))
     starts, ends = ((o, other_core(o), n, other_core(n)) for o, n in (starts, ends))
+    first = exchanged(send).reshape(wide, -1)
+    pair = [own_block, near_group(near_block)]
+    pair = jnp.where(place_z == 0, jnp.concatenate(pair), jnp.concatenate(pair[::-1]))
+    pair, starts, ends = lax.optimization_barrier((pair, starts, ends))
+    second = jnp.broadcast_to(pair[None], (owners // 2, *pair.shape))
+    second = owners_in_order(exchanged_in_plane(second), owners)
     offsets = jnp.arange(block_rows, dtype=jnp.int32)
     positions = (block_pos[0][:, None] * block_rows + offsets[None, :]).reshape(2, row_count)
     positions = jnp.where(core == 0, positions, positions[::-1]).reshape(-1)
@@ -808,7 +859,8 @@
         far=(4, 6, 7),
         far_outs=(0, 1, *range(3, 13)),
     )
-    parts = parts_of_sum(core_rows_summed(kept_part, sent_part))
+    mine = pair_sum(core_rows_summed(kept_part, sent_part))
+    mine, near, second = lax.optimization_barrier((mine, near_group(mine), second))
     scratch = [
         pltpu.VMEM((rows, wide), BF),
         pltpu.VMEM((rows, hidden), BF),
@@ -835,19 +887,21 @@
         3 * flops,
         *starts,
         *ends,
-        *parts,
-        other_rows(parts),
+        mine,
+        near,
+        other_rows(mine, near),
         vec,
         second,
         table,
         mask,
-        far=(4, 5, 6, 7, 14, 15, 16),
+        far=(4, 5, 6, 7, 12, 13, 14),
         far_outs=(0, 1, 2, 3, 4, 6, 7, 8),
     )
-    parts = parts_of_sum(core_rows_summed(*sums[2:]))
-    slab, *sums = lax.optimization_barrier((slab, *sums[:2], *parts))
-    ahead, parts = own_parts(core_rows_summed(*sums[:2])), sums[2:]
-    later = exchanged(slab.reshape(owners, depth, -1))
+    mine = pair_sum(core_rows_summed(*sums[2:]))
+    mine, slab = lax.optimization_barrier((mine, pairs_together(slab, owners)))
+    later = exchanged_in_plane(slab)
+    ahead, near = lax.optimization_barrier((sums[:2], near_group(mine)))
+    ahead = pair_sum(core_rows_summed(*ahead))
     kept_part, sent_part, slab, grad_below = call(
         functools.partial(back_kernel, layers),
         (part, part, sds((wide, width + LANES), BF), sds((row_count, wide), F32)),
@@ -861,8 +915,9 @@
         ],
         2 * flops,
         *ends,
-        *parts,
-        other_rows(parts),
+        mine,
+        near,
+        other_rows(mine, near),
         normed,
         inv_std,
         later_sums,
@@ -871,30 +926,32 @@
         place,
         table,
         *state,
-        far=(13, *range(15, 26)),
+        far=(11, *range(13, 24)),
         far_outs=(0, 1, 2),
     )
-    slab, later = lax.optimization_barrier((slab, later))
-    earlier = exchanged(slab.reshape(owners, depth, -1))
-    below = core_rows_summed(kept_part, sent_part)
-
-    (late,) = call(
-        functools.partial(gather_late_kernel, attn),
-        (sds((depth, attn + 4 * hidden), BF),),
-        [],
-        flops // 8,
-        later,
-    )
-    below, late = lax.optimization_barrier((below, late))
-    below = own_parts(below)
-    mine, small = call(
-        functools.partial(gather_kernel, attn),
-        (sds((depth, attn + 4 * hidden + LANES), BF), sds((depth, LANES), BF)),
-        [pltpu.VMEM((LANES, LANES), F32)],
-        1000,
-        earlier,
-    )
-    result, grad_tokens, grad_qkv, grad_out, grad_up, grad_down, *vectors = call(
+    slab = pairs_together(slab, owners)
+    slab, later, ahead = lax.optimization_barrier((slab, later, ahead))
+    earlier = exchanged_in_plane(slab)
+    below = pair_sum(core_rows_summed(kept_part, sent_part))
+
+    piece = sds((depth, width), BF)
+    late = call(gather_late_kernel, (piece, piece), [], flops // 8, place_at, later)
+    ends = own_parts(ahead, below)
+
+    def of_all(own, near):
+        return own, other_core(own), near_group(near), near_other_core(near)
+
+    late = of_all(*late)
+    earlier, late, ends = lax.optimization_barrier((earlier, late, ends))
+    piece = sds((depth, width + LANES), BF)
+    early = of_all(
+        *call(
+            gather_kernel, (piece, piece), [pltpu.VMEM((LANES, LANES), F32)], 1000, place_at, earlier
+        )
+    )
+    small = small_sum([part[:, width:] for part in early])
+    half = other_half(small)
+    result, grad_tokens, grad_qkv, grad_out, grad_up, grad_down, grad_b_qkv, grad_b_up = call(
         functools.partial(finish_kernel, layers),
         (sds(tokens.shape, BF),) * 2
         + tuple(
@@ -906,27 +963,28 @@
                 (layers, depth, w_down.shape[1]),
                 b_qkv.shape,
                 b_up.shape,
-                out_bias.shape,
-                norm_gain.shape,
-                norm_bias.shape,
             )
         ),
         [*vmem(sds((row_count, wide), F32), sds((row_count, 1), F32)), *copies(2)],
-        1000,
+        flops // 8,
         core_at,
-        mine,
-        other_core(mine),
-        late,
-        other_core(late),
-        other_half(small),
-        other_core_and_half(small),
-        *below,
+        place_at,
+        *early,
+        *late,
+        *ends,
         grad_below,
         state[0],
         state[1],
-        *ahead,
         result,
-        far=(12, 13),
+        far=(13, 14),
+    )
+    vectors = call(
+        functools.partial(vectors_kernel, layers),
+        tuple(sds(a.shape, F32) for a in (out_bias, norm_gain, norm_bias)),
+        [],
+        1000,
+        small,
+        half,
     )
     return (
         result,
@@ -935,6 +993,8 @@
         grad_out.transpose(0, 2, 1),
         grad_up,
         grad_down.transpose(0, 2, 1),
+        grad_b_qkv,
+        grad_b_up,
         *vectors,
     )
 

time: 244 us -> 229 us (0.939)
  waiting for transfers between devices: 107 us -> 89.8 us
  local copies, waits for them, and re-layouts: 6.17 us -> 16.4 us
  starting transfers between devices: 71.1 us -> 60.9 us
  other arithmetic: 5.6 us -> 8.18 us
    all_to_all x4 -> x1, waiting for transfers between devices: 32.2 us -> 3.94 us  [exchanged(): return lax.all_to_all(blocks, 'fsdp', 0, 0, tiled=True)]
    ppermute x6, waiting for transfers between devices: 7.69 us -> 31.6 us  [near_other_half(): return lax.ppermute(values, ('fsdp', 'tp'), pairs)]
    all_to_all x4 -> x1, starting transfers between devices: 33 us -> 9.37 us  [exchanged(): return lax.all_to_all(blocks, 'fsdp', 0, 0, tiled=True)]
    ppermute x5 -> x1, waiting for transfers between devices: 23 us -> 0.01 us  [other_half(): return lax.ppermute(values, 'tp', SWAP)]
    all_to_all x0 -> x3, starting transfers between devices: none -> 19.7 us  [exchanged_in_plane(): lax.all_to_all(blocks, 'fsdp', 0, 0, axis_index_groups=planes, tiled=True)]
    all_to_all x0 -> x3, waiting for transfers between devices: none -> 14.5 us  [exchanged_in_plane(): lax.all_to_all(blocks, 'fsdp', 0, 0, axis_index_groups=planes, tiled=True)]
    ppermute x4 -> x6, waiting for transfers between devices: 36.2 us -> 24.8 us  [near_group(): return lax.ppermute(values, 'fsdp', [(f, f ^ NEAR) for f in range(owners)])]
    ppermute x5 -> x1, starting transfers between devices: 9.92 us -> 0.73 us  [other_half(): return lax.ppermute(values, 'tp', SWAP)]
  transfers between devices with their start and end apart: 32 -> 31, of which waited for: 15 -> 20; matrix products, arithmetic and copies ran while one was open for 3% -> 8% of each run, Pallas kernels for 12% -> 13%
where the time goes in v5:
time: 229 us; the launch traced here: 228 us
  waiting for transfers between devices  89.8 us (39%)
  starting transfers between devices  60.9 us (27%)
  Pallas kernels  51.6 us (23%)
  local copies, waits for them, and re-layouts  16.4 us (7%)
  other arithmetic  8.18 us (4%)
    pallas_call x8, Pallas kernels, call(): pl.pallas_call(kernel, out_shape=outs, in_specs=[pl.BlockSpec(memory_spac...  51.6 us
    ppermute x6, waiting for transfers between devices, near_other_half(): return lax.ppermute(values, ('fsdp', 'tp'), pairs)  31.6 us
    ppermute x6, waiting for transfers between devices, near_group(): return lax.ppermute(values, 'fsdp', [(f, f ^ NEAR) for f in range(owners)])  24.8 us
    all_to_all x3, starting transfers between devices, exchanged_in_plane(): lax.all_to_all(blocks, 'fsdp', 0, 0, axis_index_groups=planes, tiled=True)  19.7 us
    all_to_all x3, waiting for transfers between devices, exchanged_in_plane(): lax.all_to_all(blocks, 'fsdp', 0, 0, axis_index_groups=planes, tiled=True)  14.5 us
    ppermute x6, starting transfers between devices, near_other_half(): return lax.ppermute(values, ('fsdp', 'tp'), pairs)  12.9 us
    ppermute x12, starting transfers between devices, other_core(): return lax.ppermute(values, 'ctx', SWAP)  11.5 us
    all_to_all x1, starting transfers between devices, exchanged(): return lax.all_to_all(blocks, 'fsdp', 0, 0, tiled=True)  9.37 us
  transfers between devices with their start and end apart: 31, of which 20 were waited for; matrix products, arithmetic and copies ran while one was open for 8% of the time, Pallas kernels for 13%

profile of v5, /device:TPU:1, one launch (start us, length us, event | category | flops | bytes accessed | tf_op | source)
XLA Modules:
  0.0 228.1 jit_solution(3447793512887586328)
XLA Ops:
  0.7 2.9 %shard_map.212 = (bf16[32,24,1664]{2,1,0:T(8,128)(2,1)}, bf16[24,1536]{1,0:T(8,128)(2,1)}, bf16[24,1536]{1,0:T(8,128)(2,1)}) custom-call(s32[1]{0:T(128)} %bitcast.core_ref, s32[1]{0:T(128)} %bitcast.1.place_ref, bf16[2,24,1152]{2,1,0:T(8,128)(2,1)} %refs_0_.1, bf16[2,24,384]{2,1,0:T(8,128)(2,1)} %bitcast.66, bf16[2,24,1536]{2,1,0:T(8,128)(2,1)} %refs_2_.1, ...), custom_call_target="tpu_custom_call" | custom-call | flops 1000 | bytes 8000000 | tf_op jit(solution)/shard_map/pallas_call | solution.py:683
  3.7 9.4 %all-to-all-start = ((bf16[32,24,1664]{2,1,0:T(8,128)(2,1)}), bf16[32,24,1664]{2,1,0:T(8,128)(2,1)S(1)}, u32[]{:S(2)}, u32[]{:S(2)}) async-start(bf16[32,24,1664]{2,1,0:T(8,128)(2,1)} %get-tuple-element.92), calls=%async_computation | async-start | bytes 5111808 | tf_op jit(solution)/shard_map/all_to_all | solution.py:58
  13.0 1.0 collective-permute-start.1
  14.1 3.6 %collective-permute-start.2 = (bf16[128,768]{1,0:T(8,128)(2,1)}, bf16[128,768]{1,0:T(8,128)(2,1)}, u32[]{:S(2)}, u32[]{:S(2)}) collective-permute-start(bf16[128,768]{1,0:T(8,128)(2,1)} %refs_0_.3), channel_id=1, source_target_pairs={{0,17},{1,16},{4,21},{5,20},{8,25},{9,24},{12,29},{13,28},{16,1},{... | collective-permute-start | bytes 589832 | tf_op jit(solution)/shard_map/ppermute | solution.py:48
  20.8 2.4 %collective-permute-done.2.refs_2_ = bf16[128,768]{1,0:T(8,128)(2,1)} collective-permute-done((bf16[128,768]{1,0:T(8,128)(2,1)}, bf16[128,768]{1,0:T(8,128)(2,1)}, u32[]{:S(2)}, u32[]{:S(2)}) %collective-permute-start.2) | collective-permute-done | bytes 196640 | tf_op jit(solution)/shard_map/ppermute | solution.py:48
  24.2 3.3 %collective-permute-done.5.refs_6_.refs_2_ = bf16[128,768]{1,0:T(8,128)(2,1)} collective-permute-done((bf16[128,768]{1,0:T(8,128)(2,1)S(1)}, bf16[128,768]{1,0:T(8,128)(2,1)}, u32[]{:S(2)}, u32[]{:S(2)}) %collective-permute-start.5) | collective-permute-done | bytes 196640 | tf_op jit(solution)/shard_map/ppermute | solution.py:48
  28.1 11.8 %collective-permute-done = bf16[24,1536]{1,0:T(8,128)(2,1)} collective-permute-done((bf16[24,1536]{1,0:T(8,128)(2,1)}, bf16[24,1536]{1,0:T(8,128)(2,1)}, u32[]{:S(2)}, u32[]{:S(2)}) %collective-permute-start) | collective-permute-done | bytes 73760 | tf_op jit(solution)/shard_map/ppermute | solution.py:42
  39.9 1.0 maximum_select_fusion
  41.0 3.9 %all-to-all-done = bf16[32,24,1664]{2,1,0:T(8,128)(2,1)S(1)} async-done(((bf16[32,24,1664]{2,1,0:T(8,128)(2,1)}), bf16[32,24,1664]{2,1,0:T(8,128)(2,1)S(1)}, u32[]{:S(2)}, u32[]{:S(2)}) %all-to-all-start) | async-done | bytes 2555936 | tf_op jit(solution)/shard_map/all_to_all | solution.py:58
  44.9 1.8 broadcast_in_dim.35
  47.1 7.0 %all-to-all-start.1 = ((bf16[16,48,1536]{2,1,0:T(8,128)(2,1)}), bf16[16,48,1536]{2,1,0:T(8,128)(2,1)}, u32[]{:S(2)}, u32[]{:S(2)}) async-start(bf16[16,48,1536]{2,1,0:T(8,128)(2,1)} %broadcast_in_dim.35), calls=%async_computation.1 | async-start | bytes 4718592 | tf_op jit(solution)/shard_map/all_to_all | solution.py:64
  55.8 8.7 %shard_map.213 = (bf16[256,768]{1,0:T(8,128)(2,1)}, bf16[256,768]{1,0:T(8,128)(2,1)}, f32[2,8,768]{2,1,0:T(8,128)}, f32[512,768]{1,0:T(8,128)}, f32[512,1]{1,0:T...) custom-call(bf16[128,768]{1,0:T(8,128)(2,1)} %refs_0_.3, ...), custom_call_target="tpu_custom_call" | custom-call | flops 1207959552 | bytes 8000000 | tf_op jit(solution)/shard_map/pallas_call | solution.py:683
  64.5 1.8 collective-permute-start.7
  66.3 1.6 collective-permute-done.7
  67.9 1.1 add_convert_fusion.3
  69.0 2.4 %collective-permute-start.8 = (bf16[256,768]{1,0:T(8,128)(2,1)S(1)}, bf16[256,768]{1,0:T(8,128)(2,1)S(1)}, u32[]{:S(2)}, u32[]{:S(2)}) collective-permute-start(bf16[256,768]{1,0:T(8,128)(2,1)S(1)} %add_convert_fusion.3), channel_id=1, source_target_pairs={{0,17},{1,16},{4,21},{5,20},{8,25},{9,24},{12,29},{13,28},{16,1},{... | collective-permute-start | bytes 1179656 | tf_op jit(solution)/shard_map/ppermute | solution.py:48
  71.4 9.3 %collective-permute-done.8 = bf16[256,768]{1,0:T(8,128)(2,1)S(1)} collective-permute-done((bf16[256,768]{1,0:T(8,128)(2,1)S(1)}, bf16[256,768]{1,0:T(8,128)(2,1)S(1)}, u32[]{:S(2)}, u32[]{:S(2)}) %collective-permute-start.8) | collective-permute-done | bytes 393248 | tf_op jit(solution)/shard_map/ppermute | solution.py:48
  81.6 4.6 %all-to-all-done.1 = bf16[16,48,1536]{2,1,0:T(8,128)(2,1)} async-done(((bf16[16,48,1536]{2,1,0:T(8,128)(2,1)}), bf16[16,48,1536]{2,1,0:T(8,128)(2,1)}, u32[]{:S(2)}, u32[]{:S(2)}) %all-to-all-start.1) | async-done | bytes 2359328 | tf_op jit(solution)/shard_map/all_to_all | solution.py:64
  86.2 3.3 %copy.33 = bf16[4,2,4,24,1536]{4,3,2,1,0:T(8,128)(2,1)} copy(bf16[4,2,4,24,1536]{4,3,1,2,0:T(8,128)(2,1)} %bitcast.14) | data formatting | bytes 4718592 | tf_op jit(solution)/shard_map/transpose | solution.py:75
  90.6 2.3 %collective-permute-start.10 = (bf16[256,768]{1,0:T(8,128)(2,1)S(1)}, bf16[256,768]{1,0:T(8,128)(2,1)S(1)}, u32[]{:S(2)}, u32[]{:S(2)}) collective-permute-start(bf16[256,768]{1,0:T(8,128)(2,1)S(1)} %fusion.4), channel_id=1, source_target_pairs={{0,2},{2,0},{1,3},{3,1},{4,6},{6,4},{5,7},{7,5},{8,10},{10,8},{9,1... | collective-permute-start | bytes 1179656 | tf_op jit(solution)/shard_map/ppermute | solution.py:29
  92.9 1.3 collective-permute-done.10.refs_10_
  95.1 15.4 %shard_map.214 = (bf16[256,768]{1,0:T(8,128)(2,1)}, bf16[256,768]{1,0:T(8,128)(2,1)}, bf16[256,768]{1,0:T(8,128)(2,1)}, bf16[256,768]{1,0:T(8,128)(2,1)}, bf16[7...) custom-call(bf16[128,768]{1,0:T(8,128)(2,1)} %refs_0_.3, ...), custom_call_target="tpu_custom_call" | custom-call | flops 3623878656 | bytes 8000000 | tf_op jit(solution)/shard_map/pallas_call | solution.py:683
  111.0 1.6 collective-permute-done.11
  112.5 1.1 add_convert_fusion.2
  113.6 3.4 %collective-permute-start.12 = (bf16[256,768]{1,0:T(8,128)(2,1)S(1)}, bf16[256,768]{1,0:T(8,128)(2,1)S(1)}, u32[]{:S(2)}, u32[]{:S(2)}) collective-permute-start(bf16[256,768]{1,0:T(8,128)(2,1)S(1)} %add_convert_fusion.2), channel_id=1, source_target_pairs={{0,17},{1,16},{4,21},{5,20},{8,25},{9,24},{12,29},{13,28},{16,1},{... | collective-permute-start | bytes 1179656 | tf_op jit(solution)/shard_map/ppermute | solution.py:48
  117.0 3.4 %copy.34 = bf16[4,2,4,24,1536]{4,3,1,2,0:T(8,128)(2,1)} copy(bf16[4,2,4,24,1536]{4,3,2,1,0:T(8,128)(2,1)} %bitcast.55) | data formatting | bytes 4718592 | tf_op jit(solution)/shard_map/reshape | solution.py:68
  120.4 5.8 %collective-permute-done.12 = bf16[256,768]{1,0:T(8,128)(2,1)S(1)} collective-permute-done((bf16[256,768]{1,0:T(8,128)(2,1)S(1)}, bf16[256,768]{1,0:T(8,128)(2,1)S(1)}, u32[]{:S(2)}, u32[]{:S(2)}) %collective-permute-start.12) | collective-permute-done | bytes 393248 | tf_op jit(solution)/shard_map/ppermute | solution.py:48
  126.4 6.0 %all-to-all-start.2 = ((bf16[16,48,1536]{2,1,0:T(8,128)(2,1)}), bf16[16,48,1536]{2,1,0:T(8,128)(2,1)}, u32[]{:S(2)}, u32[]{:S(2)}) async-start(bf16[16,48,1536]{2,1,0:T(8,128)(2,1)} %bitcast.22), calls=%async_computation.2 | async-start | bytes 4718592 | tf_op jit(solution)/shard_map/all_to_all | solution.py:64
  132.5 9.2 %collective-permute-done.13.refs_5_ = bf16[256,768]{1,0:T(8,128)(2,1)S(1)} collective-permute-done((bf16[256,768]{1,0:T(8,128)(2,1)S(1)}, bf16[256,768]{1,0:T(8,128)(2,1)S(1)}, u32[]{:S(2)}, u32[]{:S(2)}) %collective-permute-start.13) | collective-permute-done | bytes 393248 | tf_op jit(solution)/shard_map/ppermute | solution.py:42
  141.7 2.3 %collective-permute-start.15 = (bf16[256,768]{1,0:T(8,128)(2,1)S(1)}, bf16[256,768]{1,0:T(8,128)(2,1)S(1)}, u32[]{:S(2)}, u32[]{:S(2)}) collective-permute-start(bf16[256,768]{1,0:T(8,128)(2,1)S(1)} %copy-done.18), channel_id=1, source_target_pairs={{0,2},{2,0},{1,3},{3,1},{4,6},{6,4},{5,7},{7,5},{8,10},{10,8},{9,1... | collective-permute-start | bytes 1179656 | tf_op jit(solution)/shard_map/ppermute | solution.py:29
  144.3 1.1 collective-permute-done.15
  145.4 2.6 %collective-permute-start.16 = (bf16[256,768]{1,0:T(8,128)(2,1)S(1)}, bf16[256,768]{1,0:T(8,128)(2,1)S(1)}, u32[]{:S(2)}, u32[]{:S(2)}) collective-permute-start(bf16[256,768]{1,0:T(8,128)(2,1)S(1)} %add_convert_fusion.1), channel_id=1, source_target_pairs={{0,17},{1,16},{4,21},{5,20},{8,25},{9,24},{12,29},{13,28},{16,1},{... | collective-permute-start | bytes 1179656 | tf_op jit(solution)/shard_map/ppermute | solution.py:48
  148.8 14.2 %shard_map.215 = (bf16[256,768]{1,0:T(8,128)(2,1)}, bf16[256,768]{1,0:T(8,128)(2,1)}, bf16[768,1664]{1,0:T(8,128)(2,1)}, f32[128,768]{1,0:T(8,128)}) custom-call(bf16[128,768]{1,0:T(8,128)(2,1)} %refs_0_.4, bf16[128,768]{1,0:T(8,128)(2,1)} %collective-permute-done.4.refs_5_.refs_1_, bf16[128,768]{1,0:T(8,128)(2,1)} %collective-permute-done.5.refs_6_.refs_2_, ...), custom_call_target="tpu_custom_call" | custom-call | flops 2415919104 | bytes 8000000 | tf_op jit(solution)/shard_map/pallas_call | solution.py:683
  163.0 3.4 %copy.35 = bf16[4,2,4,24,1664]{4,3,1,2,0:T(8,128)(2,1)} copy(bf16[4,2,4,24,1664]{4,3,2,1,0:T(8,128)(2,1)} %bitcast.53) | data formatting | bytes 5111808 | tf_op jit(solution)/shard_map/reshape | solution.py:68
  166.5 6.7 %all-to-all-start.3 = ((bf16[16,48,1664]{2,1,0:T(8,128)(2,1)}), bf16[16,48,1664]{2,1,0:T(8,128)(2,1)}, u32[]{:S(2)}, u32[]{:S(2)}) async-start(bf16[16,48,1664]{2,1,0:T(8,128)(2,1)} %bitcast.27), calls=%async_computation.3 | async-start | bytes 5111808 | tf_op jit(solution)/shard_map/all_to_all | solution.py:64
  173.3 1.0 collective-permute-start.20
  174.3 1.3 collective-permute-done.20
  176.5 10.9 %collective-permute-done.21 = bf16[256,768]{1,0:T(8,128)(2,1)S(1)} collective-permute-done((bf16[256,768]{1,0:T(8,128)(2,1)S(1)}, bf16[256,768]{1,0:T(8,128)(2,1)S(1)}, u32[]{:S(2)}, u32[]{:S(2)}) %collective-permute-start.21) | collective-permute-done | bytes 393248 | tf_op jit(solution)/shard_map/ppermute | solution.py:48
  187.8 2.6 %shard_map.216 = (bf16[24,1536]{1,0:T(8,128)(2,1)}, bf16[24,1536]{1,0:T(8,128)(2,1)}) custom-call(s32[1]{0:T(128)} %bitcast.1.place_ref, bf16[16,48,1536]{2,1,0:T(8,128)(2,1)} %all-to-all-done.2.got_ref), custom_call_target="tpu_custom_call" | custom-call | flops 150994944 | bytes 8000000 | tf_op jit(solution)/shard_map/pallas_call | solution.py:683
  190.4 2.7 %collective-permute-start.19 = (bf16[24,1536]{1,0:T(8,128)(2,1)}, bf16[24,1536]{1,0:T(8,128)(2,1)S(1)}, u32[]{:S(2)}, u32[]{:S(2)}) collective-permute-start(bf16[24,1536]{1,0:T(8,128)(2,1)} %get-tuple-element.127), channel_id=1, source_target_pairs={{0,18},{2,16},{4,22},{6,20},{8,26},{10,24},{12,30},{14,28},{16,2},... | collective-permute-start | bytes 221192 | tf_op jit(solution)/shard_map/ppermute | solution.py:54
  194.7 6.7 %collective-permute-done.19.rest_7_ = bf16[24,1536]{1,0:T(8,128)(2,1)S(1)} collective-permute-done((bf16[24,1536]{1,0:T(8,128)(2,1)}, bf16[24,1536]{1,0:T(8,128)(2,1)S(1)}, u32[]{:S(2)}, u32[]{:S(2)}) %collective-permute-start.19) | collective-permute-done | bytes 73760 | tf_op jit(solution)/shard_map/ppermute | solution.py:54
  201.4 9.9 %all-to-all-done.3.got_ref = bf16[16,48,1664]{2,1,0:T(8,128)(2,1)} async-done(((bf16[16,48,1664]{2,1,0:T(8,128)(2,1)}), bf16[16,48,1664]{2,1,0:T(8,128)(2,1)}, u32[]{:S(2)}, u32[]{:S(2)}) %all-to-all-start.3) | async-done | bytes 2555936 | tf_op jit(solution)/shard_map/all_to_all | solution.py:64
  211.3 2.8 %shard_map.217 = (bf16[24,1664]{1,0:T(8,128)(2,1)}, bf16[24,1664]{1,0:T(8,128)(2,1)}) custom-call(s32[1]{0:T(128)} %bitcast.1.place_ref, bf16[16,48,1664]{2,1,0:T(8,128)(2,1)} %all-to-all-done.3.got_ref), custom_call_target="tpu_custom_call" | custom-call | flops 1000 | bytes 8000000 | tf_op jit(solution)/shard_map/pallas_call | solution.py:683
  214.1 1.1 collective-permute-start.25
  215.2 2.1 collective-permute-start.24
  218.2 2.8 %collective-permute-done.24.rest_2_ = bf16[24,1664]{1,0:T(8,128)(2,1)S(1)} collective-permute-done((bf16[24,1664]{1,0:T(8,128)(2,1)}, bf16[24,1664]{1,0:T(8,128)(2,1)S(1)}, u32[]{:S(2)}, u32[]{:S(2)}) %collective-permute-start.24) | collective-permute-done | bytes 79904 | tf_op jit(solution)/shard_map/ppermute | solution.py:42
  222.5 3.7 %shard_map.218 = (bf16[128,768]{1,0:T(8,128)(2,1)}, bf16[128,768]{1,0:T(8,128)(2,1)}, f32[2,24,1152]{2,1,0:T(8,128)}, f32[2,24,384]{2,1,0:T(8,128)}, f32[2,24,15...) custom-call(s32[1]{0:T(128)} %bitcast.core_ref, s32[1]{0:T(128)} %bitcast.1.place_ref, ...), custom_call_target="tpu_custom_call" | custom-call | flops 150994944 | bytes 8000000 | tf_op jit(solution)/shard_map/pallas_call | solution.py:683
  226.8 1.3 shard_map.219
  (120 shorter events, 17.2 us)
Async XLA Ops:
  3.6 14.1 %copy-start.9 = (bf16[128,768]{1,0:T(8,128)(2,1)S(1)}, bf16[128,768]{1,0:T(8,128)(2,1)}, u32[]{:S(2)}) copy-start(bf16[128,768]{1,0:T(8,128)(2,1)} %refs_0_.4) | copy-start | bytes 589828
  3.6 14.5 %copy-start.22 = (s32[1,4]{1,0:T(1,128)S(1)}, s32[1,4]{1,0:T(1,128)}, u32[]{:S(2)}) copy-start(s32[1,4]{1,0:T(1,128)} %param.15) | copy-start | bytes 52
  3.7 14.6 %copy-start.23 = (s32[1,4]{1,0:T(1,128)S(1)}, s32[1,4]{1,0:T(1,128)}, u32[]{:S(2)}) copy-start(s32[1,4]{1,0:T(1,128)} %param.16) | copy-start | bytes 52
  3.7 41.3 %all-to-all-start = ((bf16[32,24,1664]{2,1,0:T(8,128)(2,1)}), bf16[32,24,1664]{2,1,0:T(8,128)(2,1)S(1)}, u32[]{:S(2)}, u32[]{:S(2)}) async-start(bf16[32,24,1664]{2,1,0:T(8,128)(2,1)} %get-tuple-element.92), calls=%async_computation | async-start | bytes 5111808 | tf_op jit(solution)/shard_map/all_to_all | solution.py:58
  13.0 27.9 %collective-permute-start.1 = (bf16[128,768]{1,0:T(8,128)(2,1)}, bf16[128,768]{1,0:T(8,128)(2,1)}, u32[]{:S(2)}, u32[]{:S(2)}) collective-permute-start(bf16[128,768]{1,0:T(8,128)(2,1)} %refs_0_.3), channel_id=1, source_target_pairs={{0,2},{2,0},{1,3},{3,1},{4,6},{6,4},{5,7},{7,5},{8,10},{10,8},{9,1... | collective-permute-start | bytes 589832 | tf_op jit(solution)/shard_map/ppermute | solution.py:29
  14.1 9.1 %collective-permute-start.2 = (bf16[128,768]{1,0:T(8,128)(2,1)}, bf16[128,768]{1,0:T(8,128)(2,1)}, u32[]{:S(2)}, u32[]{:S(2)}) collective-permute-start(bf16[128,768]{1,0:T(8,128)(2,1)} %refs_0_.3), channel_id=1, source_target_pairs={{0,17},{1,16},{4,21},{5,20},{8,25},{9,24},{12,29},{13,28},{16,1},{... | collective-permute-start | bytes 589832 | tf_op jit(solution)/shard_map/ppermute | solution.py:48
  17.7 23.2 %collective-permute-start.4 = (bf16[128,768]{1,0:T(8,128)(2,1)S(1)}, bf16[128,768]{1,0:T(8,128)(2,1)}, u32[]{:S(2)}, u32[]{:S(2)}) collective-permute-start(bf16[128,768]{1,0:T(8,128)(2,1)S(1)} %copy-done.9), channel_id=1, source_target_pairs={{0,2},{2,0},{1,3},{3,1},{4,6},{6,4},{5,7},{7,5},{8,10},{10,8},{9,1... | collective-permute-start | bytes 589832 | tf_op jit(solution)/shard_map/ppermute | solution.py:29
  18.1 9.3 %collective-permute-start.5 = (bf16[128,768]{1,0:T(8,128)(2,1)S(1)}, bf16[128,768]{1,0:T(8,128)(2,1)}, u32[]{:S(2)}, u32[]{:S(2)}) collective-permute-start(bf16[128,768]{1,0:T(8,128)(2,1)S(1)} %copy-done.9), channel_id=1, source_target_pairs={{0,17},{1,16},{4,21},{5,20},{8,25},{9,24},{12,29},{13,28},{16,1},{... | collective-permute-start | bytes 589832 | tf_op jit(solution)/shard_map/ppermute | solution.py:48
  18.1 21.8 %collective-permute-start = (bf16[24,1536]{1,0:T(8,128)(2,1)}, bf16[24,1536]{1,0:T(8,128)(2,1)}, u32[]{:S(2)}, u32[]{:S(2)}) collective-permute-start(bf16[24,1536]{1,0:T(8,128)(2,1)} %get-tuple-element.83), channel_id=1, source_target_pairs={{0,16},{4,20},{8,24},{12,28},{16,0},{20,4},{24,8},{28,12},{32,48},... | collective-permute-start | bytes 221192 | tf_op jit(solution)/shard_map/ppermute | solution.py:42
  23.2 17.8 %collective-permute-start.3 = (bf16[128,768]{1,0:T(8,128)(2,1)}, bf16[128,768]{1,0:T(8,128)(2,1)S(1)}, u32[]{:S(2)}, u32[]{:S(2)}) collective-permute-start(bf16[128,768]{1,0:T(8,128)(2,1)} %collective-permute-done.2.refs_2_), channel_id=1, source_target_pairs={{0,2},{2,0},{1,3},{3,1},{4,6},{6,4},{5,7},{7,5},{8,10},{10,8},{9,1... | collective-permute-start | bytes 589832 | tf_op jit(solution)/shard_map/ppermute | solution.py:29
  27.4 13.6 %collective-permute-start.6 = (bf16[128,768]{1,0:T(8,128)(2,1)}, bf16[128,768]{1,0:T(8,128)(2,1)}, u32[]{:S(2)}, u32[]{:S(2)}) collective-permute-start(bf16[128,768]{1,0:T(8,128)(2,1)} %collective-permute-done.5.refs_6_.refs_2_), channel_id=1, source_target_pairs={{0,2},{2,0},{1,3},{3,1},{4,6},{6,4},{5,7},{7,5},{8,10},{10,8},{9,1... | collective-permute-start | bytes 589832 | tf_op jit(solution)/shard_map/ppermute | solution.py:29
  41.0 5.8 %copy-start.21 = (bf16[128,768]{1,0:T(8,128)(2,1)}, bf16[128,768]{1,0:T(8,128)(2,1)S(1)}, u32[]{:S(2)}) copy-start(bf16[128,768]{1,0:T(8,128)(2,1)S(1)} %collective-permute-done.3.refs_3_) | copy-start | bytes 589828
  47.1 39.1 %all-to-all-start.1 = ((bf16[16,48,1536]{2,1,0:T(8,128)(2,1)}), bf16[16,48,1536]{2,1,0:T(8,128)(2,1)}, u32[]{:S(2)}, u32[]{:S(2)}) async-start(bf16[16,48,1536]{2,1,0:T(8,128)(2,1)} %broadcast_in_dim.35), calls=%async_computation.1 | async-start | bytes 4718592 | tf_op jit(solution)/shard_map/all_to_all | solution.py:64
  64.5 3.4 %collective-permute-start.7 = (bf16[256,768]{1,0:T(8,128)(2,1)}, bf16[256,768]{1,0:T(8,128)(2,1)S(1)}, u32[]{:S(2)}, u32[]{:S(2)}) collective-permute-start(bf16[256,768]{1,0:T(8,128)(2,1)} %get-tuple-element.94), channel_id=1, source_target_pairs={{0,2},{2,0},{1,3},{3,1},{4,6},{6,4},{5,7},{7,5},{8,10},{10,8},{9,1... | collective-permute-start | bytes 1179656 | tf_op jit(solution)/shard_map/ppermute | solution.py:29
  69.0 11.7 %collective-permute-start.8 = (bf16[256,768]{1,0:T(8,128)(2,1)S(1)}, bf16[256,768]{1,0:T(8,128)(2,1)S(1)}, u32[]{:S(2)}, u32[]{:S(2)}) collective-permute-start(bf16[256,768]{1,0:T(8,128)(2,1)S(1)} %add_convert_fusion.3), channel_id=1, source_target_pairs={{0,17},{1,16},{4,21},{5,20},{8,25},{9,24},{12,29},{13,28},{16,1},{... | collective-permute-start | bytes 1179656 | tf_op jit(solution)/shard_map/ppermute | solution.py:48
  80.9 9.6 %copy-start.3 = (bf16[256,768]{1,0:T(8,128)(2,1)}, bf16[256,768]{1,0:T(8,128)(2,1)S(1)}, u32[]{:S(2)}) copy-start(bf16[256,768]{1,0:T(8,128)(2,1)S(1)} %fusion.5.refs_8_) | copy-start | bytes 1179652
  80.9 9.6 %collective-permute-start.9 = (bf16[256,768]{1,0:T(8,128)(2,1)S(1)}, bf16[256,768]{1,0:T(8,128)(2,1)S(1)}, u32[]{:S(2)}, u32[]{:S(2)}) collective-permute-start(bf16[256,768]{1,0:T(8,128)(2,1)S(1)} %fusion.5.refs_8_), channel_id=1, source_target_pairs={{0,16},{4,20},{8,24},{12,28},{16,0},{20,4},{24,8},{28,12},{32,48},... | collective-permute-start | bytes 1179656 | tf_op jit(solution)/shard_map/ppermute | solution.py:42
  90.6 3.7 %collective-permute-start.10 = (bf16[256,768]{1,0:T(8,128)(2,1)S(1)}, bf16[256,768]{1,0:T(8,128)(2,1)S(1)}, u32[]{:S(2)}, u32[]{:S(2)}) collective-permute-start(bf16[256,768]{1,0:T(8,128)(2,1)S(1)} %fusion.4), channel_id=1, source_target_pairs={{0,2},{2,0},{1,3},{3,1},{4,6},{6,4},{5,7},{7,5},{8,10},{10,8},{9,1... | collective-permute-start | bytes 1179656 | tf_op jit(solution)/shard_map/ppermute | solution.py:29
  110.5 2.0 collective-permute-start.11
  113.6 12.5 %collective-permute-start.12 = (bf16[256,768]{1,0:T(8,128)(2,1)S(1)}, bf16[256,768]{1,0:T(8,128)(2,1)S(1)}, u32[]{:S(2)}, u32[]{:S(2)}) collective-permute-start(bf16[256,768]{1,0:T(8,128)(2,1)S(1)} %add_convert_fusion.2), channel_id=1, source_target_pairs={{0,17},{1,16},{4,21},{5,20},{8,25},{9,24},{12,29},{13,28},{16,1},{... | collective-permute-start | bytes 1179656 | tf_op jit(solution)/shard_map/ppermute | solution.py:48
  126.3 17.7 %copy-start.1 = (bf16[256,768]{1,0:T(8,128)(2,1)}, bf16[256,768]{1,0:T(8,128)(2,1)S(1)}, u32[]{:S(2)}) copy-start(bf16[256,768]{1,0:T(8,128)(2,1)S(1)} %fusion.3.refs_4_) | copy-start | bytes 1179652
  126.3 15.4 %copy-start.18 = (bf16[256,768]{1,0:T(8,128)(2,1)S(1)}, bf16[256,768]{1,0:T(8,128)(2,1)}, u32[]{:S(2)}) copy-start(bf16[256,768]{1,0:T(8,128)(2,1)} %get-tuple-element.123) | copy-start | bytes 1179652
  126.3 19.0 %copy-start.7 = (bf16[256,768]{1,0:T(8,128)(2,1)S(1)}, bf16[256,768]{1,0:T(8,128)(2,1)}, u32[]{:S(2)}) copy-start(bf16[256,768]{1,0:T(8,128)(2,1)} %get-tuple-element.122) | copy-start | bytes 1179652
  126.4 40.1 %all-to-all-start.2 = ((bf16[16,48,1536]{2,1,0:T(8,128)(2,1)}), bf16[16,48,1536]{2,1,0:T(8,128)(2,1)}, u32[]{:S(2)}, u32[]{:S(2)}) async-start(bf16[16,48,1536]{2,1,0:T(8,128)(2,1)} %bitcast.22), calls=%async_computation.2 | async-start | bytes 4718592 | tf_op jit(solution)/shard_map/all_to_all | solution.py:64
  132.4 9.3 %collective-permute-start.13 = (bf16[256,768]{1,0:T(8,128)(2,1)S(1)}, bf16[256,768]{1,0:T(8,128)(2,1)S(1)}, u32[]{:S(2)}, u32[]{:S(2)}) collective-permute-start(bf16[256,768]{1,0:T(8,128)(2,1)S(1)} %fusion.3.refs_4_), channel_id=1, source_target_pairs={{0,16},{4,20},{8,24},{12,28},{16,0},{20,4},{24,8},{28,12},{32,48},... | collective-permute-start | bytes 1179656 | tf_op jit(solution)/shard_map/ppermute | solution.py:42
  141.7 6.4 %copy-start.2 = (bf16[256,768]{1,0:T(8,128)(2,1)}, bf16[256,768]{1,0:T(8,128)(2,1)S(1)}, u32[]{:S(2)}) copy-start(bf16[256,768]{1,0:T(8,128)(2,1)S(1)} %collective-permute-done.13.refs_5_) | copy-start | bytes 1179652
  141.7 3.6 %collective-permute-start.15 = (bf16[256,768]{1,0:T(8,128)(2,1)S(1)}, bf16[256,768]{1,0:T(8,128)(2,1)S(1)}, u32[]{:S(2)}, u32[]{:S(2)}) collective-permute-start(bf16[256,768]{1,0:T(8,128)(2,1)S(1)} %copy-done.18), channel_id=1, source_target_pairs={{0,2},{2,0},{1,3},{3,1},{4,6},{6,4},{5,7},{7,5},{8,10},{10,8},{9,1... | collective-permute-start | bytes 1179656 | tf_op jit(solution)/shard_map/ppermute | solution.py:29
  144.2 3.9 %collective-permute-start.14 = (bf16[256,768]{1,0:T(8,128)(2,1)S(1)}, bf16[256,768]{1,0:T(8,128)(2,1)S(1)}, u32[]{:S(2)}, u32[]{:S(2)}) collective-permute-start(bf16[256,768]{1,0:T(8,128)(2,1)S(1)} %fusion.2), channel_id=1, source_target_pairs={{0,2},{2,0},{1,3},{3,1},{4,6},{6,4},{5,7},{7,5},{8,10},{10,8},{9,1... | collective-permute-start | bytes 1179656 | tf_op jit(solution)/shard_map/ppermute | solution.py:29
  145.4 20.9 %collective-permute-start.16 = (bf16[256,768]{1,0:T(8,128)(2,1)S(1)}, bf16[256,768]{1,0:T(8,128)(2,1)S(1)}, u32[]{:S(2)}, u32[]{:S(2)}) collective-permute-start(bf16[256,768]{1,0:T(8,128)(2,1)S(1)} %add_convert_fusion.1), channel_id=1, source_target_pairs={{0,17},{1,16},{4,21},{5,20},{8,25},{9,24},{12,29},{13,28},{16,1},{... | collective-permute-start | bytes 1179656 | tf_op jit(solution)/shard_map/ppermute | solution.py:48
  166.5 6.8 %copy-start.19 = (bf16[256,768]{1,0:T(8,128)(2,1)S(1)}, bf16[256,768]{1,0:T(8,128)(2,1)}, u32[]{:S(2)}) copy-start(bf16[256,768]{1,0:T(8,128)(2,1)} %get-tuple-element.130) | copy-start | bytes 1179652
  166.5 9.1 %copy-start.8 = (bf16[256,768]{1,0:T(8,128)(2,1)S(1)}, bf16[256,768]{1,0:T(8,128)(2,1)}, u32[]{:S(2)}) copy-start(bf16[256,768]{1,0:T(8,128)(2,1)} %get-tuple-element.129) | copy-start | bytes 1179652
  166.5 44.8 %all-to-all-start.3 = ((bf16[16,48,1664]{2,1,0:T(8,128)(2,1)}), bf16[16,48,1664]{2,1,0:T(8,128)(2,1)}, u32[]{:S(2)}, u32[]{:S(2)}) async-start(bf16[16,48,1664]{2,1,0:T(8,128)(2,1)} %bitcast.27), calls=%async_computation.3 | async-start | bytes 5111808 | tf_op jit(solution)/shard_map/all_to_all | solution.py:64
  173.3 2.4 %collective-permute-start.20 = (bf16[256,768]{1,0:T(8,128)(2,1)S(1)}, bf16[256,768]{1,0:T(8,128)(2,1)S(1)}, u32[]{:S(2)}, u32[]{:S(2)}) collective-permute-start(bf16[256,768]{1,0:T(8,128)(2,1)S(1)} %copy-done.19), channel_id=1, source_target_pairs={{0,2},{2,0},{1,3},{3,1},{4,6},{6,4},{5,7},{7,5},{8,10},{10,8},{9,1... | collective-permute-start | bytes 1179656 | tf_op jit(solution)/shard_map/ppermute | solution.py:29
  175.7 11.7 %collective-permute-start.21 = (bf16[256,768]{1,0:T(8,128)(2,1)S(1)}, bf16[256,768]{1,0:T(8,128)(2,1)S(1)}, u32[]{:S(2)}, u32[]{:S(2)}) collective-permute-start(bf16[256,768]{1,0:T(8,128)(2,1)S(1)} %add_convert_fusion), channel_id=1, source_target_pairs={{0,17},{1,16},{4,21},{5,20},{8,25},{9,24},{12,29},{13,28},{16,1},{... | collective-permute-start | bytes 1179656 | tf_op jit(solution)/shard_map/ppermute | solution.py:48
  187.7 13.7 %collective-permute-start.22 = (bf16[256,768]{1,0:T(8,128)(2,1)S(1)}, bf16[256,768]{1,0:T(8,128)(2,1)S(1)}, u32[]{:S(2)}, u32[]{:S(2)}) collective-permute-start(bf16[256,768]{1,0:T(8,128)(2,1)S(1)} %pad_maximum_fusion.2), channel_id=1, source_target_pairs={{0,16},{4,20},{8,24},{12,28},{16,0},{20,4},{24,8},{28,12},{32,48},... | collective-permute-start | bytes 1179656 | tf_op jit(solution)/shard_map/ppermute | solution.py:42
  190.4 11.0 %collective-permute-start.19 = (bf16[24,1536]{1,0:T(8,128)(2,1)}, bf16[24,1536]{1,0:T(8,128)(2,1)S(1)}, u32[]{:S(2)}, u32[]{:S(2)}) collective-permute-start(bf16[24,1536]{1,0:T(8,128)(2,1)} %get-tuple-element.127), channel_id=1, source_target_pairs={{0,18},{2,16},{4,22},{6,20},{8,26},{10,24},{12,30},{14,28},{16,2},... | collective-permute-start | bytes 221192 | tf_op jit(solution)/shard_map/ppermute | solution.py:54
  193.2 8.2 %collective-permute-start.18 = (bf16[24,1536]{1,0:T(8,128)(2,1)}, bf16[24,1536]{1,0:T(8,128)(2,1)S(1)}, u32[]{:S(2)}, u32[]{:S(2)}) collective-permute-start(bf16[24,1536]{1,0:T(8,128)(2,1)} %get-tuple-element.127), channel_id=1, source_target_pairs={{0,16},{4,20},{8,24},{12,28},{16,0},{20,4},{24,8},{28,12},{32,48},... | collective-permute-start | bytes 221192 | tf_op jit(solution)/shard_map/ppermute | solution.py:42
  193.2 1.5 collective-permute-start.17
  194.7 27.8 %copy-start.15 = (bf16[24,1536]{1,0:T(8,128)(2,1)}, bf16[24,1536]{1,0:T(8,128)(2,1)S(1)}, u32[]{:S(2)}) copy-start(bf16[24,1536]{1,0:T(8,128)(2,1)S(1)} %collective-permute-done.17.rest_5_) | copy-start | bytes 221188
  201.4 21.1 %copy-start.13 = (bf16[24,1536]{1,0:T(8,128)(2,1)}, bf16[24,1536]{1,0:T(8,128)(2,1)S(1)}, u32[]{:S(2)}) copy-start(bf16[24,1536]{1,0:T(8,128)(2,1)S(1)} %collective-permute-done.19.rest_7_) | copy-start | bytes 221188
  201.4 21.1 %copy-start.14 = (bf16[24,1536]{1,0:T(8,128)(2,1)}, bf16[24,1536]{1,0:T(8,128)(2,1)S(1)}, u32[]{:S(2)}) copy-start(bf16[24,1536]{1,0:T(8,128)(2,1)S(1)} %collective-permute-done.18.rest_6_) | copy-start | bytes 221188
  201.4 21.1 %copy-start.5 = (bf16[256,768]{1,0:T(8,128)(2,1)}, bf16[256,768]{1,0:T(8,128)(2,1)S(1)}, u32[]{:S(2)}) copy-start(bf16[256,768]{1,0:T(8,128)(2,1)S(1)} %collective-permute-done.22.rest_9_) | copy-start | bytes 1179652
  214.1 4.1 %collective-permute-start.25 = (bf16[24,1664]{1,0:T(8,128)(2,1)}, bf16[24,1664]{1,0:T(8,128)(2,1)S(1)}, u32[]{:S(2)}, u32[]{:S(2)}) collective-permute-start(bf16[24,1664]{1,0:T(8,128)(2,1)} %get-tuple-element.133), channel_id=1, source_target_pairs={{0,18},{2,16},{4,22},{6,20},{8,26},{10,24},{12,30},{14,28},{16,2},... | collective-permute-start | bytes 239624 | tf_op jit(solution)/shard_map/ppermute | solution.py:54
  215.2 5.8 %collective-permute-start.24 = (bf16[24,1664]{1,0:T(8,128)(2,1)}, bf16[24,1664]{1,0:T(8,128)(2,1)S(1)}, u32[]{:S(2)}, u32[]{:S(2)}) collective-permute-start(bf16[24,1664]{1,0:T(8,128)(2,1)} %get-tuple-element.133), channel_id=1, source_target_pairs={{0,16},{4,20},{8,24},{12,28},{16,0},{20,4},{24,8},{28,12},{32,48},... | collective-permute-start | bytes 239624 | tf_op jit(solution)/shard_map/ppermute | solution.py:42
  217.3 3.7 %collective-permute-start.23 = (bf16[24,1664]{1,0:T(8,128)(2,1)}, bf16[24,1664]{1,0:T(8,128)(2,1)S(1)}, u32[]{:S(2)}, u32[]{:S(2)}) collective-permute-start(bf16[24,1664]{1,0:T(8,128)(2,1)} %get-tuple-element.132.rest_0_), channel_id=1, source_target_pairs={{0,2},{2,0},{1,3},{3,1},{4,6},{6,4},{5,7},{7,5},{8,10},{10,8},{9,1... | collective-permute-start | bytes 239624 | tf_op jit(solution)/shard_map/ppermute | solution.py:29
  218.2 4.3 %copy-start.10 = (bf16[24,1664]{1,0:T(8,128)(2,1)}, bf16[24,1664]{1,0:T(8,128)(2,1)S(1)}, u32[]{:S(2)}) copy-start(bf16[24,1664]{1,0:T(8,128)(2,1)S(1)} %collective-permute-done.25.rest_3_) | copy-start | bytes 239620
  221.7 4.5 %copy-start.16 = (f32[24,128]{1,0:T(8,128)}, f32[24,128]{1,0:T(8,128)S(1)}, u32[]{:S(2)}) copy-start(f32[24,128]{1,0:T(8,128)S(1)} %add_add_fusion.mine_ref) | copy-start | bytes 36868
  221.7 4.5 %collective-permute-start.26 = (f32[24,128]{1,0:T(8,128)S(1)}, f32[24,128]{1,0:T(8,128)S(1)}, u32[]{:S(2)}, u32[]{:S(2)}) collective-permute-start(f32[24,128]{1,0:T(8,128)S(1)} %add_add_fusion.mine_ref), channel_id=1, source_target_pairs={{0,1},{1,0},{2,3},{3,2},{4,5},{5,4},{6,7},{7,6},{8,9},{9,8},{10,11... | collective-permute-start | bytes 36872 | tf_op jit(solution)/shard_map/ppermute | solution.py:33
  (7 other events, 11.1 us)

commit v6 on v5

--- a/solution.py
+++ b/solution.py
@@ -64,9 +64,11 @@
     return lax.all_to_all(blocks, "fsdp", 0, 0, axis_index_groups=planes, tiled=True)
 
 
-def pairs_together(slab, owners):
-    blocks = slab.reshape(owners // (2 * NEAR), 2, NEAR, -1, slab.shape[1])
-    return blocks.transpose(0, 2, 1, 3, 4).reshape(owners // 2, -1, slab.shape[1])
+def pairs_together(values, owners):
+    depth = values.shape[0] // owners
+    pairs = [y * 2 * NEAR + x for y in range(owners // (2 * NEAR)) for x in range(NEAR)]
+    order = [first + z * NEAR for first in pairs for z in (0, 1)]
+    return jnp.concatenate([values[owner * depth : (owner + 1) * depth] for owner in order])
 
 
 def owners_in_order(blocks, owners):
@@ -265,7 +267,7 @@
 
 
 def backward(
-    state, grad_ref, vec_ref, slab, table_ref, parts, sums_ref, scratch, put, far_parts
+    owners, state, grad_ref, vec_ref, slab, table_ref, parts, sums_ref, scratch, put, far_parts
 ):
     low_ref, up_ref, qkv_ref, wide_ref, deep_ref = scratch
     heads_ref, w_ref = slab.heads_ref, slab.w_ref
@@ -348,9 +350,11 @@
         put.start(ref, far_part_ref)
     heads_grad = dot(state.a[...], qkv_ref[...], (0, 0))
     heads_grad = heads_grad + dot(low_ref[:group, :], state.o[...], (0, 0))
-    heads_ref[...] = heads_grad.astype(BF)
-    w_ref[:, :hidden] = dot(state.m[...], up_ref[...], (0, 0)).astype(BF)
-    w_ref[:, hidden : 2 * hidden] = dot(low, state.gl[...], (0, 0)).astype(BF)
+    heads_ref[...] = pairs_together(heads_grad, owners).astype(BF)
+    up_grad = dot(state.m[...], up_ref[...], (0, 0))
+    w_ref[:, :hidden] = pairs_together(up_grad, owners).astype(BF)
+    down_grad = dot(low, state.gl[...], (0, 0))
+    w_ref[:, hidden : 2 * hidden] = pairs_together(down_grad, owners).astype(BF)
 
 
 def first_kernel(layers, *refs):
@@ -430,7 +434,7 @@
         over_rows(own, step)
 
 
-def last_kernel(*refs):
+def last_kernel(owners, *refs):
     inputs, far_ends, parts, refs = refs[:4], refs[4:8], refs[8:10], refs[10:]
     other_ref, vec_ref, far_ref, far_table_ref, far_mask_ref, *rest = refs
     far_parts, rest = rest[:4], rest[4:]
@@ -462,12 +466,12 @@
     forward(state, vec_ref.at[1], slab, get, table_ref, mask_ref, ahead, scratch[3])
     for ref, far_part_ref in zip(ahead, far_parts[:2], strict=True):
         put.start(ref, far_part_ref)
-    backward(state, grad_ref, vec_ref.at[1], slab, table_ref, back, sums_ref, scratch, put, far_parts[2:])
+    backward(owners, state, grad_ref, vec_ref.at[1], slab, table_ref, back, sums_ref, scratch, put, far_parts[2:])
     slab.give(slab_ref.at[:, :attn], slab_ref.at[:, attn:width], arrived)
     put.wait()
 
 
-def back_kernel(layers, *refs):
+def back_kernel(layers, owners, *refs):
     inputs, parts, refs = refs[:4], refs[4:6], refs[6:]
     other_ref, normed_ref, inv_std_ref, later_ref, vec_ref, far_ref, place_ref, far_table_ref, *rest = refs
     far_state, rest = rest[:10], rest[10:]
@@ -490,7 +494,7 @@
     kept_ref[...] = below_ref[: kept_ref.shape[0], :]
     slab.wait()
     get.wait()
-    backward(state, below_ref, vec_ref.at[0], slab, table_ref, back, sums_ref, scratch, put, far_back)
+    backward(owners, state, below_ref, vec_ref.at[0], slab, table_ref, back, sums_ref, scratch, put, far_back)
     both = [sums_ref, later_ref]
     pad = jnp.zeros((8 - layers, attn), F32)
     qkv = jnp.concatenate([ref[SUM_QKV : SUM_QKV + 1, :] for ref in both] + [pad], axis=0)
@@ -503,7 +507,7 @@
     small = [ref[: SUM_SHIFT_B + 1, :] for ref in both] + spread
     used = 9 * layers
     small = jnp.concatenate(small + [jnp.zeros((LANES - used, attn), F32)], axis=0)
-    small_ref[...] = jnp.transpose(small).astype(BF)
+    small_ref[...] = pairs_together(jnp.transpose(small), owners).astype(BF)
     copy = pltpu.make_async_copy(small_ref, slab_ref.at[:, width:], arrived.at[2])
     copy.start()
     slab.give(slab_ref.at[:, :attn], slab_ref.at[:, attn:width], arrived)
@@ -869,7 +873,7 @@
         pltpu.VMEM((rows, wide), F32),
     ]
     *sums, slab, later_sums, result, normed, inv_std = call(
-        last_kernel,
+        functools.partial(last_kernel, owners),
         (
             *(part,) * 4,
             sds((wide, width), BF),
@@ -897,13 +901,13 @@
         far=(4, 5, 6, 7, 12, 13, 14),
         far_outs=(0, 1, 2, 3, 4, 6, 7, 8),
     )
-    mine = pair_sum(core_rows_summed(*sums[2:]))
-    mine, slab = lax.optimization_barrier((mine, pairs_together(slab, owners)))
-    later = exchanged_in_plane(slab)
-    ahead, near = lax.optimization_barrier((sums[:2], near_group(mine)))
+    mine, slab = lax.optimization_barrier((core_rows_summed(*sums[2:]), slab))
+    later = exchanged_in_plane(slab.reshape(owners // 2, -1, width))
+    ahead, mine = lax.optimization_barrier((sums[:2], pair_sum(mine)))
+    near = near_group(mine)
     ahead = pair_sum(core_rows_summed(*ahead))
     kept_part, sent_part, slab, grad_below = call(
-        functools.partial(back_kernel, layers),
+        functools.partial(back_kernel, layers, owners),
         (part, part, sds((wide, width + LANES), BF), sds((row_count, wide), F32)),
         [
             *vmem(table),
@@ -929,9 +933,8 @@
         far=(11, *range(13, 24)),
         far_outs=(0, 1, 2),
     )
-    slab = pairs_together(slab, owners)
     slab, later, ahead = lax.optimization_barrier((slab, later, ahead))
-    earlier = exchanged_in_plane(slab)
+    earlier = exchanged_in_plane(slab.reshape(owners // 2, -1, width + LANES))
     below = pair_sum(core_rows_summed(kept_part, sent_part))
 
     piece = sds((depth, width), BF)

time: 229 us -> 220 us (0.961)
  waiting for transfers between devices: 89.8 us -> 82.8 us
  local copies, waits for them, and re-layouts: 16.4 us -> 10.4 us
  starting transfers between devices: 60.9 us -> 64.7 us
    reshape x2 -> x0, local copies, waits for them, and re-layouts: 6.77 us -> none  [pairs_together(): blocks = slab.reshape(owners // (2 * NEAR), 2, NEAR, -1, slab.shape[1])]
    ppermute x1, starting transfers between devices: 0.73 us -> 4.28 us  [other_half(): return lax.ppermute(values, 'tp', SWAP)]
    ppermute x6, waiting for transfers between devices: 24.8 us -> 22.1 us  [near_group(): return lax.ppermute(values, 'fsdp', [(f, f ^ NEAR) for f in range(owners)])]
  transfers between devices with their start and end apart: 31 -> 31, of which waited for: 20 -> 23; matrix products, arithmetic and copies ran while one was open for 8% -> 5% of each run, Pallas kernels for 13% -> 13%
where the time goes in v6:
time: 220 us; the launch traced here: 219 us
  waiting for transfers between devices  82.8 us (38%)
  starting transfers between devices  64.7 us (29%)
  Pallas kernels  51.7 us (24%)
  local copies, waits for them, and re-layouts  10.4 us (5%)
  other arithmetic  8.19 us (4%)
    pallas_call x8, Pallas kernels, call(): pl.pallas_call(kernel, out_shape=outs, in_specs=[pl.BlockSpec(memory_spac...  51.7 us
    ppermute x6, waiting for transfers between devices, near_other_half(): return lax.ppermute(values, ('fsdp', 'tp'), pairs)  29.5 us
    ppermute x6, waiting for transfers between devices, near_group(): return lax.ppermute(values, 'fsdp', [(f, f ^ NEAR) for f in range(owners)])  22.1 us
    all_to_all x3, starting transfers between devices, exchanged_in_plane(): lax.all_to_all(blocks, 'fsdp', 0, 0, axis_index_groups=planes, tiled=True)  17.5 us
    ppermute x6, starting transfers between devices, near_other_half(): return lax.ppermute(values, ('fsdp', 'tp'), pairs)  13.7 us
    all_to_all x3, waiting for transfers between devices, exchanged_in_plane(): lax.all_to_all(blocks, 'fsdp', 0, 0, axis_index_groups=planes, tiled=True)  12.6 us
    ppermute x12, starting transfers between devices, other_core(): return lax.ppermute(values, 'ctx', SWAP)  12 us
    all_to_all x1, starting transfers between devices, exchanged(): return lax.all_to_all(blocks, 'fsdp', 0, 0, tiled=True)  9.37 us
  transfers between devices with their start and end apart: 31, of which 23 were waited for; matrix products, arithmetic and copies ran while one was open for 5% of the time, Pallas kernels for 13%

profile of v6, /device:TPU:1, one launch (start us, length us, event | category | flops | bytes accessed | tf_op | source)
XLA Modules:
  0.0 218.9 jit_solution(15425312713169061767)
XLA Ops:
  0.7 2.9 %shard_map.212 = (bf16[32,24,1664]{2,1,0:T(8,128)(2,1)}, bf16[24,1536]{1,0:T(8,128)(2,1)}, bf16[24,1536]{1,0:T(8,128)(2,1)}) custom-call(s32[1]{0:T(128)} %bitcast.core_ref, s32[1]{0:T(128)} %bitcast.1.place_ref, bf16[2,24,1152]{2,1,0:T(8,128)(2,1)} %refs_0_.1, bf16[2,24,384]{2,1,0:T(8,128)(2,1)} %bitcast.60, bf16[2,24,1536]{2,1,0:T(8,128)(2,1)} %refs_2_.1, ...), custom_call_target="tpu_custom_call" | custom-call | flops 1000 | bytes 8000000 | tf_op jit(solution)/shard_map/pallas_call | solution.py:687
  3.7 9.4 %all-to-all-start = ((bf16[32,24,1664]{2,1,0:T(8,128)(2,1)}), bf16[32,24,1664]{2,1,0:T(8,128)(2,1)S(1)}, u32[]{:S(2)}, u32[]{:S(2)}) async-start(bf16[32,24,1664]{2,1,0:T(8,128)(2,1)} %get-tuple-element.92), calls=%async_computation | async-start | bytes 5111808 | tf_op jit(solution)/shard_map/all_to_all | solution.py:58
  14.1 3.6 %collective-permute-start.2 = (bf16[128,768]{1,0:T(8,128)(2,1)}, bf16[128,768]{1,0:T(8,128)(2,1)}, u32[]{:S(2)}, u32[]{:S(2)}) collective-permute-start(bf16[128,768]{1,0:T(8,128)(2,1)} %refs_0_.3), channel_id=1, source_target_pairs={{0,17},{1,16},{4,21},{5,20},{8,25},{9,24},{12,29},{13,28},{16,1},{... | collective-permute-start | bytes 589832 | tf_op jit(solution)/shard_map/ppermute | solution.py:48
  20.8 2.4 %collective-permute-done.2.refs_2_ = bf16[128,768]{1,0:T(8,128)(2,1)} collective-permute-done((bf16[128,768]{1,0:T(8,128)(2,1)}, bf16[128,768]{1,0:T(8,128)(2,1)}, u32[]{:S(2)}, u32[]{:S(2)}) %collective-permute-start.2) | collective-permute-done | bytes 196640 | tf_op jit(solution)/shard_map/ppermute | solution.py:48
  24.2 3.3 %collective-permute-done.5.refs_6_.refs_2_ = bf16[128,768]{1,0:T(8,128)(2,1)} collective-permute-done((bf16[128,768]{1,0:T(8,128)(2,1)S(1)}, bf16[128,768]{1,0:T(8,128)(2,1)}, u32[]{:S(2)}, u32[]{:S(2)}) %collective-permute-start.5) | collective-permute-done | bytes 196640 | tf_op jit(solution)/shard_map/ppermute | solution.py:48
  28.1 11.8 %collective-permute-done = bf16[24,1536]{1,0:T(8,128)(2,1)} collective-permute-done((bf16[24,1536]{1,0:T(8,128)(2,1)}, bf16[24,1536]{1,0:T(8,128)(2,1)}, u32[]{:S(2)}, u32[]{:S(2)}) %collective-permute-start) | collective-permute-done | bytes 73760 | tf_op jit(solution)/shard_map/ppermute | solution.py:42
  41.7 3.3 %all-to-all-done = bf16[32,24,1664]{2,1,0:T(8,128)(2,1)S(1)} async-done(((bf16[32,24,1664]{2,1,0:T(8,128)(2,1)}), bf16[32,24,1664]{2,1,0:T(8,128)(2,1)S(1)}, u32[]{:S(2)}, u32[]{:S(2)}) %all-to-all-start) | async-done | bytes 2555936 | tf_op jit(solution)/shard_map/all_to_all | solution.py:58
  44.9 1.8 broadcast_in_dim.35
  47.1 7.0 %all-to-all-start.1 = ((bf16[16,48,1536]{2,1,0:T(8,128)(2,1)}), bf16[16,48,1536]{2,1,0:T(8,128)(2,1)}, u32[]{:S(2)}, u32[]{:S(2)}) async-start(bf16[16,48,1536]{2,1,0:T(8,128)(2,1)} %broadcast_in_dim.35), calls=%async_computation.1 | async-start | bytes 4718592 | tf_op jit(solution)/shard_map/all_to_all | solution.py:64
  55.8 8.7 %shard_map.213 = (bf16[256,768]{1,0:T(8,128)(2,1)}, bf16[256,768]{1,0:T(8,128)(2,1)}, f32[2,8,768]{2,1,0:T(8,128)}, f32[512,768]{1,0:T(8,128)}, f32[512,1]{1,0:T...) custom-call(bf16[128,768]{1,0:T(8,128)(2,1)} %refs_0_.3, ...), custom_call_target="tpu_custom_call" | custom-call | flops 1207959552 | bytes 8000000 | tf_op jit(solution)/shard_map/pallas_call | solution.py:687
  64.5 1.8 collective-permute-start.7
  66.3 1.6 collective-permute-done.7
  67.9 1.1 add_convert_fusion.3
  69.0 2.4 %collective-permute-start.8 = (bf16[256,768]{1,0:T(8,128)(2,1)S(1)}, bf16[256,768]{1,0:T(8,128)(2,1)S(1)}, u32[]{:S(2)}, u32[]{:S(2)}) collective-permute-start(bf16[256,768]{1,0:T(8,128)(2,1)S(1)} %add_convert_fusion.3), channel_id=1, source_target_pairs={{0,17},{1,16},{4,21},{5,20},{8,25},{9,24},{12,29},{13,28},{16,1},{... | collective-permute-start | bytes 1179656 | tf_op jit(solution)/shard_map/ppermute | solution.py:48
  71.4 9.3 %collective-permute-done.8 = bf16[256,768]{1,0:T(8,128)(2,1)S(1)} collective-permute-done((bf16[256,768]{1,0:T(8,128)(2,1)S(1)}, bf16[256,768]{1,0:T(8,128)(2,1)S(1)}, u32[]{:S(2)}, u32[]{:S(2)}) %collective-permute-start.8) | collective-permute-done | bytes 393248 | tf_op jit(solution)/shard_map/ppermute | solution.py:48
  81.6 4.6 %all-to-all-done.1 = bf16[16,48,1536]{2,1,0:T(8,128)(2,1)} async-done(((bf16[16,48,1536]{2,1,0:T(8,128)(2,1)}), bf16[16,48,1536]{2,1,0:T(8,128)(2,1)}, u32[]{:S(2)}, u32[]{:S(2)}) %all-to-all-start.1) | async-done | bytes 2359328 | tf_op jit(solution)/shard_map/all_to_all | solution.py:64
  86.2 3.4 %copy.27 = bf16[4,2,4,24,1536]{4,3,2,1,0:T(8,128)(2,1)} copy(bf16[4,2,4,24,1536]{4,3,1,2,0:T(8,128)(2,1)} %bitcast.14) | data formatting | bytes 4718592 | tf_op jit(solution)/shard_map/transpose | solution.py:77
  90.6 2.4 %collective-permute-start.10 = (bf16[256,768]{1,0:T(8,128)(2,1)S(1)}, bf16[256,768]{1,0:T(8,128)(2,1)S(1)}, u32[]{:S(2)}, u32[]{:S(2)}) collective-permute-start(bf16[256,768]{1,0:T(8,128)(2,1)S(1)} %fusion.4), channel_id=1, source_target_pairs={{0,2},{2,0},{1,3},{3,1},{4,6},{6,4},{5,7},{7,5},{8,10},{10,8},{9,1... | collective-permute-start | bytes 1179656 | tf_op jit(solution)/shard_map/ppermute | solution.py:29
  93.0 1.3 collective-permute-done.10.refs_10_
  95.1 15.5 %shard_map.214 = (bf16[256,768]{1,0:T(8,128)(2,1)}, bf16[256,768]{1,0:T(8,128)(2,1)}, bf16[256,768]{1,0:T(8,128)(2,1)}, bf16[256,768]{1,0:T(8,128)(2,1)}, bf16[7...) custom-call(bf16[128,768]{1,0:T(8,128)(2,1)} %refs_0_.3, ...), custom_call_target="tpu_custom_call" | custom-call | flops 3623878656 | bytes 8000000 | tf_op jit(solution)/shard_map/pallas_call | solution.py:687
  111.1 1.6 collective-permute-done.11
  112.7 1.1 add_convert_fusion.2
  113.8 3.4 %collective-permute-start.12 = (bf16[256,768]{1,0:T(8,128)(2,1)S(1)}, bf16[256,768]{1,0:T(8,128)(2,1)S(1)}, u32[]{:S(2)}, u32[]{:S(2)}) collective-permute-start(bf16[256,768]{1,0:T(8,128)(2,1)S(1)} %add_convert_fusion.2), channel_id=1, source_target_pairs={{0,17},{1,16},{4,21},{5,20},{8,25},{9,24},{12,29},{13,28},{16,1},{... | collective-permute-start | bytes 1179656 | tf_op jit(solution)/shard_map/ppermute | solution.py:48
  117.1 5.9 %all-to-all-start.2 = ((bf16[16,48,1536]{2,1,0:T(8,128)(2,1)}), bf16[16,48,1536]{2,1,0:T(8,128)(2,1)}, u32[]{:S(2)}, u32[]{:S(2)}) async-start(bf16[16,48,1536]{2,1,0:T(8,128)(2,1)} %bitcast.48), calls=%async_computation.2 | async-start | bytes 4718592 | tf_op jit(solution)/shard_map/all_to_all | solution.py:64
  123.1 3.3 %collective-permute-done.12 = bf16[256,768]{1,0:T(8,128)(2,1)S(1)} collective-permute-done((bf16[256,768]{1,0:T(8,128)(2,1)S(1)}, bf16[256,768]{1,0:T(8,128)(2,1)S(1)}, u32[]{:S(2)}, u32[]{:S(2)}) %collective-permute-start.12) | collective-permute-done | bytes 393248 | tf_op jit(solution)/shard_map/ppermute | solution.py:48
  127.5 1.3 collective-permute-done.15
  128.9 2.8 %collective-permute-start.16 = (bf16[256,768]{1,0:T(8,128)(2,1)S(1)}, bf16[256,768]{1,0:T(8,128)(2,1)S(1)}, u32[]{:S(2)}, u32[]{:S(2)}) collective-permute-start(bf16[256,768]{1,0:T(8,128)(2,1)S(1)} %add_convert_fusion.1), channel_id=1, source_target_pairs={{0,17},{1,16},{4,21},{5,20},{8,25},{9,24},{12,29},{13,28},{16,1},{... | collective-permute-start | bytes 1179656 | tf_op jit(solution)/shard_map/ppermute | solution.py:48
  131.7 6.6 %collective-permute-done.13.refs_5_ = bf16[256,768]{1,0:T(8,128)(2,1)S(1)} collective-permute-done((bf16[256,768]{1,0:T(8,128)(2,1)S(1)}, bf16[256,768]{1,0:T(8,128)(2,1)S(1)}, u32[]{:S(2)}, u32[]{:S(2)}) %collective-permute-start.13) | collective-permute-done | bytes 393248 | tf_op jit(solution)/shard_map/ppermute | solution.py:42
  138.4 1.1 collective-permute-start.14
  139.5 1.2 collective-permute-done.16
  141.5 14.1 %shard_map.215 = (bf16[256,768]{1,0:T(8,128)(2,1)}, bf16[256,768]{1,0:T(8,128)(2,1)}, bf16[768,1664]{1,0:T(8,128)(2,1)}, f32[128,768]{1,0:T(8,128)}) custom-call(bf16[128,768]{1,0:T(8,128)(2,1)} %refs_0_.4, bf16[128,768]{1,0:T(8,128)(2,1)} %collective-permute-done.4.refs_5_.refs_1_, bf16[128,768]{1,0:T(8,128)(2,1)} %collective-permute-done.5.refs_6_.refs_2_, ...), custom_call_target="tpu_custom_call" | custom-call | flops 2415919104 | bytes 8000000 | tf_op jit(solution)/shard_map/pallas_call | solution.py:687
  155.8 2.0 all-to-all-done.2.got_ref
  157.8 4.6 %all-to-all-start.3 = ((bf16[16,48,1664]{2,1,0:T(8,128)(2,1)}), bf16[16,48,1664]{2,1,0:T(8,128)(2,1)}, u32[]{:S(2)}, u32[]{:S(2)}) async-start(bf16[16,48,1664]{2,1,0:T(8,128)(2,1)} %bitcast.47), calls=%async_computation.3 | async-start | bytes 5111808 | tf_op jit(solution)/shard_map/all_to_all | solution.py:64
  162.4 1.9 collective-permute-start.20
  164.3 1.3 collective-permute-done.20
  165.8 1.6 collective-permute-start.21
  167.3 10.2 %collective-permute-done.21 = bf16[256,768]{1,0:T(8,128)(2,1)S(1)} collective-permute-done((bf16[256,768]{1,0:T(8,128)(2,1)S(1)}, bf16[256,768]{1,0:T(8,128)(2,1)S(1)}, u32[]{:S(2)}, u32[]{:S(2)}) %collective-permute-start.21) | collective-permute-done | bytes 393248 | tf_op jit(solution)/shard_map/ppermute | solution.py:48
  177.9 2.6 %shard_map.216 = (bf16[24,1536]{1,0:T(8,128)(2,1)}, bf16[24,1536]{1,0:T(8,128)(2,1)}) custom-call(s32[1]{0:T(128)} %bitcast.1.place_ref, bf16[16,48,1536]{2,1,0:T(8,128)(2,1)} %all-to-all-done.2.got_ref), custom_call_target="tpu_custom_call" | custom-call | flops 150994944 | bytes 8000000 | tf_op jit(solution)/shard_map/pallas_call | solution.py:687
  180.5 2.7 %collective-permute-start.19 = (bf16[24,1536]{1,0:T(8,128)(2,1)}, bf16[24,1536]{1,0:T(8,128)(2,1)S(1)}, u32[]{:S(2)}, u32[]{:S(2)}) collective-permute-start(bf16[24,1536]{1,0:T(8,128)(2,1)} %get-tuple-element.127), channel_id=1, source_target_pairs={{0,18},{2,16},{4,22},{6,20},{8,26},{10,24},{12,30},{14,28},{16,2},... | collective-permute-start | bytes 221192 | tf_op jit(solution)/shard_map/ppermute | solution.py:54
  184.8 6.7 %collective-permute-done.19.rest_7_ = bf16[24,1536]{1,0:T(8,128)(2,1)S(1)} collective-permute-done((bf16[24,1536]{1,0:T(8,128)(2,1)}, bf16[24,1536]{1,0:T(8,128)(2,1)S(1)}, u32[]{:S(2)}, u32[]{:S(2)}) %collective-permute-start.19) | collective-permute-done | bytes 73760 | tf_op jit(solution)/shard_map/ppermute | solution.py:54
  191.5 5.9 %all-to-all-done.3.got_ref = bf16[16,48,1664]{2,1,0:T(8,128)(2,1)} async-done(((bf16[16,48,1664]{2,1,0:T(8,128)(2,1)}), bf16[16,48,1664]{2,1,0:T(8,128)(2,1)}, u32[]{:S(2)}, u32[]{:S(2)}) %all-to-all-start.3) | async-done | bytes 2555936 | tf_op jit(solution)/shard_map/all_to_all | solution.py:64
  197.4 2.8 %shard_map.217 = (bf16[24,1664]{1,0:T(8,128)(2,1)}, bf16[24,1664]{1,0:T(8,128)(2,1)}) custom-call(s32[1]{0:T(128)} %bitcast.1.place_ref, bf16[16,48,1664]{2,1,0:T(8,128)(2,1)} %all-to-all-done.3.got_ref), custom_call_target="tpu_custom_call" | custom-call | flops 1000 | bytes 8000000 | tf_op jit(solution)/shard_map/pallas_call | solution.py:687
  200.2 2.9 %collective-permute-start.25 = (bf16[24,1664]{1,0:T(8,128)(2,1)}, bf16[24,1664]{1,0:T(8,128)(2,1)S(1)}, u32[]{:S(2)}, u32[]{:S(2)}) collective-permute-start(bf16[24,1664]{1,0:T(8,128)(2,1)} %get-tuple-element.133), channel_id=1, source_target_pairs={{0,18},{2,16},{4,22},{6,20},{8,26},{10,24},{12,30},{14,28},{16,2},... | collective-permute-start | bytes 239624 | tf_op jit(solution)/shard_map/ppermute | solution.py:54
  203.1 1.4 collective-permute-start.24
  205.4 2.8 %collective-permute-done.24.rest_2_ = bf16[24,1664]{1,0:T(8,128)(2,1)S(1)} collective-permute-done((bf16[24,1664]{1,0:T(8,128)(2,1)}, bf16[24,1664]{1,0:T(8,128)(2,1)S(1)}, u32[]{:S(2)}, u32[]{:S(2)}) %collective-permute-start.24) | collective-permute-done | bytes 79904 | tf_op jit(solution)/shard_map/ppermute | solution.py:42
  209.0 4.3 %collective-permute-start.26 = (f32[24,128]{1,0:T(8,128)S(1)}, f32[24,128]{1,0:T(8,128)S(1)}, u32[]{:S(2)}, u32[]{:S(2)}) collective-permute-start(f32[24,128]{1,0:T(8,128)S(1)} %add_add_fusion.mine_ref), channel_id=1, source_target_pairs={{0,1},{1,0},{2,3},{3,2},{4,5},{5,4},{6,7},{7,6},{8,9},{9,8},{10,11... | collective-permute-start | bytes 36872 | tf_op jit(solution)/shard_map/ppermute | solution.py:33
  213.3 3.7 %shard_map.218 = (bf16[128,768]{1,0:T(8,128)(2,1)}, bf16[128,768]{1,0:T(8,128)(2,1)}, f32[2,24,1152]{2,1,0:T(8,128)}, f32[2,24,384]{2,1,0:T(8,128)}, f32[2,24,15...) custom-call(s32[1]{0:T(128)} %bitcast.core_ref, s32[1]{0:T(128)} %bitcast.1.place_ref, ...), custom_call_target="tpu_custom_call" | custom-call | flops 150994944 | bytes 8000000 | tf_op jit(solution)/shard_map/pallas_call | solution.py:687
  217.6 1.3 shard_map.219
  (118 shorter events, 19.2 us)
Async XLA Ops:
  3.6 14.1 %copy-start.9 = (bf16[128,768]{1,0:T(8,128)(2,1)S(1)}, bf16[128,768]{1,0:T(8,128)(2,1)}, u32[]{:S(2)}) copy-start(bf16[128,768]{1,0:T(8,128)(2,1)} %refs_0_.4) | copy-start | bytes 589828
  3.6 14.5 %copy-start.22 = (s32[1,4]{1,0:T(1,128)S(1)}, s32[1,4]{1,0:T(1,128)}, u32[]{:S(2)}) copy-start(s32[1,4]{1,0:T(1,128)} %param.15) | copy-start | bytes 52
  3.7 14.6 %copy-start.23 = (s32[1,4]{1,0:T(1,128)S(1)}, s32[1,4]{1,0:T(1,128)}, u32[]{:S(2)}) copy-start(s32[1,4]{1,0:T(1,128)} %param.16) | copy-start | bytes 52
  3.7 41.3 %all-to-all-start = ((bf16[32,24,1664]{2,1,0:T(8,128)(2,1)}), bf16[32,24,1664]{2,1,0:T(8,128)(2,1)S(1)}, u32[]{:S(2)}, u32[]{:S(2)}) async-start(bf16[32,24,1664]{2,1,0:T(8,128)(2,1)} %get-tuple-element.92), calls=%async_computation | async-start | bytes 5111808 | tf_op jit(solution)/shard_map/all_to_all | solution.py:58
  13.0 27.9 %collective-permute-start.1 = (bf16[128,768]{1,0:T(8,128)(2,1)}, bf16[128,768]{1,0:T(8,128)(2,1)}, u32[]{:S(2)}, u32[]{:S(2)}) collective-permute-start(bf16[128,768]{1,0:T(8,128)(2,1)} %refs_0_.3), channel_id=1, source_target_pairs={{0,2},{2,0},{1,3},{3,1},{4,6},{6,4},{5,7},{7,5},{8,10},{10,8},{9,1... | collective-permute-start | bytes 589832 | tf_op jit(solution)/shard_map/ppermute | solution.py:29
  14.1 9.1 %collective-permute-start.2 = (bf16[128,768]{1,0:T(8,128)(2,1)}, bf16[128,768]{1,0:T(8,128)(2,1)}, u32[]{:S(2)}, u32[]{:S(2)}) collective-permute-start(bf16[128,768]{1,0:T(8,128)(2,1)} %refs_0_.3), channel_id=1, source_target_pairs={{0,17},{1,16},{4,21},{5,20},{8,25},{9,24},{12,29},{13,28},{16,1},{... | collective-permute-start | bytes 589832 | tf_op jit(solution)/shard_map/ppermute | solution.py:48
  17.7 23.2 %collective-permute-start.4 = (bf16[128,768]{1,0:T(8,128)(2,1)S(1)}, bf16[128,768]{1,0:T(8,128)(2,1)}, u32[]{:S(2)}, u32[]{:S(2)}) collective-permute-start(bf16[128,768]{1,0:T(8,128)(2,1)S(1)} %copy-done.9), channel_id=1, source_target_pairs={{0,2},{2,0},{1,3},{3,1},{4,6},{6,4},{5,7},{7,5},{8,10},{10,8},{9,1... | collective-permute-start | bytes 589832 | tf_op jit(solution)/shard_map/ppermute | solution.py:29
  18.1 9.3 %collective-permute-start.5 = (bf16[128,768]{1,0:T(8,128)(2,1)S(1)}, bf16[128,768]{1,0:T(8,128)(2,1)}, u32[]{:S(2)}, u32[]{:S(2)}) collective-permute-start(bf16[128,768]{1,0:T(8,128)(2,1)S(1)} %copy-done.9), channel_id=1, source_target_pairs={{0,17},{1,16},{4,21},{5,20},{8,25},{9,24},{12,29},{13,28},{16,1},{... | collective-permute-start | bytes 589832 | tf_op jit(solution)/shard_map/ppermute | solution.py:48
  18.1 21.8 %collective-permute-start = (bf16[24,1536]{1,0:T(8,128)(2,1)}, bf16[24,1536]{1,0:T(8,128)(2,1)}, u32[]{:S(2)}, u32[]{:S(2)}) collective-permute-start(bf16[24,1536]{1,0:T(8,128)(2,1)} %get-tuple-element.83), channel_id=1, source_target_pairs={{0,16},{4,20},{8,24},{12,28},{16,0},{20,4},{24,8},{28,12},{32,48},... | collective-permute-start | bytes 221192 | tf_op jit(solution)/shard_map/ppermute | solution.py:42
  23.2 17.8 %collective-permute-start.3 = (bf16[128,768]{1,0:T(8,128)(2,1)}, bf16[128,768]{1,0:T(8,128)(2,1)S(1)}, u32[]{:S(2)}, u32[]{:S(2)}) collective-permute-start(bf16[128,768]{1,0:T(8,128)(2,1)} %collective-permute-done.2.refs_2_), channel_id=1, source_target_pairs={{0,2},{2,0},{1,3},{3,1},{4,6},{6,4},{5,7},{7,5},{8,10},{10,8},{9,1... | collective-permute-start | bytes 589832 | tf_op jit(solution)/shard_map/ppermute | solution.py:29
  27.4 14.2 %collective-permute-start.6 = (bf16[128,768]{1,0:T(8,128)(2,1)}, bf16[128,768]{1,0:T(8,128)(2,1)}, u32[]{:S(2)}, u32[]{:S(2)}) collective-permute-start(bf16[128,768]{1,0:T(8,128)(2,1)} %collective-permute-done.5.refs_6_.refs_2_), channel_id=1, source_target_pairs={{0,2},{2,0},{1,3},{3,1},{4,6},{6,4},{5,7},{7,5},{8,10},{10,8},{9,1... | collective-permute-start | bytes 589832 | tf_op jit(solution)/shard_map/ppermute | solution.py:29
  47.1 39.1 %all-to-all-start.1 = ((bf16[16,48,1536]{2,1,0:T(8,128)(2,1)}), bf16[16,48,1536]{2,1,0:T(8,128)(2,1)}, u32[]{:S(2)}, u32[]{:S(2)}) async-start(bf16[16,48,1536]{2,1,0:T(8,128)(2,1)} %broadcast_in_dim.35), calls=%async_computation.1 | async-start | bytes 4718592 | tf_op jit(solution)/shard_map/all_to_all | solution.py:64
  64.5 3.4 %collective-permute-start.7 = (bf16[256,768]{1,0:T(8,128)(2,1)}, bf16[256,768]{1,0:T(8,128)(2,1)S(1)}, u32[]{:S(2)}, u32[]{:S(2)}) collective-permute-start(bf16[256,768]{1,0:T(8,128)(2,1)} %get-tuple-element.94), channel_id=1, source_target_pairs={{0,2},{2,0},{1,3},{3,1},{4,6},{6,4},{5,7},{7,5},{8,10},{10,8},{9,1... | collective-permute-start | bytes 1179656 | tf_op jit(solution)/shard_map/ppermute | solution.py:29
  69.0 11.7 %collective-permute-start.8 = (bf16[256,768]{1,0:T(8,128)(2,1)S(1)}, bf16[256,768]{1,0:T(8,128)(2,1)S(1)}, u32[]{:S(2)}, u32[]{:S(2)}) collective-permute-start(bf16[256,768]{1,0:T(8,128)(2,1)S(1)} %add_convert_fusion.3), channel_id=1, source_target_pairs={{0,17},{1,16},{4,21},{5,20},{8,25},{9,24},{12,29},{13,28},{16,1},{... | collective-permute-start | bytes 1179656 | tf_op jit(solution)/shard_map/ppermute | solution.py:48
  80.9 9.6 %copy-start.3 = (bf16[256,768]{1,0:T(8,128)(2,1)}, bf16[256,768]{1,0:T(8,128)(2,1)S(1)}, u32[]{:S(2)}) copy-start(bf16[256,768]{1,0:T(8,128)(2,1)S(1)} %fusion.5.refs_8_) | copy-start | bytes 1179652
  80.9 9.6 %collective-permute-start.9 = (bf16[256,768]{1,0:T(8,128)(2,1)S(1)}, bf16[256,768]{1,0:T(8,128)(2,1)S(1)}, u32[]{:S(2)}, u32[]{:S(2)}) collective-permute-start(bf16[256,768]{1,0:T(8,128)(2,1)S(1)} %fusion.5.refs_8_), channel_id=1, source_target_pairs={{0,16},{4,20},{8,24},{12,28},{16,0},{20,4},{24,8},{28,12},{32,48},... | collective-permute-start | bytes 1179656 | tf_op jit(solution)/shard_map/ppermute | solution.py:42
  90.6 3.7 %collective-permute-start.10 = (bf16[256,768]{1,0:T(8,128)(2,1)S(1)}, bf16[256,768]{1,0:T(8,128)(2,1)S(1)}, u32[]{:S(2)}, u32[]{:S(2)}) collective-permute-start(bf16[256,768]{1,0:T(8,128)(2,1)S(1)} %fusion.4), channel_id=1, source_target_pairs={{0,2},{2,0},{1,3},{3,1},{4,6},{6,4},{5,7},{7,5},{8,10},{10,8},{9,1... | collective-permute-start | bytes 1179656 | tf_op jit(solution)/shard_map/ppermute | solution.py:29
  110.7 2.0 collective-permute-start.11
  113.8 12.5 %collective-permute-start.12 = (bf16[256,768]{1,0:T(8,128)(2,1)S(1)}, bf16[256,768]{1,0:T(8,128)(2,1)S(1)}, u32[]{:S(2)}, u32[]{:S(2)}) collective-permute-start(bf16[256,768]{1,0:T(8,128)(2,1)S(1)} %add_convert_fusion.2), channel_id=1, source_target_pairs={{0,17},{1,16},{4,21},{5,20},{8,25},{9,24},{12,29},{13,28},{16,1},{... | collective-permute-start | bytes 1179656 | tf_op jit(solution)/shard_map/ppermute | solution.py:48
  117.1 9.4 %copy-start.18 = (bf16[256,768]{1,0:T(8,128)(2,1)S(1)}, bf16[256,768]{1,0:T(8,128)(2,1)}, u32[]{:S(2)}) copy-start(bf16[256,768]{1,0:T(8,128)(2,1)} %get-tuple-element.123) | copy-start | bytes 1179652
  117.1 11.7 %copy-start.7 = (bf16[256,768]{1,0:T(8,128)(2,1)S(1)}, bf16[256,768]{1,0:T(8,128)(2,1)}, u32[]{:S(2)}) copy-start(bf16[256,768]{1,0:T(8,128)(2,1)} %get-tuple-element.122) | copy-start | bytes 1179652
  117.1 40.7 %all-to-all-start.2 = ((bf16[16,48,1536]{2,1,0:T(8,128)(2,1)}), bf16[16,48,1536]{2,1,0:T(8,128)(2,1)}, u32[]{:S(2)}, u32[]{:S(2)}) async-start(bf16[16,48,1536]{2,1,0:T(8,128)(2,1)} %bitcast.48), calls=%async_computation.2 | async-start | bytes 4718592 | tf_op jit(solution)/shard_map/all_to_all | solution.py:64
  126.5 14.3 %copy-start.1 = (bf16[256,768]{1,0:T(8,128)(2,1)}, bf16[256,768]{1,0:T(8,128)(2,1)S(1)}, u32[]{:S(2)}) copy-start(bf16[256,768]{1,0:T(8,128)(2,1)S(1)} %fusion.3.refs_4_) | copy-start | bytes 1179652
  126.5 2.3 %collective-permute-start.15 = (bf16[256,768]{1,0:T(8,128)(2,1)S(1)}, bf16[256,768]{1,0:T(8,128)(2,1)S(1)}, u32[]{:S(2)}, u32[]{:S(2)}) collective-permute-start(bf16[256,768]{1,0:T(8,128)(2,1)S(1)} %copy-done.18), channel_id=1, source_target_pairs={{0,2},{2,0},{1,3},{3,1},{4,6},{6,4},{5,7},{7,5},{8,10},{10,8},{9,1... | collective-permute-start | bytes 1179656 | tf_op jit(solution)/shard_map/ppermute | solution.py:29
  127.5 10.8 %collective-permute-start.13 = (bf16[256,768]{1,0:T(8,128)(2,1)S(1)}, bf16[256,768]{1,0:T(8,128)(2,1)S(1)}, u32[]{:S(2)}, u32[]{:S(2)}) collective-permute-start(bf16[256,768]{1,0:T(8,128)(2,1)S(1)} %fusion.3.refs_4_), channel_id=1, source_target_pairs={{0,16},{4,20},{8,24},{12,28},{16,0},{20,4},{24,8},{28,12},{32,48},... | collective-permute-start | bytes 1179656 | tf_op jit(solution)/shard_map/ppermute | solution.py:42
  128.9 11.7 %collective-permute-start.16 = (bf16[256,768]{1,0:T(8,128)(2,1)S(1)}, bf16[256,768]{1,0:T(8,128)(2,1)S(1)}, u32[]{:S(2)}, u32[]{:S(2)}) collective-permute-start(bf16[256,768]{1,0:T(8,128)(2,1)S(1)} %add_convert_fusion.1), channel_id=1, source_target_pairs={{0,17},{1,16},{4,21},{5,20},{8,25},{9,24},{12,29},{13,28},{16,1},{... | collective-permute-start | bytes 1179656 | tf_op jit(solution)/shard_map/ppermute | solution.py:48
  138.4 2.4 %collective-permute-start.14 = (bf16[256,768]{1,0:T(8,128)(2,1)S(1)}, bf16[256,768]{1,0:T(8,128)(2,1)S(1)}, u32[]{:S(2)}, u32[]{:S(2)}) collective-permute-start(bf16[256,768]{1,0:T(8,128)(2,1)S(1)} %fusion.2), channel_id=1, source_target_pairs={{0,2},{2,0},{1,3},{3,1},{4,6},{6,4},{5,7},{7,5},{8,10},{10,8},{9,1... | collective-permute-start | bytes 1179656 | tf_op jit(solution)/shard_map/ppermute | solution.py:29
  157.8 4.6 %copy-start.19 = (bf16[256,768]{1,0:T(8,128)(2,1)S(1)}, bf16[256,768]{1,0:T(8,128)(2,1)}, u32[]{:S(2)}) copy-start(bf16[256,768]{1,0:T(8,128)(2,1)} %get-tuple-element.130) | copy-start | bytes 1179652
  157.8 7.8 %copy-start.8 = (bf16[256,768]{1,0:T(8,128)(2,1)S(1)}, bf16[256,768]{1,0:T(8,128)(2,1)}, u32[]{:S(2)}) copy-start(bf16[256,768]{1,0:T(8,128)(2,1)} %get-tuple-element.129) | copy-start | bytes 1179652
  157.8 39.6 %all-to-all-start.3 = ((bf16[16,48,1664]{2,1,0:T(8,128)(2,1)}), bf16[16,48,1664]{2,1,0:T(8,128)(2,1)}, u32[]{:S(2)}, u32[]{:S(2)}) async-start(bf16[16,48,1664]{2,1,0:T(8,128)(2,1)} %bitcast.47), calls=%async_computation.3 | async-start | bytes 5111808 | tf_op jit(solution)/shard_map/all_to_all | solution.py:64
  162.4 3.2 %collective-permute-start.20 = (bf16[256,768]{1,0:T(8,128)(2,1)S(1)}, bf16[256,768]{1,0:T(8,128)(2,1)S(1)}, u32[]{:S(2)}, u32[]{:S(2)}) collective-permute-start(bf16[256,768]{1,0:T(8,128)(2,1)S(1)} %copy-done.19), channel_id=1, source_target_pairs={{0,2},{2,0},{1,3},{3,1},{4,6},{6,4},{5,7},{7,5},{8,10},{10,8},{9,1... | collective-permute-start | bytes 1179656 | tf_op jit(solution)/shard_map/ppermute | solution.py:29
  165.8 11.7 %collective-permute-start.21 = (bf16[256,768]{1,0:T(8,128)(2,1)S(1)}, bf16[256,768]{1,0:T(8,128)(2,1)S(1)}, u32[]{:S(2)}, u32[]{:S(2)}) collective-permute-start(bf16[256,768]{1,0:T(8,128)(2,1)S(1)} %add_convert_fusion), channel_id=1, source_target_pairs={{0,17},{1,16},{4,21},{5,20},{8,25},{9,24},{12,29},{13,28},{16,1},{... | collective-permute-start | bytes 1179656 | tf_op jit(solution)/shard_map/ppermute | solution.py:48
  177.8 13.7 %collective-permute-start.22 = (bf16[256,768]{1,0:T(8,128)(2,1)S(1)}, bf16[256,768]{1,0:T(8,128)(2,1)S(1)}, u32[]{:S(2)}, u32[]{:S(2)}) collective-permute-start(bf16[256,768]{1,0:T(8,128)(2,1)S(1)} %pad_maximum_fusion.2), channel_id=1, source_target_pairs={{0,16},{4,20},{8,24},{12,28},{16,0},{20,4},{24,8},{28,12},{32,48},... | collective-permute-start | bytes 1179656 | tf_op jit(solution)/shard_map/ppermute | solution.py:42
  180.5 11.0 %collective-permute-start.19 = (bf16[24,1536]{1,0:T(8,128)(2,1)}, bf16[24,1536]{1,0:T(8,128)(2,1)S(1)}, u32[]{:S(2)}, u32[]{:S(2)}) collective-permute-start(bf16[24,1536]{1,0:T(8,128)(2,1)} %get-tuple-element.127), channel_id=1, source_target_pairs={{0,18},{2,16},{4,22},{6,20},{8,26},{10,24},{12,30},{14,28},{16,2},... | collective-permute-start | bytes 221192 | tf_op jit(solution)/shard_map/ppermute | solution.py:54
  183.2 8.2 %collective-permute-start.18 = (bf16[24,1536]{1,0:T(8,128)(2,1)}, bf16[24,1536]{1,0:T(8,128)(2,1)S(1)}, u32[]{:S(2)}, u32[]{:S(2)}) collective-permute-start(bf16[24,1536]{1,0:T(8,128)(2,1)} %get-tuple-element.127), channel_id=1, source_target_pairs={{0,16},{4,20},{8,24},{12,28},{16,0},{20,4},{24,8},{28,12},{32,48},... | collective-permute-start | bytes 221192 | tf_op jit(solution)/shard_map/ppermute | solution.py:42
  183.2 1.5 collective-permute-start.17
  184.8 28.5 %copy-start.15 = (bf16[24,1536]{1,0:T(8,128)(2,1)}, bf16[24,1536]{1,0:T(8,128)(2,1)S(1)}, u32[]{:S(2)}) copy-start(bf16[24,1536]{1,0:T(8,128)(2,1)S(1)} %collective-permute-done.17.rest_5_) | copy-start | bytes 221188
  191.5 21.8 %copy-start.13 = (bf16[24,1536]{1,0:T(8,128)(2,1)}, bf16[24,1536]{1,0:T(8,128)(2,1)S(1)}, u32[]{:S(2)}) copy-start(bf16[24,1536]{1,0:T(8,128)(2,1)S(1)} %collective-permute-done.19.rest_7_) | copy-start | bytes 221188
  191.5 21.8 %copy-start.14 = (bf16[24,1536]{1,0:T(8,128)(2,1)}, bf16[24,1536]{1,0:T(8,128)(2,1)S(1)}, u32[]{:S(2)}) copy-start(bf16[24,1536]{1,0:T(8,128)(2,1)S(1)} %collective-permute-done.18.rest_6_) | copy-start | bytes 221188
  191.5 21.8 %copy-start.5 = (bf16[256,768]{1,0:T(8,128)(2,1)}, bf16[256,768]{1,0:T(8,128)(2,1)S(1)}, u32[]{:S(2)}) copy-start(bf16[256,768]{1,0:T(8,128)(2,1)S(1)} %collective-permute-done.22.rest_9_) | copy-start | bytes 1179652
  200.2 5.2 %collective-permute-start.25 = (bf16[24,1664]{1,0:T(8,128)(2,1)}, bf16[24,1664]{1,0:T(8,128)(2,1)S(1)}, u32[]{:S(2)}, u32[]{:S(2)}) collective-permute-start(bf16[24,1664]{1,0:T(8,128)(2,1)} %get-tuple-element.133), channel_id=1, source_target_pairs={{0,18},{2,16},{4,22},{6,20},{8,26},{10,24},{12,30},{14,28},{16,2},... | collective-permute-start | bytes 239624 | tf_op jit(solution)/shard_map/ppermute | solution.py:54
  203.1 5.1 %collective-permute-start.24 = (bf16[24,1664]{1,0:T(8,128)(2,1)}, bf16[24,1664]{1,0:T(8,128)(2,1)S(1)}, u32[]{:S(2)}, u32[]{:S(2)}) collective-permute-start(bf16[24,1664]{1,0:T(8,128)(2,1)} %get-tuple-element.133), channel_id=1, source_target_pairs={{0,16},{4,20},{8,24},{12,28},{16,0},{20,4},{24,8},{28,12},{32,48},... | collective-permute-start | bytes 239624 | tf_op jit(solution)/shard_map/ppermute | solution.py:42
  204.5 3.7 %collective-permute-start.23 = (bf16[24,1664]{1,0:T(8,128)(2,1)}, bf16[24,1664]{1,0:T(8,128)(2,1)S(1)}, u32[]{:S(2)}, u32[]{:S(2)}) collective-permute-start(bf16[24,1664]{1,0:T(8,128)(2,1)} %get-tuple-element.132.rest_0_), channel_id=1, source_target_pairs={{0,2},{2,0},{1,3},{3,1},{4,6},{6,4},{5,7},{7,5},{8,10},{10,8},{9,1... | collective-permute-start | bytes 239624 | tf_op jit(solution)/shard_map/ppermute | solution.py:29
  205.4 7.8 %copy-start.10 = (bf16[24,1664]{1,0:T(8,128)(2,1)}, bf16[24,1664]{1,0:T(8,128)(2,1)S(1)}, u32[]{:S(2)}) copy-start(bf16[24,1664]{1,0:T(8,128)(2,1)S(1)} %collective-permute-done.25.rest_3_) | copy-start | bytes 239620
  208.2 5.0 %copy-start.11 = (bf16[24,1664]{1,0:T(8,128)(2,1)}, bf16[24,1664]{1,0:T(8,128)(2,1)S(1)}, u32[]{:S(2)}) copy-start(bf16[24,1664]{1,0:T(8,128)(2,1)S(1)} %collective-permute-done.24.rest_2_) | copy-start | bytes 239620
  208.3 5.0 %copy-start.12 = (bf16[24,1664]{1,0:T(8,128)(2,1)}, bf16[24,1664]{1,0:T(8,128)(2,1)S(1)}, u32[]{:S(2)}) copy-start(bf16[24,1664]{1,0:T(8,128)(2,1)S(1)} %collective-permute-done.23.rest_1_) | copy-start | bytes 239620
  209.0 8.0 %copy-start.16 = (f32[24,128]{1,0:T(8,128)}, f32[24,128]{1,0:T(8,128)S(1)}, u32[]{:S(2)}) copy-start(f32[24,128]{1,0:T(8,128)S(1)} %add_add_fusion.mine_ref) | copy-start | bytes 36868
  209.0 8.0 %collective-permute-start.26 = (f32[24,128]{1,0:T(8,128)S(1)}, f32[24,128]{1,0:T(8,128)S(1)}, u32[]{:S(2)}, u32[]{:S(2)}) collective-permute-start(f32[24,128]{1,0:T(8,128)S(1)} %add_add_fusion.mine_ref), channel_id=1, source_target_pairs={{0,1},{1,0},{2,3},{3,2},{4,5},{5,4},{6,7},{7,6},{8,9},{9,8},{10,11... | collective-permute-start | bytes 36872 | tf_op jit(solution)/shard_map/ppermute | solution.py:33
  (7 other events, 11.4 us)

commit v7 on v6

--- a/solution.py
+++ b/solution.py
@@ -86,7 +86,7 @@
     def body(at, kept):
         return step(pl.ds(pl.multiple_of(at * CHUNK, CHUNK), CHUNK), kept)
 
-    return lax.fori_loop(start // CHUNK, rows // CHUNK, body, carry)
+    return lax.fori_loop(start // CHUNK, rows // CHUNK, body, carry, unroll=True)
 
 
 def by_eights(values):
@@ -139,15 +139,17 @@
             copy.wait()
         return self.heads_ref, self.w_ref
 
-    def give(self, far_heads_ref, far_ref, sent):
-        copies = [
-            pltpu.make_async_copy(self.heads_ref, far_heads_ref, sent.at[0]),
-            pltpu.make_async_copy(self.w_ref, far_ref, sent.at[1]),
+    def give(self, put, far_ref):
+        attn, hidden = self.heads_ref.shape[1], self.w_ref.shape[1] // 2
+        self.put = put
+        self.pieces = [
+            (self.heads_ref, far_ref.at[:, :attn]),
+            (self.w_ref.at[:, :hidden], far_ref.at[:, attn : attn + hidden]),
+            (self.w_ref.at[:, hidden:], far_ref.at[:, attn + hidden : attn + 2 * hidden]),
         ]
-        for copy in copies:
-            copy.start()
-        for copy in copies:
-            copy.wait()
+
+    def sent(self, piece):
+        self.put.start(*self.pieces[piece])
 
 
 class Copies:
@@ -351,10 +353,13 @@
     heads_grad = dot(state.a[...], qkv_ref[...], (0, 0))
     heads_grad = heads_grad + dot(low_ref[:group, :], state.o[...], (0, 0))
     heads_ref[...] = pairs_together(heads_grad, owners).astype(BF)
+    slab.sent(0)
     up_grad = dot(state.m[...], up_ref[...], (0, 0))
     w_ref[:, :hidden] = pairs_together(up_grad, owners).astype(BF)
+    slab.sent(1)
     down_grad = dot(low, state.gl[...], (0, 0))
     w_ref[:, hidden : 2 * hidden] = pairs_together(down_grad, owners).astype(BF)
+    slab.sent(2)
 
 
 def first_kernel(layers, *refs):
@@ -466,8 +471,8 @@
     forward(state, vec_ref.at[1], slab, get, table_ref, mask_ref, ahead, scratch[3])
     for ref, far_part_ref in zip(ahead, far_parts[:2], strict=True):
         put.start(ref, far_part_ref)
+    slab.give(put, slab_ref)
     backward(owners, state, grad_ref, vec_ref.at[1], slab, table_ref, back, sums_ref, scratch, put, far_parts[2:])
-    slab.give(slab_ref.at[:, :attn], slab_ref.at[:, attn:width], arrived)
     put.wait()
 
 
@@ -494,6 +499,7 @@
     kept_ref[...] = below_ref[: kept_ref.shape[0], :]
     slab.wait()
     get.wait()
+    slab.give(put, slab_ref)
     backward(owners, state, below_ref, vec_ref.at[0], slab, table_ref, back, sums_ref, scratch, put, far_back)
     both = [sums_ref, later_ref]
     pad = jnp.zeros((8 - layers, attn), F32)
@@ -510,7 +516,6 @@
     small_ref[...] = pairs_together(jnp.transpose(small), owners).astype(BF)
     copy = pltpu.make_async_copy(small_ref, slab_ref.at[:, width:], arrived.at[2])
     copy.start()
-    slab.give(slab_ref.at[:, :attn], slab_ref.at[:, attn:width], arrived)
     copy.wait()
     put.wait()
 
@@ -883,7 +888,7 @@
         ),
         [
             *vmem(table, mask, sds((row_count, wide), F32)),
-            *copies(6, 7),
+            *copies(6, 10),
             *vmem(part, part, part, part, *kept, sds((rows, wide), BF)),
             *slab_scratch,
             *scratch,
@@ -911,7 +916,7 @@
         (part, part, sds((wide, width + LANES), BF), sds((row_count, wide), F32)),
         [
             *vmem(table),
-            *copies(11, 2),
+            *copies(11, 5),
             *vmem(part, part, *kept, later_sums, sds((rows, wide), F32)),
             *vmem(sds((wide, LANES), BF)),
             *slab_scratch,

time: 220 us -> 215 us (0.977)
  Pallas kernels: 51.7 us -> 47.9 us
  starting transfers between devices: 64.7 us -> 61.5 us
  waiting for transfers between devices: 82.8 us -> 85.3 us
    pallas_call x8, Pallas kernels: 51.7 us -> 47.9 us  [call(): pl.pallas_call(kernel, out_shape=outs, in_specs=[pl.BlockSpec(memory_spac...]
where the time goes in v7:
time: 215 us; the launch traced here: 214 us
  waiting for transfers between devices  85.3 us (40%)
  starting transfers between devices  61.5 us (29%)
  Pallas kernels  47.9 us (22%)
  local copies, waits for them, and re-layouts  10.4 us (5%)
  other arithmetic  8.19 us (4%)
    pallas_call x8, Pallas kernels, call(): pl.pallas_call(kernel, out_shape=outs, in_specs=[pl.BlockSpec(memory_spac...  47.9 us
    ppermute x6, waiting for transfers between devices, near_other_half(): return lax.ppermute(values, ('fsdp', 'tp'), pairs)  31.2 us
    ppermute x6, waiting for transfers between devices, near_group(): return lax.ppermute(values, 'fsdp', [(f, f ^ NEAR) for f in range(owners)])  22.1 us
    all_to_all x3, starting transfers between devices, exchanged_in_plane(): lax.all_to_all(blocks, 'fsdp', 0, 0, axis_index_groups=planes, tiled=True)  17 us
    all_to_all x3, waiting for transfers between devices, exchanged_in_plane(): lax.all_to_all(blocks, 'fsdp', 0, 0, axis_index_groups=planes, tiled=True)  14 us
    ppermute x12, starting transfers between devices, other_core(): return lax.ppermute(values, 'ctx', SWAP)  12.6 us
    ppermute x6, starting transfers between devices, near_other_half(): return lax.ppermute(values, ('fsdp', 'tp'), pairs)  12.6 us
    all_to_all x1, starting transfers between devices, exchanged(): return lax.all_to_all(blocks, 'fsdp', 0, 0, tiled=True)  9.37 us
  transfers between devices with their start and end apart: 31, of which 23 were waited for; matrix products, arithmetic and copies ran while one was open for 5% of the time, Pallas kernels for 13%

profile of v7, /device:TPU:1, one launch (start us, length us, event | category | flops | bytes accessed | tf_op | source)
XLA Modules:
  0.0 214.4 jit_solution(4587339675962325137)
XLA Ops:
  0.7 2.9 %shard_map.212 = (bf16[32,24,1664]{2,1,0:T(8,128)(2,1)}, bf16[24,1536]{1,0:T(8,128)(2,1)}, bf16[24,1536]{1,0:T(8,128)(2,1)}) custom-call(s32[1]{0:T(128)} %bitcast.core_ref, s32[1]{0:T(128)} %bitcast.1.place_ref, bf16[2,24,1152]{2,1,0:T(8,128)(2,1)} %refs_0_.1, bf16[2,24,384]{2,1,0:T(8,128)(2,1)} %bitcast.60, bf16[2,24,1536]{2,1,0:T(8,128)(2,1)} %refs_2_.1, ...), custom_call_target="tpu_custom_call" | custom-call | flops 1000 | bytes 8000000 | tf_op jit(solution)/shard_map/pallas_call | solution.py:692
  3.7 9.4 %all-to-all-start = ((bf16[32,24,1664]{2,1,0:T(8,128)(2,1)}), bf16[32,24,1664]{2,1,0:T(8,128)(2,1)S(1)}, u32[]{:S(2)}, u32[]{:S(2)}) async-start(bf16[32,24,1664]{2,1,0:T(8,128)(2,1)} %get-tuple-element.92), calls=%async_computation | async-start | bytes 5111808 | tf_op jit(solution)/shard_map/all_to_all | solution.py:58
  13.0 1.0 collective-permute-start.1
  14.1 3.6 %collective-permute-start.2 = (bf16[128,768]{1,0:T(8,128)(2,1)}, bf16[128,768]{1,0:T(8,128)(2,1)}, u32[]{:S(2)}, u32[]{:S(2)}) collective-permute-start(bf16[128,768]{1,0:T(8,128)(2,1)} %refs_0_.3), channel_id=1, source_target_pairs={{0,17},{1,16},{4,21},{5,20},{8,25},{9,24},{12,29},{13,28},{16,1},{... | collective-permute-start | bytes 589832 | tf_op jit(solution)/shard_map/ppermute | solution.py:48
  20.8 2.4 %collective-permute-done.2.refs_2_ = bf16[128,768]{1,0:T(8,128)(2,1)} collective-permute-done((bf16[128,768]{1,0:T(8,128)(2,1)}, bf16[128,768]{1,0:T(8,128)(2,1)}, u32[]{:S(2)}, u32[]{:S(2)}) %collective-permute-start.2) | collective-permute-done | bytes 196640 | tf_op jit(solution)/shard_map/ppermute | solution.py:48
  24.2 3.3 %collective-permute-done.5.refs_6_.refs_2_ = bf16[128,768]{1,0:T(8,128)(2,1)} collective-permute-done((bf16[128,768]{1,0:T(8,128)(2,1)S(1)}, bf16[128,768]{1,0:T(8,128)(2,1)}, u32[]{:S(2)}, u32[]{:S(2)}) %collective-permute-start.5) | collective-permute-done | bytes 196640 | tf_op jit(solution)/shard_map/ppermute | solution.py:48
  28.1 11.8 %collective-permute-done = bf16[24,1536]{1,0:T(8,128)(2,1)} collective-permute-done((bf16[24,1536]{1,0:T(8,128)(2,1)}, bf16[24,1536]{1,0:T(8,128)(2,1)}, u32[]{:S(2)}, u32[]{:S(2)}) %collective-permute-start) | collective-permute-done | bytes 73760 | tf_op jit(solution)/shard_map/ppermute | solution.py:42
  41.7 3.3 %all-to-all-done = bf16[32,24,1664]{2,1,0:T(8,128)(2,1)S(1)} async-done(((bf16[32,24,1664]{2,1,0:T(8,128)(2,1)}), bf16[32,24,1664]{2,1,0:T(8,128)(2,1)S(1)}, u32[]{:S(2)}, u32[]{:S(2)}) %all-to-all-start) | async-done | bytes 2555936 | tf_op jit(solution)/shard_map/all_to_all | solution.py:58
  44.9 1.8 broadcast_in_dim.35
  47.1 7.0 %all-to-all-start.1 = ((bf16[16,48,1536]{2,1,0:T(8,128)(2,1)}), bf16[16,48,1536]{2,1,0:T(8,128)(2,1)}, u32[]{:S(2)}, u32[]{:S(2)}) async-start(bf16[16,48,1536]{2,1,0:T(8,128)(2,1)} %broadcast_in_dim.35), calls=%async_computation.1 | async-start | bytes 4718592 | tf_op jit(solution)/shard_map/all_to_all | solution.py:64
  55.8 8.1 %shard_map.213 = (bf16[256,768]{1,0:T(8,128)(2,1)}, bf16[256,768]{1,0:T(8,128)(2,1)}, f32[2,8,768]{2,1,0:T(8,128)}, f32[512,768]{1,0:T(8,128)}, f32[512,1]{1,0:T...) custom-call(bf16[128,768]{1,0:T(8,128)(2,1)} %refs_0_.3, ...), custom_call_target="tpu_custom_call" | custom-call | flops 1207959552 | bytes 8000000 | tf_op jit(solution)/shard_map/pallas_call | solution.py:692
  63.9 1.8 collective-permute-start.7
  65.8 1.6 collective-permute-done.7
  67.3 1.1 add_convert_fusion.3
  68.4 2.4 %collective-permute-start.8 = (bf16[256,768]{1,0:T(8,128)(2,1)S(1)}, bf16[256,768]{1,0:T(8,128)(2,1)S(1)}, u32[]{:S(2)}, u32[]{:S(2)}) collective-permute-start(bf16[256,768]{1,0:T(8,128)(2,1)S(1)} %add_convert_fusion.3), channel_id=1, source_target_pairs={{0,17},{1,16},{4,21},{5,20},{8,25},{9,24},{12,29},{13,28},{16,1},{... | collective-permute-start | bytes 1179656 | tf_op jit(solution)/shard_map/ppermute | solution.py:48
  70.8 9.3 %collective-permute-done.8 = bf16[256,768]{1,0:T(8,128)(2,1)S(1)} collective-permute-done((bf16[256,768]{1,0:T(8,128)(2,1)S(1)}, bf16[256,768]{1,0:T(8,128)(2,1)S(1)}, u32[]{:S(2)}, u32[]{:S(2)}) %collective-permute-start.8) | collective-permute-done | bytes 393248 | tf_op jit(solution)/shard_map/ppermute | solution.py:48
  81.0 5.2 %all-to-all-done.1 = bf16[16,48,1536]{2,1,0:T(8,128)(2,1)} async-done(((bf16[16,48,1536]{2,1,0:T(8,128)(2,1)}), bf16[16,48,1536]{2,1,0:T(8,128)(2,1)}, u32[]{:S(2)}, u32[]{:S(2)}) %all-to-all-start.1) | async-done | bytes 2359328 | tf_op jit(solution)/shard_map/all_to_all | solution.py:64
  86.2 3.4 %copy.27 = bf16[4,2,4,24,1536]{4,3,2,1,0:T(8,128)(2,1)} copy(bf16[4,2,4,24,1536]{4,3,1,2,0:T(8,128)(2,1)} %bitcast.14) | data formatting | bytes 4718592 | tf_op jit(solution)/shard_map/transpose | solution.py:77
  90.1 2.9 %collective-permute-start.10 = (bf16[256,768]{1,0:T(8,128)(2,1)S(1)}, bf16[256,768]{1,0:T(8,128)(2,1)S(1)}, u32[]{:S(2)}, u32[]{:S(2)}) collective-permute-start(bf16[256,768]{1,0:T(8,128)(2,1)S(1)} %fusion.4), channel_id=1, source_target_pairs={{0,2},{2,0},{1,3},{3,1},{4,6},{6,4},{5,7},{7,5},{8,10},{10,8},{9,1... | collective-permute-start | bytes 1179656 | tf_op jit(solution)/shard_map/ppermute | solution.py:29
  93.0 1.3 collective-permute-done.10.refs_10_
  95.1 13.7 %shard_map.214 = (bf16[256,768]{1,0:T(8,128)(2,1)}, bf16[256,768]{1,0:T(8,128)(2,1)}, bf16[256,768]{1,0:T(8,128)(2,1)}, bf16[256,768]{1,0:T(8,128)(2,1)}, bf16[7...) custom-call(bf16[128,768]{1,0:T(8,128)(2,1)} %refs_0_.3, ...), custom_call_target="tpu_custom_call" | custom-call | flops 3623878656 | bytes 8000000 | tf_op jit(solution)/shard_map/pallas_call | solution.py:692
  109.2 1.6 collective-permute-done.11
  110.8 1.1 add_convert_fusion.2
  111.9 3.3 %collective-permute-start.12 = (bf16[256,768]{1,0:T(8,128)(2,1)S(1)}, bf16[256,768]{1,0:T(8,128)(2,1)S(1)}, u32[]{:S(2)}, u32[]{:S(2)}) collective-permute-start(bf16[256,768]{1,0:T(8,128)(2,1)S(1)} %add_convert_fusion.2), channel_id=1, source_target_pairs={{0,17},{1,16},{4,21},{5,20},{8,25},{9,24},{12,29},{13,28},{16,1},{... | collective-permute-start | bytes 1179656 | tf_op jit(solution)/shard_map/ppermute | solution.py:48
  115.2 5.4 %all-to-all-start.2 = ((bf16[16,48,1536]{2,1,0:T(8,128)(2,1)}), bf16[16,48,1536]{2,1,0:T(8,128)(2,1)}, u32[]{:S(2)}, u32[]{:S(2)}) async-start(bf16[16,48,1536]{2,1,0:T(8,128)(2,1)} %bitcast.48), calls=%async_computation.2 | async-start | bytes 4718592 | tf_op jit(solution)/shard_map/all_to_all | solution.py:64
  120.6 3.8 %collective-permute-done.12 = bf16[256,768]{1,0:T(8,128)(2,1)S(1)} collective-permute-done((bf16[256,768]{1,0:T(8,128)(2,1)S(1)}, bf16[256,768]{1,0:T(8,128)(2,1)S(1)}, u32[]{:S(2)}, u32[]{:S(2)}) %collective-permute-start.12) | collective-permute-done | bytes 393248 | tf_op jit(solution)/shard_map/ppermute | solution.py:48
  125.6 1.3 collective-permute-done.15
  127.0 2.8 %collective-permute-start.16 = (bf16[256,768]{1,0:T(8,128)(2,1)S(1)}, bf16[256,768]{1,0:T(8,128)(2,1)S(1)}, u32[]{:S(2)}, u32[]{:S(2)}) collective-permute-start(bf16[256,768]{1,0:T(8,128)(2,1)S(1)} %add_convert_fusion.1), channel_id=1, source_target_pairs={{0,17},{1,16},{4,21},{5,20},{8,25},{9,24},{12,29},{13,28},{16,1},{... | collective-permute-start | bytes 1179656 | tf_op jit(solution)/shard_map/ppermute | solution.py:48
  129.8 6.6 %collective-permute-done.13.refs_5_ = bf16[256,768]{1,0:T(8,128)(2,1)S(1)} collective-permute-done((bf16[256,768]{1,0:T(8,128)(2,1)S(1)}, bf16[256,768]{1,0:T(8,128)(2,1)S(1)}, u32[]{:S(2)}, u32[]{:S(2)}) %collective-permute-start.13) | collective-permute-done | bytes 393248 | tf_op jit(solution)/shard_map/ppermute | solution.py:42
  136.5 1.1 collective-permute-start.14
  137.6 1.2 collective-permute-done.16
  139.7 12.8 %shard_map.215 = (bf16[256,768]{1,0:T(8,128)(2,1)}, bf16[256,768]{1,0:T(8,128)(2,1)}, bf16[768,1664]{1,0:T(8,128)(2,1)}, f32[128,768]{1,0:T(8,128)}) custom-call(bf16[128,768]{1,0:T(8,128)(2,1)} %refs_0_.4, bf16[128,768]{1,0:T(8,128)(2,1)} %collective-permute-done.4.refs_5_.refs_1_, bf16[128,768]{1,0:T(8,128)(2,1)} %collective-permute-done.5.refs_6_.refs_2_, ...), custom_call_target="tpu_custom_call" | custom-call | flops 2415919104 | bytes 8000000 | tf_op jit(solution)/shard_map/pallas_call | solution.py:692
  152.6 2.8 %all-to-all-done.2.got_ref = bf16[16,48,1536]{2,1,0:T(8,128)(2,1)} async-done(((bf16[16,48,1536]{2,1,0:T(8,128)(2,1)}), bf16[16,48,1536]{2,1,0:T(8,128)(2,1)}, u32[]{:S(2)}, u32[]{:S(2)}) %all-to-all-start.2) | async-done | bytes 2359328 | tf_op jit(solution)/shard_map/all_to_all | solution.py:64
  155.4 4.6 %all-to-all-start.3 = ((bf16[16,48,1664]{2,1,0:T(8,128)(2,1)}), bf16[16,48,1664]{2,1,0:T(8,128)(2,1)}, u32[]{:S(2)}, u32[]{:S(2)}) async-start(bf16[16,48,1664]{2,1,0:T(8,128)(2,1)} %bitcast.47), calls=%async_computation.3 | async-start | bytes 5111808 | tf_op jit(solution)/shard_map/all_to_all | solution.py:64
  160.0 1.9 collective-permute-start.20
  161.9 1.3 collective-permute-done.20
  163.8 11.3 %collective-permute-done.21 = bf16[256,768]{1,0:T(8,128)(2,1)S(1)} collective-permute-done((bf16[256,768]{1,0:T(8,128)(2,1)S(1)}, bf16[256,768]{1,0:T(8,128)(2,1)S(1)}, u32[]{:S(2)}, u32[]{:S(2)}) %collective-permute-start.21) | collective-permute-done | bytes 393248 | tf_op jit(solution)/shard_map/ppermute | solution.py:48
  175.5 2.6 %shard_map.216 = (bf16[24,1536]{1,0:T(8,128)(2,1)}, bf16[24,1536]{1,0:T(8,128)(2,1)}) custom-call(s32[1]{0:T(128)} %bitcast.1.place_ref, bf16[16,48,1536]{2,1,0:T(8,128)(2,1)} %all-to-all-done.2.got_ref), custom_call_target="tpu_custom_call" | custom-call | flops 150994944 | bytes 8000000 | tf_op jit(solution)/shard_map/pallas_call | solution.py:692
  178.1 2.7 %collective-permute-start.19 = (bf16[24,1536]{1,0:T(8,128)(2,1)}, bf16[24,1536]{1,0:T(8,128)(2,1)S(1)}, u32[]{:S(2)}, u32[]{:S(2)}) collective-permute-start(bf16[24,1536]{1,0:T(8,128)(2,1)} %get-tuple-element.127), channel_id=1, source_target_pairs={{0,18},{2,16},{4,22},{6,20},{8,26},{10,24},{12,30},{14,28},{16,2},... | collective-permute-start | bytes 221192 | tf_op jit(solution)/shard_map/ppermute | solution.py:54
  182.4 6.7 %collective-permute-done.19.rest_7_ = bf16[24,1536]{1,0:T(8,128)(2,1)S(1)} collective-permute-done((bf16[24,1536]{1,0:T(8,128)(2,1)}, bf16[24,1536]{1,0:T(8,128)(2,1)S(1)}, u32[]{:S(2)}, u32[]{:S(2)}) %collective-permute-start.19) | collective-permute-done | bytes 73760 | tf_op jit(solution)/shard_map/ppermute | solution.py:54
  189.1 6.0 %all-to-all-done.3.got_ref = bf16[16,48,1664]{2,1,0:T(8,128)(2,1)} async-done(((bf16[16,48,1664]{2,1,0:T(8,128)(2,1)}), bf16[16,48,1664]{2,1,0:T(8,128)(2,1)}, u32[]{:S(2)}, u32[]{:S(2)}) %all-to-all-start.3) | async-done | bytes 2555936 | tf_op jit(solution)/shard_map/all_to_all | solution.py:64
  195.0 2.8 %shard_map.217 = (bf16[24,1664]{1,0:T(8,128)(2,1)}, bf16[24,1664]{1,0:T(8,128)(2,1)}) custom-call(s32[1]{0:T(128)} %bitcast.1.place_ref, bf16[16,48,1664]{2,1,0:T(8,128)(2,1)} %all-to-all-done.3.got_ref), custom_call_target="tpu_custom_call" | custom-call | flops 1000 | bytes 8000000 | tf_op jit(solution)/shard_map/pallas_call | solution.py:692
  197.8 2.4 %collective-permute-start.25 = (bf16[24,1664]{1,0:T(8,128)(2,1)}, bf16[24,1664]{1,0:T(8,128)(2,1)S(1)}, u32[]{:S(2)}, u32[]{:S(2)}) collective-permute-start(bf16[24,1664]{1,0:T(8,128)(2,1)} %get-tuple-element.133), channel_id=1, source_target_pairs={{0,18},{2,16},{4,22},{6,20},{8,26},{10,24},{12,30},{14,28},{16,2},... | collective-permute-start | bytes 239624 | tf_op jit(solution)/shard_map/ppermute | solution.py:54
  200.2 1.9 collective-permute-start.24
  202.5 3.3 %collective-permute-done.24.rest_2_ = bf16[24,1664]{1,0:T(8,128)(2,1)S(1)} collective-permute-done((bf16[24,1664]{1,0:T(8,128)(2,1)}, bf16[24,1664]{1,0:T(8,128)(2,1)S(1)}, u32[]{:S(2)}, u32[]{:S(2)}) %collective-permute-start.24) | collective-permute-done | bytes 79904 | tf_op jit(solution)/shard_map/ppermute | solution.py:42
  206.6 2.1 %collective-permute-start.26 = (f32[24,128]{1,0:T(8,128)S(1)}, f32[24,128]{1,0:T(8,128)S(1)}, u32[]{:S(2)}, u32[]{:S(2)}) collective-permute-start(f32[24,128]{1,0:T(8,128)S(1)} %add_add_fusion.mine_ref), channel_id=1, source_target_pairs={{0,1},{1,0},{2,3},{3,2},{4,5},{5,4},{6,7},{7,6},{8,9},{9,8},{10,11... | collective-permute-start | bytes 36872 | tf_op jit(solution)/shard_map/ppermute | solution.py:33
  208.8 3.7 %shard_map.218 = (bf16[128,768]{1,0:T(8,128)(2,1)}, bf16[128,768]{1,0:T(8,128)(2,1)}, f32[2,24,1152]{2,1,0:T(8,128)}, f32[2,24,384]{2,1,0:T(8,128)}, f32[2,24,15...) custom-call(s32[1]{0:T(128)} %bitcast.core_ref, s32[1]{0:T(128)} %bitcast.1.place_ref, ...), custom_call_target="tpu_custom_call" | custom-call | flops 150994944 | bytes 8000000 | tf_op jit(solution)/shard_map/pallas_call | solution.py:692
  213.1 1.3 shard_map.219
  (118 shorter events, 17.5 us)
Async XLA Ops:
  3.6 14.1 %copy-start.9 = (bf16[128,768]{1,0:T(8,128)(2,1)S(1)}, bf16[128,768]{1,0:T(8,128)(2,1)}, u32[]{:S(2)}) copy-start(bf16[128,768]{1,0:T(8,128)(2,1)} %refs_0_.4) | copy-start | bytes 589828
  3.6 14.5 %copy-start.22 = (s32[1,4]{1,0:T(1,128)S(1)}, s32[1,4]{1,0:T(1,128)}, u32[]{:S(2)}) copy-start(s32[1,4]{1,0:T(1,128)} %param.15) | copy-start | bytes 52
  3.7 14.6 %copy-start.23 = (s32[1,4]{1,0:T(1,128)S(1)}, s32[1,4]{1,0:T(1,128)}, u32[]{:S(2)}) copy-start(s32[1,4]{1,0:T(1,128)} %param.16) | copy-start | bytes 52
  3.7 41.3 %all-to-all-start = ((bf16[32,24,1664]{2,1,0:T(8,128)(2,1)}), bf16[32,24,1664]{2,1,0:T(8,128)(2,1)S(1)}, u32[]{:S(2)}, u32[]{:S(2)}) async-start(bf16[32,24,1664]{2,1,0:T(8,128)(2,1)} %get-tuple-element.92), calls=%async_computation | async-start | bytes 5111808 | tf_op jit(solution)/shard_map/all_to_all | solution.py:58
  13.0 27.9 %collective-permute-start.1 = (bf16[128,768]{1,0:T(8,128)(2,1)}, bf16[128,768]{1,0:T(8,128)(2,1)}, u32[]{:S(2)}, u32[]{:S(2)}) collective-permute-start(bf16[128,768]{1,0:T(8,128)(2,1)} %refs_0_.3), channel_id=1, source_target_pairs={{0,2},{2,0},{1,3},{3,1},{4,6},{6,4},{5,7},{7,5},{8,10},{10,8},{9,1... | collective-permute-start | bytes 589832 | tf_op jit(solution)/shard_map/ppermute | solution.py:29
  14.1 9.1 %collective-permute-start.2 = (bf16[128,768]{1,0:T(8,128)(2,1)}, bf16[128,768]{1,0:T(8,128)(2,1)}, u32[]{:S(2)}, u32[]{:S(2)}) collective-permute-start(bf16[128,768]{1,0:T(8,128)(2,1)} %refs_0_.3), channel_id=1, source_target_pairs={{0,17},{1,16},{4,21},{5,20},{8,25},{9,24},{12,29},{13,28},{16,1},{... | collective-permute-start | bytes 589832 | tf_op jit(solution)/shard_map/ppermute | solution.py:48
  17.7 23.2 %collective-permute-start.4 = (bf16[128,768]{1,0:T(8,128)(2,1)S(1)}, bf16[128,768]{1,0:T(8,128)(2,1)}, u32[]{:S(2)}, u32[]{:S(2)}) collective-permute-start(bf16[128,768]{1,0:T(8,128)(2,1)S(1)} %copy-done.9), channel_id=1, source_target_pairs={{0,2},{2,0},{1,3},{3,1},{4,6},{6,4},{5,7},{7,5},{8,10},{10,8},{9,1... | collective-permute-start | bytes 589832 | tf_op jit(solution)/shard_map/ppermute | solution.py:29
  18.1 9.3 %collective-permute-start.5 = (bf16[128,768]{1,0:T(8,128)(2,1)S(1)}, bf16[128,768]{1,0:T(8,128)(2,1)}, u32[]{:S(2)}, u32[]{:S(2)}) collective-permute-start(bf16[128,768]{1,0:T(8,128)(2,1)S(1)} %copy-done.9), channel_id=1, source_target_pairs={{0,17},{1,16},{4,21},{5,20},{8,25},{9,24},{12,29},{13,28},{16,1},{... | collective-permute-start | bytes 589832 | tf_op jit(solution)/shard_map/ppermute | solution.py:48
  18.1 21.8 %collective-permute-start = (bf16[24,1536]{1,0:T(8,128)(2,1)}, bf16[24,1536]{1,0:T(8,128)(2,1)}, u32[]{:S(2)}, u32[]{:S(2)}) collective-permute-start(bf16[24,1536]{1,0:T(8,128)(2,1)} %get-tuple-element.83), channel_id=1, source_target_pairs={{0,16},{4,20},{8,24},{12,28},{16,0},{20,4},{24,8},{28,12},{32,48},... | collective-permute-start | bytes 221192 | tf_op jit(solution)/shard_map/ppermute | solution.py:42
  23.2 17.8 %collective-permute-start.3 = (bf16[128,768]{1,0:T(8,128)(2,1)}, bf16[128,768]{1,0:T(8,128)(2,1)S(1)}, u32[]{:S(2)}, u32[]{:S(2)}) collective-permute-start(bf16[128,768]{1,0:T(8,128)(2,1)} %collective-permute-done.2.refs_2_), channel_id=1, source_target_pairs={{0,2},{2,0},{1,3},{3,1},{4,6},{6,4},{5,7},{7,5},{8,10},{10,8},{9,1... | collective-permute-start | bytes 589832 | tf_op jit(solution)/shard_map/ppermute | solution.py:29
  27.4 14.2 %collective-permute-start.6 = (bf16[128,768]{1,0:T(8,128)(2,1)}, bf16[128,768]{1,0:T(8,128)(2,1)}, u32[]{:S(2)}, u32[]{:S(2)}) collective-permute-start(bf16[128,768]{1,0:T(8,128)(2,1)} %collective-permute-done.5.refs_6_.refs_2_), channel_id=1, source_target_pairs={{0,2},{2,0},{1,3},{3,1},{4,6},{6,4},{5,7},{7,5},{8,10},{10,8},{9,1... | collective-permute-start | bytes 589832 | tf_op jit(solution)/shard_map/ppermute | solution.py:29
  47.1 39.1 %all-to-all-start.1 = ((bf16[16,48,1536]{2,1,0:T(8,128)(2,1)}), bf16[16,48,1536]{2,1,0:T(8,128)(2,1)}, u32[]{:S(2)}, u32[]{:S(2)}) async-start(bf16[16,48,1536]{2,1,0:T(8,128)(2,1)} %broadcast_in_dim.35), calls=%async_computation.1 | async-start | bytes 4718592 | tf_op jit(solution)/shard_map/all_to_all | solution.py:64
  63.9 3.4 %collective-permute-start.7 = (bf16[256,768]{1,0:T(8,128)(2,1)}, bf16[256,768]{1,0:T(8,128)(2,1)S(1)}, u32[]{:S(2)}, u32[]{:S(2)}) collective-permute-start(bf16[256,768]{1,0:T(8,128)(2,1)} %get-tuple-element.94), channel_id=1, source_target_pairs={{0,2},{2,0},{1,3},{3,1},{4,6},{6,4},{5,7},{7,5},{8,10},{10,8},{9,1... | collective-permute-start | bytes 1179656 | tf_op jit(solution)/shard_map/ppermute | solution.py:29
  68.4 11.7 %collective-permute-start.8 = (bf16[256,768]{1,0:T(8,128)(2,1)S(1)}, bf16[256,768]{1,0:T(8,128)(2,1)S(1)}, u32[]{:S(2)}, u32[]{:S(2)}) collective-permute-start(bf16[256,768]{1,0:T(8,128)(2,1)S(1)} %add_convert_fusion.3), channel_id=1, source_target_pairs={{0,17},{1,16},{4,21},{5,20},{8,25},{9,24},{12,29},{13,28},{16,1},{... | collective-permute-start | bytes 1179656 | tf_op jit(solution)/shard_map/ppermute | solution.py:48
  80.3 9.6 %copy-start.3 = (bf16[256,768]{1,0:T(8,128)(2,1)}, bf16[256,768]{1,0:T(8,128)(2,1)S(1)}, u32[]{:S(2)}) copy-start(bf16[256,768]{1,0:T(8,128)(2,1)S(1)} %fusion.5.refs_8_) | copy-start | bytes 1179652
  80.3 9.6 %collective-permute-start.9 = (bf16[256,768]{1,0:T(8,128)(2,1)S(1)}, bf16[256,768]{1,0:T(8,128)(2,1)S(1)}, u32[]{:S(2)}, u32[]{:S(2)}) collective-permute-start(bf16[256,768]{1,0:T(8,128)(2,1)S(1)} %fusion.5.refs_8_), channel_id=1, source_target_pairs={{0,16},{4,20},{8,24},{12,28},{16,0},{20,4},{24,8},{28,12},{32,48},... | collective-permute-start | bytes 1179656 | tf_op jit(solution)/shard_map/ppermute | solution.py:42
  89.9 4.5 %copy-start.6 = (bf16[256,768]{1,0:T(8,128)(2,1)}, bf16[256,768]{1,0:T(8,128)(2,1)S(1)}, u32[]{:S(2)}) copy-start(bf16[256,768]{1,0:T(8,128)(2,1)S(1)} %collective-permute-done.9.refs_9_) | copy-start | bytes 1179652
  90.1 4.3 %collective-permute-start.10 = (bf16[256,768]{1,0:T(8,128)(2,1)S(1)}, bf16[256,768]{1,0:T(8,128)(2,1)S(1)}, u32[]{:S(2)}, u32[]{:S(2)}) collective-permute-start(bf16[256,768]{1,0:T(8,128)(2,1)S(1)} %fusion.4), channel_id=1, source_target_pairs={{0,2},{2,0},{1,3},{3,1},{4,6},{6,4},{5,7},{7,5},{8,10},{10,8},{9,1... | collective-permute-start | bytes 1179656 | tf_op jit(solution)/shard_map/ppermute | solution.py:29
  108.8 2.0 collective-permute-start.11
  111.9 12.5 %collective-permute-start.12 = (bf16[256,768]{1,0:T(8,128)(2,1)S(1)}, bf16[256,768]{1,0:T(8,128)(2,1)S(1)}, u32[]{:S(2)}, u32[]{:S(2)}) collective-permute-start(bf16[256,768]{1,0:T(8,128)(2,1)S(1)} %add_convert_fusion.2), channel_id=1, source_target_pairs={{0,17},{1,16},{4,21},{5,20},{8,25},{9,24},{12,29},{13,28},{16,1},{... | collective-permute-start | bytes 1179656 | tf_op jit(solution)/shard_map/ppermute | solution.py:48
  115.2 9.4 %copy-start.18 = (bf16[256,768]{1,0:T(8,128)(2,1)S(1)}, bf16[256,768]{1,0:T(8,128)(2,1)}, u32[]{:S(2)}) copy-start(bf16[256,768]{1,0:T(8,128)(2,1)} %get-tuple-element.123) | copy-start | bytes 1179652
  115.2 11.7 %copy-start.7 = (bf16[256,768]{1,0:T(8,128)(2,1)S(1)}, bf16[256,768]{1,0:T(8,128)(2,1)}, u32[]{:S(2)}) copy-start(bf16[256,768]{1,0:T(8,128)(2,1)} %get-tuple-element.122) | copy-start | bytes 1179652
  115.2 40.2 %all-to-all-start.2 = ((bf16[16,48,1536]{2,1,0:T(8,128)(2,1)}), bf16[16,48,1536]{2,1,0:T(8,128)(2,1)}, u32[]{:S(2)}, u32[]{:S(2)}) async-start(bf16[16,48,1536]{2,1,0:T(8,128)(2,1)} %bitcast.48), calls=%async_computation.2 | async-start | bytes 4718592 | tf_op jit(solution)/shard_map/all_to_all | solution.py:64
  124.6 14.3 %copy-start.1 = (bf16[256,768]{1,0:T(8,128)(2,1)}, bf16[256,768]{1,0:T(8,128)(2,1)S(1)}, u32[]{:S(2)}) copy-start(bf16[256,768]{1,0:T(8,128)(2,1)S(1)} %fusion.3.refs_4_) | copy-start | bytes 1179652
  124.6 2.3 %collective-permute-start.15 = (bf16[256,768]{1,0:T(8,128)(2,1)S(1)}, bf16[256,768]{1,0:T(8,128)(2,1)S(1)}, u32[]{:S(2)}, u32[]{:S(2)}) collective-permute-start(bf16[256,768]{1,0:T(8,128)(2,1)S(1)} %copy-done.18), channel_id=1, source_target_pairs={{0,2},{2,0},{1,3},{3,1},{4,6},{6,4},{5,7},{7,5},{8,10},{10,8},{9,1... | collective-permute-start | bytes 1179656 | tf_op jit(solution)/shard_map/ppermute | solution.py:29
  125.6 10.8 %collective-permute-start.13 = (bf16[256,768]{1,0:T(8,128)(2,1)S(1)}, bf16[256,768]{1,0:T(8,128)(2,1)S(1)}, u32[]{:S(2)}, u32[]{:S(2)}) collective-permute-start(bf16[256,768]{1,0:T(8,128)(2,1)S(1)} %fusion.3.refs_4_), channel_id=1, source_target_pairs={{0,16},{4,20},{8,24},{12,28},{16,0},{20,4},{24,8},{28,12},{32,48},... | collective-permute-start | bytes 1179656 | tf_op jit(solution)/shard_map/ppermute | solution.py:42
  127.0 11.7 %collective-permute-start.16 = (bf16[256,768]{1,0:T(8,128)(2,1)S(1)}, bf16[256,768]{1,0:T(8,128)(2,1)S(1)}, u32[]{:S(2)}, u32[]{:S(2)}) collective-permute-start(bf16[256,768]{1,0:T(8,128)(2,1)S(1)} %add_convert_fusion.1), channel_id=1, source_target_pairs={{0,17},{1,16},{4,21},{5,20},{8,25},{9,24},{12,29},{13,28},{16,1},{... | collective-permute-start | bytes 1179656 | tf_op jit(solution)/shard_map/ppermute | solution.py:48
  136.5 2.4 %collective-permute-start.14 = (bf16[256,768]{1,0:T(8,128)(2,1)S(1)}, bf16[256,768]{1,0:T(8,128)(2,1)S(1)}, u32[]{:S(2)}, u32[]{:S(2)}) collective-permute-start(bf16[256,768]{1,0:T(8,128)(2,1)S(1)} %fusion.2), channel_id=1, source_target_pairs={{0,2},{2,0},{1,3},{3,1},{4,6},{6,4},{5,7},{7,5},{8,10},{10,8},{9,1... | collective-permute-start | bytes 1179656 | tf_op jit(solution)/shard_map/ppermute | solution.py:29
  155.4 4.6 %copy-start.19 = (bf16[256,768]{1,0:T(8,128)(2,1)S(1)}, bf16[256,768]{1,0:T(8,128)(2,1)}, u32[]{:S(2)}) copy-start(bf16[256,768]{1,0:T(8,128)(2,1)} %get-tuple-element.130) | copy-start | bytes 1179652
  155.4 7.8 %copy-start.8 = (bf16[256,768]{1,0:T(8,128)(2,1)S(1)}, bf16[256,768]{1,0:T(8,128)(2,1)}, u32[]{:S(2)}) copy-start(bf16[256,768]{1,0:T(8,128)(2,1)} %get-tuple-element.129) | copy-start | bytes 1179652
  155.4 39.6 %all-to-all-start.3 = ((bf16[16,48,1664]{2,1,0:T(8,128)(2,1)}), bf16[16,48,1664]{2,1,0:T(8,128)(2,1)}, u32[]{:S(2)}, u32[]{:S(2)}) async-start(bf16[16,48,1664]{2,1,0:T(8,128)(2,1)} %bitcast.47), calls=%async_computation.3 | async-start | bytes 5111808 | tf_op jit(solution)/shard_map/all_to_all | solution.py:64
  160.0 3.2 %collective-permute-start.20 = (bf16[256,768]{1,0:T(8,128)(2,1)S(1)}, bf16[256,768]{1,0:T(8,128)(2,1)S(1)}, u32[]{:S(2)}, u32[]{:S(2)}) collective-permute-start(bf16[256,768]{1,0:T(8,128)(2,1)S(1)} %copy-done.19), channel_id=1, source_target_pairs={{0,2},{2,0},{1,3},{3,1},{4,6},{6,4},{5,7},{7,5},{8,10},{10,8},{9,1... | collective-permute-start | bytes 1179656 | tf_op jit(solution)/shard_map/ppermute | solution.py:29
  163.4 11.7 %collective-permute-start.21 = (bf16[256,768]{1,0:T(8,128)(2,1)S(1)}, bf16[256,768]{1,0:T(8,128)(2,1)S(1)}, u32[]{:S(2)}, u32[]{:S(2)}) collective-permute-start(bf16[256,768]{1,0:T(8,128)(2,1)S(1)} %add_convert_fusion), channel_id=1, source_target_pairs={{0,17},{1,16},{4,21},{5,20},{8,25},{9,24},{12,29},{13,28},{16,1},{... | collective-permute-start | bytes 1179656 | tf_op jit(solution)/shard_map/ppermute | solution.py:48
  175.4 13.7 %collective-permute-start.22 = (bf16[256,768]{1,0:T(8,128)(2,1)S(1)}, bf16[256,768]{1,0:T(8,128)(2,1)S(1)}, u32[]{:S(2)}, u32[]{:S(2)}) collective-permute-start(bf16[256,768]{1,0:T(8,128)(2,1)S(1)} %pad_maximum_fusion.2), channel_id=1, source_target_pairs={{0,16},{4,20},{8,24},{12,28},{16,0},{20,4},{24,8},{28,12},{32,48},... | collective-permute-start | bytes 1179656 | tf_op jit(solution)/shard_map/ppermute | solution.py:42
  178.1 11.0 %collective-permute-start.19 = (bf16[24,1536]{1,0:T(8,128)(2,1)}, bf16[24,1536]{1,0:T(8,128)(2,1)S(1)}, u32[]{:S(2)}, u32[]{:S(2)}) collective-permute-start(bf16[24,1536]{1,0:T(8,128)(2,1)} %get-tuple-element.127), channel_id=1, source_target_pairs={{0,18},{2,16},{4,22},{6,20},{8,26},{10,24},{12,30},{14,28},{16,2},... | collective-permute-start | bytes 221192 | tf_op jit(solution)/shard_map/ppermute | solution.py:54
  180.8 8.2 %collective-permute-start.18 = (bf16[24,1536]{1,0:T(8,128)(2,1)}, bf16[24,1536]{1,0:T(8,128)(2,1)S(1)}, u32[]{:S(2)}, u32[]{:S(2)}) collective-permute-start(bf16[24,1536]{1,0:T(8,128)(2,1)} %get-tuple-element.127), channel_id=1, source_target_pairs={{0,16},{4,20},{8,24},{12,28},{16,0},{20,4},{24,8},{28,12},{32,48},... | collective-permute-start | bytes 221192 | tf_op jit(solution)/shard_map/ppermute | solution.py:42
  180.8 1.5 collective-permute-start.17
  182.4 26.4 %copy-start.15 = (bf16[24,1536]{1,0:T(8,128)(2,1)}, bf16[24,1536]{1,0:T(8,128)(2,1)S(1)}, u32[]{:S(2)}) copy-start(bf16[24,1536]{1,0:T(8,128)(2,1)S(1)} %collective-permute-done.17.rest_5_) | copy-start | bytes 221188
  189.0 19.7 %copy-start.13 = (bf16[24,1536]{1,0:T(8,128)(2,1)}, bf16[24,1536]{1,0:T(8,128)(2,1)S(1)}, u32[]{:S(2)}) copy-start(bf16[24,1536]{1,0:T(8,128)(2,1)S(1)} %collective-permute-done.19.rest_7_) | copy-start | bytes 221188
  189.1 19.7 %copy-start.14 = (bf16[24,1536]{1,0:T(8,128)(2,1)}, bf16[24,1536]{1,0:T(8,128)(2,1)S(1)}, u32[]{:S(2)}) copy-start(bf16[24,1536]{1,0:T(8,128)(2,1)S(1)} %collective-permute-done.18.rest_6_) | copy-start | bytes 221188
  189.1 19.7 %copy-start.5 = (bf16[256,768]{1,0:T(8,128)(2,1)}, bf16[256,768]{1,0:T(8,128)(2,1)S(1)}, u32[]{:S(2)}) copy-start(bf16[256,768]{1,0:T(8,128)(2,1)S(1)} %collective-permute-done.22.rest_9_) | copy-start | bytes 1179652
  197.8 4.7 %collective-permute-start.25 = (bf16[24,1664]{1,0:T(8,128)(2,1)}, bf16[24,1664]{1,0:T(8,128)(2,1)S(1)}, u32[]{:S(2)}, u32[]{:S(2)}) collective-permute-start(bf16[24,1664]{1,0:T(8,128)(2,1)} %get-tuple-element.133), channel_id=1, source_target_pairs={{0,18},{2,16},{4,22},{6,20},{8,26},{10,24},{12,30},{14,28},{16,2},... | collective-permute-start | bytes 239624 | tf_op jit(solution)/shard_map/ppermute | solution.py:54
  200.2 5.6 %collective-permute-start.24 = (bf16[24,1664]{1,0:T(8,128)(2,1)}, bf16[24,1664]{1,0:T(8,128)(2,1)S(1)}, u32[]{:S(2)}, u32[]{:S(2)}) collective-permute-start(bf16[24,1664]{1,0:T(8,128)(2,1)} %get-tuple-element.133), channel_id=1, source_target_pairs={{0,16},{4,20},{8,24},{12,28},{16,0},{20,4},{24,8},{28,12},{32,48},... | collective-permute-start | bytes 239624 | tf_op jit(solution)/shard_map/ppermute | solution.py:42
  202.1 3.7 %collective-permute-start.23 = (bf16[24,1664]{1,0:T(8,128)(2,1)}, bf16[24,1664]{1,0:T(8,128)(2,1)S(1)}, u32[]{:S(2)}, u32[]{:S(2)}) collective-permute-start(bf16[24,1664]{1,0:T(8,128)(2,1)} %get-tuple-element.132.rest_0_), channel_id=1, source_target_pairs={{0,2},{2,0},{1,3},{3,1},{4,6},{6,4},{5,7},{7,5},{8,10},{10,8},{9,1... | collective-permute-start | bytes 239624 | tf_op jit(solution)/shard_map/ppermute | solution.py:29
  202.5 6.2 %copy-start.10 = (bf16[24,1664]{1,0:T(8,128)(2,1)}, bf16[24,1664]{1,0:T(8,128)(2,1)S(1)}, u32[]{:S(2)}) copy-start(bf16[24,1664]{1,0:T(8,128)(2,1)S(1)} %collective-permute-done.25.rest_3_) | copy-start | bytes 239620
  205.9 2.9 %copy-start.12 = (bf16[24,1664]{1,0:T(8,128)(2,1)}, bf16[24,1664]{1,0:T(8,128)(2,1)S(1)}, u32[]{:S(2)}) copy-start(bf16[24,1664]{1,0:T(8,128)(2,1)S(1)} %collective-permute-done.23.rest_1_) | copy-start | bytes 239620
  206.6 5.9 %copy-start.16 = (f32[24,128]{1,0:T(8,128)}, f32[24,128]{1,0:T(8,128)S(1)}, u32[]{:S(2)}) copy-start(f32[24,128]{1,0:T(8,128)S(1)} %add_add_fusion.mine_ref) | copy-start | bytes 36868
  206.6 5.9 %collective-permute-start.26 = (f32[24,128]{1,0:T(8,128)S(1)}, f32[24,128]{1,0:T(8,128)S(1)}, u32[]{:S(2)}, u32[]{:S(2)}) collective-permute-start(f32[24,128]{1,0:T(8,128)S(1)} %add_add_fusion.mine_ref), channel_id=1, source_target_pairs={{0,1},{1,0},{2,3},{3,2},{4,5},{5,4},{6,7},{7,6},{8,9},{9,8},{10,11... | collective-permute-start | bytes 36872 | tf_op jit(solution)/shard_map/ppermute | solution.py:33
  (7 other events, 10.4 us)

commit v8 on v7

--- a/solution.py
+++ b/solution.py
@@ -580,6 +580,15 @@
     return [wide[z][1] for z in at]
 
 
+def spread_kernel(place_ref, own_ref, near_ref, send_ref):
+    own, near = own_ref[...].astype(F32), near_ref[...].astype(F32)
+    first = place_ref[0] == 0
+    rows = [jnp.where(first, own, near), jnp.where(first, near, own)]
+    rows = jnp.concatenate(rows, axis=0).astype(BF)
+    for pair in range(send_ref.shape[0]):
+        send_ref[pair] = rows
+
+
 def sum_of(got_ref, columns):
     total = got_ref[0, :, columns].astype(F32)
     for sender in range(1, got_ref.shape[0]):
@@ -812,10 +821,16 @@
     starts, ends = ((own, near_other_half(own)) for own in (tokens, cotangent))
     starts, ends = ((o, other_core(o), n, other_core(n)) for o, n in (starts, ends))
     first = exchanged(send).reshape(wide, -1)
-    pair = [own_block, near_group(near_block)]
-    pair = jnp.where(place_z == 0, jnp.concatenate(pair), jnp.concatenate(pair[::-1]))
-    pair, starts, ends = lax.optimization_barrier((pair, starts, ends))
-    second = jnp.broadcast_to(pair[None], (owners // 2, *pair.shape))
+    near_rows, starts, ends = lax.optimization_barrier((near_group(near_block), starts, ends))
+    (second,) = call(
+        spread_kernel,
+        (sds((owners // 2, 2 * depth, width), BF),),
+        [],
+        100_000_000,
+        place_at,
+        own_block,
+        near_rows,
+    )
     second = owners_in_order(exchanged_in_plane(second), owners)
     offsets = jnp.arange(block_rows, dtype=jnp.int32)
     positions = (block_pos[0][:, None] * block_rows + offsets[None, :]).reshape(2, row_count)

time: 215 us -> 215 us (level)
  Pallas kernels: 47.9 us -> 50.7 us
    reshape x0 -> x1, local copies, waits for them, and re-layouts: none -> 3.37 us  [owners_in_order(): blocks = blocks.reshape(owners // (2 * NEAR), NEAR, 2, -1, width)]
    transpose x1 -> x0, local copies, waits for them, and re-layouts: 3.37 us -> none  [owners_in_order(): return blocks.transpose(0, 2, 1, 3, 4).reshape(-1, width)]
    pallas_call x8 -> x9, Pallas kernels: 47.9 us -> 50.7 us  [call(): pl.pallas_call(kernel, out_shape=outs, in_specs=[pl.BlockSpec(memory_spac...]
    ppermute x6, starting transfers between devices: 12.6 us -> 10.1 us  [near_other_half(): return lax.ppermute(values, ('fsdp', 'tp'), pairs)]
    all_to_all x3, starting transfers between devices: 17 us -> 19.4 us  [exchanged_in_plane(): lax.all_to_all(blocks, 'fsdp', 0, 0, axis_index_groups=planes, tiled=True)]
  transfers between devices with their start and end apart: 31 -> 31, of which waited for: 23 -> 22; matrix products, arithmetic and copies ran while one was open for 5% -> 5% of each run, Pallas kernels for 13% -> 14%
where the time goes in v8:
time: 215 us; the launch traced here: 214 us
  waiting for transfers between devices  85.8 us (40%)
  starting transfers between devices  61.2 us (28%)
  Pallas kernels  50.7 us (24%)
  local copies, waits for them, and re-layouts  8.27 us (4%)
  other arithmetic  7.17 us (3%)
    pallas_call x9, Pallas kernels, call(): pl.pallas_call(kernel, out_shape=outs, in_specs=[pl.BlockSpec(memory_spac...  50.7 us
    ppermute x6, waiting for transfers between devices, near_other_half(): return lax.ppermute(values, ('fsdp', 'tp'), pairs)  31.3 us
    ppermute x6, waiting for transfers between devices, near_group(): return lax.ppermute(values, 'fsdp', [(f, f ^ NEAR) for f in range(owners)])  22.8 us
    all_to_all x3, starting transfers between devices, exchanged_in_plane(): lax.all_to_all(blocks, 'fsdp', 0, 0, axis_index_groups=planes, tiled=True)  19.4 us
    all_to_all x3, waiting for transfers between devices, exchanged_in_plane(): lax.all_to_all(blocks, 'fsdp', 0, 0, axis_index_groups=planes, tiled=True)  15.7 us
    ppermute x12, starting transfers between devices, other_core(): return lax.ppermute(values, 'ctx', SWAP)  12 us
    ppermute x6, starting transfers between devices, near_other_half(): return lax.ppermute(values, ('fsdp', 'tp'), pairs)  10.1 us
    all_to_all x1, starting transfers between devices, exchanged(): return lax.all_to_all(blocks, 'fsdp', 0, 0, tiled=True)  9.48 us
  transfers between devices with their start and end apart: 31, of which 22 were waited for; matrix products, arithmetic and copies ran while one was open for 5% of the time, Pallas kernels for 14%

profile of v8, /device:TPU:1, one launch (start us, length us, event | category | flops | bytes accessed | tf_op | source)
XLA Modules:
  0.0 214.3 jit_solution(2355366366787936604)
XLA Ops:
  0.7 3.0 %shard_map.212 = (bf16[32,24,1664]{2,1,0:T(8,128)(2,1)}, bf16[24,1536]{1,0:T(8,128)(2,1)}, bf16[24,1536]{1,0:T(8,128)(2,1)}) custom-call(s32[1]{0:T(128)} %bitcast.core_ref, s32[1]{0:T(128)} %bitcast.1.place_ref, bf16[2,24,1152]{2,1,0:T(8,128)(2,1)} %refs_0_.1, bf16[2,24,384]{2,1,0:T(8,128)(2,1)} %bitcast.58, bf16[2,24,1536]{2,1,0:T(8,128)(2,1)} %refs_2_.1, ...), custom_call_target="tpu_custom_call" | custom-call | flops 1000 | bytes 8000000 | tf_op jit(solution)/shard_map/pallas_call | solution.py:701
  3.7 9.5 %all-to-all-start = ((bf16[32,24,1664]{2,1,0:T(8,128)(2,1)}), bf16[32,24,1664]{2,1,0:T(8,128)(2,1)}, u32[]{:S(2)}, u32[]{:S(2)}) async-start(bf16[32,24,1664]{2,1,0:T(8,128)(2,1)} %get-tuple-element.91), calls=%async_computation | async-start | bytes 5111808 | tf_op jit(solution)/shard_map/all_to_all | solution.py:58
  13.2 1.0 collective-permute-start.1
  14.3 3.6 %collective-permute-start.2 = (bf16[128,768]{1,0:T(8,128)(2,1)S(1)}, bf16[128,768]{1,0:T(8,128)(2,1)S(1)}, u32[]{:S(2)}, u32[]{:S(2)}) collective-permute-start(bf16[128,768]{1,0:T(8,128)(2,1)S(1)} %copy-done.24), channel_id=1, source_target_pairs={{0,17},{1,16},{4,21},{5,20},{8,25},{9,24},{12,29},{13,28},{16,1},{... | collective-permute-start | bytes 589832 | tf_op jit(solution)/shard_map/ppermute | solution.py:48
  20.2 2.9 %collective-permute-done.2.refs_2_ = bf16[128,768]{1,0:T(8,128)(2,1)S(1)} collective-permute-done((bf16[128,768]{1,0:T(8,128)(2,1)S(1)}, bf16[128,768]{1,0:T(8,128)(2,1)S(1)}, u32[]{:S(2)}, u32[]{:S(2)}) %collective-permute-start.2) | collective-permute-done | bytes 196640 | tf_op jit(solution)/shard_map/ppermute | solution.py:48
  24.0 3.4 %collective-permute-done.5.refs_6_.refs_2_ = bf16[128,768]{1,0:T(8,128)(2,1)S(1)} collective-permute-done((bf16[128,768]{1,0:T(8,128)(2,1)S(1)}, bf16[128,768]{1,0:T(8,128)(2,1)S(1)}, u32[]{:S(2)}, u32[]{:S(2)}) %collective-permute-start.5) | collective-permute-done | bytes 196640 | tf_op jit(solution)/shard_map/ppermute | solution.py:48
  28.7 11.3 %collective-permute-done.near_ref = bf16[24,1536]{1,0:T(8,128)(2,1)S(1)} collective-permute-done((bf16[24,1536]{1,0:T(8,128)(2,1)S(1)}, bf16[24,1536]{1,0:T(8,128)(2,1)S(1)}, u32[]{:S(2)}, u32[]{:S(2)}) %collective-permute-start) | collective-permute-done | bytes 73760 | tf_op jit(solution)/shard_map/ppermute | solution.py:42
  40.8 2.6 %shard_map.214 = bf16[16,48,1536]{2,1,0:T(8,128)(2,1)} custom-call(s32[1]{0:T(128)} %bitcast.1.place_ref, bf16[24,1536]{1,0:T(8,128)(2,1)} %get-tuple-element.94.own_ref, bf16[24,1536]{1,0:T(8,128)(2,1)} %copy-done.15), custom_call_target="tpu_custom_call" | custom-call | flops 100000000 | bytes 8000000 | tf_op jit(solution)/shard_map/pallas_call | solution.py:701
  43.4 1.7 all-to-all-done
  45.1 7.8 %all-to-all-start.1 = ((bf16[16,48,1536]{2,1,0:T(8,128)(2,1)}), bf16[16,48,1536]{2,1,0:T(8,128)(2,1)}, u32[]{:S(2)}, u32[]{:S(2)}) async-start(bf16[16,48,1536]{2,1,0:T(8,128)(2,1)} %shard_map.214), calls=%async_computation.1 | async-start | bytes 4718592 | tf_op jit(solution)/shard_map/all_to_all | solution.py:64
  54.6 8.2 %shard_map.213 = (bf16[256,768]{1,0:T(8,128)(2,1)}, bf16[256,768]{1,0:T(8,128)(2,1)}, f32[2,8,768]{2,1,0:T(8,128)}, f32[512,768]{1,0:T(8,128)}, f32[512,1]{1,0:T...) custom-call(bf16[128,768]{1,0:T(8,128)(2,1)} %refs_0_.3, ...), custom_call_target="tpu_custom_call" | custom-call | flops 1207959552 | bytes 8000000 | tf_op jit(solution)/shard_map/pallas_call | solution.py:701
  62.8 1.3 collective-permute-start.7
  64.2 1.6 collective-permute-done.7
  65.7 1.1 add_convert_fusion.3
  66.8 3.4 %collective-permute-start.8 = (bf16[256,768]{1,0:T(8,128)(2,1)S(1)}, bf16[256,768]{1,0:T(8,128)(2,1)S(1)}, u32[]{:S(2)}, u32[]{:S(2)}) collective-permute-start(bf16[256,768]{1,0:T(8,128)(2,1)S(1)} %add_convert_fusion.3), channel_id=1, source_target_pairs={{0,17},{1,16},{4,21},{5,20},{8,25},{9,24},{12,29},{13,28},{16,1},{... | collective-permute-start | bytes 1179656 | tf_op jit(solution)/shard_map/ppermute | solution.py:48
  70.2 9.3 %collective-permute-done.8 = bf16[256,768]{1,0:T(8,128)(2,1)S(1)} collective-permute-done((bf16[256,768]{1,0:T(8,128)(2,1)S(1)}, bf16[256,768]{1,0:T(8,128)(2,1)S(1)}, u32[]{:S(2)}, u32[]{:S(2)}) %collective-permute-start.8) | collective-permute-done | bytes 393248 | tf_op jit(solution)/shard_map/ppermute | solution.py:48
  79.7 6.8 %all-to-all-done.1 = bf16[16,48,1536]{2,1,0:T(8,128)(2,1)} async-done(((bf16[16,48,1536]{2,1,0:T(8,128)(2,1)}), bf16[16,48,1536]{2,1,0:T(8,128)(2,1)}, u32[]{:S(2)}, u32[]{:S(2)}) %all-to-all-start.1) | async-done | bytes 2359328 | tf_op jit(solution)/shard_map/all_to_all | solution.py:64
  86.5 3.4 %copy.27 = bf16[4,4,2,24,1536]{4,3,1,2,0:T(8,128)(2,1)} copy(bf16[4,4,2,24,1536]{4,3,2,1,0:T(8,128)(2,1)} %bitcast.13) | data formatting | bytes 4718592 | tf_op jit(solution)/shard_map/reshape | solution.py:76
  90.0 2.7 %collective-permute-start.10 = (bf16[256,768]{1,0:T(8,128)(2,1)S(1)}, bf16[256,768]{1,0:T(8,128)(2,1)S(1)}, u32[]{:S(2)}, u32[]{:S(2)}) collective-permute-start(bf16[256,768]{1,0:T(8,128)(2,1)S(1)} %fusion.4), channel_id=1, source_target_pairs={{0,2},{2,0},{1,3},{3,1},{4,6},{6,4},{5,7},{7,5},{8,10},{10,8},{9,1... | collective-permute-start | bytes 1179656 | tf_op jit(solution)/shard_map/ppermute | solution.py:29
  92.7 1.3 collective-permute-done.10.refs_10_
  94.8 13.7 %shard_map.215 = (bf16[256,768]{1,0:T(8,128)(2,1)}, bf16[256,768]{1,0:T(8,128)(2,1)}, bf16[256,768]{1,0:T(8,128)(2,1)}, bf16[256,768]{1,0:T(8,128)(2,1)}, bf16[7...) custom-call(bf16[128,768]{1,0:T(8,128)(2,1)} %refs_0_.3, ...), custom_call_target="tpu_custom_call" | custom-call | flops 3623878656 | bytes 8000000 | tf_op jit(solution)/shard_map/pallas_call | solution.py:701
  109.0 1.6 collective-permute-done.11
  110.6 1.1 add_convert_fusion.2
  111.7 1.4 collective-permute-start.12
  113.1 7.0 %all-to-all-start.2 = ((bf16[16,48,1536]{2,1,0:T(8,128)(2,1)}), bf16[16,48,1536]{2,1,0:T(8,128)(2,1)}, u32[]{:S(2)}, u32[]{:S(2)}) async-start(bf16[16,48,1536]{2,1,0:T(8,128)(2,1)} %bitcast.46), calls=%async_computation.2 | async-start | bytes 4718592 | tf_op jit(solution)/shard_map/all_to_all | solution.py:64
  120.0 3.3 %collective-permute-done.12 = bf16[256,768]{1,0:T(8,128)(2,1)S(1)} collective-permute-done((bf16[256,768]{1,0:T(8,128)(2,1)S(1)}, bf16[256,768]{1,0:T(8,128)(2,1)S(1)}, u32[]{:S(2)}, u32[]{:S(2)}) %collective-permute-start.12) | collective-permute-done | bytes 393248 | tf_op jit(solution)/shard_map/ppermute | solution.py:48
  123.5 1.3 collective-permute-start.15
  126.2 1.4 collective-permute-start.16
  127.6 7.9 %collective-permute-done.13.refs_5_ = bf16[256,768]{1,0:T(8,128)(2,1)S(1)} collective-permute-done((bf16[256,768]{1,0:T(8,128)(2,1)S(1)}, bf16[256,768]{1,0:T(8,128)(2,1)S(1)}, u32[]{:S(2)}, u32[]{:S(2)}) %collective-permute-start.13) | collective-permute-done | bytes 393248 | tf_op jit(solution)/shard_map/ppermute | solution.py:42
  135.7 1.1 collective-permute-start.14
  136.8 1.2 collective-permute-done.16
  138.8 12.8 %shard_map.216 = (bf16[256,768]{1,0:T(8,128)(2,1)}, bf16[256,768]{1,0:T(8,128)(2,1)}, bf16[768,1664]{1,0:T(8,128)(2,1)}, f32[128,768]{1,0:T(8,128)}) custom-call(bf16[128,768]{1,0:T(8,128)(2,1)} %refs_0_.4, bf16[128,768]{1,0:T(8,128)(2,1)} %copy-done.9, bf16[128,768]{1,0:T(8,128)(2,1)} %copy-done.10, bf16[128,768]{1,0:T(8,128)(2,1)} %copy-done.11, ...), custom_call_target="tpu_custom_call" | custom-call | flops 2415919104 | bytes 8000000 | tf_op jit(solution)/shard_map/pallas_call | solution.py:701
  151.8 3.0 %all-to-all-done.2.got_ref = bf16[16,48,1536]{2,1,0:T(8,128)(2,1)} async-done(((bf16[16,48,1536]{2,1,0:T(8,128)(2,1)}), bf16[16,48,1536]{2,1,0:T(8,128)(2,1)}, u32[]{:S(2)}, u32[]{:S(2)}) %all-to-all-start.2) | async-done | bytes 2359328 | tf_op jit(solution)/shard_map/all_to_all | solution.py:64
  154.8 4.6 %all-to-all-start.3 = ((bf16[16,48,1664]{2,1,0:T(8,128)(2,1)}), bf16[16,48,1664]{2,1,0:T(8,128)(2,1)}, u32[]{:S(2)}, u32[]{:S(2)}) async-start(bf16[16,48,1664]{2,1,0:T(8,128)(2,1)} %bitcast.45), calls=%async_computation.3 | async-start | bytes 5111808 | tf_op jit(solution)/shard_map/all_to_all | solution.py:64
  159.4 1.9 collective-permute-start.20
  161.3 1.3 collective-permute-done.20
  163.1 11.3 %collective-permute-done.21 = bf16[256,768]{1,0:T(8,128)(2,1)S(1)} collective-permute-done((bf16[256,768]{1,0:T(8,128)(2,1)S(1)}, bf16[256,768]{1,0:T(8,128)(2,1)S(1)}, u32[]{:S(2)}, u32[]{:S(2)}) %collective-permute-start.21) | collective-permute-done | bytes 393248 | tf_op jit(solution)/shard_map/ppermute | solution.py:48
  174.8 2.6 %shard_map.217 = (bf16[24,1536]{1,0:T(8,128)(2,1)}, bf16[24,1536]{1,0:T(8,128)(2,1)}) custom-call(s32[1]{0:T(128)} %bitcast.1.place_ref, bf16[16,48,1536]{2,1,0:T(8,128)(2,1)} %all-to-all-done.2.got_ref), custom_call_target="tpu_custom_call" | custom-call | flops 150994944 | bytes 8000000 | tf_op jit(solution)/shard_map/pallas_call | solution.py:701
  177.5 2.7 %collective-permute-start.19 = (bf16[24,1536]{1,0:T(8,128)(2,1)}, bf16[24,1536]{1,0:T(8,128)(2,1)S(1)}, u32[]{:S(2)}, u32[]{:S(2)}) collective-permute-start(bf16[24,1536]{1,0:T(8,128)(2,1)} %get-tuple-element.127), channel_id=1, source_target_pairs={{0,18},{2,16},{4,22},{6,20},{8,26},{10,24},{12,30},{14,28},{16,2},... | collective-permute-start | bytes 221192 | tf_op jit(solution)/shard_map/ppermute | solution.py:54
  181.7 6.7 %collective-permute-done.19.rest_7_ = bf16[24,1536]{1,0:T(8,128)(2,1)S(1)} collective-permute-done((bf16[24,1536]{1,0:T(8,128)(2,1)}, bf16[24,1536]{1,0:T(8,128)(2,1)S(1)}, u32[]{:S(2)}, u32[]{:S(2)}) %collective-permute-start.19) | collective-permute-done | bytes 73760 | tf_op jit(solution)/shard_map/ppermute | solution.py:54
  188.5 5.9 %all-to-all-done.3.got_ref = bf16[16,48,1664]{2,1,0:T(8,128)(2,1)} async-done(((bf16[16,48,1664]{2,1,0:T(8,128)(2,1)}), bf16[16,48,1664]{2,1,0:T(8,128)(2,1)}, u32[]{:S(2)}, u32[]{:S(2)}) %all-to-all-start.3) | async-done | bytes 2555936 | tf_op jit(solution)/shard_map/all_to_all | solution.py:64
  194.4 2.8 %shard_map.218 = (bf16[24,1664]{1,0:T(8,128)(2,1)}, bf16[24,1664]{1,0:T(8,128)(2,1)}) custom-call(s32[1]{0:T(128)} %bitcast.1.place_ref, bf16[16,48,1664]{2,1,0:T(8,128)(2,1)} %all-to-all-done.3.got_ref), custom_call_target="tpu_custom_call" | custom-call | flops 1000 | bytes 8000000 | tf_op jit(solution)/shard_map/pallas_call | solution.py:701
  197.1 2.3 %collective-permute-start.25 = (bf16[24,1664]{1,0:T(8,128)(2,1)}, bf16[24,1664]{1,0:T(8,128)(2,1)S(1)}, u32[]{:S(2)}, u32[]{:S(2)}) collective-permute-start(bf16[24,1664]{1,0:T(8,128)(2,1)} %get-tuple-element.133), channel_id=1, source_target_pairs={{0,18},{2,16},{4,22},{6,20},{8,26},{10,24},{12,30},{14,28},{16,2},... | collective-permute-start | bytes 239624 | tf_op jit(solution)/shard_map/ppermute | solution.py:54
  199.4 2.1 collective-permute-start.24
  201.7 3.5 %collective-permute-done.24.rest_2_ = bf16[24,1664]{1,0:T(8,128)(2,1)S(1)} collective-permute-done((bf16[24,1664]{1,0:T(8,128)(2,1)}, bf16[24,1664]{1,0:T(8,128)(2,1)S(1)}, u32[]{:S(2)}, u32[]{:S(2)}) %collective-permute-start.24) | collective-permute-done | bytes 79904 | tf_op jit(solution)/shard_map/ppermute | solution.py:42
  205.9 2.7 %collective-permute-start.26 = (f32[24,128]{1,0:T(8,128)S(1)}, f32[24,128]{1,0:T(8,128)S(1)}, u32[]{:S(2)}, u32[]{:S(2)}) collective-permute-start(f32[24,128]{1,0:T(8,128)S(1)} %add_add_fusion.mine_ref), channel_id=1, source_target_pairs={{0,1},{1,0},{2,3},{3,2},{4,5},{5,4},{6,7},{7,6},{8,9},{9,8},{10,11... | collective-permute-start | bytes 36872 | tf_op jit(solution)/shard_map/ppermute | solution.py:33
  208.7 3.7 %shard_map.219 = (bf16[128,768]{1,0:T(8,128)(2,1)}, bf16[128,768]{1,0:T(8,128)(2,1)}, f32[2,24,1152]{2,1,0:T(8,128)}, f32[2,24,384]{2,1,0:T(8,128)}, f32[2,24,15...) custom-call(s32[1]{0:T(128)} %bitcast.core_ref, s32[1]{0:T(128)} %bitcast.1.place_ref, ...), custom_call_target="tpu_custom_call" | custom-call | flops 150994944 | bytes 8000000 | tf_op jit(solution)/shard_map/pallas_call | solution.py:701
  213.0 1.3 shard_map.220
  (131 shorter events, 15.2 us)
Async XLA Ops:
  3.7 9.6 %copy-start.24 = (bf16[128,768]{1,0:T(8,128)(2,1)S(1)}, bf16[128,768]{1,0:T(8,128)(2,1)}, u32[]{:S(2)}) copy-start(bf16[128,768]{1,0:T(8,128)(2,1)} %refs_0_.3) | copy-start | bytes 589828
  3.7 14.2 %copy-start.8 = (bf16[128,768]{1,0:T(8,128)(2,1)S(1)}, bf16[128,768]{1,0:T(8,128)(2,1)}, u32[]{:S(2)}) copy-start(bf16[128,768]{1,0:T(8,128)(2,1)} %refs_0_.4) | copy-start | bytes 589828
  3.7 14.5 %copy-start.28 = (bf16[24,1536]{1,0:T(8,128)(2,1)S(1)}, bf16[24,1536]{1,0:T(8,128)(2,1)}, u32[]{:S(2)}) copy-start(bf16[24,1536]{1,0:T(8,128)(2,1)} %get-tuple-element.82) | copy-start | bytes 221188
  3.7 14.5 %copy-start.29 = (s32[1,4]{1,0:T(1,128)S(1)}, s32[1,4]{1,0:T(1,128)}, u32[]{:S(2)}) copy-start(s32[1,4]{1,0:T(1,128)} %param.15) | copy-start | bytes 52
  3.7 14.7 %copy-start.30 = (s32[1,4]{1,0:T(1,128)S(1)}, s32[1,4]{1,0:T(1,128)}, u32[]{:S(2)}) copy-start(s32[1,4]{1,0:T(1,128)} %param.16) | copy-start | bytes 52
  3.7 41.4 %all-to-all-start = ((bf16[32,24,1664]{2,1,0:T(8,128)(2,1)}), bf16[32,24,1664]{2,1,0:T(8,128)(2,1)}, u32[]{:S(2)}, u32[]{:S(2)}) async-start(bf16[32,24,1664]{2,1,0:T(8,128)(2,1)} %get-tuple-element.91), calls=%async_computation | async-start | bytes 5111808 | tf_op jit(solution)/shard_map/all_to_all | solution.py:58
  13.2 26.8 %collective-permute-start.1 = (bf16[128,768]{1,0:T(8,128)(2,1)S(1)}, bf16[128,768]{1,0:T(8,128)(2,1)S(1)}, u32[]{:S(2)}, u32[]{:S(2)}) collective-permute-start(bf16[128,768]{1,0:T(8,128)(2,1)S(1)} %copy-done.24), channel_id=1, source_target_pairs={{0,2},{2,0},{1,3},{3,1},{4,6},{6,4},{5,7},{7,5},{8,10},{10,8},{9,1... | collective-permute-start | bytes 589832 | tf_op jit(solution)/shard_map/ppermute | solution.py:29
  14.3 8.8 %collective-permute-start.2 = (bf16[128,768]{1,0:T(8,128)(2,1)S(1)}, bf16[128,768]{1,0:T(8,128)(2,1)S(1)}, u32[]{:S(2)}, u32[]{:S(2)}) collective-permute-start(bf16[128,768]{1,0:T(8,128)(2,1)S(1)} %copy-done.24), channel_id=1, source_target_pairs={{0,17},{1,16},{4,21},{5,20},{8,25},{9,24},{12,29},{13,28},{16,1},{... | collective-permute-start | bytes 589832 | tf_op jit(solution)/shard_map/ppermute | solution.py:48
  17.8 22.2 %collective-permute-start.4 = (bf16[128,768]{1,0:T(8,128)(2,1)S(1)}, bf16[128,768]{1,0:T(8,128)(2,1)S(1)}, u32[]{:S(2)}, u32[]{:S(2)}) collective-permute-start(bf16[128,768]{1,0:T(8,128)(2,1)S(1)} %copy-done.8), channel_id=1, source_target_pairs={{0,2},{2,0},{1,3},{3,1},{4,6},{6,4},{5,7},{7,5},{8,10},{10,8},{9,1... | collective-permute-start | bytes 589832 | tf_op jit(solution)/shard_map/ppermute | solution.py:29
  18.2 9.1 %collective-permute-start.5 = (bf16[128,768]{1,0:T(8,128)(2,1)S(1)}, bf16[128,768]{1,0:T(8,128)(2,1)S(1)}, u32[]{:S(2)}, u32[]{:S(2)}) collective-permute-start(bf16[128,768]{1,0:T(8,128)(2,1)S(1)} %copy-done.8), channel_id=1, source_target_pairs={{0,17},{1,16},{4,21},{5,20},{8,25},{9,24},{12,29},{13,28},{16,1},{... | collective-permute-start | bytes 589832 | tf_op jit(solution)/shard_map/ppermute | solution.py:48
  18.2 21.8 %collective-permute-start = (bf16[24,1536]{1,0:T(8,128)(2,1)S(1)}, bf16[24,1536]{1,0:T(8,128)(2,1)S(1)}, u32[]{:S(2)}, u32[]{:S(2)}) collective-permute-start(bf16[24,1536]{1,0:T(8,128)(2,1)S(1)} %copy-done.28), channel_id=1, source_target_pairs={{0,16},{4,20},{8,24},{12,28},{16,0},{20,4},{24,8},{28,12},{32,48},... | collective-permute-start | bytes 221192 | tf_op jit(solution)/shard_map/ppermute | solution.py:42
  23.1 31.5 %copy-start.26 = (bf16[128,768]{1,0:T(8,128)(2,1)}, bf16[128,768]{1,0:T(8,128)(2,1)S(1)}, u32[]{:S(2)}) copy-start(bf16[128,768]{1,0:T(8,128)(2,1)S(1)} %collective-permute-done.2.refs_2_) | copy-start | bytes 589828
  23.1 16.9 %collective-permute-start.3 = (bf16[128,768]{1,0:T(8,128)(2,1)S(1)}, bf16[128,768]{1,0:T(8,128)(2,1)S(1)}, u32[]{:S(2)}, u32[]{:S(2)}) collective-permute-start(bf16[128,768]{1,0:T(8,128)(2,1)S(1)} %collective-permute-done.2.refs_2_), channel_id=1, source_target_pairs={{0,2},{2,0},{1,3},{3,1},{4,6},{6,4},{5,7},{7,5},{8,10},{10,8},{9,1... | collective-permute-start | bytes 589832 | tf_op jit(solution)/shard_map/ppermute | solution.py:29
  27.3 17.8 %copy-start.10 = (bf16[128,768]{1,0:T(8,128)(2,1)}, bf16[128,768]{1,0:T(8,128)(2,1)S(1)}, u32[]{:S(2)}) copy-start(bf16[128,768]{1,0:T(8,128)(2,1)S(1)} %collective-permute-done.5.refs_6_.refs_2_) | copy-start | bytes 589828
  27.3 12.7 %collective-permute-start.6 = (bf16[128,768]{1,0:T(8,128)(2,1)S(1)}, bf16[128,768]{1,0:T(8,128)(2,1)S(1)}, u32[]{:S(2)}, u32[]{:S(2)}) collective-permute-start(bf16[128,768]{1,0:T(8,128)(2,1)S(1)} %collective-permute-done.5.refs_6_.refs_2_), channel_id=1, source_target_pairs={{0,2},{2,0},{1,3},{3,1},{4,6},{6,4},{5,7},{7,5},{8,10},{10,8},{9,1... | collective-permute-start | bytes 589832 | tf_op jit(solution)/shard_map/ppermute | solution.py:29
  45.1 41.4 %all-to-all-start.1 = ((bf16[16,48,1536]{2,1,0:T(8,128)(2,1)}), bf16[16,48,1536]{2,1,0:T(8,128)(2,1)}, u32[]{:S(2)}, u32[]{:S(2)}) async-start(bf16[16,48,1536]{2,1,0:T(8,128)(2,1)} %shard_map.214), calls=%async_computation.1 | async-start | bytes 4718592 | tf_op jit(solution)/shard_map/all_to_all | solution.py:64
  62.8 2.9 %collective-permute-start.7 = (bf16[256,768]{1,0:T(8,128)(2,1)}, bf16[256,768]{1,0:T(8,128)(2,1)S(1)}, u32[]{:S(2)}, u32[]{:S(2)}) collective-permute-start(bf16[256,768]{1,0:T(8,128)(2,1)} %get-tuple-element.93), channel_id=1, source_target_pairs={{0,2},{2,0},{1,3},{3,1},{4,6},{6,4},{5,7},{7,5},{8,10},{10,8},{9,1... | collective-permute-start | bytes 1179656 | tf_op jit(solution)/shard_map/ppermute | solution.py:29
  66.8 12.7 %collective-permute-start.8 = (bf16[256,768]{1,0:T(8,128)(2,1)S(1)}, bf16[256,768]{1,0:T(8,128)(2,1)S(1)}, u32[]{:S(2)}, u32[]{:S(2)}) collective-permute-start(bf16[256,768]{1,0:T(8,128)(2,1)S(1)} %add_convert_fusion.3), channel_id=1, source_target_pairs={{0,17},{1,16},{4,21},{5,20},{8,25},{9,24},{12,29},{13,28},{16,1},{... | collective-permute-start | bytes 1179656 | tf_op jit(solution)/shard_map/ppermute | solution.py:48
  79.6 10.3 %copy-start.2 = (bf16[256,768]{1,0:T(8,128)(2,1)}, bf16[256,768]{1,0:T(8,128)(2,1)S(1)}, u32[]{:S(2)}) copy-start(bf16[256,768]{1,0:T(8,128)(2,1)S(1)} %fusion.5.refs_8_) | copy-start | bytes 1179652
  79.6 10.2 %collective-permute-start.9 = (bf16[256,768]{1,0:T(8,128)(2,1)S(1)}, bf16[256,768]{1,0:T(8,128)(2,1)S(1)}, u32[]{:S(2)}, u32[]{:S(2)}) collective-permute-start(bf16[256,768]{1,0:T(8,128)(2,1)S(1)} %fusion.5.refs_8_), channel_id=1, source_target_pairs={{0,16},{4,20},{8,24},{12,28},{16,0},{20,4},{24,8},{28,12},{32,48},... | collective-permute-start | bytes 1179656 | tf_op jit(solution)/shard_map/ppermute | solution.py:42
  90.0 4.0 %collective-permute-start.10 = (bf16[256,768]{1,0:T(8,128)(2,1)S(1)}, bf16[256,768]{1,0:T(8,128)(2,1)S(1)}, u32[]{:S(2)}, u32[]{:S(2)}) collective-permute-start(bf16[256,768]{1,0:T(8,128)(2,1)S(1)} %fusion.4), channel_id=1, source_target_pairs={{0,2},{2,0},{1,3},{3,1},{4,6},{6,4},{5,7},{7,5},{8,10},{10,8},{9,1... | collective-permute-start | bytes 1179656 | tf_op jit(solution)/shard_map/ppermute | solution.py:29
  108.6 2.0 collective-permute-start.11
  111.7 11.6 %collective-permute-start.12 = (bf16[256,768]{1,0:T(8,128)(2,1)S(1)}, bf16[256,768]{1,0:T(8,128)(2,1)S(1)}, u32[]{:S(2)}, u32[]{:S(2)}) collective-permute-start(bf16[256,768]{1,0:T(8,128)(2,1)S(1)} %add_convert_fusion.2), channel_id=1, source_target_pairs={{0,17},{1,16},{4,21},{5,20},{8,25},{9,24},{12,29},{13,28},{16,1},{... | collective-permute-start | bytes 1179656 | tf_op jit(solution)/shard_map/ppermute | solution.py:48
  113.1 10.4 %copy-start.21 = (bf16[256,768]{1,0:T(8,128)(2,1)S(1)}, bf16[256,768]{1,0:T(8,128)(2,1)}, u32[]{:S(2)}) copy-start(bf16[256,768]{1,0:T(8,128)(2,1)} %get-tuple-element.123) | copy-start | bytes 1179652
  113.1 13.0 %copy-start.6 = (bf16[256,768]{1,0:T(8,128)(2,1)S(1)}, bf16[256,768]{1,0:T(8,128)(2,1)}, u32[]{:S(2)}) copy-start(bf16[256,768]{1,0:T(8,128)(2,1)} %get-tuple-element.122) | copy-start | bytes 1179652
  113.1 41.7 %all-to-all-start.2 = ((bf16[16,48,1536]{2,1,0:T(8,128)(2,1)}), bf16[16,48,1536]{2,1,0:T(8,128)(2,1)}, u32[]{:S(2)}, u32[]{:S(2)}) async-start(bf16[16,48,1536]{2,1,0:T(8,128)(2,1)} %bitcast.46), calls=%async_computation.2 | async-start | bytes 4718592 | tf_op jit(solution)/shard_map/all_to_all | solution.py:64
  123.5 14.7 %copy-start = (bf16[256,768]{1,0:T(8,128)(2,1)}, bf16[256,768]{1,0:T(8,128)(2,1)S(1)}, u32[]{:S(2)}) copy-start(bf16[256,768]{1,0:T(8,128)(2,1)S(1)} %fusion.3.refs_4_) | copy-start | bytes 1179652
  123.5 2.6 %collective-permute-start.15 = (bf16[256,768]{1,0:T(8,128)(2,1)S(1)}, bf16[256,768]{1,0:T(8,128)(2,1)S(1)}, u32[]{:S(2)}, u32[]{:S(2)}) collective-permute-start(bf16[256,768]{1,0:T(8,128)(2,1)S(1)} %copy-done.21), channel_id=1, source_target_pairs={{0,2},{2,0},{1,3},{3,1},{4,6},{6,4},{5,7},{7,5},{8,10},{10,8},{9,1... | collective-permute-start | bytes 1179656 | tf_op jit(solution)/shard_map/ppermute | solution.py:29
  124.8 10.8 %collective-permute-start.13 = (bf16[256,768]{1,0:T(8,128)(2,1)S(1)}, bf16[256,768]{1,0:T(8,128)(2,1)S(1)}, u32[]{:S(2)}, u32[]{:S(2)}) collective-permute-start(bf16[256,768]{1,0:T(8,128)(2,1)S(1)} %fusion.3.refs_4_), channel_id=1, source_target_pairs={{0,16},{4,20},{8,24},{12,28},{16,0},{20,4},{24,8},{28,12},{32,48},... | collective-permute-start | bytes 1179656 | tf_op jit(solution)/shard_map/ppermute | solution.py:42
  126.2 11.7 %collective-permute-start.16 = (bf16[256,768]{1,0:T(8,128)(2,1)S(1)}, bf16[256,768]{1,0:T(8,128)(2,1)S(1)}, u32[]{:S(2)}, u32[]{:S(2)}) collective-permute-start(bf16[256,768]{1,0:T(8,128)(2,1)S(1)} %add_convert_fusion.1), channel_id=1, source_target_pairs={{0,17},{1,16},{4,21},{5,20},{8,25},{9,24},{12,29},{13,28},{16,1},{... | collective-permute-start | bytes 1179656 | tf_op jit(solution)/shard_map/ppermute | solution.py:48
  135.7 2.4 %collective-permute-start.14 = (bf16[256,768]{1,0:T(8,128)(2,1)S(1)}, bf16[256,768]{1,0:T(8,128)(2,1)S(1)}, u32[]{:S(2)}, u32[]{:S(2)}) collective-permute-start(bf16[256,768]{1,0:T(8,128)(2,1)S(1)} %fusion.2), channel_id=1, source_target_pairs={{0,2},{2,0},{1,3},{3,1},{4,6},{6,4},{5,7},{7,5},{8,10},{10,8},{9,1... | collective-permute-start | bytes 1179656 | tf_op jit(solution)/shard_map/ppermute | solution.py:29
  154.8 7.9 %copy-start.7 = (bf16[256,768]{1,0:T(8,128)(2,1)S(1)}, bf16[256,768]{1,0:T(8,128)(2,1)}, u32[]{:S(2)}) copy-start(bf16[256,768]{1,0:T(8,128)(2,1)} %get-tuple-element.129) | copy-start | bytes 1179652
  154.8 39.6 %all-to-all-start.3 = ((bf16[16,48,1664]{2,1,0:T(8,128)(2,1)}), bf16[16,48,1664]{2,1,0:T(8,128)(2,1)}, u32[]{:S(2)}, u32[]{:S(2)}) async-start(bf16[16,48,1664]{2,1,0:T(8,128)(2,1)} %bitcast.45), calls=%async_computation.3 | async-start | bytes 5111808 | tf_op jit(solution)/shard_map/all_to_all | solution.py:64
  159.4 3.2 %collective-permute-start.20 = (bf16[256,768]{1,0:T(8,128)(2,1)S(1)}, bf16[256,768]{1,0:T(8,128)(2,1)S(1)}, u32[]{:S(2)}, u32[]{:S(2)}) collective-permute-start(bf16[256,768]{1,0:T(8,128)(2,1)S(1)} %copy-done.22), channel_id=1, source_target_pairs={{0,2},{2,0},{1,3},{3,1},{4,6},{6,4},{5,7},{7,5},{8,10},{10,8},{9,1... | collective-permute-start | bytes 1179656 | tf_op jit(solution)/shard_map/ppermute | solution.py:29
  162.7 11.7 %collective-permute-start.21 = (bf16[256,768]{1,0:T(8,128)(2,1)S(1)}, bf16[256,768]{1,0:T(8,128)(2,1)S(1)}, u32[]{:S(2)}, u32[]{:S(2)}) collective-permute-start(bf16[256,768]{1,0:T(8,128)(2,1)S(1)} %add_convert_fusion), channel_id=1, source_target_pairs={{0,17},{1,16},{4,21},{5,20},{8,25},{9,24},{12,29},{13,28},{16,1},{... | collective-permute-start | bytes 1179656 | tf_op jit(solution)/shard_map/ppermute | solution.py:48
  174.7 13.7 %collective-permute-start.22 = (bf16[256,768]{1,0:T(8,128)(2,1)S(1)}, bf16[256,768]{1,0:T(8,128)(2,1)S(1)}, u32[]{:S(2)}, u32[]{:S(2)}) collective-permute-start(bf16[256,768]{1,0:T(8,128)(2,1)S(1)} %pad_maximum_fusion.2), channel_id=1, source_target_pairs={{0,16},{4,20},{8,24},{12,28},{16,0},{20,4},{24,8},{28,12},{32,48},... | collective-permute-start | bytes 1179656 | tf_op jit(solution)/shard_map/ppermute | solution.py:42
  177.5 11.0 %collective-permute-start.19 = (bf16[24,1536]{1,0:T(8,128)(2,1)}, bf16[24,1536]{1,0:T(8,128)(2,1)S(1)}, u32[]{:S(2)}, u32[]{:S(2)}) collective-permute-start(bf16[24,1536]{1,0:T(8,128)(2,1)} %get-tuple-element.127), channel_id=1, source_target_pairs={{0,18},{2,16},{4,22},{6,20},{8,26},{10,24},{12,30},{14,28},{16,2},... | collective-permute-start | bytes 221192 | tf_op jit(solution)/shard_map/ppermute | solution.py:54
  180.2 8.2 %collective-permute-start.18 = (bf16[24,1536]{1,0:T(8,128)(2,1)}, bf16[24,1536]{1,0:T(8,128)(2,1)S(1)}, u32[]{:S(2)}, u32[]{:S(2)}) collective-permute-start(bf16[24,1536]{1,0:T(8,128)(2,1)} %get-tuple-element.127), channel_id=1, source_target_pairs={{0,16},{4,20},{8,24},{12,28},{16,0},{20,4},{24,8},{28,12},{32,48},... | collective-permute-start | bytes 221192 | tf_op jit(solution)/shard_map/ppermute | solution.py:42
  180.2 1.5 collective-permute-start.17
  181.7 26.9 %copy-start.18 = (bf16[24,1536]{1,0:T(8,128)(2,1)}, bf16[24,1536]{1,0:T(8,128)(2,1)S(1)}, u32[]{:S(2)}) copy-start(bf16[24,1536]{1,0:T(8,128)(2,1)S(1)} %collective-permute-done.17.rest_5_) | copy-start | bytes 221188
  188.4 20.2 %copy-start.16 = (bf16[24,1536]{1,0:T(8,128)(2,1)}, bf16[24,1536]{1,0:T(8,128)(2,1)S(1)}, u32[]{:S(2)}) copy-start(bf16[24,1536]{1,0:T(8,128)(2,1)S(1)} %collective-permute-done.19.rest_7_) | copy-start | bytes 221188
  188.4 20.2 %copy-start.17 = (bf16[24,1536]{1,0:T(8,128)(2,1)}, bf16[24,1536]{1,0:T(8,128)(2,1)S(1)}, u32[]{:S(2)}) copy-start(bf16[24,1536]{1,0:T(8,128)(2,1)S(1)} %collective-permute-done.18.rest_6_) | copy-start | bytes 221188
  188.4 20.2 %copy-start.4 = (bf16[256,768]{1,0:T(8,128)(2,1)}, bf16[256,768]{1,0:T(8,128)(2,1)S(1)}, u32[]{:S(2)}) copy-start(bf16[256,768]{1,0:T(8,128)(2,1)S(1)} %collective-permute-done.22.rest_9_) | copy-start | bytes 1179652
  197.1 4.6 %collective-permute-start.25 = (bf16[24,1664]{1,0:T(8,128)(2,1)}, bf16[24,1664]{1,0:T(8,128)(2,1)S(1)}, u32[]{:S(2)}, u32[]{:S(2)}) collective-permute-start(bf16[24,1664]{1,0:T(8,128)(2,1)} %get-tuple-element.133), channel_id=1, source_target_pairs={{0,18},{2,16},{4,22},{6,20},{8,26},{10,24},{12,30},{14,28},{16,2},... | collective-permute-start | bytes 239624 | tf_op jit(solution)/shard_map/ppermute | solution.py:54
  199.4 5.8 %collective-permute-start.24 = (bf16[24,1664]{1,0:T(8,128)(2,1)}, bf16[24,1664]{1,0:T(8,128)(2,1)S(1)}, u32[]{:S(2)}, u32[]{:S(2)}) collective-permute-start(bf16[24,1664]{1,0:T(8,128)(2,1)} %get-tuple-element.133), channel_id=1, source_target_pairs={{0,16},{4,20},{8,24},{12,28},{16,0},{20,4},{24,8},{28,12},{32,48},... | collective-permute-start | bytes 239624 | tf_op jit(solution)/shard_map/ppermute | solution.py:42
  201.5 3.7 %collective-permute-start.23 = (bf16[24,1664]{1,0:T(8,128)(2,1)}, bf16[24,1664]{1,0:T(8,128)(2,1)S(1)}, u32[]{:S(2)}, u32[]{:S(2)}) collective-permute-start(bf16[24,1664]{1,0:T(8,128)(2,1)} %get-tuple-element.132.rest_0_), channel_id=1, source_target_pairs={{0,2},{2,0},{1,3},{3,1},{4,6},{6,4},{5,7},{7,5},{8,10},{10,8},{9,1... | collective-permute-start | bytes 239624 | tf_op jit(solution)/shard_map/ppermute | solution.py:29
  201.7 6.9 %copy-start.12 = (bf16[24,1664]{1,0:T(8,128)(2,1)}, bf16[24,1664]{1,0:T(8,128)(2,1)S(1)}, u32[]{:S(2)}) copy-start(bf16[24,1664]{1,0:T(8,128)(2,1)S(1)} %collective-permute-done.25.rest_3_) | copy-start | bytes 239620
  205.9 6.5 %collective-permute-start.26 = (f32[24,128]{1,0:T(8,128)S(1)}, f32[24,128]{1,0:T(8,128)S(1)}, u32[]{:S(2)}, u32[]{:S(2)}) collective-permute-start(f32[24,128]{1,0:T(8,128)S(1)} %add_add_fusion.mine_ref), channel_id=1, source_target_pairs={{0,1},{1,0},{2,3},{3,2},{4,5},{5,4},{6,7},{7,6},{8,9},{9,8},{10,11... | collective-permute-start | bytes 36872 | tf_op jit(solution)/shard_map/ppermute | solution.py:33
  (14 other events, 43.0 us)
